TPU v7x, 512 devices: a whole 4x4x16 slice. The times are simulated.
512 devices in a mesh: sect: 8 (over z_hi, core), blk: 64 (over x, y, z_lo).
Axes of the slice: x: 4, y: 4, z: 16 (z_hi: 4, z_lo: 4; z = z_hi * 4 + z_lo), core: 2. Of those that a mesh axis runs over, the one named last changes fastest.
Arguments:
- gas_field: float32 [5, 128, 32, 8192], P(None, 'sect', None, 'blk'), may hold values from -6 to 6
- diffusion: float32 [128, 32, 8192], P('sect', None, 'blk'), may hold values from 0.02 to 0.16
- reaction: float32 [5, 5], replicated, may hold values from -2.5 to 2.5
- particles: float32 [16, 1048576], P(None, ('sect', 'blk')), may hold values from -6 to 6
- mixing: float32 [16, 16], replicated, may hold values from -1.5 to 1.5
- heating: float32 [16], replicated, may hold values from -3 to 3
- wall_cell: int32 [1048576], P(('sect', 'blk')), may hold values from 0 to 2047
- tile_hop: int32 [1048576, 1], P(('sect', 'blk')), may hold values from 0 to 4; in each aligned block of 2048 rows (0 to 2047, 2048 to 4095, ...) at most 1024 rows name the same one
Outputs:
- gas_next: float32 [5, 128, 32, 8192], P(None, 'sect', None, 'blk')
- arrived: float32 [16, 2621440], P(None, ('sect', 'blk'))
Inputs may be any that keep to these rules, and one draw needn't show every extreme that they name: `tile_hop`: among the 2048 particles of one device, at most 1024 have the same move, and in some devices exactly 1024 do.
All inputs are finite; a program needn't handle non-finite values.
Results may differ from a plain program's by a relative error of at most 0.0001.
Values sent between devices are 32-bit elements; how exact they have to be, the bound alone decides.
No kernel may reach another device: no remote copies, remote signals or barrier semaphores. Data moves between devices by JAX's collectives and lax.ppermute only.
A program may use at most 64 MiB of HBM per device.

v0:
```python
import jax
import jax.numpy as jnp
from jax import lax
from jax.sharding import PartitionSpec as P

REACH = 2
ITERS = 3


DIFFUSE = (1.0, 0.8, 0.6, 0.9, 0.7)


def extended(x, sides, width, wrap):
    for axis, dim in sides:
        size, length = (lax.axis_size(axis), x.shape[dim])
        up = [(i, (i + 1) % size) for i in range(size if wrap else size - 1)]
        down = [(j, i) for i, j in up]
        last = lax.slice_in_dim(x, length - width, length, axis=dim)
        first = lax.slice_in_dim(x, 0, width, axis=dim)
        before = lax.ppermute(last, axis, up)
        after = lax.ppermute(first, axis, down)
        x = jnp.concatenate([before, x, after], axis=dim)
    return x


def passed_along(x, axis, by):
    size = lax.axis_size(axis)
    pairs = [(i, i + by) for i in range(size) if 0 <= i + by < size]
    return lax.ppermute(x, axis, pairs)


def passed_along_2(x, axis, by):
    size = lax.axis_size(axis)
    return lax.ppermute(x, axis, [(i, (i + by) % size) for i in range(size)])


def advance(field, kappa, reaction, axial_pad, loop_pad):
    radial_pad = jnp.concatenate([field[:, :, :1], field, field[:, :, -1:]], axis=2)
    laplace = axial_pad[:, 2:] + axial_pad[:, :-2]
    laplace = laplace + radial_pad[:, :, 2:] + radial_pad[:, :, :-2]
    laplace = laplace + loop_pad[..., 2:] + loop_pad[..., :-2] - 6.0 * field
    rates = jnp.asarray(DIFFUSE, jnp.float32)[:, None, None, None]
    coupled = jnp.tensordot(reaction, field, axes=(1, 0), precision=lax.Precision.HIGHEST)
    return field + rates * kappa[None] * laplace + 0.3 * coupled


def local(gas_field, diffusion, reaction, particles, mixing, heating, wall_cell, tile_hop):
    field = gas_field
    for sweep in range(ITERS):
        loop_pad = extended(field, (("blk", 3),), 1, True)
        axial_pad = extended(field, (("sect", 1),), 1, False)
        field = advance(field, diffusion, reaction, axial_pad, loop_pad)
    wall_rows = field[0, :, field.shape[2] - 1, :]
    earlier = passed_along(wall_rows, "sect", 1)
    flux = (0.5 * (wall_rows + earlier)).reshape(-1)
    look = jnp.take(flux, wall_cell, axis=0)
    heated = particles + 0.5 * jnp.dot(mixing, particles, precision=lax.Precision.HIGHEST)
    heated = heated + heating[:, None] * (look - particles[0])[None, :]
    count = particles.shape[1]
    capacity = count // 2
    spread = 2 * REACH + 1
    moves = tile_hop[:, 0]
    one_hot = (moves[None, :] == lax.broadcasted_iota(jnp.int32, (spread, count), 0)).astype(
        jnp.int32
    )
    ranks = jnp.cumsum(one_hot, axis=1) - 1
    rank_each = jnp.sum(ranks * one_hot, axis=0)
    position = moves * capacity + rank_each
    packed = (
        jnp.zeros((particles.shape[0], spread * capacity), jnp.float32).at[:, position].set(heated)
    )
    blocks = [packed[:, j * capacity : (j + 1) * capacity] for j in range(spread)]
    pieces = list(blocks)
    for offset_index in range(spread):
        if offset_index != REACH:
            pieces[offset_index] = passed_along_2(blocks[offset_index], "blk", offset_index - REACH)
    arrived = jnp.concatenate(pieces, axis=1)
    return (field, arrived)


def solution(mesh):
    in_specs = (
        P(None, "sect", None, "blk"),
        P("sect", None, "blk"),
        P(),
        P(None, ("sect", "blk")),
        P(),
        P(),
        P(("sect", "blk")),
        P(("sect", "blk"), None),
    )
    out_specs = (P(None, "sect", None, "blk"), P(None, ("sect", "blk")))
    return jax.shard_map(local, mesh=mesh, in_specs=in_specs, out_specs=out_specs, check_vma=False)
```

profile of v0, /device:TPU:1, one launch (start us, length us, event | category | flops | bytes accessed | tf_op | source)
XLA Modules:
  0.0 225.3 jit_solution(2019234591093803621)
XLA Ops:
  0.7 2.3 %copy.64 = f32[5,16,32,128]{3,0,2,1:T(8,128)S(1)} copy(f32[5,16,32,128]{3,2,1,0:T(8,128)} %param.11) | data formatting | bytes 2621440 | tf_op args[0]
  3.0 8.8 %collective-permute-start = (f32[5,1,32,128]{3,0,2,1:T(8,128)S(1)}, f32[5,1,32,128]{3,0,2,1:T(8,128)S(1)}, u32[]{:S(2)}, u32[]{:S(2)}) collective-permute-start(f32[5,1,32,128]{3,0,2,1:T(8,128)S(1)} %get-tuple-element.25), channel_id=1, source_target_pairs={{64,0},{128,64},{192,128},{256,192},{320,256},{384,320},{448,384},... | collective-permute-start | bytes 245768 | tf_op jit(solution)/shard_map/ppermute | solution.py:21
  11.8 3.3 %collective-permute-start.1 = (f32[5,1,32,128]{3,0,2,1:T(8,128)S(1)}, f32[5,1,32,128]{3,0,2,1:T(8,128)S(1)}, u32[]{:S(2)}, u32[]{:S(2)}) collective-permute-start(f32[5,1,32,128]{3,0,2,1:T(8,128)S(1)} %get-tuple-element.26), channel_id=1, source_target_pairs={{0,64},{64,128},{128,192},{192,256},{256,320},{320,384},{384,448},... | collective-permute-start | bytes 245768 | tf_op jit(solution)/shard_map/ppermute | solution.py:20
  16.2 10.9 %collective-permute-start.2 = (f32[5,16,32,1]{2,1,3,0:T(8,128)S(1)}, f32[5,16,32,1]{2,1,3,0:T(8,128)S(1)}, u32[]{:S(2)}, u32[]{:S(2)}) collective-permute-start(f32[5,16,32,1]{2,1,3,0:T(8,128)S(1)} %copy.82), channel_id=1, source_target_pairs={{1,0},{2,1},{3,2},{4,3},{5,4},{6,5},{7,6},{8,7},{9,8},{10,9},{11,1... | collective-permute-start | bytes 30728 | tf_op jit(solution)/shard_map/ppermute | solution.py:21
  27.6 1.9 collective-permute-start.3
  29.6 1.4 reduce-window.6
  31.5 0.9 fusion.42
  32.5 2.1 copy.59
  34.6 3.8 %collective-permute-done.3 = f32[5,16,32,1]{2,1,3,0:T(8,128)S(1)} collective-permute-done((f32[5,16,32,1]{2,1,3,0:T(8,128)S(1)}, f32[5,16,32,1]{2,1,3,0:T(8,128)S(1)}, u32[]{:S(2)}, u32[]{:S(2)}) %collective-permute-start.3) | collective-permute-done | bytes 10272 | tf_op jit(solution)/shard_map/ppermute | solution.py:20
  38.4 2.0 copy.61
  40.4 11.0 %fusion.4 = f32[5,16,32,128]{3,0,2,1:T(8,128)S(1)} fusion(f32[5,16,32,128]{3,0,2,1:T(8,128)} %copy-done.3, f32[5,16,32,1]{3,0,2,1:T(8,128)} %copy.61, f32[5,16,32,1]{3,0,2,1:T(8,128)} %copy.59, f32[5,16,1,128]{3,0,2,1:T(8,128)S(1)} %get-tuple-element.28, f32[5,16,1,128]{3,0,2,1:T(8,128)S(1)} %get-tuple-element.27, ...), kind=kOutput, calls=%fused_computation.10 | convolution fusion | flops 25559040 | bytes 3149944 | tf_op jit(solution)/shard_map/dot_general | solution.py:43
  51.4 2.8 %fusion.40 = (f32[5,16,32,1]{3,0,2,1:T(8,128)}, f32[5,16,32,1]{3,0,2,1:T(8,128)}) fusion(f32[5,16,32,128]{3,0,2,1:T(8,128)S(1)} %fusion.4), kind=kLoop, calls=%fused_computation.77 | loop fusion | bytes 40960 | tf_op jit(solution)/shard_map/slice | solution.py:19
  54.3 2.1 copy.66
  56.4 5.6 %collective-permute-start.6 = (f32[5,16,32,1]{2,1,3,0:T(8,128)S(1)}, f32[5,16,32,1]{2,1,3,0:T(8,128)S(1)}, u32[]{:S(2)}, u32[]{:S(2)}) collective-permute-start(f32[5,16,32,1]{2,1,3,0:T(8,128)S(1)} %copy.66), channel_id=1, source_target_pairs={{1,0},{2,1},{3,2},{4,3},{5,4},{6,5},{7,6},{8,7},{9,8},{10,9},{11,1... | collective-permute-start | bytes 30728 | tf_op jit(solution)/shard_map/ppermute | solution.py:21
  62.0 2.1 copy.68
  64.1 1.9 collective-permute-start.7
  66.0 1.9 collective-permute-start.4
  67.9 7.7 %collective-permute-start.5 = (f32[5,1,32,128]{3,0,2,1:T(8,128)S(1)}, f32[5,1,32,128]{3,0,2,1:T(8,128)S(1)}, u32[]{:S(2)}, u32[]{:S(2)}) collective-permute-start(f32[5,1,32,128]{3,0,2,1:T(8,128)S(1)} %get-tuple-element.20), channel_id=1, source_target_pairs={{0,64},{64,128},{128,192},{192,256},{256,320},{320,384},{384,448},... | collective-permute-start | bytes 245768 | tf_op jit(solution)/shard_map/ppermute | solution.py:20
  75.7 2.1 copy.67
  77.8 2.0 copy.69
  79.9 11.0 %fusion.6 = f32[5,16,32,128]{3,0,2,1:T(8,128)S(1)} fusion(f32[5,16,32,128]{3,0,2,1:T(8,128)} %copy-done.2, f32[5,16,32,1]{3,0,2,1:T(8,128)} %copy.69, f32[5,16,32,1]{3,0,2,1:T(8,128)} %copy.67, f32[5,16,1,128]{3,0,2,1:T(8,128)S(1)} %get-tuple-element.22, f32[5,16,1,128]{3,0,2,1:T(8,128)S(1)} %get-tuple-element.21, ...), kind=kOutput, calls=%fused_computation.12 | convolution fusion | flops 25559040 | bytes 3149944 | tf_op jit(solution)/shard_map/dot_general | solution.py:43
  90.9 2.7 %fusion.37 = (f32[5,16,32,1]{3,0,2,1:T(8,128)}, f32[5,16,32,1]{3,0,2,1:T(8,128)}) fusion(f32[5,16,32,128]{3,0,2,1:T(8,128)S(1)} %fusion.6), kind=kLoop, calls=%fused_computation.74 | loop fusion | bytes 40960 | tf_op jit(solution)/shard_map/slice | solution.py:19
  93.6 2.1 copy.70
  95.8 9.4 %collective-permute-start.10 = (f32[5,16,32,1]{2,1,3,0:T(8,128)S(1)}, f32[5,16,32,1]{2,1,3,0:T(8,128)S(1)}, u32[]{:S(2)}, u32[]{:S(2)}) collective-permute-start(f32[5,16,32,1]{2,1,3,0:T(8,128)S(1)} %copy.70), channel_id=1, source_target_pairs={{1,0},{2,1},{3,2},{4,3},{5,4},{6,5},{7,6},{8,7},{9,8},{10,9},{11,1... | collective-permute-start | bytes 30728 | tf_op jit(solution)/shard_map/ppermute | solution.py:21
  105.1 2.1 copy.72
  107.3 1.9 collective-permute-start.11
  109.2 1.9 collective-permute-start.8
  111.1 7.5 %collective-permute-start.9 = (f32[5,1,32,128]{3,0,2,1:T(8,128)S(1)}, f32[5,1,32,128]{3,0,2,1:T(8,128)S(1)}, u32[]{:S(2)}, u32[]{:S(2)}) collective-permute-start(f32[5,1,32,128]{3,0,2,1:T(8,128)S(1)} %get-tuple-element.14), channel_id=1, source_target_pairs={{0,64},{64,128},{128,192},{192,256},{256,320},{320,384},{384,448},... | collective-permute-start | bytes 245768 | tf_op jit(solution)/shard_map/ppermute | solution.py:20
  118.7 2.0 copy.71
  120.7 2.1 copy.73
  122.8 5.8 %fusion.8 = f32[5,16,32,128]{3,0,2,1:T(8,128)S(1)} fusion(f32[5,16,32,128]{3,0,2,1:T(8,128)S(1)} %fusion.6, f32[5,16,32,1]{3,0,2,1:T(8,128)} %copy.73, f32[5,16,32,1]{3,0,2,1:T(8,128)} %copy.71, f32[5,16,1,128]{3,0,2,1:T(8,128)S(1)} %get-tuple-element.16, f32[5,16,1,128]{3,0,2,1:T(8,128)S(1)} %get-tuple-element.15, ...), kind=kOutput, calls=%fused_computation.14 | convolution fusion | flops 25559040 | bytes 3149944 | tf_op jit(solution)/shard_map/dot_general | solution.py:43
  128.7 6.0 %collective-permute-start.12 = (f32[16,128]{1,0:T(8,128)S(1)}, f32[16,128]{1,0:T(8,128)S(1)}, u32[]{:S(2)}, u32[]{:S(2)}) collective-permute-start(f32[16,128]{1,0:T(8,128)S(1)} %bitcast.34), channel_id=1, source_target_pairs={{0,64},{64,128},{128,192},{192,256},{256,320},{320,384},{384,448},... | collective-permute-start | bytes 24584 | tf_op jit(solution)/shard_map/ppermute | solution.py:29
  134.7 0.7 collective-permute-done.12
  135.5 11.8 %gather_fusion = f32[2048]{0:T(1024)S(1)} fusion(f32[2048]{0:T(1024)S(1)} %multiply_bitcast_fusion, s32[2048]{0:T(1024)S(1)} %fusion.30), kind=kCustom, calls=%fused_computation | custom fusion | bytes 24576 | tf_op jit(solution)/shard_map/jit(_take)/gather | solution.py:56
  147.6 1.3 copy.74
  148.9 6.6 %scatter_custom_fusion = f32[16,5120]{0,1:T(8,128)S(1)} fusion(s32[2048]{0:T(1024)S(1)} %bitcast.37, f32[2048,16]{1,0:T(8,128)} %copy.74, f32[]{:T(128)} %constant.14.clone.1), kind=kCustom, calls=%fused_computation.51 | custom fusion | bytes 328192 | tf_op jit(solution)/shard_map/scatter | solution.py:70
  155.5 1.4 fusion.34
  156.9 2.3 %collective-permute-start.13 = (f32[16,1024]{0,1:T(8,128)}, f32[16,1024]{0,1:T(8,128)}, u32[]{:S(2)}, u32[]{:S(2)}) collective-permute-start(f32[16,1024]{0,1:T(8,128)} %get-tuple-element.12), channel_id=1, source_target_pairs={{0,62},{1,63},{2,0},{3,1},{4,2},{5,3},{6,4},{7,5},{8,6},{9,7},{10,... | collective-permute-start | bytes 196616 | tf_op jit(solution)/shard_map/ppermute | solution.py:34
  159.2 1.3 copy.80
  160.5 9.1 %collective-permute-start.14 = (f32[16,1024]{0,1:T(8,128)}, f32[16,1024]{0,1:T(8,128)S(1)}, u32[]{:S(2)}, u32[]{:S(2)}) collective-permute-start(f32[16,1024]{0,1:T(8,128)} %get-tuple-element.11), channel_id=1, source_target_pairs={{0,63},{1,0},{2,1},{3,2},{4,3},{5,4},{6,5},{7,6},{8,7},{9,8},{10,9... | collective-permute-start | bytes 196616 | tf_op jit(solution)/shard_map/ppermute | solution.py:34
  169.8 2.2 collective-permute-start.15
  172.0 3.1 %collective-permute-start.16 = (f32[16,1024]{0,1:T(8,128)S(1)}, f32[16,1024]{0,1:T(8,128)S(1)}, u32[]{:S(2)}, u32[]{:S(2)}) collective-permute-start(f32[16,1024]{0,1:T(8,128)S(1)} %copy-done.6), channel_id=1, source_target_pairs={{0,2},{1,3},{2,4},{3,5},{4,6},{5,7},{6,8},{7,9},{8,10},{9,11},{10,... | collective-permute-start | bytes 196616 | tf_op jit(solution)/shard_map/ppermute | solution.py:34
  175.1 3.2 %collective-permute-done.13 = f32[16,1024]{0,1:T(8,128)} collective-permute-done((f32[16,1024]{0,1:T(8,128)}, f32[16,1024]{0,1:T(8,128)}, u32[]{:S(2)}, u32[]{:S(2)}) %collective-permute-start.13) | collective-permute-done | bytes 65568 | tf_op jit(solution)/shard_map/ppermute | solution.py:34
  178.3 1.2 copy.75
  179.6 18.6 %collective-permute-done.14 = f32[16,1024]{0,1:T(8,128)S(1)} collective-permute-done((f32[16,1024]{0,1:T(8,128)}, f32[16,1024]{0,1:T(8,128)S(1)}, u32[]{:S(2)}, u32[]{:S(2)}) %collective-permute-start.14) | collective-permute-done | bytes 65568 | tf_op jit(solution)/shard_map/ppermute | solution.py:34
  198.4 3.1 %collective-permute-done.15 = f32[16,1024]{0,1:T(8,128)S(1)} collective-permute-done((f32[16,1024]{0,1:T(8,128)S(1)}, f32[16,1024]{0,1:T(8,128)S(1)}, u32[]{:S(2)}, u32[]{:S(2)}) %collective-permute-start.15) | collective-permute-done | bytes 65568 | tf_op jit(solution)/shard_map/ppermute | solution.py:34
  201.6 22.8 %collective-permute-done.16 = f32[16,1024]{0,1:T(8,128)S(1)} collective-permute-done((f32[16,1024]{0,1:T(8,128)S(1)}, f32[16,1024]{0,1:T(8,128)S(1)}, u32[]{:S(2)}, u32[]{:S(2)}) %collective-permute-start.16) | collective-permute-done | bytes 65568 | tf_op jit(solution)/shard_map/ppermute | solution.py:34
  224.6 0.7 copy-done.11
  (70 shorter events, 3.2 us)
Async XLA Ops:
  0.6 146.7 %copy-start = (f32[16,16]{1,0:T(8,128)S(1)}, f32[16,16]{1,0:T(8,128)}, u32[]{:S(2)}) copy-start(f32[16,16]{1,0:T(8,128)} %param.15) | copy-start | bytes 3076
  0.6 14.5 %copy-start.1 = (f32[5,16,32,128]{3,2,1,0:T(8,128)S(1)}, f32[5,16,32,128]{3,2,1,0:T(8,128)}, u32[]{:S(2)}) copy-start(f32[5,16,32,128]{3,2,1,0:T(8,128)} %param.11) | copy-start | bytes 3932164
  3.0 8.8 %copy-start.3 = (f32[5,16,32,128]{3,0,2,1:T(8,128)}, f32[5,16,32,128]{3,0,2,1:T(8,128)S(1)}, u32[]{:S(2)}) copy-start(f32[5,16,32,128]{3,0,2,1:T(8,128)S(1)} %copy.64) | copy-start | bytes 3932164
  3.0 37.4 %collective-permute-start = (f32[5,1,32,128]{3,0,2,1:T(8,128)S(1)}, f32[5,1,32,128]{3,0,2,1:T(8,128)S(1)}, u32[]{:S(2)}, u32[]{:S(2)}) collective-permute-start(f32[5,1,32,128]{3,0,2,1:T(8,128)S(1)} %get-tuple-element.25), channel_id=1, source_target_pairs={{64,0},{128,64},{192,128},{256,192},{320,256},{384,320},{448,384},... | collective-permute-start | bytes 245768 | tf_op jit(solution)/shard_map/ppermute | solution.py:21
  11.8 28.6 %collective-permute-start.1 = (f32[5,1,32,128]{3,0,2,1:T(8,128)S(1)}, f32[5,1,32,128]{3,0,2,1:T(8,128)S(1)}, u32[]{:S(2)}, u32[]{:S(2)}) collective-permute-start(f32[5,1,32,128]{3,0,2,1:T(8,128)S(1)} %get-tuple-element.26), channel_id=1, source_target_pairs={{0,64},{64,128},{128,192},{192,256},{256,320},{320,384},{384,448},... | collective-permute-start | bytes 245768 | tf_op jit(solution)/shard_map/ppermute | solution.py:20
  15.6 13.9 %copy-start.9 = (s32[2048,1]{0,1:T(1,128)S(1)}, s32[2048,1]{0,1:T(1,128)}, u32[]{:S(2)}) copy-start(s32[2048,1]{0,1:T(1,128)} %param.18) | copy-start | bytes 24580
  16.2 16.3 %collective-permute-start.2 = (f32[5,16,32,1]{2,1,3,0:T(8,128)S(1)}, f32[5,16,32,1]{2,1,3,0:T(8,128)S(1)}, u32[]{:S(2)}, u32[]{:S(2)}) collective-permute-start(f32[5,16,32,1]{2,1,3,0:T(8,128)S(1)} %copy.82), channel_id=1, source_target_pairs={{1,0},{2,1},{3,2},{4,3},{5,4},{6,5},{7,6},{8,7},{9,8},{10,9},{11,1... | collective-permute-start | bytes 30728 | tf_op jit(solution)/shard_map/ppermute | solution.py:21
  27.6 10.8 %collective-permute-start.3 = (f32[5,16,32,1]{2,1,3,0:T(8,128)S(1)}, f32[5,16,32,1]{2,1,3,0:T(8,128)S(1)}, u32[]{:S(2)}, u32[]{:S(2)}) collective-permute-start(f32[5,16,32,1]{2,1,3,0:T(8,128)S(1)} %copy.83), channel_id=1, source_target_pairs={{0,1},{1,2},{2,3},{3,4},{4,5},{5,6},{6,7},{7,8},{8,9},{9,10},{10,1... | collective-permute-start | bytes 30728 | tf_op jit(solution)/shard_map/ppermute | solution.py:20
  32.4 8.0 %copy-start.13 = (f32[16,32,128]{2,1,0:T(8,128)S(1)}, f32[16,32,128]{2,1,0:T(8,128)}, u32[]{:S(2)}) copy-start(f32[16,32,128]{2,1,0:T(8,128)} %param.12) | copy-start | bytes 786436
  32.4 8.0 %copy-start.14 = (f32[5,5]{1,0:T(8,128)S(1)}, f32[5,5]{1,0:T(8,128)}, u32[]{:S(2)}) copy-start(f32[5,5]{1,0:T(8,128)} %param.13) | copy-start | bytes 304
  32.4 8.0 %copy-start.15 = (f32[5]{0:T(128)S(1)}, f32[5]{0:T(128)}, u32[]{:S(2)}) copy-start(f32[5]{0:T(128)} %constant.40.clone) | copy-start | bytes 64
  51.4 24.2 %copy-start.2 = (f32[5,16,32,128]{3,0,2,1:T(8,128)}, f32[5,16,32,128]{3,0,2,1:T(8,128)S(1)}, u32[]{:S(2)}) copy-start(f32[5,16,32,128]{3,0,2,1:T(8,128)S(1)} %fusion.4) | copy-start | bytes 3932164
  56.4 19.3 %collective-permute-start.6 = (f32[5,16,32,1]{2,1,3,0:T(8,128)S(1)}, f32[5,16,32,1]{2,1,3,0:T(8,128)S(1)}, u32[]{:S(2)}, u32[]{:S(2)}) collective-permute-start(f32[5,16,32,1]{2,1,3,0:T(8,128)S(1)} %copy.66), channel_id=1, source_target_pairs={{1,0},{2,1},{3,2},{4,3},{5,4},{6,5},{7,6},{8,7},{9,8},{10,9},{11,1... | collective-permute-start | bytes 30728 | tf_op jit(solution)/shard_map/ppermute | solution.py:21
  64.1 13.7 %collective-permute-start.7 = (f32[5,16,32,1]{2,1,3,0:T(8,128)S(1)}, f32[5,16,32,1]{2,1,3,0:T(8,128)S(1)}, u32[]{:S(2)}, u32[]{:S(2)}) collective-permute-start(f32[5,16,32,1]{2,1,3,0:T(8,128)S(1)} %copy.68), channel_id=1, source_target_pairs={{0,1},{1,2},{2,3},{3,4},{4,5},{5,6},{6,7},{7,8},{8,9},{9,10},{10,1... | collective-permute-start | bytes 30728 | tf_op jit(solution)/shard_map/ppermute | solution.py:20
  66.0 13.9 %collective-permute-start.4 = (f32[5,1,32,128]{3,0,2,1:T(8,128)S(1)}, f32[5,1,32,128]{3,0,2,1:T(8,128)S(1)}, u32[]{:S(2)}, u32[]{:S(2)}) collective-permute-start(f32[5,1,32,128]{3,0,2,1:T(8,128)S(1)} %get-tuple-element.19), channel_id=1, source_target_pairs={{64,0},{128,64},{192,128},{256,192},{320,256},{384,320},{448,384},... | collective-permute-start | bytes 245768 | tf_op jit(solution)/shard_map/ppermute | solution.py:21
  67.9 11.9 %collective-permute-start.5 = (f32[5,1,32,128]{3,0,2,1:T(8,128)S(1)}, f32[5,1,32,128]{3,0,2,1:T(8,128)S(1)}, u32[]{:S(2)}, u32[]{:S(2)}) collective-permute-start(f32[5,1,32,128]{3,0,2,1:T(8,128)S(1)} %get-tuple-element.20), channel_id=1, source_target_pairs={{0,64},{64,128},{128,192},{192,256},{256,320},{320,384},{384,448},... | collective-permute-start | bytes 245768 | tf_op jit(solution)/shard_map/ppermute | solution.py:20
  95.8 22.9 %collective-permute-start.10 = (f32[5,16,32,1]{2,1,3,0:T(8,128)S(1)}, f32[5,16,32,1]{2,1,3,0:T(8,128)S(1)}, u32[]{:S(2)}, u32[]{:S(2)}) collective-permute-start(f32[5,16,32,1]{2,1,3,0:T(8,128)S(1)} %copy.70), channel_id=1, source_target_pairs={{1,0},{2,1},{3,2},{4,3},{5,4},{6,5},{7,6},{8,7},{9,8},{10,9},{11,1... | collective-permute-start | bytes 30728 | tf_op jit(solution)/shard_map/ppermute | solution.py:21
  107.3 13.5 %collective-permute-start.11 = (f32[5,16,32,1]{2,1,3,0:T(8,128)S(1)}, f32[5,16,32,1]{2,1,3,0:T(8,128)S(1)}, u32[]{:S(2)}, u32[]{:S(2)}) collective-permute-start(f32[5,16,32,1]{2,1,3,0:T(8,128)S(1)} %copy.72), channel_id=1, source_target_pairs={{0,1},{1,2},{2,3},{3,4},{4,5},{5,6},{6,7},{7,8},{8,9},{9,10},{10,1... | collective-permute-start | bytes 30728 | tf_op jit(solution)/shard_map/ppermute | solution.py:20
  109.2 13.6 %collective-permute-start.8 = (f32[5,1,32,128]{3,0,2,1:T(8,128)S(1)}, f32[5,1,32,128]{3,0,2,1:T(8,128)S(1)}, u32[]{:S(2)}, u32[]{:S(2)}) collective-permute-start(f32[5,1,32,128]{3,0,2,1:T(8,128)S(1)} %get-tuple-element.13), channel_id=1, source_target_pairs={{64,0},{128,64},{192,128},{256,192},{320,256},{384,320},{448,384},... | collective-permute-start | bytes 245768 | tf_op jit(solution)/shard_map/ppermute | solution.py:21
  111.1 11.7 %collective-permute-start.9 = (f32[5,1,32,128]{3,0,2,1:T(8,128)S(1)}, f32[5,1,32,128]{3,0,2,1:T(8,128)S(1)}, u32[]{:S(2)}, u32[]{:S(2)}) collective-permute-start(f32[5,1,32,128]{3,0,2,1:T(8,128)S(1)} %get-tuple-element.14), channel_id=1, source_target_pairs={{0,64},{64,128},{128,192},{192,256},{256,320},{320,384},{384,448},... | collective-permute-start | bytes 245768 | tf_op jit(solution)/shard_map/ppermute | solution.py:20
  122.8 11.9 %copy-start.10 = (s32[2048]{0:T(1024)S(1)}, s32[2048]{0:T(1024)}, u32[]{:S(2)}) copy-start(s32[2048]{0:T(1024)} %param.17) | copy-start | bytes 24580
  128.7 6.1 %copy-start.4 = (f32[5,16,32,128]{3,0,2,1:T(8,128)}, f32[5,16,32,128]{3,0,2,1:T(8,128)S(1)}, u32[]{:S(2)}) copy-start(f32[5,16,32,128]{3,0,2,1:T(8,128)S(1)} %fusion.8) | copy-start | bytes 3932164
  128.7 6.8 %collective-permute-start.12 = (f32[16,128]{1,0:T(8,128)S(1)}, f32[16,128]{1,0:T(8,128)S(1)}, u32[]{:S(2)}, u32[]{:S(2)}) collective-permute-start(f32[16,128]{1,0:T(8,128)S(1)} %bitcast.34), channel_id=1, source_target_pairs={{0,64},{64,128},{128,192},{192,256},{256,320},{320,384},{384,448},... | collective-permute-start | bytes 24584 | tf_op jit(solution)/shard_map/ppermute | solution.py:29
  135.5 11.8 %copy-start.8 = (f32[16,2048]{1,0:T(8,128)S(1)}, f32[16,2048]{1,0:T(8,128)}, u32[]{:S(2)}) copy-start(f32[16,2048]{1,0:T(8,128)} %param.14) | copy-start | bytes 393220
  135.5 11.8 %copy-start.12 = (f32[16]{0:T(128)S(1)}, f32[16]{0:T(128)}, u32[]{:S(2)}) copy-start(f32[16]{0:T(128)} %param.16) | copy-start | bytes 196
  155.5 3.7 %copy-start.5 = (f32[5,16,32,128]{3,0,2,1:T(8,128)S(1)}, f32[5,16,32,128]{3,0,2,1:T(8,128)}, u32[]{:S(2)}) copy-start(f32[5,16,32,128]{3,0,2,1:T(8,128)} %copy-done.4) | copy-start | bytes 3932164
  156.9 12.9 %copy-start.7 = (f32[16,1024]{0,1:T(8,128)S(1)}, f32[16,1024]{0,1:T(8,128)}, u32[]{:S(2)}) copy-start(f32[16,1024]{0,1:T(8,128)} %get-tuple-element.9) | copy-start | bytes 196612
  156.9 15.1 %copy-start.6 = (f32[16,1024]{0,1:T(8,128)S(1)}, f32[16,1024]{0,1:T(8,128)}, u32[]{:S(2)}) copy-start(f32[16,1024]{0,1:T(8,128)} %get-tuple-element.8) | copy-start | bytes 196612
  156.9 21.4 %collective-permute-start.13 = (f32[16,1024]{0,1:T(8,128)}, f32[16,1024]{0,1:T(8,128)}, u32[]{:S(2)}, u32[]{:S(2)}) collective-permute-start(f32[16,1024]{0,1:T(8,128)} %get-tuple-element.12), channel_id=1, source_target_pairs={{0,62},{1,63},{2,0},{3,1},{4,2},{5,3},{6,4},{7,5},{8,6},{9,7},{10,... | collective-permute-start | bytes 196616 | tf_op jit(solution)/shard_map/ppermute | solution.py:34
  160.5 37.7 %collective-permute-start.14 = (f32[16,1024]{0,1:T(8,128)}, f32[16,1024]{0,1:T(8,128)S(1)}, u32[]{:S(2)}, u32[]{:S(2)}) collective-permute-start(f32[16,1024]{0,1:T(8,128)} %get-tuple-element.11), channel_id=1, source_target_pairs={{0,63},{1,0},{2,1},{3,2},{4,3},{5,4},{6,5},{7,6},{8,7},{9,8},{10,9... | collective-permute-start | bytes 196616 | tf_op jit(solution)/shard_map/ppermute | solution.py:34
  169.8 31.6 %collective-permute-start.15 = (f32[16,1024]{0,1:T(8,128)S(1)}, f32[16,1024]{0,1:T(8,128)S(1)}, u32[]{:S(2)}, u32[]{:S(2)}) collective-permute-start(f32[16,1024]{0,1:T(8,128)S(1)} %copy-done.7), channel_id=1, source_target_pairs={{0,1},{1,2},{2,3},{3,4},{4,5},{5,6},{6,7},{7,8},{8,9},{9,10},{10,1... | collective-permute-start | bytes 196616 | tf_op jit(solution)/shard_map/ppermute | solution.py:34
  172.0 52.4 %collective-permute-start.16 = (f32[16,1024]{0,1:T(8,128)S(1)}, f32[16,1024]{0,1:T(8,128)S(1)}, u32[]{:S(2)}, u32[]{:S(2)}) collective-permute-start(f32[16,1024]{0,1:T(8,128)S(1)} %copy-done.6), channel_id=1, source_target_pairs={{0,2},{1,3},{2,4},{3,5},{4,6},{5,7},{6,8},{7,9},{8,10},{9,11},{10,... | collective-permute-start | bytes 196616 | tf_op jit(solution)/shard_map/ppermute | solution.py:34
  224.6 0.7 copy-start.11
where the time goes:
time: 227 us; the launch traced here: 225 us
  starting transfers between devices  85.5 us (38%)
  local copies, waits for them, and re-layouts  56.5 us (25%)
  waiting for transfers between devices  52.3 us (23%)
  matrix products  28.1 us (12%)
    ppermute x4, waiting for transfers between devices, passed_along_2(): return lax.ppermute(x, axis, [(i, (i + by) % size) for i in range(size)])  47.8 us
    ppermute x6, starting transfers between devices, extended(): after = lax.ppermute(first, axis, down)  38.5 us
    dot_general x3, matrix products, advance(): jnp.tensordot(reaction, field, axes=(1, 0), precision=lax.Precision.HIGHEST)  27.8 us
    ppermute x6, starting transfers between devices, extended(): before = lax.ppermute(last, axis, up)  24.4 us
    ppermute x4, starting transfers between devices, passed_along_2(): return lax.ppermute(x, axis, [(i, (i + by) % size) for i in range(size)])  16.7 us
    gather x1, local copies, waits for them, and re-layouts, local(): look = jnp.take(flux, wall_cell, axis=0)  11.8 us
    slice x8, local copies, waits for them, and re-layouts, extended(): first = lax.slice_in_dim(x, 0, width, axis=dim)  10.3 us
    scatter x1, local copies, waits for them, and re-layouts, local(): jnp.zeros((particles.shape[0], spread * capacity), jnp.float32)  6.6 us
  transfers between devices with their start and end apart: 17, of which 6 were waited for; matrix products, arithmetic and copies ran while one was open for 11% of the time, Pallas kernels for 0%

commit v1 on v0

v1 whole, which is shorter than its diff:
```python
import jax
import jax.numpy as jnp
from jax import lax
from jax.experimental import pallas as pl
from jax.experimental.pallas import tpu as pltpu
from jax.sharding import PartitionSpec as P

REACH = 2
MOVES = 2 * REACH + 1
ITERS = 3
DIFFUSE = (1.0, 0.8, 0.6, 0.9, 0.7)
COMP = 5
GX = 16
GR = 32
GA = 128
TILES = GR // 8
EXT = GX + 2 * ITERS
CHUNKS = 16
VALS = 16
CAP = 1024
SPOTS = CAP // 128

FIELD_COLUMNS = (3, 2, 1, 0, -1)
KAPPA_COLUMNS = (2, 1, 0)
STRIPS = [(c, k) for c in range(COMP) for k in FIELD_COLUMNS] + [(COMP, k) for k in KAPPA_COLUMNS]
STRIP_AT = {key: i for i, key in enumerate(STRIPS)}
CORNERS = [(c, 1) for c in range(COMP)] + [(c, 2) for c in range(COMP)] + [(COMP, 1)] + [(c, 0) for c in range(COMP)]
LAYERS = 3 * COMP + 2 + 1

VMEM = pl.BlockSpec(memory_space=pltpu.VMEM)
SMEM = pl.BlockSpec(memory_space=pltpu.SMEM)


def f32(*shape):
    return jax.ShapeDtypeStruct(shape, jnp.float32)


def i32(*shape):
    return jax.ShapeDtypeStruct(shape, jnp.int32)


def lanes(shape=(8, 128)):
    return lax.broadcasted_iota(jnp.int32, shape, len(shape) - 1)


def pick(x, index):
    return jnp.take_along_axis(x, index, axis=1, mode="promise_in_bounds")


def rows(tile):
    return slice(8 * tile, 8 * tile + 8)


def call(kernel, outs, scratch=(), specs=None, flops=0, moved=0, limit=16):
    return pl.pallas_call(
        kernel,
        out_shape=outs,
        in_specs=specs,
        out_specs=jax.tree.map(lambda _: VMEM, outs),
        scratch_shapes=list(scratch),
        cost_estimate=pl.CostEstimate(flops=flops, bytes_accessed=moved, transcendentals=0),
        compiler_params=pltpu.CompilerParams(vmem_limit_bytes=limit << 20),
    )


def edges_kernel(gas, kappa, to_right, to_left):
    lane = lanes()
    within = lane & 63
    depth, cell = within >> 4, within & 15
    high = jnp.maximum(6 * cell + 2 - depth, 0)
    low = 6 * cell + 3 + depth
    for tile in range(TILES):
        packed = [jnp.zeros((8, 128), jnp.float32) for _ in range(COMP + 1)]
        for x in range(GX):
            here = (lane >= 6 * x) & (lane < 6 * x + 6)
            for q in range(COMP + 1):
                slab = gas[q, x, rows(tile), :] if q < COMP else kappa[x, rows(tile), :]
                packed[q] = jnp.where(here, pltpu.roll(slab, 6 * x + 3, 1), packed[q])
        for s in range((COMP + 1) // 2):
            for out, index in ((to_right, high), (to_left, low)):
                out[s, rows(tile), :] = jnp.where(lane < 64, pick(packed[2 * s], index), pick(packed[2 * s + 1], index))


def strips_kernel(gas, kappa, to_right, to_left, from_left, from_right, strips, send_a, send_wall, send_rest):
    lane = lanes()
    low_side = (lane & 1) == 1
    cell = jnp.clip((lane >> 1) - 3, 0, GX - 1)
    odd = lax.rem(lax.axis_index("sect"), 2)
    even = odd == 0
    for tile in range(TILES):
        held = {}
        for q, k in STRIPS:
            depth = k - 1 if k > 0 else -k
            index = cell + ((q % 2) * 64 + depth * 16)
            low, high = (from_left, from_right) if k > 0 else (to_left, to_right)
            value = jnp.where(low_side, pick(low[q // 2, rows(tile), :], index), pick(high[q // 2, rows(tile), :], index))
            strips[STRIP_AT[q, k], rows(tile), :] = value
            held[q, k] = value
        top = jnp.zeros((8, 128), jnp.float32)
        bottom = top
        for i, key in enumerate(CORNERS):
            here = (lane >> 2) == i
            top = jnp.where(here, pltpu.roll(held[key], (4 * i - 34) % 128, 1), top)
            bottom = jnp.where(here, pltpu.roll(held[key], (4 * i - 6) % 128, 1), bottom)
        for_a = jnp.where(even, top, bottom)
        for_b = jnp.where(even, bottom, top)
        send_a[LAYERS - 1, rows(tile), :] = for_a
        if tile == TILES - 1:
            send_wall[LAYERS - 1] = for_b
        else:
            send_rest[LAYERS - 1, rows(tile), :] = for_b
    at_a, at_b = jnp.where(even, GX - 3, 0), jnp.where(even, 0, GX - 3)
    kappa_a, kappa_b = jnp.where(even, GX - 2, 0), jnp.where(even, 0, GX - 2)
    split = GR - 8
    for c in range(COMP):
        for layer in range(3):
            send_a[3 * c + layer] = gas[c, at_a + layer]
            send_wall[3 * c + layer] = gas[c, at_b + layer, split:, :]
            send_rest[3 * c + layer] = gas[c, at_b + layer, :split, :]
    for layer in range(2):
        send_a[3 * COMP + layer] = kappa[kappa_a + layer]
        send_wall[3 * COMP + layer] = kappa[kappa_b + layer, split:, :]
        send_rest[3 * COMP + layer] = kappa[kappa_b + layer, :split, :]


def coupling(reaction):
    return [[0.3 * reaction[c, d] + (1.0 if c == d else 0.0) for d in range(COMP)] for c in range(COMP)]


def updated(c, values, neighbours, kappa, mix):
    total = mix[c][0] * values[0]
    for d in range(1, COMP):
        total = total + mix[c][d] * values[d]
    rate = kappa if DIFFUSE[c] == 1.0 else DIFFUSE[c] * kappa
    return total + rate * (neighbours - 6.0 * values[c])


def radial_sum(tiles, wall_only):
    sub = lax.broadcasted_iota(jnp.int32, (8, 128), 0)
    down = [pltpu.roll(t, 1, 0) for t in tiles]
    up = [pltpu.roll(t, 7, 0) for t in tiles]
    last = len(tiles) - 1
    sums = []
    for i, t in enumerate(tiles):
        if wall_only:
            below = down[i]
        else:
            below = jnp.where(sub == 0, down[i - 1] if i > 0 else t, down[i])
        above = jnp.where(sub == 7, up[i + 1] if i < last else t, up[i])
        sums.append(below + above)
    return sums


def strip_levels(strips, low_corner, high_corner, mix, edge, tiles):
    lane = lanes()
    wall_only = len(tiles) == 1
    from_low = (lane >= 2) & (lane < 6)
    from_high = (lane >= 38) & (lane < 42)
    held = {}
    for key in STRIPS:
        held[key] = [strips[STRIP_AT[key], rows(t), :] for t in tiles]
    for i, key in enumerate(CORNERS):
        for n in range(len(tiles)):
            value = jnp.where(from_low, pltpu.roll(low_corner[n], (2 - 4 * i) % 128, 1), held[key][n])
            held[key][n] = jnp.where(from_high, pltpu.roll(high_corner[n], (38 - 4 * i) % 128, 1), value)
    for step in range(ITERS):
        for c in range(COMP):
            for n in range(len(tiles)):
                edge[step, c, rows(n), :] = held[c, 1][n]
        if step == ITERS - 1:
            break
        later = {}
        for k in (2, 1, 0) if step == 0 else (1,):
            for c in range(COMP):
                radial = radial_sum(held[c, k], wall_only)
                later[c, k] = []
                for n in range(len(tiles)):
                    value = held[c, k][n]
                    around = held[c, k + 1][n] + held[c, k - 1][n]
                    around = around + pltpu.roll(value, 2, 1) + pltpu.roll(value, 126, 1) + radial[n]
                    later[c, k].append(updated(c, [held[d, k][n] for d in range(COMP)], around, held[COMP, k][n], mix))
        for key in [key for key in held if key[0] == COMP]:
            later[key] = held[key]
        held = later


def plane(src, kappa, edge, step, at, mix, count, wall_only, comps):
    lane = lanes()
    first, last = lane == 0, lane == 127
    shift = 127 - 2 * at
    values = [[src[c, at, rows(t), :] for t in range(count)] for c in range(COMP)]
    kap = [kappa[at, rows(t), :] for t in range(count)]
    out = {}
    for c in comps:
        radial = radial_sum(values[c], wall_only)
        for t in range(count):
            value = values[c][t]
            beyond = pltpu.roll(edge[step, c, rows(t), :], shift, 1)
            around = src[c, at - 1, rows(t), :] + src[c, at + 1, rows(t), :] + radial[t]
            around = around + jnp.where(first, beyond, pltpu.roll(value, 1, 1))
            around = around + jnp.where(last, beyond, pltpu.roll(value, 127, 1))
            out[c, t] = updated(c, [values[d][t] for d in range(COMP)], around, kap[t], mix)
    return out


def steps(count, wall_only, now, later, kappa, edge, mix, finish):
    for step in range(ITERS):
        src, dst = (now, later) if step % 2 == 0 else (later, now)
        final = step == ITERS - 1

        def body(at, carry, step=step, src=src, dst=dst, final=final):
            comps = (0,) if final and wall_only else range(COMP)
            out = plane(src, kappa, edge, step, at, mix, count, wall_only, comps)
            if final:
                finish(at, out)
            else:
                for (c, t), value in out.items():
                    dst[c, at, rows(t), :] = value
            return carry

        lax.fori_loop(step + 1, EXT - 1 - step, body, 0)


def wall_kernel(gas, kappa, strips, recv_a, recv_wall, reaction, wall, now, later, kap, edge):
    odd = lax.rem(lax.axis_index("sect"), 2)
    even = odd == 0
    mix = coupling(reaction)
    top = slice(GR - 8, GR)
    at_a, at_b = jnp.where(even, GX + 3, 0), jnp.where(even, 0, GX + 3)
    kappa_a, kappa_b = jnp.where(even, GX + 3, 1), jnp.where(even, 1, GX + 3)
    for c in range(COMP):
        for x in range(GX):
            now[c, x + 3] = gas[c, x, top, :]
        for layer in range(3):
            now[c, at_a + layer] = recv_a[3 * c + layer, top, :]
            now[c, at_b + layer] = recv_wall[3 * c + layer]
    for x in range(GX):
        kap[x + 3] = kappa[x, top, :]
    for layer in range(2):
        kap[kappa_a + layer] = recv_a[3 * COMP + layer, top, :]
        kap[kappa_b + layer] = recv_wall[3 * COMP + layer]
    corner_a, corner_b = recv_a[LAYERS - 1, top, :], recv_wall[LAYERS - 1]
    low, high = jnp.where(even, corner_b, corner_a), jnp.where(even, corner_a, corner_b)
    strip_levels(strips, [low], [high], mix, edge, [TILES - 1])

    def finish(at, out):
        wall[pl.ds(at - 3, 1), :] = out[0, 0][7:8, :]

    steps(1, True, now, later, kap, edge, mix, finish)


def gas_kernel(gas, kappa, strips, recv_a, recv_wall, recv_rest, reaction, result, now, later, kap, edge):
    odd = lax.rem(lax.axis_index("sect"), 2)
    even = odd == 0
    mix = coupling(reaction)
    split = GR - 8
    at_a, at_b = jnp.where(even, GX + 3, 0), jnp.where(even, 0, GX + 3)
    kappa_a, kappa_b = jnp.where(even, GX + 3, 1), jnp.where(even, 1, GX + 3)
    for c in range(COMP):
        now[c, 3 : GX + 3] = gas[c]
        for layer in range(3):
            now[c, at_a + layer] = recv_a[3 * c + layer]
            now[c, at_b + layer, split:, :] = recv_wall[3 * c + layer]
            now[c, at_b + layer, :split, :] = recv_rest[3 * c + layer]
    kap[3 : GX + 3] = kappa[...]
    for layer in range(2):
        kap[kappa_a + layer] = recv_a[3 * COMP + layer]
        kap[kappa_b + layer, split:, :] = recv_wall[3 * COMP + layer]
        kap[kappa_b + layer, :split, :] = recv_rest[3 * COMP + layer]
    low, high = [], []
    for t in range(TILES):
        corner_a = recv_a[LAYERS - 1, rows(t), :]
        corner_b = recv_wall[LAYERS - 1] if t == TILES - 1 else recv_rest[LAYERS - 1, rows(t), :]
        low.append(jnp.where(even, corner_b, corner_a))
        high.append(jnp.where(even, corner_a, corner_b))
    strip_levels(strips, low, high, mix, edge, list(range(TILES)))

    def finish(at, out):
        for (c, t), value in out.items():
            result[c, at - 3, rows(t), :] = value

    steps(TILES, False, now, later, kap, edge, mix, finish)


def pack_kernel(hop, cell, particles, mixing, heating, packed, cells, spread, ordered, source, begin, end):
    lane = lanes()
    square = (128, 128)
    down, across = lax.broadcasted_iota(jnp.int32, square, 0), lanes(square)
    moves = hop[...]
    named = [moves == j for j in range(MOVES)]
    table = jnp.concatenate(
        [jnp.where(m, 1.0, 0.0) for m in named] + [jnp.zeros((128 - MOVES * CHUNKS, 128), jnp.float32)], axis=0
    )
    running = jnp.dot(table, jnp.where(down <= across, 1.0, 0.0), preferred_element_type=jnp.float32)
    count = jnp.dot(table, jnp.ones(square, jnp.float32), preferred_element_type=jnp.float32)
    before = jnp.where(((down >> 4) == (across >> 4)) & (across < down), 1.0, 0.0)
    base = jnp.dot(before, count, preferred_element_type=jnp.float32)
    offset = jnp.zeros((CHUNKS, 128), jnp.float32)
    place = jnp.zeros((CHUNKS, 128), jnp.float32)
    across16 = lanes((CHUNKS, 128))
    for j in range(MOVES):
        part = slice(CHUNKS * j, CHUNKS * (j + 1))
        place = jnp.where(named[j], offset + running[part] - 1.0, place)
        first = base[part].astype(jnp.int32)
        source[part, :] = (across16 + offset.astype(jnp.int32) - first) & 127
        begin[part, :] = across16 - first
        end[part, :] = across16 - first - count[part].astype(jnp.int32)
        offset = offset + count[part]
    own = lax.broadcasted_iota(jnp.int32, (VALS, VALS), 0) == lax.broadcasted_iota(jnp.int32, (VALS, VALS), 1)
    weights = 0.5 * mixing[...] + jnp.where(own, 1.0, 0.0)
    first_value = lax.broadcasted_iota(jnp.int32, (VALS, VALS), 1) == 0
    weights = weights - jnp.where(first_value, heating[...], 0.0)
    for v in range(VALS):
        spread[v] = jnp.broadcast_to(weights[:, v : v + 1], (VALS, 128))
    place = place.astype(jnp.int32)
    position = lane.astype(jnp.float32)
    for chunk in range(CHUNKS):
        part = slice(128 * chunk, 128 * (chunk + 1))
        total = spread[0] * particles[0:1, part]
        for v in range(1, VALS):
            total = total + spread[v] * particles[v : v + 1, part]
        hot = jnp.where(down == place[chunk : chunk + 1, :], 1.0, 0.0)
        order = lax.dot_general(position, hot, (((1,), (1,)), ((), ())), preferred_element_type=jnp.float32)
        order = order.astype(jnp.int32)
        ordered[chunk, 0:8, :] = pick(total[0:8], order)
        ordered[chunk, 8:16, :] = pick(total[8:16], order)
        ordered[chunk, 16:24, :] = pick(
            jnp.broadcast_to(cell[chunk : chunk + 1, :], (8, 128)).astype(jnp.float32), order
        )

    def block(j, carry):
        held = [[jnp.zeros((8, 128), jnp.float32)] * 2 + [jnp.full((8, 128), -1.0)] for _ in range(SPOTS)]
        for chunk in range(CHUNKS):
            row = pl.ds(CHUNKS * j + chunk, 1)
            index = jnp.broadcast_to(source[row, :], (8, 128))
            parts = [pick(ordered[chunk, rows(n), :], index) for n in range(3)]
            start = jnp.broadcast_to(begin[row, :], (8, 128))
            stop = jnp.broadcast_to(end[row, :], (8, 128))
            for spot in range(SPOTS):
                here = (start >= -128 * spot) & (stop < -128 * spot)
                held[spot] = [jnp.where(here, new, old) for new, old in zip(parts, held[spot])]
        for spot in range(SPOTS):
            part = slice(128 * spot, 128 * (spot + 1))
            packed[j, 0:8, part] = held[spot][0]
            packed[j, 8:16, part] = held[spot][1]
            cells[j, spot : spot + 1, :] = held[spot][2][0:1, :].astype(jnp.int32)
        return carry

    lax.fori_loop(0, MOVES, block, 0)


def heat_kernel(wall, earlier, packed, cells, heating, *refs):
    outs, look = refs[:MOVES], refs[MOVES]
    flux = 0.5 * (wall[...] + earlier[...])
    heat = jnp.broadcast_to(heating[...], (VALS, 128))
    for j in range(MOVES):
        where_to = cells[j]
        row, column = where_to >> 7, where_to & 127
        found = jnp.zeros((8, 128), jnp.float32)
        for x in range(GX):
            line = jnp.broadcast_to(flux[x : x + 1, :], (8, 128))
            found = jnp.where(row == x, pick(line, column), found)
        look[j] = found
    for j in range(MOVES):
        for spot in range(SPOTS):
            part = slice(128 * spot, 128 * (spot + 1))
            outs[j][:, part] = packed[j, :, part] + heat * look[j, spot : spot + 1, :]


def ring(x, axis, by):
    size = lax.axis_size(axis)
    return lax.ppermute(x, axis, [(i, (i + by) % size) for i in range(size)])


def swap(x, axis, first):
    size = lax.axis_size(axis)
    pairs = [(i, i + 1) for i in range(first, size - 1, 2)]
    return lax.ppermute(x, axis, pairs + [(j, i) for i, j in pairs])


def local(gas, kappa, reaction, particles, mixing, heating, wall_cell, tile_hop):
    strip_shape = (3, GR, GA)
    to_right, to_left = call(edges_kernel, (f32(*strip_shape), f32(*strip_shape)), specs=[VMEM] * 2, moved=2 << 20)(gas, kappa)
    from_left = ring(to_right, "blk", 1)
    from_right = ring(to_left, "blk", -1)

    heating_column = heating.reshape(VALS, 1)
    packed, cells = call(
        pack_kernel,
        (f32(MOVES, VALS, CAP), i32(MOVES, SPOTS, 128)),
        scratch=[
            pltpu.VMEM((VALS, VALS, 128), jnp.float32),
            pltpu.VMEM((CHUNKS, 24, 128), jnp.float32),
            pltpu.VMEM((MOVES * CHUNKS, 128), jnp.int32),
            pltpu.VMEM((MOVES * CHUNKS, 128), jnp.int32),
            pltpu.VMEM((MOVES * CHUNKS, 128), jnp.int32),
        ],
        specs=[VMEM] * 5,
        moved=8 << 20,
    )(tile_hop.reshape(CHUNKS, 128), wall_cell.reshape(CHUNKS, 128), particles, mixing, heating_column)

    strips, send_a, send_wall, send_rest = call(
        strips_kernel,
        (f32(len(STRIPS), GR, GA), f32(LAYERS, GR, GA), f32(LAYERS, 8, GA), f32(LAYERS, GR - 8, GA)),
        specs=[VMEM] * 6,
        moved=2 << 20,
    )(gas, kappa, to_right, to_left, from_left, from_right)
    recv_wall = swap(send_wall, "sect", 1)
    recv_a = swap(send_a, "sect", 0)
    recv_rest = swap(send_rest, "sect", 1)

    wall = call(
        wall_kernel,
        f32(GX, GA),
        scratch=[
            pltpu.VMEM((COMP, EXT, 8, GA), jnp.float32),
            pltpu.VMEM((COMP, EXT, 8, GA), jnp.float32),
            pltpu.VMEM((EXT, 8, GA), jnp.float32),
            pltpu.VMEM((ITERS, COMP, 8, GA), jnp.float32),
        ],
        specs=[VMEM] * 5 + [SMEM],
        moved=4 << 20,
    )(gas, kappa, strips, recv_a, recv_wall, reaction)
    size = lax.axis_size("sect")
    earlier = lax.ppermute(wall, "sect", [(i, i + 1) for i in range(size - 1)])

    blocks = call(
        heat_kernel,
        (f32(VALS, CAP),) * MOVES,
        scratch=[pltpu.VMEM((MOVES, SPOTS, 128), jnp.float32)],
        specs=[VMEM] * 5,
        moved=2 << 20,
    )(wall, earlier, packed, cells, heating_column)
    pieces = [block if j == REACH else ring(block, "blk", j - REACH) for j, block in enumerate(blocks)]

    field = call(
        gas_kernel,
        f32(COMP, GX, GR, GA),
        scratch=[
            pltpu.VMEM((COMP, EXT, GR, GA), jnp.float32),
            pltpu.VMEM((COMP, EXT, GR, GA), jnp.float32),
            pltpu.VMEM((EXT, GR, GA), jnp.float32),
            pltpu.VMEM((ITERS, COMP, GR, GA), jnp.float32),
        ],
        specs=[VMEM] * 6 + [SMEM],
        moved=20 << 20,
    )(gas, kappa, strips, recv_a, recv_wall, recv_rest, reaction)
    return field, jnp.concatenate(pieces, axis=1)


def solution(mesh):
    in_specs = (
        P(None, "sect", None, "blk"),
        P("sect", None, "blk"),
        P(),
        P(None, ("sect", "blk")),
        P(),
        P(),
        P(("sect", "blk")),
        P(("sect", "blk"), None),
    )
    out_specs = (P(None, "sect", None, "blk"), P(None, ("sect", "blk")))
    return jax.shard_map(local, mesh=mesh, in_specs=in_specs, out_specs=out_specs, check_vma=False)
```

time: 227 us -> 91.2 us (0.40)
  local copies, waits for them, and re-layouts: 56.5 us -> 3.14 us
  waiting for transfers between devices: 52.3 us -> 13 us
  starting transfers between devices: 85.5 us -> 54.9 us
  matrix products: 28.1 us -> 0 us
  Pallas kernels: 0 us -> 18.8 us
    ppermute x17 -> x10, waiting for transfers between devices: 52.3 us -> 13 us  [the longest x6 8.3 us: ring(): return lax.ppermute(x, axis, [(i, (i + by) % size) for i in range(size)])]
    ppermute x17 -> x10, starting transfers between devices: 85.5 us -> 54.9 us  [the longest x6 32.9 us: ring(): return lax.ppermute(x, axis, [(i, (i + by) % size) for i in range(size)])]
    dot_general x4 -> x0, matrix products: 28.1 us -> none  [the longest x3 27.8 us: advance(): jnp.tensordot(reaction, field, axes=(1, 0), precision=lax.Precision.HIGHEST)]
    pallas_call x0 -> x6, Pallas kernels: none -> 18.8 us  [the longest x1 9.75 us: local(): call(gas_kernel, f32(COMP, GX, GR, GA), scratch=[pltpu.VMEM((COMP, EXT, G...]
    slice x17 -> x0, local copies, waits for them, and re-layouts: 17.2 us -> none  [the longest x8 10.3 us: extended(): first = lax.slice_in_dim(x, 0, width, axis=dim)]
    ppermute x10 -> x0, local copies, waits for them, and re-layouts: 14.1 us -> none  [the longest x3 6.24 us: extended(): after = lax.ppermute(first, axis, down)]
    gather x1 -> x0, local copies, waits for them, and re-layouts: 11.8 us -> none  [local(): look = jnp.take(flux, wall_cell, axis=0)]
    scatter x1 -> x0, local copies, waits for them, and re-layouts: 6.6 us -> none  [local(): jnp.zeros((particles.shape[0], spread * capacity), jnp.float32)]
  transfers between devices with their start and end apart: 17 -> 10, of which waited for: 6 -> 4; matrix products, arithmetic and copies ran while one was open for 11% -> 0% of each run, Pallas kernels for 0% -> 19%
where the time goes in v1:
time: 91.2 us; the launch traced here: 90.8 us
  starting transfers between devices  54.9 us (60%)
  Pallas kernels  18.8 us (21%)
  waiting for transfers between devices  13 us (14%)
  local copies, waits for them, and re-layouts  3.14 us (3%)
    ppermute x6, starting transfers between devices, ring(): return lax.ppermute(x, axis, [(i, (i + by) % size) for i in range(size)])  32.9 us
    ppermute x3, starting transfers between devices, swap(): return lax.ppermute(x, axis, pairs + [(j, i) for i, j in pairs])  17.2 us
    pallas_call x1, Pallas kernels, local(): call(gas_kernel, f32(COMP, GX, GR, GA), scratch=[pltpu.VMEM((COMP, EXT, G...  9.75 us
    ppermute x6, waiting for transfers between devices, ring(): return lax.ppermute(x, axis, [(i, (i + by) % size) for i in range(size)])  8.3 us
    pallas_call x1, Pallas kernels, local(): call(wall_kernel, f32(GX, GA), scratch=[pltpu.VMEM((COMP, EXT, 8, GA), jn...  5.49 us
    ppermute x1, starting transfers between devices, local(): earlier = lax.ppermute(wall, 'sect', [(i, i + 1) for i in range(size - 1)])  4.87 us
    ppermute x3, waiting for transfers between devices, swap(): return lax.ppermute(x, axis, pairs + [(j, i) for i, j in pairs])  4.71 us
    unnamed x26, local copies, waits for them, and re-layouts  3.05 us
  transfers between devices with their start and end apart: 10, of which 4 were waited for; matrix products, arithmetic and copies ran while one was open for 0% of the time, Pallas kernels for 19%

profile of v1, /device:TPU:1, one launch (start us, length us, event | category | flops | bytes accessed | tf_op | source)
XLA Modules:
  0.0 90.8 jit_solution(14525993855257357271)
XLA Ops:
  0.6 0.0 copy-start
  0.6 1.3 %copy-done = f32[5,16,32,128]{3,2,1,0:T(8,128)S(1)} copy-done((f32[5,16,32,128]{3,2,1,0:T(8,128)S(1)}, f32[5,16,32,128]{3,2,1,0:T(8,128)}, u32[]{:S(2)}) %copy-start) | copy-done | bytes 1310744
  1.9 0.0 copy-start.2
  2.0 0.9 %copy-done.2 = f32[16,32,128]{2,1,0:T(8,128)S(1)} copy-done((f32[16,32,128]{2,1,0:T(8,128)S(1)}, f32[16,32,128]{2,1,0:T(8,128)}, u32[]{:S(2)}) %copy-start.2) | copy-done | bytes 262168
  2.9 0.0 copy-start.5
  2.9 0.8 shard_map.95
  3.7 4.4 %collective-permute-start = (f32[3,32,128]{2,1,0:T(8,128)S(1)}, f32[3,32,128]{2,1,0:T(8,128)S(1)}, u32[]{:S(2)}, u32[]{:S(2)}) collective-permute-start(f32[3,32,128]{2,1,0:T(8,128)S(1)} %get-tuple-element.15.to_right), channel_id=1, source_target_pairs={{0,1},{1,2},{2,3},{3,4},{4,5},{5,6},{6,7},{7,8},{8,9},{9,10},{10,1... | collective-permute-start | bytes 147464 | tf_op jit(solution)/shard_map/ppermute | solution.py:372
  8.1 9.3 %collective-permute-start.1 = (f32[3,32,128]{2,1,0:T(8,128)S(1)}, f32[3,32,128]{2,1,0:T(8,128)S(1)}, u32[]{:S(2)}, u32[]{:S(2)}) collective-permute-start(f32[3,32,128]{2,1,0:T(8,128)S(1)} %get-tuple-element.16.to_left), channel_id=1, source_target_pairs={{0,63},{1,0},{2,1},{3,2},{4,3},{5,4},{6,5},{7,6},{8,7},{9,8},{10,9... | collective-permute-start | bytes 147464 | tf_op jit(solution)/shard_map/ppermute | solution.py:372
  17.4 0.0 collective-permute-done.from_left
  17.4 1.1 %collective-permute-done.1.from_right = f32[3,32,128]{2,1,0:T(8,128)S(1)} collective-permute-done((f32[3,32,128]{2,1,0:T(8,128)S(1)}, f32[3,32,128]{2,1,0:T(8,128)S(1)}, u32[]{:S(2)}, u32[]{:S(2)}) %collective-permute-start.1) | collective-permute-done | bytes 49184 | tf_op jit(solution)/shard_map/ppermute | solution.py:372
  18.5 0.8 shard_map.96
  19.4 0.0 copy-start.10
  19.4 0.0 copy-start.4
  19.4 0.0 copy-start.6
  19.4 0.0 copy-start.7
  19.4 0.0 copy-start.8
  19.4 7.7 %collective-permute-start.2 = (f32[18,32,128]{2,1,0:T(8,128)S(1)}, f32[18,32,128]{2,1,0:T(8,128)S(1)}, u32[]{:S(2)}, u32[]{:S(2)}) collective-permute-start(f32[18,32,128]{2,1,0:T(8,128)S(1)} %get-tuple-element.18), channel_id=1, source_target_pairs={{0,64},{128,192},{256,320},{384,448},{64,0},{192,128},{320,256},{4... | collective-permute-start | bytes 884744 | tf_op jit(solution)/shard_map/ppermute | solution.py:378
  27.2 4.6 %collective-permute-start.4 = (f32[18,24,128]{2,1,0:T(8,128)S(1)}, f32[18,24,128]{2,1,0:T(8,128)S(1)}, u32[]{:S(2)}, u32[]{:S(2)}) collective-permute-start(f32[18,24,128]{2,1,0:T(8,128)S(1)} %get-tuple-element.20), channel_id=1, source_target_pairs={{64,128},{192,256},{320,384},{128,64},{256,192},{384,320},{65,129}... | collective-permute-start | bytes 663560 | tf_op jit(solution)/shard_map/ppermute | solution.py:378
  31.7 4.9 %collective-permute-start.3 = (f32[18,8,128]{2,1,0:T(8,128)S(1)}, f32[18,8,128]{2,1,0:T(8,128)S(1)}, u32[]{:S(2)}, u32[]{:S(2)}) collective-permute-start(f32[18,8,128]{2,1,0:T(8,128)S(1)} %get-tuple-element.19), channel_id=1, source_target_pairs={{64,128},{192,256},{320,384},{128,64},{256,192},{384,320},{65,129}... | collective-permute-start | bytes 221192 | tf_op jit(solution)/shard_map/ppermute | solution.py:378
  36.6 4.7 %collective-permute-done.3.recv_wall = f32[18,8,128]{2,1,0:T(8,128)S(1)} collective-permute-done((f32[18,8,128]{2,1,0:T(8,128)S(1)}, f32[18,8,128]{2,1,0:T(8,128)S(1)}, u32[]{:S(2)}, u32[]{:S(2)}) %collective-permute-start.3) | collective-permute-done | bytes 73760 | tf_op jit(solution)/shard_map/ppermute | solution.py:378
  41.4 0.0 collective-permute-done.2.recv_a
  41.4 0.0 copy-done.5
  41.4 0.0 copy-start.1
  41.4 0.0 copy-start.3
  41.4 5.5 %shard_map.98.wall = f32[16,128]{1,0:T(8,128)S(1)} custom-call(f32[5,16,32,128]{3,2,1,0:T(8,128)S(1)} %copy-done, f32[16,32,128]{2,1,0:T(8,128)S(1)} %copy-done.2, f32[28,32,128]{2,1,0:T(8,128)S(1)} %get-tuple-element.17.strips, f32[18,32,128]{2,1,0:T(8,128)S(1)} %collective-permute-done.2.recv_a, f32[18,8,128]{2,1,0:T(8,128)S(1)} %collective-permute-done.3.recv_wall, ...), custom_call_target="tpu_custom_call" | custom-call | bytes 4194304 | tf_op jit(solution)/shard_map/pallas_call | solution.py:412
  46.9 4.9 %collective-permute-start.5 = (f32[16,128]{1,0:T(8,128)S(1)}, f32[16,128]{1,0:T(8,128)S(1)}, u32[]{:S(2)}, u32[]{:S(2)}) collective-permute-start(f32[16,128]{1,0:T(8,128)S(1)} %shard_map.98.wall), channel_id=1, source_target_pairs={{0,64},{64,128},{128,192},{192,256},{256,320},{320,384},{384,448},... | collective-permute-start | bytes 24584 | tf_op jit(solution)/shard_map/ppermute | solution.py:425
  51.7 0.0 copy-done.10
  51.7 0.1 copy.10.heating
  51.8 0.0 copy-done.4
  51.8 0.0 copy-done.6
  51.8 0.0 copy-done.7
  51.8 0.0 copy-done.8
  51.9 1.7 %shard_map.99 = (f32[5,16,1024]{2,1,0:T(8,128)S(1)}, s32[5,8,128]{2,1,0:T(8,128)S(1)}) custom-call(s32[16,128]{1,0:T(8,128)S(1)} %bitcast.3, s32[16,128]{1,0:T(8,128)S(1)} %bitcast.4, f32[16,2048]{1,0:T(8,128)S(1)} %copy-done.4, f32[16,16]{1,0:T(8,128)S(1)} %copy-done.8, f32[16,1]{1,0:T(8,128)S(1)} %copy.10.heating), custom_call_target="tpu_custom_call" | custom-call | bytes 8388608 | tf_op jit(solution)/shard_map/pallas_call | solution.py:388
  53.6 0.0 collective-permute-done.5.earlier
  53.6 0.2 shard_map.100
  53.8 8.1 %collective-permute-start.6 = (f32[16,1024]{1,0:T(8,128)S(1)}, f32[16,1024]{1,0:T(8,128)S(1)}, u32[]{:S(2)}, u32[]{:S(2)}) collective-permute-start(f32[16,1024]{1,0:T(8,128)S(1)} %get-tuple-element.23), channel_id=1, source_target_pairs={{0,62},{1,63},{2,0},{3,1},{4,2},{5,3},{6,4},{7,5},{8,6},{9,7},{10,... | collective-permute-start | bytes 196616 | tf_op jit(solution)/shard_map/ppermute | solution.py:372
  61.9 0.0 collective-permute-done.4.recv_rest
  61.9 0.0 copy-done.1
  61.9 0.0 copy-done.3
  61.9 9.7 %shard_map.97 = f32[5,16,32,128]{3,2,1,0:T(8,128)} custom-call(f32[5,16,32,128]{3,2,1,0:T(8,128)S(1)} %copy-done.1, f32[16,32,128]{2,1,0:T(8,128)S(1)} %copy-done.3, f32[28,32,128]{2,1,0:T(8,128)S(1)} %get-tuple-element.17.strips, f32[18,32,128]{2,1,0:T(8,128)S(1)} %collective-permute-done.2.recv_a, f32[18,8,128]{2,1,0:T(8,128)S(1)} %collective-permute-done.3.recv_wall, ...), custom_call_target="tpu_custom_call" | custom-call | bytes 20971520 | tf_op jit(solution)/shard_map/pallas_call | solution.py:436
  71.6 5.9 %collective-permute-start.7 = (f32[16,1024]{1,0:T(8,128)S(1)}, f32[16,1024]{1,0:T(8,128)S(1)}, u32[]{:S(2)}, u32[]{:S(2)}) collective-permute-start(f32[16,1024]{1,0:T(8,128)S(1)} %get-tuple-element.24), channel_id=1, source_target_pairs={{0,63},{1,0},{2,1},{3,2},{4,3},{5,4},{6,5},{7,6},{8,7},{9,8},{10,9... | collective-permute-start | bytes 196616 | tf_op jit(solution)/shard_map/ppermute | solution.py:372
  77.5 2.2 %collective-permute-start.8 = (f32[16,1024]{1,0:T(8,128)S(1)}, f32[16,1024]{1,0:T(8,128)S(1)}, u32[]{:S(2)}, u32[]{:S(2)}) collective-permute-start(f32[16,1024]{1,0:T(8,128)S(1)} %get-tuple-element.26), channel_id=1, source_target_pairs={{0,1},{1,2},{2,3},{3,4},{4,5},{5,6},{6,7},{7,8},{8,9},{9,10},{10,1... | collective-permute-start | bytes 196616 | tf_op jit(solution)/shard_map/ppermute | solution.py:372
  79.7 3.1 %collective-permute-start.9 = (f32[16,1024]{1,0:T(8,128)S(1)}, f32[16,1024]{1,0:T(8,128)S(1)}, u32[]{:S(2)}, u32[]{:S(2)}) collective-permute-start(f32[16,1024]{1,0:T(8,128)S(1)} %get-tuple-element.27), channel_id=1, source_target_pairs={{0,2},{1,3},{2,4},{3,5},{4,6},{5,7},{6,8},{7,9},{8,10},{9,11},{10,... | collective-permute-start | bytes 196616 | tf_op jit(solution)/shard_map/ppermute | solution.py:372
  82.8 0.0 collective-permute-done.6
  82.8 0.0 collective-permute-done.7
  82.9 5.7 %collective-permute-done.8 = f32[16,1024]{1,0:T(8,128)S(1)} collective-permute-done((f32[16,1024]{1,0:T(8,128)S(1)}, f32[16,1024]{1,0:T(8,128)S(1)}, u32[]{:S(2)}, u32[]{:S(2)}) %collective-permute-start.8) | collective-permute-done | bytes 65568 | tf_op jit(solution)/shard_map/ppermute | solution.py:372
  88.5 1.5 %collective-permute-done.9 = f32[16,1024]{1,0:T(8,128)S(1)} collective-permute-done((f32[16,1024]{1,0:T(8,128)S(1)}, f32[16,1024]{1,0:T(8,128)S(1)}, u32[]{:S(2)}, u32[]{:S(2)}) %collective-permute-start.9) | collective-permute-done | bytes 65568 | tf_op jit(solution)/shard_map/ppermute | solution.py:372
  90.0 0.7 copy-done.9
  (6 shorter events, 0.0 us)
Async XLA Ops:
  0.6 1.3 %copy-start = (f32[5,16,32,128]{3,2,1,0:T(8,128)S(1)}, f32[5,16,32,128]{3,2,1,0:T(8,128)}, u32[]{:S(2)}) copy-start(f32[5,16,32,128]{3,2,1,0:T(8,128)} %gas.7) | copy-start | bytes 3932164
  1.9 0.9 %copy-start.2 = (f32[16,32,128]{2,1,0:T(8,128)S(1)}, f32[16,32,128]{2,1,0:T(8,128)}, u32[]{:S(2)}) copy-start(f32[16,32,128]{2,1,0:T(8,128)} %kappa.7) | copy-start | bytes 786436
  2.9 38.5 %copy-start.5 = (f32[5,5]{1,0:T(8,128)S(1)}, f32[5,5]{1,0:T(8,128)}, u32[]{:S(2)}) copy-start(f32[5,5]{1,0:T(8,128)} %reaction.3) | copy-start | bytes 304
  3.7 13.7 %collective-permute-start = (f32[3,32,128]{2,1,0:T(8,128)S(1)}, f32[3,32,128]{2,1,0:T(8,128)S(1)}, u32[]{:S(2)}, u32[]{:S(2)}) collective-permute-start(f32[3,32,128]{2,1,0:T(8,128)S(1)} %get-tuple-element.15.to_right), channel_id=1, source_target_pairs={{0,1},{1,2},{2,3},{3,4},{4,5},{5,6},{6,7},{7,8},{8,9},{9,10},{10,1... | collective-permute-start | bytes 147464 | tf_op jit(solution)/shard_map/ppermute | solution.py:372
  8.1 10.4 %collective-permute-start.1 = (f32[3,32,128]{2,1,0:T(8,128)S(1)}, f32[3,32,128]{2,1,0:T(8,128)S(1)}, u32[]{:S(2)}, u32[]{:S(2)}) collective-permute-start(f32[3,32,128]{2,1,0:T(8,128)S(1)} %get-tuple-element.16.to_left), channel_id=1, source_target_pairs={{0,63},{1,0},{2,1},{3,2},{4,3},{5,4},{6,5},{7,6},{8,7},{9,8},{10,9... | collective-permute-start | bytes 147464 | tf_op jit(solution)/shard_map/ppermute | solution.py:372
  19.4 32.4 %copy-start.10 = (f32[16]{0:T(128)S(1)}, f32[16]{0:T(128)}, u32[]{:S(2)}) copy-start(f32[16]{0:T(128)} %param.13) | copy-start | bytes 196
  19.4 32.4 %copy-start.4 = (f32[16,2048]{1,0:T(8,128)S(1)}, f32[16,2048]{1,0:T(8,128)}, u32[]{:S(2)}) copy-start(f32[16,2048]{1,0:T(8,128)} %particles.1) | copy-start | bytes 393220
  19.4 32.4 %copy-start.6 = (s32[2048,1]{0,1:T(1,128)S(1)}, s32[2048,1]{0,1:T(1,128)}, u32[]{:S(2)}) copy-start(s32[2048,1]{0,1:T(1,128)} %param.15) | copy-start | bytes 24580
  19.4 32.4 %copy-start.7 = (s32[2048]{0:T(1024)S(1)}, s32[2048]{0:T(1024)}, u32[]{:S(2)}) copy-start(s32[2048]{0:T(1024)} %param.14) | copy-start | bytes 24580
  19.4 32.4 %copy-start.8 = (f32[16,16]{1,0:T(8,128)S(1)}, f32[16,16]{1,0:T(8,128)}, u32[]{:S(2)}) copy-start(f32[16,16]{1,0:T(8,128)} %mixing.1) | copy-start | bytes 3076
  19.4 21.9 %collective-permute-start.2 = (f32[18,32,128]{2,1,0:T(8,128)S(1)}, f32[18,32,128]{2,1,0:T(8,128)S(1)}, u32[]{:S(2)}, u32[]{:S(2)}) collective-permute-start(f32[18,32,128]{2,1,0:T(8,128)S(1)} %get-tuple-element.18), channel_id=1, source_target_pairs={{0,64},{128,192},{256,320},{384,448},{64,0},{192,128},{320,256},{4... | collective-permute-start | bytes 884744 | tf_op jit(solution)/shard_map/ppermute | solution.py:378
  27.2 34.7 %collective-permute-start.4 = (f32[18,24,128]{2,1,0:T(8,128)S(1)}, f32[18,24,128]{2,1,0:T(8,128)S(1)}, u32[]{:S(2)}, u32[]{:S(2)}) collective-permute-start(f32[18,24,128]{2,1,0:T(8,128)S(1)} %get-tuple-element.20), channel_id=1, source_target_pairs={{64,128},{192,256},{320,384},{128,64},{256,192},{384,320},{65,129}... | collective-permute-start | bytes 663560 | tf_op jit(solution)/shard_map/ppermute | solution.py:378
  31.7 9.6 %collective-permute-start.3 = (f32[18,8,128]{2,1,0:T(8,128)S(1)}, f32[18,8,128]{2,1,0:T(8,128)S(1)}, u32[]{:S(2)}, u32[]{:S(2)}) collective-permute-start(f32[18,8,128]{2,1,0:T(8,128)S(1)} %get-tuple-element.19), channel_id=1, source_target_pairs={{64,128},{192,256},{320,384},{128,64},{256,192},{384,320},{65,129}... | collective-permute-start | bytes 221192 | tf_op jit(solution)/shard_map/ppermute | solution.py:378
  41.4 20.5 %copy-start.1 = (f32[5,16,32,128]{3,2,1,0:T(8,128)S(1)}, f32[5,16,32,128]{3,2,1,0:T(8,128)}, u32[]{:S(2)}) copy-start(f32[5,16,32,128]{3,2,1,0:T(8,128)} %gas.7) | copy-start | bytes 3932164
  41.4 20.5 %copy-start.3 = (f32[16,32,128]{2,1,0:T(8,128)S(1)}, f32[16,32,128]{2,1,0:T(8,128)}, u32[]{:S(2)}) copy-start(f32[16,32,128]{2,1,0:T(8,128)} %kappa.7) | copy-start | bytes 786436
  46.9 6.7 %collective-permute-start.5 = (f32[16,128]{1,0:T(8,128)S(1)}, f32[16,128]{1,0:T(8,128)S(1)}, u32[]{:S(2)}, u32[]{:S(2)}) collective-permute-start(f32[16,128]{1,0:T(8,128)S(1)} %shard_map.98.wall), channel_id=1, source_target_pairs={{0,64},{64,128},{128,192},{192,256},{256,320},{320,384},{384,448},... | collective-permute-start | bytes 24584 | tf_op jit(solution)/shard_map/ppermute | solution.py:425
  53.8 29.0 %collective-permute-start.6 = (f32[16,1024]{1,0:T(8,128)S(1)}, f32[16,1024]{1,0:T(8,128)S(1)}, u32[]{:S(2)}, u32[]{:S(2)}) collective-permute-start(f32[16,1024]{1,0:T(8,128)S(1)} %get-tuple-element.23), channel_id=1, source_target_pairs={{0,62},{1,63},{2,0},{3,1},{4,2},{5,3},{6,4},{7,5},{8,6},{9,7},{10,... | collective-permute-start | bytes 196616 | tf_op jit(solution)/shard_map/ppermute | solution.py:372
  71.6 11.2 %collective-permute-start.7 = (f32[16,1024]{1,0:T(8,128)S(1)}, f32[16,1024]{1,0:T(8,128)S(1)}, u32[]{:S(2)}, u32[]{:S(2)}) collective-permute-start(f32[16,1024]{1,0:T(8,128)S(1)} %get-tuple-element.24), channel_id=1, source_target_pairs={{0,63},{1,0},{2,1},{3,2},{4,3},{5,4},{6,5},{7,6},{8,7},{9,8},{10,9... | collective-permute-start | bytes 196616 | tf_op jit(solution)/shard_map/ppermute | solution.py:372
  77.5 11.0 %collective-permute-start.8 = (f32[16,1024]{1,0:T(8,128)S(1)}, f32[16,1024]{1,0:T(8,128)S(1)}, u32[]{:S(2)}, u32[]{:S(2)}) collective-permute-start(f32[16,1024]{1,0:T(8,128)S(1)} %get-tuple-element.26), channel_id=1, source_target_pairs={{0,1},{1,2},{2,3},{3,4},{4,5},{5,6},{6,7},{7,8},{8,9},{9,10},{10,1... | collective-permute-start | bytes 196616 | tf_op jit(solution)/shard_map/ppermute | solution.py:372
  79.7 10.3 %collective-permute-start.9 = (f32[16,1024]{1,0:T(8,128)S(1)}, f32[16,1024]{1,0:T(8,128)S(1)}, u32[]{:S(2)}, u32[]{:S(2)}) collective-permute-start(f32[16,1024]{1,0:T(8,128)S(1)} %get-tuple-element.27), channel_id=1, source_target_pairs={{0,2},{1,3},{2,4},{3,5},{4,6},{5,7},{6,8},{7,9},{8,10},{9,11},{10,... | collective-permute-start | bytes 196616 | tf_op jit(solution)/shard_map/ppermute | solution.py:372
  90.0 0.7 copy-start.9

commit v2 on v1

--- a/solution.py
+++ b/solution.py
@@ -29,6 +29,8 @@
 
 VMEM = pl.BlockSpec(memory_space=pltpu.VMEM)
 SMEM = pl.BlockSpec(memory_space=pltpu.SMEM)
+ANY = pl.BlockSpec(memory_space=pl.ANY)
+HBM = pl.BlockSpec(memory_space=pltpu.HBM)
 
 
 def f32(*shape):
@@ -51,37 +53,45 @@
     return slice(8 * tile, 8 * tile + 8)
 
 
-def call(kernel, outs, scratch=(), specs=None, flops=0, moved=0, limit=16):
+def call(kernel, outs, scratch=(), specs=None, out_specs=None, flops=0, moved=0, limit=16):
     return pl.pallas_call(
         kernel,
         out_shape=outs,
         in_specs=specs,
-        out_specs=jax.tree.map(lambda _: VMEM, outs),
+        out_specs=jax.tree.map(lambda _: VMEM, outs) if out_specs is None else out_specs,
         scratch_shapes=list(scratch),
         cost_estimate=pl.CostEstimate(flops=flops, bytes_accessed=moved, transcendentals=0),
-        compiler_params=pltpu.CompilerParams(vmem_limit_bytes=limit << 20),
+        compiler_params=pltpu.CompilerParams(vmem_limit_bytes=int(limit * 2**20)),
     )
 
 
-def edges_kernel(gas, kappa, to_right, to_left):
+def edges_kernel(gas, kappa, to_right, to_left, held, arrived):
+    copies = [pltpu.make_async_copy(gas.at[q], held.at[q], arrived.at[q]) for q in range(COMP)]
+    copies.append(pltpu.make_async_copy(kappa, held.at[COMP], arrived.at[COMP]))
+    for copy in copies:
+        copy.start()
     lane = lanes()
     within = lane & 63
     depth, cell = within >> 4, within & 15
     high = jnp.maximum(6 * cell + 2 - depth, 0)
     low = 6 * cell + 3 + depth
-    for tile in range(TILES):
-        packed = [jnp.zeros((8, 128), jnp.float32) for _ in range(COMP + 1)]
-        for x in range(GX):
-            here = (lane >= 6 * x) & (lane < 6 * x + 6)
-            for q in range(COMP + 1):
-                slab = gas[q, x, rows(tile), :] if q < COMP else kappa[x, rows(tile), :]
-                packed[q] = jnp.where(here, pltpu.roll(slab, 6 * x + 3, 1), packed[q])
-        for s in range((COMP + 1) // 2):
+    for pair in range((COMP + 1) // 2):
+        packed = {}
+        for q in (2 * pair, 2 * pair + 1):
+            copies[q].wait()
+            for tile in range(TILES):
+                total = jnp.zeros((8, 128), jnp.float32)
+                for x in range(GX):
+                    here = (lane >= 6 * x) & (lane < 6 * x + 6)
+                    total = jnp.where(here, pltpu.roll(held[q, x, rows(tile), :], 6 * x + 3, 1), total)
+                packed[q, tile] = total
+        for tile in range(TILES):
+            first, second = packed[2 * pair, tile], packed[2 * pair + 1, tile]
             for out, index in ((to_right, high), (to_left, low)):
-                out[s, rows(tile), :] = jnp.where(lane < 64, pick(packed[2 * s], index), pick(packed[2 * s + 1], index))
-
-
-def strips_kernel(gas, kappa, to_right, to_left, from_left, from_right, strips, send_a, send_wall, send_rest):
+                out[pair, rows(tile), :] = jnp.where(lane < 64, pick(first, index), pick(second, index))
+
+
+def strips_kernel(gas, kappa, to_right, to_left, from_left, from_right, strips, send_a, send_wall):
     lane = lanes()
     low_side = (lane & 1) == 1
     cell = jnp.clip((lane >> 1) - 3, 0, GX - 1)
@@ -105,10 +115,7 @@
         for_a = jnp.where(even, top, bottom)
         for_b = jnp.where(even, bottom, top)
         send_a[LAYERS - 1, rows(tile), :] = for_a
-        if tile == TILES - 1:
-            send_wall[LAYERS - 1] = for_b
-        else:
-            send_rest[LAYERS - 1, rows(tile), :] = for_b
+        send_wall[LAYERS - 1 + tile] = for_b
     at_a, at_b = jnp.where(even, GX - 3, 0), jnp.where(even, 0, GX - 3)
     kappa_a, kappa_b = jnp.where(even, GX - 2, 0), jnp.where(even, 0, GX - 2)
     split = GR - 8
@@ -116,11 +123,20 @@
         for layer in range(3):
             send_a[3 * c + layer] = gas[c, at_a + layer]
             send_wall[3 * c + layer] = gas[c, at_b + layer, split:, :]
-            send_rest[3 * c + layer] = gas[c, at_b + layer, :split, :]
     for layer in range(2):
         send_a[3 * COMP + layer] = kappa[kappa_a + layer]
         send_wall[3 * COMP + layer] = kappa[kappa_b + layer, split:, :]
-        send_rest[3 * COMP + layer] = kappa[kappa_b + layer, :split, :]
+
+
+def rest_kernel(gas, kappa, _, send_rest):
+    even = lax.rem(lax.axis_index("sect"), 2) == 0
+    split = GR - 8
+    from_b, from_kappa = jnp.where(even, 0, GX - 3), jnp.where(even, 0, GX - 2)
+    for c in range(COMP):
+        for layer in range(3):
+            send_rest[3 * c + layer] = gas[c, from_b + layer, :split, :]
+    for layer in range(2):
+        send_rest[3 * COMP + layer] = kappa[from_kappa + layer, :split, :]
 
 
 def coupling(reaction):
@@ -203,7 +219,7 @@
     return out
 
 
-def steps(count, wall_only, now, later, kappa, edge, mix, finish):
+def steps(count, wall_only, now, later, kappa, edge, mix, finish, unroll):
     for step in range(ITERS):
         src, dst = (now, later) if step % 2 == 0 else (later, now)
         final = step == ITERS - 1
@@ -218,7 +234,11 @@
                     dst[c, at, rows(t), :] = value
             return carry
 
-        lax.fori_loop(step + 1, EXT - 1 - step, body, 0)
+        if unroll is None:
+            for at in range(step + 1, EXT - 1 - step):
+                body(at, 0)
+        else:
+            lax.fori_loop(step + 1, EXT - 1 - step, body, 0, unroll=unroll)
 
 
 def wall_kernel(gas, kappa, strips, recv_a, recv_wall, reaction, wall, now, later, kap, edge):
@@ -239,17 +259,18 @@
     for layer in range(2):
         kap[kappa_a + layer] = recv_a[3 * COMP + layer, top, :]
         kap[kappa_b + layer] = recv_wall[3 * COMP + layer]
-    corner_a, corner_b = recv_a[LAYERS - 1, top, :], recv_wall[LAYERS - 1]
+    corner_a, corner_b = recv_a[LAYERS - 1, top, :], recv_wall[LAYERS + TILES - 2]
     low, high = jnp.where(even, corner_b, corner_a), jnp.where(even, corner_a, corner_b)
     strip_levels(strips, [low], [high], mix, edge, [TILES - 1])
 
     def finish(at, out):
-        wall[pl.ds(at - 3, 1), :] = out[0, 0][7:8, :]
-
-    steps(1, True, now, later, kap, edge, mix, finish)
-
-
-def gas_kernel(gas, kappa, strips, recv_a, recv_wall, recv_rest, reaction, result, now, later, kap, edge):
+        wall[at - 3 : at - 2, :] = out[0, 0][7:8, :]
+
+    steps(1, True, now, later, kap, edge, mix, finish, unroll=None)
+
+
+def gas_kernel(gas, kappa, strips, recv_a, recv_wall, recv_rest, reaction, _, result, token, now, later, kap, edge):
+    token[...] = jnp.zeros((8, 128), jnp.float32)
     odd = lax.rem(lax.axis_index("sect"), 2)
     even = odd == 0
     mix = coupling(reaction)
@@ -270,7 +291,7 @@
     low, high = [], []
     for t in range(TILES):
         corner_a = recv_a[LAYERS - 1, rows(t), :]
-        corner_b = recv_wall[LAYERS - 1] if t == TILES - 1 else recv_rest[LAYERS - 1, rows(t), :]
+        corner_b = recv_wall[LAYERS - 1 + t]
         low.append(jnp.where(even, corner_b, corner_a))
         high.append(jnp.where(even, corner_a, corner_b))
     strip_levels(strips, low, high, mix, edge, list(range(TILES)))
@@ -279,10 +300,10 @@
         for (c, t), value in out.items():
             result[c, at - 3, rows(t), :] = value
 
-    steps(TILES, False, now, later, kap, edge, mix, finish)
-
-
-def pack_kernel(hop, cell, particles, mixing, heating, packed, cells, spread, ordered, source, begin, end):
+    steps(TILES, False, now, later, kap, edge, mix, finish, unroll=2)
+
+
+def pack_kernel(hop, cell, particles, mixing, heating, _, packed, cells, spread, ordered, source, begin, end):
     lane = lanes()
     square = (128, 128)
     down, across = lax.broadcasted_iota(jnp.int32, square, 0), lanes(square)
@@ -367,6 +388,17 @@
             outs[j][:, part] = packed[j, :, part] + heat * look[j, spot : spot + 1, :]
 
 
+def join_kernel(*refs):
+    pieces, out, done = refs[:MOVES], refs[MOVES + 1], refs[MOVES + 2]
+    copies = [
+        pltpu.make_async_copy(piece, out.at[:, j * CAP : (j + 1) * CAP], done.at[j]) for j, piece in enumerate(pieces)
+    ]
+    for copy in copies:
+        copy.start()
+    for copy in copies:
+        copy.wait()
+
+
 def ring(x, axis, by):
     size = lax.axis_size(axis)
     return lax.ppermute(x, axis, [(i, (i + by) % size) for i in range(size)])
@@ -380,33 +412,26 @@
 
 def local(gas, kappa, reaction, particles, mixing, heating, wall_cell, tile_hop):
     strip_shape = (3, GR, GA)
-    to_right, to_left = call(edges_kernel, (f32(*strip_shape), f32(*strip_shape)), specs=[VMEM] * 2, moved=2 << 20)(gas, kappa)
+    to_right, to_left = call(
+        edges_kernel,
+        (f32(*strip_shape), f32(*strip_shape)),
+        scratch=[pltpu.VMEM((COMP + 1, GX, GR, GA), jnp.float32), pltpu.SemaphoreType.DMA((COMP + 1,))],
+        specs=[HBM] * 2,
+        moved=2 << 20,
+        limit=53.75,
+    )(gas, kappa)
     from_left = ring(to_right, "blk", 1)
     from_right = ring(to_left, "blk", -1)
 
-    heating_column = heating.reshape(VALS, 1)
-    packed, cells = call(
-        pack_kernel,
-        (f32(MOVES, VALS, CAP), i32(MOVES, SPOTS, 128)),
-        scratch=[
-            pltpu.VMEM((VALS, VALS, 128), jnp.float32),
-            pltpu.VMEM((CHUNKS, 24, 128), jnp.float32),
-            pltpu.VMEM((MOVES * CHUNKS, 128), jnp.int32),
-            pltpu.VMEM((MOVES * CHUNKS, 128), jnp.int32),
-            pltpu.VMEM((MOVES * CHUNKS, 128), jnp.int32),
-        ],
-        specs=[VMEM] * 5,
-        moved=8 << 20,
-    )(tile_hop.reshape(CHUNKS, 128), wall_cell.reshape(CHUNKS, 128), particles, mixing, heating_column)
-
-    strips, send_a, send_wall, send_rest = call(
+    strips, send_a, send_wall = call(
         strips_kernel,
-        (f32(len(STRIPS), GR, GA), f32(LAYERS, GR, GA), f32(LAYERS, 8, GA), f32(LAYERS, GR - 8, GA)),
+        (f32(len(STRIPS), GR, GA), f32(LAYERS, GR, GA), f32(LAYERS - 1 + TILES, 8, GA)),
         specs=[VMEM] * 6,
         moved=2 << 20,
     )(gas, kappa, to_right, to_left, from_left, from_right)
     recv_wall = swap(send_wall, "sect", 1)
     recv_a = swap(send_a, "sect", 0)
+    send_rest = call(rest_kernel, f32(LAYERS - 1, GR - 8, GA), specs=[VMEM] * 2 + [ANY], moved=1 << 20)(gas, kappa, recv_wall)
     recv_rest = swap(send_rest, "sect", 1)
 
     wall = call(
@@ -421,6 +446,20 @@
         specs=[VMEM] * 5 + [SMEM],
         moved=4 << 20,
     )(gas, kappa, strips, recv_a, recv_wall, reaction)
+    heating_column = heating.reshape(VALS, 1)
+    packed, cells = call(
+        pack_kernel,
+        (f32(MOVES, VALS, CAP), i32(MOVES, SPOTS, 128)),
+        scratch=[
+            pltpu.VMEM((VALS, VALS, 128), jnp.float32),
+            pltpu.VMEM((CHUNKS, 24, 128), jnp.float32),
+            pltpu.VMEM((MOVES * CHUNKS, 128), jnp.int32),
+            pltpu.VMEM((MOVES * CHUNKS, 128), jnp.int32),
+            pltpu.VMEM((MOVES * CHUNKS, 128), jnp.int32),
+        ],
+        specs=[VMEM] * 5 + [ANY],
+        moved=4 << 20,
+    )(tile_hop.reshape(CHUNKS, 128), wall_cell.reshape(CHUNKS, 128), particles, mixing, heating_column, wall)
     size = lax.axis_size("sect")
     earlier = lax.ppermute(wall, "sect", [(i, i + 1) for i in range(size - 1)])
 
@@ -433,19 +472,27 @@
     )(wall, earlier, packed, cells, heating_column)
     pieces = [block if j == REACH else ring(block, "blk", j - REACH) for j, block in enumerate(blocks)]
 
-    field = call(
+    field, token = call(
         gas_kernel,
-        f32(COMP, GX, GR, GA),
+        (f32(COMP, GX, GR, GA), f32(8, 128)),
         scratch=[
             pltpu.VMEM((COMP, EXT, GR, GA), jnp.float32),
             pltpu.VMEM((COMP, EXT, GR, GA), jnp.float32),
             pltpu.VMEM((EXT, GR, GA), jnp.float32),
             pltpu.VMEM((ITERS, COMP, GR, GA), jnp.float32),
         ],
-        specs=[VMEM] * 6 + [SMEM],
+        specs=[VMEM] * 6 + [SMEM, ANY],
         moved=20 << 20,
-    )(gas, kappa, strips, recv_a, recv_wall, recv_rest, reaction)
-    return field, jnp.concatenate(pieces, axis=1)
+    )(gas, kappa, strips, recv_a, recv_wall, recv_rest, reaction, pieces[0])
+    arrived = call(
+        join_kernel,
+        f32(VALS, MOVES * CAP),
+        scratch=[pltpu.SemaphoreType.DMA((MOVES,))],
+        specs=[VMEM] * MOVES + [ANY],
+        out_specs=HBM,
+        moved=1 << 20,
+    )(*pieces, token)
+    return field, arrived
 
 
 def solution(mesh):

time: 91.2 us -> 75.8 us (0.83)
  waiting for transfers between devices: 13 us -> 6.99 us
  Pallas kernels: 18.8 us -> 14.8 us
  local copies, waits for them, and re-layouts: 3.14 us -> 0.13 us
  starting transfers between devices: 54.9 us -> 52.7 us
    ppermute x6, waiting for transfers between devices: 8.3 us -> 1.86 us  [ring(): return lax.ppermute(x, axis, [(i, (i + by) % size) for i in range(size)])]
    pallas_call x1, Pallas kernels: 5.49 us -> 1.45 us  [local(): call(wall_kernel, f32(GX, GA), scratch=[pltpu.VMEM((COMP, EXT, 8, GA), jn...]
    unnamed x26 -> x16, local copies, waits for them, and re-layouts: 3.05 us -> 0.05 us
    ppermute x6, starting transfers between devices: 32.9 us -> 30.9 us  [ring(): return lax.ppermute(x, axis, [(i, (i + by) % size) for i in range(size)])]
    pallas_call x2 -> x4, Pallas kernels: 10.6 us -> 10.6 us  [the longest x1 7.63 us: local(): call(gas_kernel, (f32(COMP, GX, GR, GA), f32(8, 128)), scratch=[pltpu.VME...]
  transfers between devices with their start and end apart: 10 -> 10, of which waited for: 4 -> 3; matrix products, arithmetic and copies ran while one was open for 0% -> 0% of each run, Pallas kernels for 19% -> 15%
where the time goes in v2:
time: 75.8 us; the launch traced here: 75.5 us
  starting transfers between devices  52.7 us (70%)
  Pallas kernels  14.8 us (20%)
  waiting for transfers between devices  6.99 us (9%)
  between operations  0.88 us (1%)
    ppermute x6, starting transfers between devices, ring(): return lax.ppermute(x, axis, [(i, (i + by) % size) for i in range(size)])  30.9 us
    ppermute x3, starting transfers between devices, swap(): return lax.ppermute(x, axis, pairs + [(j, i) for i, j in pairs])  16.9 us
    pallas_call x1, Pallas kernels, local(): call(gas_kernel, (f32(COMP, GX, GR, GA), f32(8, 128)), scratch=[pltpu.VME...  7.63 us
    ppermute x3, waiting for transfers between devices, swap(): return lax.ppermute(x, axis, pairs + [(j, i) for i, j in pairs])  5.13 us
    ppermute x1, starting transfers between devices, local(): earlier = lax.ppermute(wall, 'sect', [(i, i + 1) for i in range(size - 1)])  4.89 us
    pallas_call x1, Pallas kernels, local(): call(edges_kernel, (f32(*strip_shape), f32(*strip_shape)), scratch=[pltpu...  2.18 us
    ppermute x6, waiting for transfers between devices, ring(): return lax.ppermute(x, axis, [(i, (i + by) % size) for i in range(size)])  1.86 us
    pallas_call x1, Pallas kernels, local(): call(pack_kernel, (f32(MOVES, VALS, CAP), i32(MOVES, SPOTS, 128)), scratc...  1.74 us
  transfers between devices with their start and end apart: 10, of which 3 were waited for; matrix products, arithmetic and copies ran while one was open for 0% of the time, Pallas kernels for 15%

profile of v2, /device:TPU:1, one launch (start us, length us, event | category | flops | bytes accessed | tf_op | source)
XLA Modules:
  0.0 75.5 jit_solution(3083641461694741911)
XLA Ops:
  0.6 0.0 copy-start.1
  0.6 0.0 copy-start
  0.6 2.2 %shard_map.95 = (f32[3,32,128]{2,1,0:T(8,128)S(1)}, f32[3,32,128]{2,1,0:T(8,128)S(1)}) custom-call(f32[5,16,32,128]{3,2,1,0:T(8,128)} %gas.9, f32[16,32,128]{2,1,0:T(8,128)} %kappa.9), custom_call_target="tpu_custom_call" | custom-call | bytes 2097152 | tf_op jit(solution)/shard_map/pallas_call | solution.py:415
  2.8 4.4 %collective-permute-start = (f32[3,32,128]{2,1,0:T(8,128)S(1)}, f32[3,32,128]{2,1,0:T(8,128)S(1)}, u32[]{:S(2)}, u32[]{:S(2)}) collective-permute-start(f32[3,32,128]{2,1,0:T(8,128)S(1)} %get-tuple-element.16.to_right), channel_id=1, source_target_pairs={{0,1},{1,2},{2,3},{3,4},{4,5},{5,6},{6,7},{7,8},{8,9},{9,10},{10,1... | collective-permute-start | bytes 147464 | tf_op jit(solution)/shard_map/ppermute | solution.py:404
  7.2 9.3 %collective-permute-start.1 = (f32[3,32,128]{2,1,0:T(8,128)S(1)}, f32[3,32,128]{2,1,0:T(8,128)S(1)}, u32[]{:S(2)}, u32[]{:S(2)}) collective-permute-start(f32[3,32,128]{2,1,0:T(8,128)S(1)} %get-tuple-element.17.to_left), channel_id=1, source_target_pairs={{0,63},{1,0},{2,1},{3,2},{4,3},{5,4},{6,5},{7,6},{8,7},{9,8},{10,9... | collective-permute-start | bytes 147464 | tf_op jit(solution)/shard_map/ppermute | solution.py:404
  16.5 0.0 collective-permute-done.from_left
  16.5 1.1 %collective-permute-done.1.from_right = f32[3,32,128]{2,1,0:T(8,128)S(1)} collective-permute-done((f32[3,32,128]{2,1,0:T(8,128)S(1)}, f32[3,32,128]{2,1,0:T(8,128)S(1)}, u32[]{:S(2)}, u32[]{:S(2)}) %collective-permute-start.1) | collective-permute-done | bytes 49184 | tf_op jit(solution)/shard_map/ppermute | solution.py:404
  17.7 0.0 copy-done.1
  17.7 0.0 copy-done
  17.7 0.8 %shard_map.96 = (f32[28,32,128]{2,1,0:T(8,128)S(1)}, f32[18,32,128]{2,1,0:T(8,128)S(1)}, f32[21,8,128]{2,1,0:T(8,128)S(1)}) custom-call(f32[5,16,32,128]{3,2,1,0:T(8,128)S(1)} %copy-done, f32[16,32,128]{2,1,0:T(8,128)S(1)} %copy-done.1, f32[3,32,128]{2,1,0:T(8,128)S(1)} %get-tuple-element.16.to_right, f32[3,32,128]{2,1,0:T(8,128)S(1)} %get-tuple-element.17.to_left, ...), custom_call_target="tpu_custom_call" | custom-call | bytes 2097152 | tf_op jit(solution)/shard_map/pallas_call | solution.py:426
  18.5 0.0 copy-start.3
  18.5 7.6 %collective-permute-start.2 = (f32[18,32,128]{2,1,0:T(8,128)S(1)}, f32[18,32,128]{2,1,0:T(8,128)S(1)}, u32[]{:S(2)}, u32[]{:S(2)}) collective-permute-start(f32[18,32,128]{2,1,0:T(8,128)S(1)} %get-tuple-element.19), channel_id=1, source_target_pairs={{0,64},{128,192},{256,320},{384,448},{64,0},{192,128},{320,256},{4... | collective-permute-start | bytes 884744 | tf_op jit(solution)/shard_map/ppermute | solution.py:410
  26.1 4.6 %collective-permute-start.3 = (f32[21,8,128]{2,1,0:T(8,128)S(1)}, f32[21,8,128]{2,1,0:T(8,128)S(1)}, u32[]{:S(2)}, u32[]{:S(2)}) collective-permute-start(f32[21,8,128]{2,1,0:T(8,128)S(1)} %get-tuple-element.20), channel_id=1, source_target_pairs={{64,128},{192,256},{320,384},{128,64},{256,192},{384,320},{65,129}... | collective-permute-start | bytes 258056 | tf_op jit(solution)/shard_map/ppermute | solution.py:410
  30.7 5.1 %collective-permute-done.3._.recv_wall = f32[21,8,128]{2,1,0:T(8,128)S(1)} collective-permute-done((f32[21,8,128]{2,1,0:T(8,128)S(1)}, f32[21,8,128]{2,1,0:T(8,128)S(1)}, u32[]{:S(2)}, u32[]{:S(2)}) %collective-permute-start.3) | collective-permute-done | bytes 86048 | tf_op jit(solution)/shard_map/ppermute | solution.py:410
  35.8 0.0 copy-start.7
  35.8 0.0 copy-start.2
  35.9 0.0 copy-start.4
  35.9 0.0 copy-start.5
  35.9 0.0 copy-start.6
  35.9 4.7 %collective-permute-start.4 = (f32[17,24,128]{2,1,0:T(8,128)S(1)}, f32[17,24,128]{2,1,0:T(8,128)S(1)}, u32[]{:S(2)}, u32[]{:S(2)}) collective-permute-start(f32[17,24,128]{2,1,0:T(8,128)S(1)} %shard_map.97), channel_id=1, source_target_pairs={{64,128},{192,256},{320,384},{128,64},{256,192},{384,320},{65,129}... | collective-permute-start | bytes 626696 | tf_op jit(solution)/shard_map/ppermute | solution.py:410
  40.6 0.0 collective-permute-done.2.recv_a
  40.6 0.0 copy-done.3
  40.6 1.4 %shard_map.98._.wall = f32[16,128]{1,0:T(8,128)S(1)} custom-call(f32[5,16,32,128]{3,2,1,0:T(8,128)S(1)} %copy-done, f32[16,32,128]{2,1,0:T(8,128)S(1)} %copy-done.1, f32[28,32,128]{2,1,0:T(8,128)S(1)} %get-tuple-element.18.strips, f32[18,32,128]{2,1,0:T(8,128)S(1)} %collective-permute-done.2.recv_a, f32[21,8,128]{2,1,0:T(8,128)S(1)} %collective-permute-done.3._.recv_wall, ...), custom_call_target="tpu_custom_call" | custom-call | bytes 4194304 | tf_op jit(solution)/shard_map/pallas_call | solution.py:437
  42.1 4.9 %collective-permute-start.5 = (f32[16,128]{1,0:T(8,128)S(1)}, f32[16,128]{1,0:T(8,128)S(1)}, u32[]{:S(2)}, u32[]{:S(2)}) collective-permute-start(f32[16,128]{1,0:T(8,128)S(1)} %shard_map.98._.wall), channel_id=1, source_target_pairs={{0,64},{64,128},{128,192},{192,256},{256,320},{320,384},{384,448},... | collective-permute-start | bytes 24584 | tf_op jit(solution)/shard_map/ppermute | solution.py:464
  47.0 0.0 copy-done.7
  47.0 0.1 copy.10.heating
  47.1 0.0 copy-done.2
  47.1 0.0 copy-done.4
  47.1 0.0 copy-done.5
  47.1 0.0 copy-done.6
  47.1 1.7 %shard_map.99 = (f32[5,16,1024]{2,1,0:T(8,128)S(1)}, s32[5,8,128]{2,1,0:T(8,128)S(1)}) custom-call(s32[16,128]{1,0:T(8,128)S(1)} %bitcast.3, s32[16,128]{1,0:T(8,128)S(1)} %bitcast.4, f32[16,2048]{1,0:T(8,128)S(1)} %copy-done.2, f32[16,16]{1,0:T(8,128)S(1)} %copy-done.6, f32[16,1]{1,0:T(8,128)S(1)} %copy.10.heating, f32[16,128]{1,0:T(8,128)S(1)} %shard_map.98._.wall), custom_call_target="tpu_custom_call" | custom-call | bytes 4194304 | tf_op jit(solution)/shard_map/pallas_call | solution.py:450
  48.8 0.0 collective-permute-done.5.earlier
  48.9 0.2 shard_map.100
  49.1 3.6 %collective-permute-start.6 = (f32[16,1024]{1,0:T(8,128)S(1)}, f32[16,1024]{1,0:T(8,128)S(1)}, u32[]{:S(2)}, u32[]{:S(2)}) collective-permute-start(f32[16,1024]{1,0:T(8,128)S(1)} %get-tuple-element.23), channel_id=1, source_target_pairs={{0,62},{1,63},{2,0},{3,1},{4,2},{5,3},{6,4},{7,5},{8,6},{9,7},{10,... | collective-permute-start | bytes 196616 | tf_op jit(solution)/shard_map/ppermute | solution.py:404
  52.7 8.4 %collective-permute-start.7 = (f32[16,1024]{1,0:T(8,128)S(1)}, f32[16,1024]{1,0:T(8,128)S(1)}, u32[]{:S(2)}, u32[]{:S(2)}) collective-permute-start(f32[16,1024]{1,0:T(8,128)S(1)} %get-tuple-element.25), channel_id=1, source_target_pairs={{0,63},{1,0},{2,1},{3,2},{4,3},{5,4},{6,5},{7,6},{8,7},{9,8},{10,9... | collective-permute-start | bytes 196616 | tf_op jit(solution)/shard_map/ppermute | solution.py:404
  61.0 2.2 %collective-permute-start.8 = (f32[16,1024]{1,0:T(8,128)S(1)}, f32[16,1024]{1,0:T(8,128)S(1)}, u32[]{:S(2)}, u32[]{:S(2)}) collective-permute-start(f32[16,1024]{1,0:T(8,128)S(1)} %get-tuple-element.27), channel_id=1, source_target_pairs={{0,1},{1,2},{2,3},{3,4},{4,5},{5,6},{6,7},{7,8},{8,9},{9,10},{10,1... | collective-permute-start | bytes 196616 | tf_op jit(solution)/shard_map/ppermute | solution.py:404
  63.2 3.1 %collective-permute-start.9 = (f32[16,1024]{1,0:T(8,128)S(1)}, f32[16,1024]{1,0:T(8,128)S(1)}, u32[]{:S(2)}, u32[]{:S(2)}) collective-permute-start(f32[16,1024]{1,0:T(8,128)S(1)} %get-tuple-element.28), channel_id=1, source_target_pairs={{0,2},{1,3},{2,4},{3,5},{4,6},{5,7},{6,8},{7,9},{8,10},{9,11},{10,... | collective-permute-start | bytes 196616 | tf_op jit(solution)/shard_map/ppermute | solution.py:404
  66.3 0.0 collective-permute-done.4.recv_rest
  66.4 0.0 collective-permute-done.6._.refs_0_
  66.4 7.6 %shard_map.101 = (f32[5,16,32,128]{3,2,1,0:T(8,128)}, f32[8,128]{1,0:T(8,128)S(1)}) custom-call(f32[5,16,32,128]{3,2,1,0:T(8,128)S(1)} %copy-done, f32[16,32,128]{2,1,0:T(8,128)S(1)} %copy-done.1, f32[28,32,128]{2,1,0:T(8,128)S(1)} %get-tuple-element.18.strips, f32[18,32,128]{2,1,0:T(8,128)S(1)} %collective-permute-done.2.recv_a, ...), custom_call_target="tpu_custom_call" | custom-call | bytes 20971520 | tf_op jit(solution)/shard_map/pallas_call | solution.py:475
  74.0 0.0 collective-permute-done.7.refs_1_
  74.0 0.0 collective-permute-done.8.refs_3_
  74.0 0.7 collective-permute-done.9.refs_4_
  74.7 0.8 %shard_map.102 = f32[16,5120]{1,0:T(8,128)} custom-call(f32[16,1024]{1,0:T(8,128)S(1)} %collective-permute-done.6._.refs_0_, f32[16,1024]{1,0:T(8,128)S(1)} %collective-permute-done.7.refs_1_, f32[16,1024]{1,0:T(8,128)S(1)} %get-tuple-element.26.refs_2_, f32[16,1024]{1,0:T(8,128)S(1)} %collective-permute-done.8.refs_3_, ...), custom_call_target="tpu_custom_call" | custom-call | bytes 1048576 | tf_op jit(solution)/shard_map/pallas_call | solution.py:487
  (1 shorter events, 0.0 us)
Async XLA Ops:
  0.6 17.0 %copy-start.1 = (f32[16,32,128]{2,1,0:T(8,128)S(1)}, f32[16,32,128]{2,1,0:T(8,128)}, u32[]{:S(2)}) copy-start(f32[16,32,128]{2,1,0:T(8,128)} %kappa.9) | copy-start | bytes 786436
  0.6 17.0 %copy-start = (f32[5,16,32,128]{3,2,1,0:T(8,128)S(1)}, f32[5,16,32,128]{3,2,1,0:T(8,128)}, u32[]{:S(2)}) copy-start(f32[5,16,32,128]{3,2,1,0:T(8,128)} %gas.9) | copy-start | bytes 3932164
  2.8 13.7 %collective-permute-start = (f32[3,32,128]{2,1,0:T(8,128)S(1)}, f32[3,32,128]{2,1,0:T(8,128)S(1)}, u32[]{:S(2)}, u32[]{:S(2)}) collective-permute-start(f32[3,32,128]{2,1,0:T(8,128)S(1)} %get-tuple-element.16.to_right), channel_id=1, source_target_pairs={{0,1},{1,2},{2,3},{3,4},{4,5},{5,6},{6,7},{7,8},{8,9},{9,10},{10,1... | collective-permute-start | bytes 147464 | tf_op jit(solution)/shard_map/ppermute | solution.py:404
  7.2 10.4 %collective-permute-start.1 = (f32[3,32,128]{2,1,0:T(8,128)S(1)}, f32[3,32,128]{2,1,0:T(8,128)S(1)}, u32[]{:S(2)}, u32[]{:S(2)}) collective-permute-start(f32[3,32,128]{2,1,0:T(8,128)S(1)} %get-tuple-element.17.to_left), channel_id=1, source_target_pairs={{0,63},{1,0},{2,1},{3,2},{4,3},{5,4},{6,5},{7,6},{8,7},{9,8},{10,9... | collective-permute-start | bytes 147464 | tf_op jit(solution)/shard_map/ppermute | solution.py:404
  18.5 22.1 %copy-start.3 = (f32[5,5]{1,0:T(8,128)S(1)}, f32[5,5]{1,0:T(8,128)}, u32[]{:S(2)}) copy-start(f32[5,5]{1,0:T(8,128)} %reaction.3) | copy-start | bytes 304
  18.5 22.1 %collective-permute-start.2 = (f32[18,32,128]{2,1,0:T(8,128)S(1)}, f32[18,32,128]{2,1,0:T(8,128)S(1)}, u32[]{:S(2)}, u32[]{:S(2)}) collective-permute-start(f32[18,32,128]{2,1,0:T(8,128)S(1)} %get-tuple-element.19), channel_id=1, source_target_pairs={{0,64},{128,192},{256,320},{384,448},{64,0},{192,128},{320,256},{4... | collective-permute-start | bytes 884744 | tf_op jit(solution)/shard_map/ppermute | solution.py:410
  26.1 9.7 %collective-permute-start.3 = (f32[21,8,128]{2,1,0:T(8,128)S(1)}, f32[21,8,128]{2,1,0:T(8,128)S(1)}, u32[]{:S(2)}, u32[]{:S(2)}) collective-permute-start(f32[21,8,128]{2,1,0:T(8,128)S(1)} %get-tuple-element.20), channel_id=1, source_target_pairs={{64,128},{192,256},{320,384},{128,64},{256,192},{384,320},{65,129}... | collective-permute-start | bytes 258056 | tf_op jit(solution)/shard_map/ppermute | solution.py:410
  35.8 11.2 %copy-start.7 = (f32[16]{0:T(128)S(1)}, f32[16]{0:T(128)}, u32[]{:S(2)}) copy-start(f32[16]{0:T(128)} %param.13) | copy-start | bytes 196
  35.8 11.2 %copy-start.2 = (f32[16,2048]{1,0:T(8,128)S(1)}, f32[16,2048]{1,0:T(8,128)}, u32[]{:S(2)}) copy-start(f32[16,2048]{1,0:T(8,128)} %particles.1) | copy-start | bytes 393220
  35.9 11.2 %copy-start.4 = (s32[2048,1]{0,1:T(1,128)S(1)}, s32[2048,1]{0,1:T(1,128)}, u32[]{:S(2)}) copy-start(s32[2048,1]{0,1:T(1,128)} %param.15) | copy-start | bytes 24580
  35.9 11.2 %copy-start.5 = (s32[2048]{0:T(1024)S(1)}, s32[2048]{0:T(1024)}, u32[]{:S(2)}) copy-start(s32[2048]{0:T(1024)} %param.14) | copy-start | bytes 24580
  35.9 11.2 %copy-start.6 = (f32[16,16]{1,0:T(8,128)S(1)}, f32[16,16]{1,0:T(8,128)}, u32[]{:S(2)}) copy-start(f32[16,16]{1,0:T(8,128)} %mixing.1) | copy-start | bytes 3076
  35.9 30.5 %collective-permute-start.4 = (f32[17,24,128]{2,1,0:T(8,128)S(1)}, f32[17,24,128]{2,1,0:T(8,128)S(1)}, u32[]{:S(2)}, u32[]{:S(2)}) collective-permute-start(f32[17,24,128]{2,1,0:T(8,128)S(1)} %shard_map.97), channel_id=1, source_target_pairs={{64,128},{192,256},{320,384},{128,64},{256,192},{384,320},{65,129}... | collective-permute-start | bytes 626696 | tf_op jit(solution)/shard_map/ppermute | solution.py:410
  42.1 6.8 %collective-permute-start.5 = (f32[16,128]{1,0:T(8,128)S(1)}, f32[16,128]{1,0:T(8,128)S(1)}, u32[]{:S(2)}, u32[]{:S(2)}) collective-permute-start(f32[16,128]{1,0:T(8,128)S(1)} %shard_map.98._.wall), channel_id=1, source_target_pairs={{0,64},{64,128},{128,192},{192,256},{256,320},{320,384},{384,448},... | collective-permute-start | bytes 24584 | tf_op jit(solution)/shard_map/ppermute | solution.py:464
  49.1 17.3 %collective-permute-start.6 = (f32[16,1024]{1,0:T(8,128)S(1)}, f32[16,1024]{1,0:T(8,128)S(1)}, u32[]{:S(2)}, u32[]{:S(2)}) collective-permute-start(f32[16,1024]{1,0:T(8,128)S(1)} %get-tuple-element.23), channel_id=1, source_target_pairs={{0,62},{1,63},{2,0},{3,1},{4,2},{5,3},{6,4},{7,5},{8,6},{9,7},{10,... | collective-permute-start | bytes 196616 | tf_op jit(solution)/shard_map/ppermute | solution.py:404
  52.7 21.3 %collective-permute-start.7 = (f32[16,1024]{1,0:T(8,128)S(1)}, f32[16,1024]{1,0:T(8,128)S(1)}, u32[]{:S(2)}, u32[]{:S(2)}) collective-permute-start(f32[16,1024]{1,0:T(8,128)S(1)} %get-tuple-element.25), channel_id=1, source_target_pairs={{0,63},{1,0},{2,1},{3,2},{4,3},{5,4},{6,5},{7,6},{8,7},{9,8},{10,9... | collective-permute-start | bytes 196616 | tf_op jit(solution)/shard_map/ppermute | solution.py:404
  61.0 13.0 %collective-permute-start.8 = (f32[16,1024]{1,0:T(8,128)S(1)}, f32[16,1024]{1,0:T(8,128)S(1)}, u32[]{:S(2)}, u32[]{:S(2)}) collective-permute-start(f32[16,1024]{1,0:T(8,128)S(1)} %get-tuple-element.27), channel_id=1, source_target_pairs={{0,1},{1,2},{2,3},{3,4},{4,5},{5,6},{6,7},{7,8},{8,9},{9,10},{10,1... | collective-permute-start | bytes 196616 | tf_op jit(solution)/shard_map/ppermute | solution.py:404
  63.2 11.5 %collective-permute-start.9 = (f32[16,1024]{1,0:T(8,128)S(1)}, f32[16,1024]{1,0:T(8,128)S(1)}, u32[]{:S(2)}, u32[]{:S(2)}) collective-permute-start(f32[16,1024]{1,0:T(8,128)S(1)} %get-tuple-element.28), channel_id=1, source_target_pairs={{0,2},{1,3},{2,4},{3,5},{4,6},{5,7},{6,8},{7,9},{8,10},{9,11},{10,... | collective-permute-start | bytes 196616 | tf_op jit(solution)/shard_map/ppermute | solution.py:404

commit v3 on v2

--- a/solution.py
+++ b/solution.py
@@ -65,7 +65,7 @@
     )
 
 
-def edges_kernel(gas, kappa, to_right, to_left, held, arrived):
+def edges_kernel(gas, kappa, send_q, send_p, held, arrived):
     copies = [pltpu.make_async_copy(gas.at[q], held.at[q], arrived.at[q]) for q in range(COMP)]
     copies.append(pltpu.make_async_copy(kappa, held.at[COMP], arrived.at[COMP]))
     for copy in copies:
@@ -75,6 +75,8 @@
     depth, cell = within >> 4, within & 15
     high = jnp.maximum(6 * cell + 2 - depth, 0)
     low = 6 * cell + 3 + depth
+    odd = lax.rem(lax.axis_index("blk"), 2) == 1
+    index_q, index_p = jnp.where(odd, high, low), jnp.where(odd, low, high)
     for pair in range((COMP + 1) // 2):
         packed = {}
         for q in (2 * pair, 2 * pair + 1):
@@ -87,23 +89,29 @@
                 packed[q, tile] = total
         for tile in range(TILES):
             first, second = packed[2 * pair, tile], packed[2 * pair + 1, tile]
-            for out, index in ((to_right, high), (to_left, low)):
+            for out, index in ((send_q, index_q), (send_p, index_p)):
                 out[pair, rows(tile), :] = jnp.where(lane < 64, pick(first, index), pick(second, index))
 
 
-def strips_kernel(gas, kappa, to_right, to_left, from_left, from_right, strips, send_a, send_wall):
+def strips_kernel(gas, kappa, send_q, send_p, recv_q, recv_p, _, strips, send_a, send_wall):
     lane = lanes()
     low_side = (lane & 1) == 1
     cell = jnp.clip((lane >> 1) - 3, 0, GX - 1)
-    odd = lax.rem(lax.axis_index("sect"), 2)
-    even = odd == 0
+    even = lax.rem(lax.axis_index("sect"), 2) == 0
+    odd_tile = lax.rem(lax.axis_index("blk"), 2) == 1
     for tile in range(TILES):
         held = {}
+        slabs = [[ref[s, rows(tile), :] for s in range(3)] for ref in (send_q, send_p, recv_q, recv_p)]
+        own_q, own_p, got_q, got_p = slabs
+        to_left = [jnp.where(odd_tile, p, q) for q, p in zip(own_q, own_p)]
+        to_right = [jnp.where(odd_tile, q, p) for q, p in zip(own_q, own_p)]
+        from_left = [jnp.where(odd_tile, p, q) for q, p in zip(got_q, got_p)]
+        from_right = [jnp.where(odd_tile, q, p) for q, p in zip(got_q, got_p)]
         for q, k in STRIPS:
             depth = k - 1 if k > 0 else -k
             index = cell + ((q % 2) * 64 + depth * 16)
             low, high = (from_left, from_right) if k > 0 else (to_left, to_right)
-            value = jnp.where(low_side, pick(low[q // 2, rows(tile), :], index), pick(high[q // 2, rows(tile), :], index))
+            value = jnp.where(low_side, pick(low[q // 2], index), pick(high[q // 2], index))
             strips[STRIP_AT[q, k], rows(tile), :] = value
             held[q, k] = value
         top = jnp.zeros((8, 128), jnp.float32)
@@ -128,7 +136,7 @@
         send_wall[3 * COMP + layer] = kappa[kappa_b + layer, split:, :]
 
 
-def rest_kernel(gas, kappa, _, send_rest):
+def rest_kernel(gas, kappa, send_rest):
     even = lax.rem(lax.axis_index("sect"), 2) == 0
     split = GR - 8
     from_b, from_kappa = jnp.where(even, 0, GX - 3), jnp.where(even, 0, GX - 2)
@@ -167,6 +175,17 @@
     return sums
 
 
+def radial_sum_of(src, c, at, values):
+    sub = lax.broadcasted_iota(jnp.int32, (8, 128), 0)
+    sums = []
+    for t in range(TILES):
+        first, last = t == 0, t == TILES - 1
+        below = jnp.where(sub == 0, values[t], pltpu.roll(values[t], 1, 0)) if first else src[c, at, 8 * t - 1 : 8 * t + 7, :]
+        above = jnp.where(sub == 7, values[t], pltpu.roll(values[t], 7, 0)) if last else src[c, at, 8 * t + 1 : 8 * t + 9, :]
+        sums.append(below + above)
+    return sums
+
+
 def strip_levels(strips, low_corner, high_corner, mix, edge, tiles):
     lane = lanes()
     wall_only = len(tiles) == 1
@@ -175,7 +194,7 @@
     held = {}
     for key in STRIPS:
         held[key] = [strips[STRIP_AT[key], rows(t), :] for t in tiles]
-    for i, key in enumerate(CORNERS):
+    for i, key in enumerate(CORNERS if low_corner else ()):
         for n in range(len(tiles)):
             value = jnp.where(from_low, pltpu.roll(low_corner[n], (2 - 4 * i) % 128, 1), held[key][n])
             held[key][n] = jnp.where(from_high, pltpu.roll(high_corner[n], (38 - 4 * i) % 128, 1), value)
@@ -200,15 +219,15 @@
         held = later
 
 
-def plane(src, kappa, edge, step, at, mix, count, wall_only, comps):
+def plane(src, kappa, edge, step, at, x, mix, count, comps):
     lane = lanes()
     first, last = lane == 0, lane == 127
-    shift = 127 - 2 * at
+    shift = 121 - 2 * x
     values = [[src[c, at, rows(t), :] for t in range(count)] for c in range(COMP)]
     kap = [kappa[at, rows(t), :] for t in range(count)]
     out = {}
     for c in comps:
-        radial = radial_sum(values[c], wall_only)
+        radial = radial_sum(values[c], True) if count == 1 else radial_sum_of(src, c, at, values[c])
         for t in range(count):
             value = values[c][t]
             beyond = pltpu.roll(edge[step, c, rows(t), :], shift, 1)
@@ -219,29 +238,7 @@
     return out
 
 
-def steps(count, wall_only, now, later, kappa, edge, mix, finish, unroll):
-    for step in range(ITERS):
-        src, dst = (now, later) if step % 2 == 0 else (later, now)
-        final = step == ITERS - 1
-
-        def body(at, carry, step=step, src=src, dst=dst, final=final):
-            comps = (0,) if final and wall_only else range(COMP)
-            out = plane(src, kappa, edge, step, at, mix, count, wall_only, comps)
-            if final:
-                finish(at, out)
-            else:
-                for (c, t), value in out.items():
-                    dst[c, at, rows(t), :] = value
-            return carry
-
-        if unroll is None:
-            for at in range(step + 1, EXT - 1 - step):
-                body(at, 0)
-        else:
-            lax.fori_loop(step + 1, EXT - 1 - step, body, 0, unroll=unroll)
-
-
-def wall_kernel(gas, kappa, strips, recv_a, recv_wall, reaction, wall, now, later, kap, edge):
+def wall_kernel(gas, kappa, strips, recv_a, recv_wall, reaction, _, wall, now, later, kap, edge):
     odd = lax.rem(lax.axis_index("sect"), 2)
     even = odd == 0
     mix = coupling(reaction)
@@ -263,31 +260,63 @@
     low, high = jnp.where(even, corner_b, corner_a), jnp.where(even, corner_a, corner_b)
     strip_levels(strips, [low], [high], mix, edge, [TILES - 1])
 
-    def finish(at, out):
-        wall[at - 3 : at - 2, :] = out[0, 0][7:8, :]
-
-    steps(1, True, now, later, kap, edge, mix, finish, unroll=None)
-
-
-def gas_kernel(gas, kappa, strips, recv_a, recv_wall, recv_rest, reaction, _, result, token, now, later, kap, edge):
+    for step, (src, dst) in enumerate(((now, later), (later, now), (now, None))):
+        comps = (0,) if step == ITERS - 1 else range(COMP)
+        for at in range(step + 1, EXT - 1 - step):
+            out = plane(src, kap, edge, step, at, at - 3, mix, 1, comps)
+            if step == ITERS - 1:
+                wall[at - 3 : at - 2, :] = out[0, 0][7:8, :]
+                continue
+            for c in comps:
+                dst[c, at] = out[c, 0]
+
+
+def inner_kernel(gas, kappa, strips, reaction, first, second, middle, edge):
+    mix = coupling(reaction)
+    strip_levels(strips, None, None, mix, edge, list(range(TILES)))
+    for step, (src, dst) in enumerate(((gas, first), (first, second), (second, middle))):
+
+        def body(x, carry, step=step, src=src, dst=dst):
+            out = plane(src, kappa, edge, step, x, x, mix, TILES, range(COMP))
+            into = x - 3 if step == ITERS - 1 else x
+            for (c, t), value in out.items():
+                dst[c, into, rows(t), :] = value
+            return carry
+
+        lax.fori_loop(step + 1, GX - 1 - step, body, 0, unroll=2)
+
+
+def outer_kernel(
+    gas, kappa, strips, first, second, middle, recv_a, recv_wall, both_rest, reaction, _, result, token, now, later, kap, edge
+):
     token[...] = jnp.zeros((8, 128), jnp.float32)
-    odd = lax.rem(lax.axis_index("sect"), 2)
-    even = odd == 0
+    even = lax.rem(lax.axis_index("sect"), 2) == 0
     mix = coupling(reaction)
     split = GR - 8
+    section, sections = lax.axis_index("sect"), lax.axis_size("sect")
+    inside = (section > 0) & (section < sections - 1)
+    other = jnp.where(even, 0, 1)
+
+    def recv_rest(layer):
+        return jnp.where(inside, both_rest[other, layer], 0.0)
+
     at_a, at_b = jnp.where(even, GX + 3, 0), jnp.where(even, 0, GX + 3)
     kappa_a, kappa_b = jnp.where(even, GX + 3, 1), jnp.where(even, 1, GX + 3)
     for c in range(COMP):
-        now[c, 3 : GX + 3] = gas[c]
+        for x in (0, 1, GX - 2, GX - 1):
+            now[c, x + 3] = gas[c, x]
         for layer in range(3):
             now[c, at_a + layer] = recv_a[3 * c + layer]
             now[c, at_b + layer, split:, :] = recv_wall[3 * c + layer]
-            now[c, at_b + layer, :split, :] = recv_rest[3 * c + layer]
-    kap[3 : GX + 3] = kappa[...]
+            now[c, at_b + layer, :split, :] = recv_rest(3 * c + layer)
+        for x in (1, 2, GX - 3, GX - 2):
+            later[c, x + 3] = first[c, x]
+    for x in (0, 1, 2, GX - 3, GX - 2, GX - 1):
+        kap[x + 3] = kappa[x]
     for layer in range(2):
         kap[kappa_a + layer] = recv_a[3 * COMP + layer]
         kap[kappa_b + layer, split:, :] = recv_wall[3 * COMP + layer]
-        kap[kappa_b + layer, :split, :] = recv_rest[3 * COMP + layer]
+        kap[kappa_b + layer, :split, :] = recv_rest(3 * COMP + layer)
     low, high = [], []
     for t in range(TILES):
         corner_a = recv_a[LAYERS - 1, rows(t), :]
@@ -295,12 +324,21 @@
         low.append(jnp.where(even, corner_b, corner_a))
         high.append(jnp.where(even, corner_a, corner_b))
     strip_levels(strips, low, high, mix, edge, list(range(TILES)))
-
-    def finish(at, out):
-        for (c, t), value in out.items():
-            result[c, at - 3, rows(t), :] = value
-
-    steps(TILES, False, now, later, kap, edge, mix, finish, unroll=2)
+    for c in range(COMP):
+        result[c, 3 : GX - 3] = middle[c]
+    for step, (src, dst) in enumerate(((now, later), (later, now), (now, None))):
+        if step == ITERS - 1:
+            for c in range(COMP):
+                for x in (2, 3, GX - 4, GX - 3):
+                    now[c, x + 3] = second[c, x]
+        for i in range(3):
+            for at in (step + 1 + i, GX + 2 - step + i):
+                out = plane(src, kap, edge, step, at, at - 3, mix, TILES, range(COMP))
+                for (c, t), value in out.items():
+                    if step == ITERS - 1:
+                        result[c, at - 3, rows(t), :] = value
+                    else:
+                        dst[c, at, rows(t), :] = value
 
 
 def pack_kernel(hop, cell, particles, mixing, heating, _, packed, cells, spread, ordered, source, begin, end):
@@ -370,8 +408,13 @@
     lax.fori_loop(0, MOVES, block, 0)
 
 
-def heat_kernel(wall, earlier, packed, cells, heating, *refs):
-    outs, look = refs[:MOVES], refs[MOVES]
+def moves_of_swaps():
+    tile = lax.axis_index("blk")
+    odd, late = lax.rem(tile, 2), lax.rem(tile, 4) >> 1
+    return [REACH - 1 + 2 * odd, 2 * REACH * late, 2 * REACH * (1 - late), REACH + 1 - 2 * odd]
+
+
+def heat_kernel(wall, earlier, packed, cells, heating, own, send_q, send_s, send_r, send_p, look):
     flux = 0.5 * (wall[...] + earlier[...])
     heat = jnp.broadcast_to(heating[...], (VALS, 128))
     for j in range(MOVES):
@@ -382,57 +425,67 @@
             line = jnp.broadcast_to(flux[x : x + 1, :], (8, 128))
             found = jnp.where(row == x, pick(line, column), found)
         look[j] = found
-    for j in range(MOVES):
+    for out, j in zip((own, send_q, send_s, send_r, send_p), [REACH] + moves_of_swaps()):
         for spot in range(SPOTS):
             part = slice(128 * spot, 128 * (spot + 1))
-            outs[j][:, part] = packed[j, :, part] + heat * look[j, spot : spot + 1, :]
-
-
-def join_kernel(*refs):
-    pieces, out, done = refs[:MOVES], refs[MOVES + 1], refs[MOVES + 2]
-    copies = [
-        pltpu.make_async_copy(piece, out.at[:, j * CAP : (j + 1) * CAP], done.at[j]) for j, piece in enumerate(pieces)
-    ]
+            out[:, part] = packed[j, :, part] + heat * look[j, spot : spot + 1, :]
+
+
+def join_kernel(own, recv_q, recv_s, recv_r, recv_p, _, out, done):
+    copies = []
+    for n, (piece, j) in enumerate(zip((own, recv_q, recv_s, recv_r, recv_p), [REACH] + moves_of_swaps())):
+        place = pl.multiple_of((2 * REACH - j) * CAP, CAP)
+        copies.append(pltpu.make_async_copy(piece, out.at[:, pl.ds(place, CAP)], done.at[n]))
     for copy in copies:
         copy.start()
     for copy in copies:
         copy.wait()
 
 
-def ring(x, axis, by):
-    size = lax.axis_size(axis)
-    return lax.ppermute(x, axis, [(i, (i + by) % size) for i in range(size)])
-
-
-def swap(x, axis, first):
-    size = lax.axis_size(axis)
-    pairs = [(i, i + 1) for i in range(first, size - 1, 2)]
+def swap(x, axis, pairs):
     return lax.ppermute(x, axis, pairs + [(j, i) for i, j in pairs])
 
 
 def local(gas, kappa, reaction, particles, mixing, heating, wall_cell, tile_hop):
-    strip_shape = (3, GR, GA)
-    to_right, to_left = call(
+    sections, tiles = lax.axis_size("sect"), lax.axis_size("blk")
+    pairs_a = [(i, i + 1) for i in range(0, sections, 2)]
+    pairs_b = [(i, i + 1) for i in range(1, sections - 1, 2)]
+    pairs_q = [(i, (i + 1) % tiles) for i in range(1, tiles, 2)]
+    pairs_p = [(i, i + 1) for i in range(0, tiles, 2)]
+    pairs_s = [(i, (i + 2) % tiles) for i in range(tiles) if i % 4 >= 2]
+    pairs_r = [(i, i + 2) for i in range(tiles) if i % 4 < 2]
+
+    send_q, send_p = call(
         edges_kernel,
-        (f32(*strip_shape), f32(*strip_shape)),
+        (f32(3, GR, GA), f32(3, GR, GA)),
         scratch=[pltpu.VMEM((COMP + 1, GX, GR, GA), jnp.float32), pltpu.SemaphoreType.DMA((COMP + 1,))],
         specs=[HBM] * 2,
         moved=2 << 20,
         limit=53.75,
     )(gas, kappa)
-    from_left = ring(to_right, "blk", 1)
-    from_right = ring(to_left, "blk", -1)
+    recv_q = swap(send_q, "blk", pairs_q)
+    recv_p = swap(send_p, "blk", pairs_p)
+    send_rest = call(rest_kernel, f32(LAYERS - 1, GR - 8, GA), specs=[VMEM] * 2, moved=1 << 18)(gas, kappa)
+    groups = [list(pair) for pair in pairs_b] + [[0, sections - 1]]
+    both_rest = lax.all_gather(send_rest, "sect", axis_index_groups=groups)
 
     strips, send_a, send_wall = call(
         strips_kernel,
         (f32(len(STRIPS), GR, GA), f32(LAYERS, GR, GA), f32(LAYERS - 1 + TILES, 8, GA)),
-        specs=[VMEM] * 6,
+        specs=[VMEM] * 6 + [ANY],
         moved=2 << 20,
-    )(gas, kappa, to_right, to_left, from_left, from_right)
-    recv_wall = swap(send_wall, "sect", 1)
-    recv_a = swap(send_a, "sect", 0)
-    send_rest = call(rest_kernel, f32(LAYERS - 1, GR - 8, GA), specs=[VMEM] * 2 + [ANY], moved=1 << 20)(gas, kappa, recv_wall)
-    recv_rest = swap(send_rest, "sect", 1)
+    )(gas, kappa, send_q, send_p, recv_q, recv_p, send_rest)
+    recv_wall = swap(send_wall, "sect", pairs_b)
+    recv_a = swap(send_a, "sect", pairs_a)
+
+    whole = f32(COMP, GX, GR, GA)
+    first, second, middle = call(
+        inner_kernel,
+        (whole, whole, f32(COMP, GX - 6, GR, GA)),
+        scratch=[pltpu.VMEM((ITERS, COMP, GR, GA), jnp.float32)],
+        specs=[VMEM] * 3 + [SMEM],
+        moved=12 << 20,
+    )(gas, kappa, strips, reaction)
 
     wall = call(
         wall_kernel,
@@ -443,9 +496,11 @@
             pltpu.VMEM((EXT, 8, GA), jnp.float32),
             pltpu.VMEM((ITERS, COMP, 8, GA), jnp.float32),
         ],
-        specs=[VMEM] * 5 + [SMEM],
+        specs=[VMEM] * 5 + [SMEM, ANY],
         moved=4 << 20,
-    )(gas, kappa, strips, recv_a, recv_wall, reaction)
+    )(gas, kappa, strips, recv_a, recv_wall, reaction, middle)
+    earlier = lax.ppermute(wall, "sect", [(i, i + 1) for i in range(sections - 1)])
+
     heating_column = heating.reshape(VALS, 1)
     packed, cells = call(
         pack_kernel,
@@ -460,30 +515,27 @@
         specs=[VMEM] * 5 + [ANY],
         moved=4 << 20,
     )(tile_hop.reshape(CHUNKS, 128), wall_cell.reshape(CHUNKS, 128), particles, mixing, heating_column, wall)
-    size = lax.axis_size("sect")
-    earlier = lax.ppermute(wall, "sect", [(i, i + 1) for i in range(size - 1)])
-
-    blocks = call(
+    own, *sends = call(
         heat_kernel,
         (f32(VALS, CAP),) * MOVES,
         scratch=[pltpu.VMEM((MOVES, SPOTS, 128), jnp.float32)],
         specs=[VMEM] * 5,
         moved=2 << 20,
     )(wall, earlier, packed, cells, heating_column)
-    pieces = [block if j == REACH else ring(block, "blk", j - REACH) for j, block in enumerate(blocks)]
+    pieces = [swap(x, "blk", pairs) for x, pairs in zip(sends, (pairs_q, pairs_s, pairs_r, pairs_p))]
 
     field, token = call(
-        gas_kernel,
-        (f32(COMP, GX, GR, GA), f32(8, 128)),
+        outer_kernel,
+        (whole, f32(8, 128)),
         scratch=[
             pltpu.VMEM((COMP, EXT, GR, GA), jnp.float32),
             pltpu.VMEM((COMP, EXT, GR, GA), jnp.float32),
             pltpu.VMEM((EXT, GR, GA), jnp.float32),
             pltpu.VMEM((ITERS, COMP, GR, GA), jnp.float32),
         ],
-        specs=[VMEM] * 6 + [SMEM, ANY],
-        moved=20 << 20,
-    )(gas, kappa, strips, recv_a, recv_wall, recv_rest, reaction, pieces[0])
+        specs=[VMEM] * 9 + [SMEM, ANY],
+        moved=8 << 20,
+    )(gas, kappa, strips, first, second, middle, recv_a, recv_wall, both_rest, reaction, pieces[0])
     arrived = call(
         join_kernel,
         f32(VALS, MOVES * CAP),
@@ -491,7 +543,7 @@
         specs=[VMEM] * MOVES + [ANY],
         out_specs=HBM,
         moved=1 << 20,
-    )(*pieces, token)
+    )(own, *pieces, token)
     return field, arrived
 
 

time: 75.8 us -> 84.9 us (1.12)
  blocking collectives: 0 us -> 15.1 us
  starting transfers between devices: 52.7 us -> 45.5 us
  local copies, waits for them, and re-layouts: 0.13 us -> 4.71 us
  waiting for transfers between devices: 6.99 us -> 3.14 us
    ppermute x7 -> x1, starting transfers between devices: 35.8 us -> 4.04 us  [local(): lax.ppermute(wall, 'sect', [(i, i + 1) for i in range(sections - 1)])]
    ppermute x3 -> x8, starting transfers between devices: 16.9 us -> 41.5 us  [swap(): return lax.ppermute(x, axis, pairs + [(j, i) for i, j in pairs])]
    all_gather x0 -> x1, blocking collectives: none -> 15.1 us  [local(): both_rest = lax.all_gather(send_rest, 'sect', axis_index_groups=groups)]
    unnamed x16 -> x24, local copies, waits for them, and re-layouts: 0.05 us -> 4.63 us
    ppermute x3 -> x8, waiting for transfers between devices: 5.13 us -> 3.14 us  [swap(): return lax.ppermute(x, axis, pairs + [(j, i) for i, j in pairs])]
    ppermute x7 -> x1, waiting for transfers between devices: 1.86 us -> 0.01 us  [local(): lax.ppermute(wall, 'sect', [(i, i + 1) for i in range(sections - 1)])]
    pallas_call x3 -> x4, Pallas kernels: 9.83 us -> 10.1 us  [the longest x1 4.56 us: local(): call(inner_kernel, (whole, whole, f32(COMP, GX - 6, GR, GA)), scratch=[pl...]
  transfers between devices with their start and end apart: 10 -> 9, of which waited for: 3 -> 1; matrix products, arithmetic and copies ran while one was open for 0% -> 0% of each run, Pallas kernels for 15% -> 11%
where the time goes in v3:
time: 84.9 us; the launch traced here: 84.5 us
  starting transfers between devices  45.5 us (54%)
  Pallas kernels  15.1 us (18%)
  blocking collectives  15.1 us (18%)
  local copies, waits for them, and re-layouts  4.71 us (6%)
  waiting for transfers between devices  3.14 us (4%)
  between operations  0.9 us (1%)
    ppermute x8, starting transfers between devices, swap(): return lax.ppermute(x, axis, pairs + [(j, i) for i, j in pairs])  41.5 us
    all_gather x1, blocking collectives, local(): both_rest = lax.all_gather(send_rest, 'sect', axis_index_groups=groups)  15.1 us
    unnamed x24, local copies, waits for them, and re-layouts  4.63 us
    pallas_call x1, Pallas kernels, local(): call(inner_kernel, (whole, whole, f32(COMP, GX - 6, GR, GA)), scratch=[pl...  4.56 us
    ppermute x1, starting transfers between devices, local(): lax.ppermute(wall, 'sect', [(i, i + 1) for i in range(sections - 1)])  4.04 us
    pallas_call x1, Pallas kernels, local(): call(outer_kernel, (whole, f32(8, 128)), scratch=[pltpu.VMEM((COMP, EXT,...  3.35 us
    ppermute x8, waiting for transfers between devices, swap(): return lax.ppermute(x, axis, pairs + [(j, i) for i, j in pairs])  3.14 us
    pallas_call x1, Pallas kernels, local(): call(edges_kernel, (f32(3, GR, GA), f32(3, GR, GA)), scratch=[pltpu.VMEM(...  2.18 us
  transfers between devices with their start and end apart: 9, of which 1 were waited for; matrix products, arithmetic and copies ran while one was open for 0% of the time, Pallas kernels for 11%

profile of v3, /device:TPU:1, one launch (start us, length us, event | category | flops | bytes accessed | tf_op | source)
XLA Modules:
  0.0 84.5 jit_solution(10944784919289935685)
XLA Ops:
  0.6 0.0 copy-start.1
  0.6 0.0 copy-start
  0.6 2.2 %shard_map.95 = (f32[3,32,128]{2,1,0:T(8,128)S(1)}, f32[3,32,128]{2,1,0:T(8,128)S(1)}) custom-call(f32[5,16,32,128]{3,2,1,0:T(8,128)} %gas.11, f32[16,32,128]{2,1,0:T(8,128)} %kappa.11), custom_call_target="tpu_custom_call" | custom-call | bytes 2097152 | tf_op jit(solution)/shard_map/pallas_call | solution.py:458
  2.8 11.7 %collective-permute-start = (f32[3,32,128]{2,1,0:T(8,128)S(1)}, f32[3,32,128]{2,1,0:T(8,128)S(1)}, u32[]{:S(2)}, u32[]{:S(2)}) collective-permute-start(f32[3,32,128]{2,1,0:T(8,128)S(1)} %get-tuple-element.19.send_q), channel_id=1, source_target_pairs={{1,2},{3,4},{5,6},{7,8},{9,10},{11,12},{13,14},{15,16},{17,18},{19... | collective-permute-start | bytes 147464 | tf_op jit(solution)/shard_map/ppermute | solution.py:446
  14.6 1.9 %collective-permute-start.1 = (f32[3,32,128]{2,1,0:T(8,128)S(1)}, f32[3,32,128]{2,1,0:T(8,128)S(1)}, u32[]{:S(2)}, u32[]{:S(2)}) collective-permute-start(f32[3,32,128]{2,1,0:T(8,128)S(1)} %get-tuple-element.20.send_p), channel_id=1, source_target_pairs={{0,1},{2,3},{4,5},{6,7},{8,9},{10,11},{12,13},{14,15},{16,17},{18,... | collective-permute-start | bytes 147464 | tf_op jit(solution)/shard_map/ppermute | solution.py:446
  16.5 0.0 copy-done.1
  16.5 0.0 copy-done
  16.6 0.0 copy-start.7
  16.6 0.0 collective-permute-done.recv_q
  16.6 3.1 %collective-permute-done.1.recv_p = f32[3,32,128]{2,1,0:T(8,128)S(1)} collective-permute-done((f32[3,32,128]{2,1,0:T(8,128)S(1)}, f32[3,32,128]{2,1,0:T(8,128)S(1)}, u32[]{:S(2)}, u32[]{:S(2)}) %collective-permute-start.1) | collective-permute-done | bytes 49184 | tf_op jit(solution)/shard_map/ppermute | solution.py:446
  19.7 0.8 shard_map.97
  20.6 4.0 %collective-permute-start.2 = (f32[18,32,128]{2,1,0:T(8,128)S(1)}, f32[18,32,128]{2,1,0:T(8,128)S(1)}, u32[]{:S(2)}, u32[]{:S(2)}) collective-permute-start(f32[18,32,128]{2,1,0:T(8,128)S(1)} %get-tuple-element.25), channel_id=1, source_target_pairs={{0,64},{128,192},{256,320},{384,448},{64,0},{192,128},{320,256},{4... | collective-permute-start | bytes 884744 | tf_op jit(solution)/shard_map/ppermute | solution.py:446
  24.6 8.4 %collective-permute-start.3 = (f32[21,8,128]{2,1,0:T(8,128)S(1)}, f32[21,8,128]{2,1,0:T(8,128)S(1)}, u32[]{:S(2)}, u32[]{:S(2)}) collective-permute-start(f32[21,8,128]{2,1,0:T(8,128)S(1)} %get-tuple-element.26), channel_id=1, source_target_pairs={{64,128},{192,256},{320,384},{128,64},{256,192},{384,320},{65,129}... | collective-permute-start | bytes 258056 | tf_op jit(solution)/shard_map/ppermute | solution.py:446
  33.0 0.0 copy-done.7
  33.0 4.6 %shard_map.98 = (f32[5,16,32,128]{3,2,1,0:T(8,128)S(1)}, f32[5,16,32,128]{3,2,1,0:T(8,128)S(1)}, f32[5,10,32,128]{3,2,1,0:T(8,128)S(1)}) custom-call(f32[5,16,32,128]{3,2,1,0:T(8,128)S(1)} %copy-done, f32[16,32,128]{2,1,0:T(8,128)S(1)} %copy-done.1, f32[28,32,128]{2,1,0:T(8,128)S(1)} %get-tuple-element.21.strips, f32[5,5]{1,0:T(8,128)S(1)} %copy-done.7), custom_call_target="tpu_custom_call" | custom-call | bytes 12582912 | tf_op jit(solution)/shard_map/pallas_call | solution.py:482
  37.6 0.0 copy-start.2
  37.6 1.0 %copy-done.2 = f32[5,16,32,128]{3,2,1,0:T(8,128)} copy-done((f32[5,16,32,128]{3,2,1,0:T(8,128)}, f32[5,16,32,128]{3,2,1,0:T(8,128)S(1)}, u32[]{:S(2)}) %copy-start.2) | copy-done | bytes 1310744
  38.6 0.0 collective-permute-done.3.recv_wall
  38.6 0.0 collective-permute-done.2.recv_a
  38.6 0.0 copy-start.11
  38.7 0.0 copy-start.8
  38.7 0.0 copy-start.9
  38.7 0.0 copy-start.10
  38.7 1.4 %shard_map.99._.wall = f32[16,128]{1,0:T(8,128)S(1)} custom-call(f32[5,16,32,128]{3,2,1,0:T(8,128)S(1)} %copy-done, f32[16,32,128]{2,1,0:T(8,128)S(1)} %copy-done.1, f32[28,32,128]{2,1,0:T(8,128)S(1)} %get-tuple-element.21.strips, f32[18,32,128]{2,1,0:T(8,128)S(1)} %collective-permute-done.2.recv_a, f32[21,8,128]{2,1,0:T(8,128)S(1)} %collective-permute-done.3.recv_wall, ...), custom_call_target="tpu_custom_call" | custom-call | bytes 4194304 | tf_op jit(solution)/shard_map/pallas_call | solution.py:490
  40.1 0.0 copy-done.4
  40.2 4.0 %collective-permute-start.4 = (f32[16,128]{1,0:T(8,128)S(1)}, f32[16,128]{1,0:T(8,128)S(1)}, u32[]{:S(2)}, u32[]{:S(2)}) collective-permute-start(f32[16,128]{1,0:T(8,128)S(1)} %shard_map.99._.wall), channel_id=1, source_target_pairs={{0,64},{64,128},{128,192},{192,256},{256,320},{320,384},{384,448},... | collective-permute-start | bytes 24584 | tf_op jit(solution)/shard_map/ppermute | solution.py:502
  44.2 0.0 copy-done.11
  44.2 0.1 copy.12.heating
  44.3 0.0 copy-done.8
  44.3 0.0 copy-done.9
  44.3 0.0 copy-start.6
  44.3 0.9 %copy-done.6 = f32[16,2048]{1,0:T(8,128)S(1)} copy-done((f32[16,2048]{1,0:T(8,128)S(1)}, f32[16,2048]{1,0:T(8,128)}, u32[]{:S(2)}) %copy-start.6) | copy-done | bytes 131096
  45.2 1.7 %shard_map.100 = (f32[5,16,1024]{2,1,0:T(8,128)S(1)}, s32[5,8,128]{2,1,0:T(8,128)S(1)}) custom-call(s32[16,128]{1,0:T(8,128)S(1)} %bitcast.5, s32[16,128]{1,0:T(8,128)S(1)} %bitcast.6, f32[16,2048]{1,0:T(8,128)S(1)} %copy-done.6, f32[16,16]{1,0:T(8,128)S(1)} %copy-done.10, f32[16,1]{1,0:T(8,128)S(1)} %copy.12.heating, f32[16,128]{1,0:T(8,128)S(1)} %shard_map.99._.wall), custom_call_target="tpu_custom_call" | custom-call | bytes 4194304 | tf_op jit(solution)/shard_map/pallas_call | solution.py:505
  47.0 0.0 collective-permute-done.4.earlier
  47.0 0.2 shard_map.101
  47.2 6.0 %collective-permute-start.5 = (f32[16,1024]{1,0:T(8,128)S(1)}, f32[16,1024]{1,0:T(8,128)S(1)}, u32[]{:S(2)}, u32[]{:S(2)}) collective-permute-start(f32[16,1024]{1,0:T(8,128)S(1)} %get-tuple-element.29), channel_id=1, source_target_pairs={{1,2},{3,4},{5,6},{7,8},{9,10},{11,12},{13,14},{15,16},{17,18},{19... | collective-permute-start | bytes 196616 | tf_op jit(solution)/shard_map/ppermute | solution.py:446
  53.2 1.9 %collective-permute-start.6 = (f32[16,1024]{1,0:T(8,128)S(1)}, f32[16,1024]{1,0:T(8,128)S(1)}, u32[]{:S(2)}, u32[]{:S(2)}) collective-permute-start(f32[16,1024]{1,0:T(8,128)S(1)} %get-tuple-element.32), channel_id=1, source_target_pairs={{2,4},{3,5},{6,8},{7,9},{10,12},{11,13},{14,16},{15,17},{18,20},{1... | collective-permute-start | bytes 196616 | tf_op jit(solution)/shard_map/ppermute | solution.py:446
  55.1 1.9 %collective-permute-start.7 = (f32[16,1024]{1,0:T(8,128)S(1)}, f32[16,1024]{1,0:T(8,128)S(1)}, u32[]{:S(2)}, u32[]{:S(2)}) collective-permute-start(f32[16,1024]{1,0:T(8,128)S(1)} %get-tuple-element.33), channel_id=1, source_target_pairs={{0,2},{1,3},{4,6},{5,7},{8,10},{9,11},{12,14},{13,15},{16,18},{17,... | collective-permute-start | bytes 196616 | tf_op jit(solution)/shard_map/ppermute | solution.py:446
  57.0 5.6 %collective-permute-start.8 = (f32[16,1024]{1,0:T(8,128)S(1)}, f32[16,1024]{1,0:T(8,128)S(1)}, u32[]{:S(2)}, u32[]{:S(2)}) collective-permute-start(f32[16,1024]{1,0:T(8,128)S(1)} %get-tuple-element.34), channel_id=1, source_target_pairs={{0,1},{2,3},{4,5},{6,7},{8,9},{10,11},{12,13},{14,15},{16,17},{18,... | collective-permute-start | bytes 196616 | tf_op jit(solution)/shard_map/ppermute | solution.py:446
  62.6 15.1 %all-gather = f32[34,24,128]{2,1,0:T(8,128)S(1)} all-gather(f32[17,24,128]{2,1,0:T(8,128)S(1)} %shard_map.96._), channel_id=2, replica_groups={{64,128},{192,256},{320,384},{0,448},{65,129},{193,257},{321,385},{1,44..., dimensions={0}, use_global_device_ids=true | all-gather | bytes 626688 | tf_op jit(solution)/shard_map/all_gather | solution.py:470
  77.8 0.0 collective-permute-done.5._.recv_q
  77.8 1.3 %copy-done.3 = f32[5,16,32,128]{3,2,1,0:T(8,128)S(1)} copy-done((f32[5,16,32,128]{3,2,1,0:T(8,128)S(1)}, f32[5,16,32,128]{3,2,1,0:T(8,128)}, u32[]{:S(2)}) %copy-start.3) | copy-done | bytes 1310744
  79.1 1.3 %copy-done.5 = f32[5,16,32,128]{3,2,1,0:T(8,128)S(1)} copy-done((f32[5,16,32,128]{3,2,1,0:T(8,128)S(1)}, f32[5,16,32,128]{3,2,1,0:T(8,128)}, u32[]{:S(2)}) %copy-start.5) | copy-done | bytes 1310744
  80.4 3.3 %shard_map.102 = (f32[5,16,32,128]{3,2,1,0:T(8,128)}, f32[8,128]{1,0:T(8,128)S(1)}) custom-call(f32[5,16,32,128]{3,2,1,0:T(8,128)S(1)} %copy-done, f32[16,32,128]{2,1,0:T(8,128)S(1)} %copy-done.1, f32[28,32,128]{2,1,0:T(8,128)S(1)} %get-tuple-element.21.strips, f32[5,16,32,128]{3,2,1,0:T(8,128)S(1)} %copy-done.3, f32[5,16,32,128]{3,2,1,0:T(8,128)S(1)} %copy-done.5, ...), custom_call_target="tpu_custom_call" | custom-call | bytes 8388608 | tf_op jit(solution)/shard_map/pallas_call | solution.py:527
  83.7 0.0 collective-permute-done.6.recv_s
  83.8 0.0 collective-permute-done.7.recv_r
  83.8 0.0 collective-permute-done.8.recv_p
  83.8 0.8 shard_map.103
  (5 shorter events, 0.0 us)
Async XLA Ops:
  0.6 15.9 %copy-start.1 = (f32[16,32,128]{2,1,0:T(8,128)S(1)}, f32[16,32,128]{2,1,0:T(8,128)}, u32[]{:S(2)}) copy-start(f32[16,32,128]{2,1,0:T(8,128)} %kappa.11) | copy-start | bytes 786436
  0.6 15.9 %copy-start = (f32[5,16,32,128]{3,2,1,0:T(8,128)S(1)}, f32[5,16,32,128]{3,2,1,0:T(8,128)}, u32[]{:S(2)}) copy-start(f32[5,16,32,128]{3,2,1,0:T(8,128)} %gas.11) | copy-start | bytes 3932164
  2.8 13.7 %collective-permute-start = (f32[3,32,128]{2,1,0:T(8,128)S(1)}, f32[3,32,128]{2,1,0:T(8,128)S(1)}, u32[]{:S(2)}, u32[]{:S(2)}) collective-permute-start(f32[3,32,128]{2,1,0:T(8,128)S(1)} %get-tuple-element.19.send_q), channel_id=1, source_target_pairs={{1,2},{3,4},{5,6},{7,8},{9,10},{11,12},{13,14},{15,16},{17,18},{19... | collective-permute-start | bytes 147464 | tf_op jit(solution)/shard_map/ppermute | solution.py:446
  14.6 5.1 %collective-permute-start.1 = (f32[3,32,128]{2,1,0:T(8,128)S(1)}, f32[3,32,128]{2,1,0:T(8,128)S(1)}, u32[]{:S(2)}, u32[]{:S(2)}) collective-permute-start(f32[3,32,128]{2,1,0:T(8,128)S(1)} %get-tuple-element.20.send_p), channel_id=1, source_target_pairs={{0,1},{2,3},{4,5},{6,7},{8,9},{10,11},{12,13},{14,15},{16,17},{18,... | collective-permute-start | bytes 147464 | tf_op jit(solution)/shard_map/ppermute | solution.py:446
  16.6 16.4 %copy-start.7 = (f32[5,5]{1,0:T(8,128)S(1)}, f32[5,5]{1,0:T(8,128)}, u32[]{:S(2)}) copy-start(f32[5,5]{1,0:T(8,128)} %reaction.5) | copy-start | bytes 304
  20.6 18.1 %collective-permute-start.2 = (f32[18,32,128]{2,1,0:T(8,128)S(1)}, f32[18,32,128]{2,1,0:T(8,128)S(1)}, u32[]{:S(2)}, u32[]{:S(2)}) collective-permute-start(f32[18,32,128]{2,1,0:T(8,128)S(1)} %get-tuple-element.25), channel_id=1, source_target_pairs={{0,64},{128,192},{256,320},{384,448},{64,0},{192,128},{320,256},{4... | collective-permute-start | bytes 884744 | tf_op jit(solution)/shard_map/ppermute | solution.py:446
  24.6 14.0 %collective-permute-start.3 = (f32[21,8,128]{2,1,0:T(8,128)S(1)}, f32[21,8,128]{2,1,0:T(8,128)S(1)}, u32[]{:S(2)}, u32[]{:S(2)}) collective-permute-start(f32[21,8,128]{2,1,0:T(8,128)S(1)} %get-tuple-element.26), channel_id=1, source_target_pairs={{64,128},{192,256},{320,384},{128,64},{256,192},{384,320},{65,129}... | collective-permute-start | bytes 258056 | tf_op jit(solution)/shard_map/ppermute | solution.py:446
  37.6 1.1 %copy-start.2 = (f32[5,16,32,128]{3,2,1,0:T(8,128)}, f32[5,16,32,128]{3,2,1,0:T(8,128)S(1)}, u32[]{:S(2)}) copy-start(f32[5,16,32,128]{3,2,1,0:T(8,128)S(1)} %get-tuple-element.22.first) | copy-start | bytes 3932164
  38.6 1.5 %copy-start.4 = (f32[5,16,32,128]{3,2,1,0:T(8,128)}, f32[5,16,32,128]{3,2,1,0:T(8,128)S(1)}, u32[]{:S(2)}) copy-start(f32[5,16,32,128]{3,2,1,0:T(8,128)S(1)} %get-tuple-element.23.second) | copy-start | bytes 3932164
  38.6 5.6 %copy-start.11 = (f32[16]{0:T(128)S(1)}, f32[16]{0:T(128)}, u32[]{:S(2)}) copy-start(f32[16]{0:T(128)} %param.13) | copy-start | bytes 196
  38.7 5.6 %copy-start.8 = (s32[2048,1]{0,1:T(1,128)S(1)}, s32[2048,1]{0,1:T(1,128)}, u32[]{:S(2)}) copy-start(s32[2048,1]{0,1:T(1,128)} %param.15) | copy-start | bytes 24580
  38.7 5.6 %copy-start.9 = (s32[2048]{0:T(1024)S(1)}, s32[2048]{0:T(1024)}, u32[]{:S(2)}) copy-start(s32[2048]{0:T(1024)} %param.14) | copy-start | bytes 24580
  38.7 5.6 %copy-start.10 = (f32[16,16]{1,0:T(8,128)S(1)}, f32[16,16]{1,0:T(8,128)}, u32[]{:S(2)}) copy-start(f32[16,16]{1,0:T(8,128)} %mixing.1) | copy-start | bytes 3076
  40.2 6.8 %collective-permute-start.4 = (f32[16,128]{1,0:T(8,128)S(1)}, f32[16,128]{1,0:T(8,128)S(1)}, u32[]{:S(2)}, u32[]{:S(2)}) collective-permute-start(f32[16,128]{1,0:T(8,128)S(1)} %shard_map.99._.wall), channel_id=1, source_target_pairs={{0,64},{64,128},{128,192},{192,256},{256,320},{320,384},{384,448},... | collective-permute-start | bytes 24584 | tf_op jit(solution)/shard_map/ppermute | solution.py:502
  44.3 0.9 %copy-start.6 = (f32[16,2048]{1,0:T(8,128)S(1)}, f32[16,2048]{1,0:T(8,128)}, u32[]{:S(2)}) copy-start(f32[16,2048]{1,0:T(8,128)} %particles.1) | copy-start | bytes 393220
  47.2 30.6 %collective-permute-start.5 = (f32[16,1024]{1,0:T(8,128)S(1)}, f32[16,1024]{1,0:T(8,128)S(1)}, u32[]{:S(2)}, u32[]{:S(2)}) collective-permute-start(f32[16,1024]{1,0:T(8,128)S(1)} %get-tuple-element.29), channel_id=1, source_target_pairs={{1,2},{3,4},{5,6},{7,8},{9,10},{11,12},{13,14},{15,16},{17,18},{19... | collective-permute-start | bytes 196616 | tf_op jit(solution)/shard_map/ppermute | solution.py:446
  53.2 30.6 %collective-permute-start.6 = (f32[16,1024]{1,0:T(8,128)S(1)}, f32[16,1024]{1,0:T(8,128)S(1)}, u32[]{:S(2)}, u32[]{:S(2)}) collective-permute-start(f32[16,1024]{1,0:T(8,128)S(1)} %get-tuple-element.32), channel_id=1, source_target_pairs={{2,4},{3,5},{6,8},{7,9},{10,12},{11,13},{14,16},{15,17},{18,20},{1... | collective-permute-start | bytes 196616 | tf_op jit(solution)/shard_map/ppermute | solution.py:446
  55.1 28.6 %collective-permute-start.7 = (f32[16,1024]{1,0:T(8,128)S(1)}, f32[16,1024]{1,0:T(8,128)S(1)}, u32[]{:S(2)}, u32[]{:S(2)}) collective-permute-start(f32[16,1024]{1,0:T(8,128)S(1)} %get-tuple-element.33), channel_id=1, source_target_pairs={{0,2},{1,3},{4,6},{5,7},{8,10},{9,11},{12,14},{13,15},{16,18},{17,... | collective-permute-start | bytes 196616 | tf_op jit(solution)/shard_map/ppermute | solution.py:446
  57.0 26.7 %collective-permute-start.8 = (f32[16,1024]{1,0:T(8,128)S(1)}, f32[16,1024]{1,0:T(8,128)S(1)}, u32[]{:S(2)}, u32[]{:S(2)}) collective-permute-start(f32[16,1024]{1,0:T(8,128)S(1)} %get-tuple-element.34), channel_id=1, source_target_pairs={{0,1},{2,3},{4,5},{6,7},{8,9},{10,11},{12,13},{14,15},{16,17},{18,... | collective-permute-start | bytes 196616 | tf_op jit(solution)/shard_map/ppermute | solution.py:446
  77.8 1.3 %copy-start.3 = (f32[5,16,32,128]{3,2,1,0:T(8,128)S(1)}, f32[5,16,32,128]{3,2,1,0:T(8,128)}, u32[]{:S(2)}) copy-start(f32[5,16,32,128]{3,2,1,0:T(8,128)} %copy-done.2) | copy-start | bytes 3932164
  79.1 1.3 %copy-start.5 = (f32[5,16,32,128]{3,2,1,0:T(8,128)S(1)}, f32[5,16,32,128]{3,2,1,0:T(8,128)}, u32[]{:S(2)}) copy-start(f32[5,16,32,128]{3,2,1,0:T(8,128)} %copy-done.4) | copy-start | bytes 3932164

commit v4 on v3

--- a/solution.py
+++ b/solution.py
@@ -26,6 +26,7 @@
 STRIP_AT = {key: i for i, key in enumerate(STRIPS)}
 CORNERS = [(c, 1) for c in range(COMP)] + [(c, 2) for c in range(COMP)] + [(COMP, 1)] + [(c, 0) for c in range(COMP)]
 LAYERS = 3 * COMP + 2 + 1
+SEAM = (1, 2, GX - 3, GX - 2)
 
 VMEM = pl.BlockSpec(memory_space=pltpu.VMEM)
 SMEM = pl.BlockSpec(memory_space=pltpu.SMEM)
@@ -123,22 +124,23 @@
         for_a = jnp.where(even, top, bottom)
         for_b = jnp.where(even, bottom, top)
         send_a[LAYERS - 1, rows(tile), :] = for_a
-        send_wall[LAYERS - 1 + tile] = for_b
+        send_wall[2 * (LAYERS - 1) + tile] = for_b
     at_a, at_b = jnp.where(even, GX - 3, 0), jnp.where(even, 0, GX - 3)
     kappa_a, kappa_b = jnp.where(even, GX - 2, 0), jnp.where(even, 0, GX - 2)
-    split = GR - 8
     for c in range(COMP):
         for layer in range(3):
             send_a[3 * c + layer] = gas[c, at_a + layer]
-            send_wall[3 * c + layer] = gas[c, at_b + layer, split:, :]
+            for half in range(2):
+                send_wall[2 * (3 * c + layer) + half] = gas[c, at_b + layer, rows(2 + half), :]
     for layer in range(2):
         send_a[3 * COMP + layer] = kappa[kappa_a + layer]
-        send_wall[3 * COMP + layer] = kappa[kappa_b + layer, split:, :]
-
-
-def rest_kernel(gas, kappa, send_rest):
+        for half in range(2):
+            send_wall[2 * (3 * COMP + layer) + half] = kappa[kappa_b + layer, rows(2 + half), :]
+
+
+def rest_kernel(gas, kappa, _, send_rest):
     even = lax.rem(lax.axis_index("sect"), 2) == 0
-    split = GR - 8
+    split = GR // 2
     from_b, from_kappa = jnp.where(even, 0, GX - 3), jnp.where(even, 0, GX - 2)
     for c in range(COMP):
         for layer in range(3):
@@ -238,7 +240,7 @@
     return out
 
 
-def wall_kernel(gas, kappa, strips, recv_a, recv_wall, reaction, _, wall, now, later, kap, edge):
+def wall_kernel(gas, kappa, strips, recv_wall, recv_a, reaction, _, wall, now, later, kap, edge):
     odd = lax.rem(lax.axis_index("sect"), 2)
     even = odd == 0
     mix = coupling(reaction)
@@ -250,13 +252,13 @@
             now[c, x + 3] = gas[c, x, top, :]
         for layer in range(3):
             now[c, at_a + layer] = recv_a[3 * c + layer, top, :]
-            now[c, at_b + layer] = recv_wall[3 * c + layer]
+            now[c, at_b + layer] = recv_wall[2 * (3 * c + layer) + 1]
     for x in range(GX):
         kap[x + 3] = kappa[x, top, :]
     for layer in range(2):
         kap[kappa_a + layer] = recv_a[3 * COMP + layer, top, :]
-        kap[kappa_b + layer] = recv_wall[3 * COMP + layer]
-    corner_a, corner_b = recv_a[LAYERS - 1, top, :], recv_wall[LAYERS + TILES - 2]
+        kap[kappa_b + layer] = recv_wall[2 * (3 * COMP + layer) + 1]
+    corner_a, corner_b = recv_a[LAYERS - 1, top, :], recv_wall[2 * (LAYERS - 1) + TILES - 1]
     low, high = jnp.where(even, corner_b, corner_a), jnp.where(even, corner_a, corner_b)
     strip_levels(strips, [low], [high], mix, edge, [TILES - 1])
 
@@ -271,10 +273,10 @@
                 dst[c, at] = out[c, 0]
 
 
-def inner_kernel(gas, kappa, strips, reaction, first, second, middle, edge):
+def inner_kernel(gas, kappa, strips, reaction, first, second, middle, one, two, edge):
     mix = coupling(reaction)
     strip_levels(strips, None, None, mix, edge, list(range(TILES)))
-    for step, (src, dst) in enumerate(((gas, first), (first, second), (second, middle))):
+    for step, (src, dst) in enumerate(((gas, one), (one, two), (two, middle))):
 
         def body(x, carry, step=step, src=src, dst=dst):
             out = plane(src, kappa, edge, step, x, x, mix, TILES, range(COMP))
@@ -284,22 +286,19 @@
             return carry
 
         lax.fori_loop(step + 1, GX - 1 - step, body, 0, unroll=2)
+    for c in range(COMP):
+        for i, x in enumerate(SEAM):
+            first[c, i] = one[c, x]
+            second[c, i] = two[c, x + 1 if i < 2 else x - 1]
 
 
 def outer_kernel(
-    gas, kappa, strips, first, second, middle, recv_a, recv_wall, both_rest, reaction, _, result, token, now, later, kap, edge
+    _, gas, kappa, strips, first, second, middle, recv_wall, recv_a, recv_rest, reaction, result, token, now, later, kap, edge
 ):
     token[...] = jnp.zeros((8, 128), jnp.float32)
     even = lax.rem(lax.axis_index("sect"), 2) == 0
     mix = coupling(reaction)
-    split = GR - 8
-    section, sections = lax.axis_index("sect"), lax.axis_size("sect")
-    inside = (section > 0) & (section < sections - 1)
-    other = jnp.where(even, 0, 1)
-
-    def recv_rest(layer):
-        return jnp.where(inside, both_rest[other, layer], 0.0)
-
+    split = GR // 2
     at_a, at_b = jnp.where(even, GX + 3, 0), jnp.where(even, 0, GX + 3)
     kappa_a, kappa_b = jnp.where(even, GX + 3, 1), jnp.where(even, 1, GX + 3)
     for c in range(COMP):
@@ -307,20 +306,22 @@
             now[c, x + 3] = gas[c, x]
         for layer in range(3):
             now[c, at_a + layer] = recv_a[3 * c + layer]
-            now[c, at_b + layer, split:, :] = recv_wall[3 * c + layer]
-            now[c, at_b + layer, :split, :] = recv_rest(3 * c + layer)
-        for x in (1, 2, GX - 3, GX - 2):
-            later[c, x + 3] = first[c, x]
+            for half in range(2):
+                now[c, at_b + layer, rows(2 + half), :] = recv_wall[2 * (3 * c + layer) + half]
+            now[c, at_b + layer, :split, :] = recv_rest[3 * c + layer]
+        for i, x in enumerate(SEAM):
+            later[c, x + 3] = first[c, i]
     for x in (0, 1, 2, GX - 3, GX - 2, GX - 1):
         kap[x + 3] = kappa[x]
     for layer in range(2):
         kap[kappa_a + layer] = recv_a[3 * COMP + layer]
-        kap[kappa_b + layer, split:, :] = recv_wall[3 * COMP + layer]
-        kap[kappa_b + layer, :split, :] = recv_rest(3 * COMP + layer)
+        for half in range(2):
+            kap[kappa_b + layer, rows(2 + half), :] = recv_wall[2 * (3 * COMP + layer) + half]
+        kap[kappa_b + layer, :split, :] = recv_rest[3 * COMP + layer]
     low, high = [], []
     for t in range(TILES):
         corner_a = recv_a[LAYERS - 1, rows(t), :]
-        corner_b = recv_wall[LAYERS - 1 + t]
+        corner_b = recv_wall[2 * (LAYERS - 1) + t]
         low.append(jnp.where(even, corner_b, corner_a))
         high.append(jnp.where(even, corner_a, corner_b))
     strip_levels(strips, low, high, mix, edge, list(range(TILES)))
@@ -329,8 +330,8 @@
     for step, (src, dst) in enumerate(((now, later), (later, now), (now, None))):
         if step == ITERS - 1:
             for c in range(COMP):
-                for x in (2, 3, GX - 4, GX - 3):
-                    now[c, x + 3] = second[c, x]
+                for i, x in enumerate(SEAM):
+                    now[c, (x + 1 if i < 2 else x - 1) + 3] = second[c, i]
         for i in range(3):
             for at in (step + 1 + i, GX + 2 - step + i):
                 out = plane(src, kap, edge, step, at, at - 3, mix, TILES, range(COMP))
@@ -465,42 +466,6 @@
     )(gas, kappa)
     recv_q = swap(send_q, "blk", pairs_q)
     recv_p = swap(send_p, "blk", pairs_p)
-    send_rest = call(rest_kernel, f32(LAYERS - 1, GR - 8, GA), specs=[VMEM] * 2, moved=1 << 18)(gas, kappa)
-    groups = [list(pair) for pair in pairs_b] + [[0, sections - 1]]
-    both_rest = lax.all_gather(send_rest, "sect", axis_index_groups=groups)
-
-    strips, send_a, send_wall = call(
-        strips_kernel,
-        (f32(len(STRIPS), GR, GA), f32(LAYERS, GR, GA), f32(LAYERS - 1 + TILES, 8, GA)),
-        specs=[VMEM] * 6 + [ANY],
-        moved=2 << 20,
-    )(gas, kappa, send_q, send_p, recv_q, recv_p, send_rest)
-    recv_wall = swap(send_wall, "sect", pairs_b)
-    recv_a = swap(send_a, "sect", pairs_a)
-
-    whole = f32(COMP, GX, GR, GA)
-    first, second, middle = call(
-        inner_kernel,
-        (whole, whole, f32(COMP, GX - 6, GR, GA)),
-        scratch=[pltpu.VMEM((ITERS, COMP, GR, GA), jnp.float32)],
-        specs=[VMEM] * 3 + [SMEM],
-        moved=12 << 20,
-    )(gas, kappa, strips, reaction)
-
-    wall = call(
-        wall_kernel,
-        f32(GX, GA),
-        scratch=[
-            pltpu.VMEM((COMP, EXT, 8, GA), jnp.float32),
-            pltpu.VMEM((COMP, EXT, 8, GA), jnp.float32),
-            pltpu.VMEM((EXT, 8, GA), jnp.float32),
-            pltpu.VMEM((ITERS, COMP, 8, GA), jnp.float32),
-        ],
-        specs=[VMEM] * 5 + [SMEM, ANY],
-        moved=4 << 20,
-    )(gas, kappa, strips, recv_a, recv_wall, reaction, middle)
-    earlier = lax.ppermute(wall, "sect", [(i, i + 1) for i in range(sections - 1)])
-
     heating_column = heating.reshape(VALS, 1)
     packed, cells = call(
         pack_kernel,
@@ -514,7 +479,47 @@
         ],
         specs=[VMEM] * 5 + [ANY],
         moved=4 << 20,
-    )(tile_hop.reshape(CHUNKS, 128), wall_cell.reshape(CHUNKS, 128), particles, mixing, heating_column, wall)
+    )(tile_hop.reshape(CHUNKS, 128), wall_cell.reshape(CHUNKS, 128), particles, mixing, heating_column, send_p)
+
+    strips, send_a, send_wall = call(
+        strips_kernel,
+        (f32(len(STRIPS), GR, GA), f32(LAYERS, GR, GA), f32(2 * (LAYERS - 1) + TILES, 8, GA)),
+        specs=[VMEM] * 6 + [ANY],
+        moved=2 << 20,
+    )(gas, kappa, send_q, send_p, recv_q, recv_p, cells)
+    recv_wall = swap(send_wall, "sect", pairs_b)
+    recv_a = swap(send_a, "sect", pairs_a)
+
+    whole = f32(COMP, GX, GR, GA)
+    first, second, middle = call(
+        inner_kernel,
+        (f32(COMP, len(SEAM), GR, GA), f32(COMP, len(SEAM), GR, GA), f32(COMP, GX - 6, GR, GA)),
+        scratch=[
+            pltpu.VMEM((COMP, GX, GR, GA), jnp.float32),
+            pltpu.VMEM((COMP, GX, GR, GA), jnp.float32),
+            pltpu.VMEM((ITERS, COMP, GR, GA), jnp.float32),
+        ],
+        specs=[VMEM] * 3 + [SMEM],
+        moved=12 << 20,
+    )(gas, kappa, strips, reaction)
+
+    send_rest = call(rest_kernel, f32(LAYERS - 1, GR // 2, GA), specs=[VMEM] * 2 + [ANY], moved=1 << 18)(gas, kappa, middle)
+    recv_rest = swap(send_rest, "sect", pairs_b)
+
+    wall = call(
+        wall_kernel,
+        f32(GX, GA),
+        scratch=[
+            pltpu.VMEM((COMP, EXT, 8, GA), jnp.float32),
+            pltpu.VMEM((COMP, EXT, 8, GA), jnp.float32),
+            pltpu.VMEM((EXT, 8, GA), jnp.float32),
+            pltpu.VMEM((ITERS, COMP, 8, GA), jnp.float32),
+        ],
+        specs=[VMEM] * 5 + [SMEM, ANY],
+        moved=4 << 20,
+    )(gas, kappa, strips, recv_wall, recv_a, reaction, send_rest)
+    earlier = lax.ppermute(wall, "sect", [(i, i + 1) for i in range(sections - 1)])
+
     own, *sends = call(
         heat_kernel,
         (f32(VALS, CAP),) * MOVES,
@@ -533,9 +538,9 @@
             pltpu.VMEM((EXT, GR, GA), jnp.float32),
             pltpu.VMEM((ITERS, COMP, GR, GA), jnp.float32),
         ],
-        specs=[VMEM] * 9 + [SMEM, ANY],
+        specs=[ANY] + [VMEM] * 9 + [SMEM],
         moved=8 << 20,
-    )(gas, kappa, strips, first, second, middle, recv_a, recv_wall, both_rest, reaction, pieces[0])
+    )(pieces[0], gas, kappa, strips, first, second, middle, recv_wall, recv_a, recv_rest, reaction)
     arrived = call(
         join_kernel,
         f32(VALS, MOVES * CAP),

time: 84.9 us -> 69.8 us (0.82)
  blocking collectives: 15.1 us -> 0 us
  starting transfers between devices: 45.5 us -> 50.1 us
  waiting for transfers between devices: 3.14 us -> 0.79 us
  local copies, waits for them, and re-layouts: 4.71 us -> 2.4 us
    all_gather x1 -> x0, blocking collectives: 15.1 us -> none  [local(): both_rest = lax.all_gather(send_rest, 'sect', axis_index_groups=groups)]
    ppermute x1, starting transfers between devices: 4.04 us -> 7.55 us  [local(): lax.ppermute(wall, 'sect', [(i, i + 1) for i in range(sections - 1)])]
    ppermute x8 -> x9, waiting for transfers between devices: 3.14 us -> 0.02 us  [swap(): return lax.ppermute(x, axis, pairs + [(j, i) for i, j in pairs])]
    unnamed x24 -> x16, local copies, waits for them, and re-layouts: 4.63 us -> 2.32 us
    ppermute x8 -> x9, starting transfers between devices: 41.5 us -> 42.6 us  [swap(): return lax.ppermute(x, axis, pairs + [(j, i) for i, j in pairs])]
  transfers between devices with their start and end apart: 9 -> 10, of which waited for: 1 -> 1; matrix products, arithmetic and copies ran while one was open for 0% -> 0% of each run, Pallas kernels for 11% -> 16%
where the time goes in v4:
time: 69.8 us; the launch traced here: 69.4 us
  starting transfers between devices  50.1 us (72%)
  Pallas kernels  15.2 us (22%)
  local copies, waits for them, and re-layouts  2.4 us (3%)
  between operations  0.89 us (1%)
  waiting for transfers between devices  0.79 us (1%)
    ppermute x9, starting transfers between devices, swap(): return lax.ppermute(x, axis, pairs + [(j, i) for i, j in pairs])  42.6 us
    ppermute x1, starting transfers between devices, local(): lax.ppermute(wall, 'sect', [(i, i + 1) for i in range(sections - 1)])  7.55 us
    pallas_call x1, Pallas kernels, local(): call(inner_kernel, (f32(COMP, len(SEAM), GR, GA), f32(COMP, len(SEAM), GR...  4.56 us
    pallas_call x1, Pallas kernels, local(): call(outer_kernel, (whole, f32(8, 128)), scratch=[pltpu.VMEM((COMP, EXT,...  3.41 us
    unnamed x16, local copies, waits for them, and re-layouts  2.32 us
    pallas_call x1, Pallas kernels, local(): call(edges_kernel, (f32(3, GR, GA), f32(3, GR, GA)), scratch=[pltpu.VMEM(...  2.18 us
    pallas_call x1, Pallas kernels, local(): call(pack_kernel, (f32(MOVES, VALS, CAP), i32(MOVES, SPOTS, 128)), scratc...  1.74 us
    pallas_call x1, Pallas kernels, local(): call(wall_kernel, f32(GX, GA), scratch=[pltpu.VMEM((COMP, EXT, 8, GA), jn...  1.45 us
  transfers between devices with their start and end apart: 10, of which 1 were waited for; matrix products, arithmetic and copies ran while one was open for 0% of the time, Pallas kernels for 16%

profile of v4, /device:TPU:1, one launch (start us, length us, event | category | flops | bytes accessed | tf_op | source)
XLA Modules:
  0.0 69.4 jit_solution(2514669295753097650)
XLA Ops:
  0.6 0.0 copy-start.1
  0.6 0.0 copy-start
  0.7 0.0 copy-start.7
  0.7 0.0 copy-start.4
  0.7 2.2 %shard_map.95 = (f32[3,32,128]{2,1,0:T(8,128)S(1)}, f32[3,32,128]{2,1,0:T(8,128)S(1)}) custom-call(f32[5,16,32,128]{3,2,1,0:T(8,128)} %gas.11, f32[16,32,128]{2,1,0:T(8,128)} %kappa.11), custom_call_target="tpu_custom_call" | custom-call | bytes 2097152 | tf_op jit(solution)/shard_map/pallas_call | solution.py:459
  2.9 0.0 copy-start.3
  2.9 11.7 %collective-permute-start = (f32[3,32,128]{2,1,0:T(8,128)S(1)}, f32[3,32,128]{2,1,0:T(8,128)S(1)}, u32[]{:S(2)}, u32[]{:S(2)}) collective-permute-start(f32[3,32,128]{2,1,0:T(8,128)S(1)} %get-tuple-element.19.send_q), channel_id=1, source_target_pairs={{1,2},{3,4},{5,6},{7,8},{9,10},{11,12},{13,14},{15,16},{17,18},{19... | collective-permute-start | bytes 147464 | tf_op jit(solution)/shard_map/ppermute | solution.py:447
  14.6 1.9 %collective-permute-start.1 = (f32[3,32,128]{2,1,0:T(8,128)S(1)}, f32[3,32,128]{2,1,0:T(8,128)S(1)}, u32[]{:S(2)}, u32[]{:S(2)}) collective-permute-start(f32[3,32,128]{2,1,0:T(8,128)S(1)} %get-tuple-element.20._.send_p), channel_id=1, source_target_pairs={{0,1},{2,3},{4,5},{6,7},{8,9},{10,11},{12,13},{14,15},{16,17},{18,... | collective-permute-start | bytes 147464 | tf_op jit(solution)/shard_map/ppermute | solution.py:447
  16.5 0.0 copy-done.7
  16.5 0.1 copy.10.heating
  16.6 0.0 copy-done.4
  16.6 0.0 copy-start.2
  16.6 0.9 %copy-done.2 = f32[16,2048]{1,0:T(8,128)S(1)} copy-done((f32[16,2048]{1,0:T(8,128)S(1)}, f32[16,2048]{1,0:T(8,128)}, u32[]{:S(2)}) %copy-start.2) | copy-done | bytes 131096
  17.5 0.0 copy-start.5
  17.5 0.7 %copy-done.5 = s32[2048]{0:T(1024)S(1)} copy-done((s32[2048]{0:T(1024)S(1)}, s32[2048]{0:T(1024)}, u32[]{:S(2)}) %copy-start.5) | copy-done | bytes 8216
  18.2 0.0 copy-start.6
  18.2 0.7 %copy-done.6 = f32[16,16]{1,0:T(8,128)S(1)} copy-done((f32[16,16]{1,0:T(8,128)S(1)}, f32[16,16]{1,0:T(8,128)}, u32[]{:S(2)}) %copy-start.6) | copy-done | bytes 1048
  18.9 1.7 %shard_map.96 = (f32[5,16,1024]{2,1,0:T(8,128)S(1)}, s32[5,8,128]{2,1,0:T(8,128)S(1)}) custom-call(s32[16,128]{1,0:T(8,128)S(1)} %bitcast.3, s32[16,128]{1,0:T(8,128)S(1)} %bitcast.4, f32[16,2048]{1,0:T(8,128)S(1)} %copy-done.2, f32[16,16]{1,0:T(8,128)S(1)} %copy-done.6, f32[16,1]{1,0:T(8,128)S(1)} %copy.10.heating, f32[3,32,128]{2,1,0:T(8,128)S(1)} %get-tuple-element.20._.send_p), custom_call_target="tpu_custom_call" | custom-call | bytes 4194304 | tf_op jit(solution)/shard_map/pallas_call | solution.py:470
  20.7 0.0 collective-permute-done.recv_q
  20.7 0.0 collective-permute-done.1.recv_p
  20.7 0.0 copy-done.1
  20.7 0.0 copy-done
  20.7 0.8 %shard_map.97 = (f32[28,32,128]{2,1,0:T(8,128)S(1)}, f32[18,32,128]{2,1,0:T(8,128)S(1)}, f32[38,8,128]{2,1,0:T(8,128)S(1)}) custom-call(f32[5,16,32,128]{3,2,1,0:T(8,128)S(1)} %copy-done, f32[16,32,128]{2,1,0:T(8,128)S(1)} %copy-done.1, f32[3,32,128]{2,1,0:T(8,128)S(1)} %get-tuple-element.19.send_q, f32[3,32,128]{2,1,0:T(8,128)S(1)} %get-tuple-element.20._.send_p, ...), custom_call_target="tpu_custom_call" | custom-call | bytes 2097152 | tf_op jit(solution)/shard_map/pallas_call | solution.py:484
  21.6 3.1 %collective-permute-start.3 = (f32[18,32,128]{2,1,0:T(8,128)S(1)}, f32[18,32,128]{2,1,0:T(8,128)S(1)}, u32[]{:S(2)}, u32[]{:S(2)}) collective-permute-start(f32[18,32,128]{2,1,0:T(8,128)S(1)} %get-tuple-element.24), channel_id=1, source_target_pairs={{0,64},{128,192},{256,320},{384,448},{64,0},{192,128},{320,256},{4... | collective-permute-start | bytes 884744 | tf_op jit(solution)/shard_map/ppermute | solution.py:447
  24.6 8.5 %collective-permute-start.2 = (f32[38,8,128]{2,1,0:T(8,128)S(1)}, f32[38,8,128]{2,1,0:T(8,128)S(1)}, u32[]{:S(2)}, u32[]{:S(2)}) collective-permute-start(f32[38,8,128]{2,1,0:T(8,128)S(1)} %get-tuple-element.23), channel_id=1, source_target_pairs={{64,128},{192,256},{320,384},{128,64},{256,192},{384,320},{65,129}... | collective-permute-start | bytes 466952 | tf_op jit(solution)/shard_map/ppermute | solution.py:447
  33.2 0.0 copy-done.3
  33.2 4.6 %shard_map.98 = (f32[5,4,32,128]{3,2,1,0:T(8,128)S(1)}, f32[5,4,32,128]{3,2,1,0:T(8,128)S(1)}, f32[5,10,32,128]{3,2,1,0:T(8,128)S(1)}) custom-call(f32[5,16,32,128]{3,2,1,0:T(8,128)S(1)} %copy-done, f32[16,32,128]{2,1,0:T(8,128)S(1)} %copy-done.1, f32[28,32,128]{2,1,0:T(8,128)S(1)} %get-tuple-element.22.strips, f32[5,5]{1,0:T(8,128)S(1)} %copy-done.3), custom_call_target="tpu_custom_call" | custom-call | bytes 12582912 | tf_op jit(solution)/shard_map/pallas_call | solution.py:494
  37.8 1.9 %collective-permute-start.6 = (f32[17,16,128]{2,1,0:T(8,128)S(1)}, f32[17,16,128]{2,1,0:T(8,128)S(1)}, u32[]{:S(2)}, u32[]{:S(2)}) collective-permute-start(f32[17,16,128]{2,1,0:T(8,128)S(1)} %shard_map.99._), channel_id=1, source_target_pairs={{64,128},{192,256},{320,384},{128,64},{256,192},{384,320},{65,129}... | collective-permute-start | bytes 417800 | tf_op jit(solution)/shard_map/ppermute | solution.py:447
  39.7 0.0 collective-permute-done.2.recv_wall
  39.7 0.0 collective-permute-done.3.recv_a
  39.7 1.5 %shard_map.100.wall = f32[16,128]{1,0:T(8,128)S(1)} custom-call(f32[5,16,32,128]{3,2,1,0:T(8,128)S(1)} %copy-done, f32[16,32,128]{2,1,0:T(8,128)S(1)} %copy-done.1, f32[28,32,128]{2,1,0:T(8,128)S(1)} %get-tuple-element.22.strips, f32[38,8,128]{2,1,0:T(8,128)S(1)} %collective-permute-done.2.recv_wall, f32[18,32,128]{2,1,0:T(8,128)S(1)} %collective-permute-done.3.recv_a, ...), custom_call_target="tpu_custom_call" | custom-call | bytes 4194304 | tf_op jit(solution)/shard_map/pallas_call | solution.py:509
  41.2 7.5 %collective-permute-start.4 = (f32[16,128]{1,0:T(8,128)S(1)}, f32[16,128]{1,0:T(8,128)S(1)}, u32[]{:S(2)}, u32[]{:S(2)}) collective-permute-start(f32[16,128]{1,0:T(8,128)S(1)} %shard_map.100.wall), channel_id=1, source_target_pairs={{0,64},{64,128},{128,192},{192,256},{256,320},{320,384},{384,448},... | collective-permute-start | bytes 24584 | tf_op jit(solution)/shard_map/ppermute | solution.py:521
  48.7 0.8 %collective-permute-done.4.earlier = f32[16,128]{1,0:T(8,128)S(1)} collective-permute-done((f32[16,128]{1,0:T(8,128)S(1)}, f32[16,128]{1,0:T(8,128)S(1)}, u32[]{:S(2)}, u32[]{:S(2)}) %collective-permute-start.4) | collective-permute-done | bytes 8224 | tf_op jit(solution)/shard_map/ppermute | solution.py:521
  49.5 0.2 shard_map.101
  49.7 5.6 %collective-permute-start.5 = (f32[16,1024]{1,0:T(8,128)S(1)}, f32[16,1024]{1,0:T(8,128)S(1)}, u32[]{:S(2)}, u32[]{:S(2)}) collective-permute-start(f32[16,1024]{1,0:T(8,128)S(1)} %get-tuple-element.27), channel_id=1, source_target_pairs={{1,2},{3,4},{5,6},{7,8},{9,10},{11,12},{13,14},{15,16},{17,18},{19... | collective-permute-start | bytes 196616 | tf_op jit(solution)/shard_map/ppermute | solution.py:447
  55.3 1.9 %collective-permute-start.7 = (f32[16,1024]{1,0:T(8,128)S(1)}, f32[16,1024]{1,0:T(8,128)S(1)}, u32[]{:S(2)}, u32[]{:S(2)}) collective-permute-start(f32[16,1024]{1,0:T(8,128)S(1)} %get-tuple-element.32), channel_id=1, source_target_pairs={{2,4},{3,5},{6,8},{7,9},{10,12},{11,13},{14,16},{15,17},{18,20},{1... | collective-permute-start | bytes 196616 | tf_op jit(solution)/shard_map/ppermute | solution.py:447
  57.3 1.9 %collective-permute-start.8 = (f32[16,1024]{1,0:T(8,128)S(1)}, f32[16,1024]{1,0:T(8,128)S(1)}, u32[]{:S(2)}, u32[]{:S(2)}) collective-permute-start(f32[16,1024]{1,0:T(8,128)S(1)} %get-tuple-element.33), channel_id=1, source_target_pairs={{0,2},{1,3},{4,6},{5,7},{8,10},{9,11},{12,14},{13,15},{16,18},{17,... | collective-permute-start | bytes 196616 | tf_op jit(solution)/shard_map/ppermute | solution.py:447
  59.2 6.0 %collective-permute-start.9 = (f32[16,1024]{1,0:T(8,128)S(1)}, f32[16,1024]{1,0:T(8,128)S(1)}, u32[]{:S(2)}, u32[]{:S(2)}) collective-permute-start(f32[16,1024]{1,0:T(8,128)S(1)} %get-tuple-element.34), channel_id=1, source_target_pairs={{0,1},{2,3},{4,5},{6,7},{8,9},{10,11},{12,13},{14,15},{16,17},{18,... | collective-permute-start | bytes 196616 | tf_op jit(solution)/shard_map/ppermute | solution.py:447
  65.2 0.0 collective-permute-done.6.recv_rest
  65.2 0.0 collective-permute-done.5._.recv_q
  65.2 3.4 %shard_map.102 = (f32[5,16,32,128]{3,2,1,0:T(8,128)}, f32[8,128]{1,0:T(8,128)S(1)}) custom-call(f32[16,1024]{1,0:T(8,128)S(1)} %collective-permute-done.5._.recv_q, f32[5,16,32,128]{3,2,1,0:T(8,128)S(1)} %copy-done, f32[16,32,128]{2,1,0:T(8,128)S(1)} %copy-done.1, f32[28,32,128]{2,1,0:T(8,128)S(1)} %get-tuple-element.22.strips, ...), custom_call_target="tpu_custom_call" | custom-call | bytes 8388608 | tf_op jit(solution)/shard_map/pallas_call | solution.py:532
  68.6 0.0 collective-permute-done.7.recv_s
  68.6 0.0 collective-permute-done.8.recv_r
  68.6 0.0 collective-permute-done.9.recv_p
  68.6 0.8 %shard_map.103 = f32[16,5120]{1,0:T(8,128)} custom-call(f32[16,1024]{1,0:T(8,128)S(1)} %get-tuple-element.31.own, f32[16,1024]{1,0:T(8,128)S(1)} %collective-permute-done.5._.recv_q, f32[16,1024]{1,0:T(8,128)S(1)} %collective-permute-done.7.recv_s, f32[16,1024]{1,0:T(8,128)S(1)} %collective-permute-done.8.recv_r, ...), custom_call_target="tpu_custom_call" | custom-call | bytes 1048576 | tf_op jit(solution)/shard_map/pallas_call | solution.py:544
  (1 shorter events, 0.0 us)
Async XLA Ops:
  0.6 20.1 %copy-start.1 = (f32[16,32,128]{2,1,0:T(8,128)S(1)}, f32[16,32,128]{2,1,0:T(8,128)}, u32[]{:S(2)}) copy-start(f32[16,32,128]{2,1,0:T(8,128)} %kappa.11) | copy-start | bytes 786436
  0.6 20.1 %copy-start = (f32[5,16,32,128]{3,2,1,0:T(8,128)S(1)}, f32[5,16,32,128]{3,2,1,0:T(8,128)}, u32[]{:S(2)}) copy-start(f32[5,16,32,128]{3,2,1,0:T(8,128)} %gas.11) | copy-start | bytes 3932164
  0.7 15.9 %copy-start.7 = (f32[16]{0:T(128)S(1)}, f32[16]{0:T(128)}, u32[]{:S(2)}) copy-start(f32[16]{0:T(128)} %param.13) | copy-start | bytes 196
  0.7 16.0 %copy-start.4 = (s32[2048,1]{0,1:T(1,128)S(1)}, s32[2048,1]{0,1:T(1,128)}, u32[]{:S(2)}) copy-start(s32[2048,1]{0,1:T(1,128)} %param.15) | copy-start | bytes 24580
  2.9 30.3 %copy-start.3 = (f32[5,5]{1,0:T(8,128)S(1)}, f32[5,5]{1,0:T(8,128)}, u32[]{:S(2)}) copy-start(f32[5,5]{1,0:T(8,128)} %reaction.5) | copy-start | bytes 304
  2.9 17.8 %collective-permute-start = (f32[3,32,128]{2,1,0:T(8,128)S(1)}, f32[3,32,128]{2,1,0:T(8,128)S(1)}, u32[]{:S(2)}, u32[]{:S(2)}) collective-permute-start(f32[3,32,128]{2,1,0:T(8,128)S(1)} %get-tuple-element.19.send_q), channel_id=1, source_target_pairs={{1,2},{3,4},{5,6},{7,8},{9,10},{11,12},{13,14},{15,16},{17,18},{19... | collective-permute-start | bytes 147464 | tf_op jit(solution)/shard_map/ppermute | solution.py:447
  14.6 6.1 %collective-permute-start.1 = (f32[3,32,128]{2,1,0:T(8,128)S(1)}, f32[3,32,128]{2,1,0:T(8,128)S(1)}, u32[]{:S(2)}, u32[]{:S(2)}) collective-permute-start(f32[3,32,128]{2,1,0:T(8,128)S(1)} %get-tuple-element.20._.send_p), channel_id=1, source_target_pairs={{0,1},{2,3},{4,5},{6,7},{8,9},{10,11},{12,13},{14,15},{16,17},{18,... | collective-permute-start | bytes 147464 | tf_op jit(solution)/shard_map/ppermute | solution.py:447
  16.6 0.9 %copy-start.2 = (f32[16,2048]{1,0:T(8,128)S(1)}, f32[16,2048]{1,0:T(8,128)}, u32[]{:S(2)}) copy-start(f32[16,2048]{1,0:T(8,128)} %particles.1) | copy-start | bytes 393220
  17.5 0.7 %copy-start.5 = (s32[2048]{0:T(1024)S(1)}, s32[2048]{0:T(1024)}, u32[]{:S(2)}) copy-start(s32[2048]{0:T(1024)} %param.14) | copy-start | bytes 24580
  18.2 0.7 %copy-start.6 = (f32[16,16]{1,0:T(8,128)S(1)}, f32[16,16]{1,0:T(8,128)}, u32[]{:S(2)}) copy-start(f32[16,16]{1,0:T(8,128)} %mixing.1) | copy-start | bytes 3076
  21.6 18.1 %collective-permute-start.3 = (f32[18,32,128]{2,1,0:T(8,128)S(1)}, f32[18,32,128]{2,1,0:T(8,128)S(1)}, u32[]{:S(2)}, u32[]{:S(2)}) collective-permute-start(f32[18,32,128]{2,1,0:T(8,128)S(1)} %get-tuple-element.24), channel_id=1, source_target_pairs={{0,64},{128,192},{256,320},{384,448},{64,0},{192,128},{320,256},{4... | collective-permute-start | bytes 884744 | tf_op jit(solution)/shard_map/ppermute | solution.py:447
  24.6 15.1 %collective-permute-start.2 = (f32[38,8,128]{2,1,0:T(8,128)S(1)}, f32[38,8,128]{2,1,0:T(8,128)S(1)}, u32[]{:S(2)}, u32[]{:S(2)}) collective-permute-start(f32[38,8,128]{2,1,0:T(8,128)S(1)} %get-tuple-element.23), channel_id=1, source_target_pairs={{64,128},{192,256},{320,384},{128,64},{256,192},{384,320},{65,129}... | collective-permute-start | bytes 466952 | tf_op jit(solution)/shard_map/ppermute | solution.py:447
  37.8 27.4 %collective-permute-start.6 = (f32[17,16,128]{2,1,0:T(8,128)S(1)}, f32[17,16,128]{2,1,0:T(8,128)S(1)}, u32[]{:S(2)}, u32[]{:S(2)}) collective-permute-start(f32[17,16,128]{2,1,0:T(8,128)S(1)} %shard_map.99._), channel_id=1, source_target_pairs={{64,128},{192,256},{320,384},{128,64},{256,192},{384,320},{65,129}... | collective-permute-start | bytes 417800 | tf_op jit(solution)/shard_map/ppermute | solution.py:447
  41.2 8.3 %collective-permute-start.4 = (f32[16,128]{1,0:T(8,128)S(1)}, f32[16,128]{1,0:T(8,128)S(1)}, u32[]{:S(2)}, u32[]{:S(2)}) collective-permute-start(f32[16,128]{1,0:T(8,128)S(1)} %shard_map.100.wall), channel_id=1, source_target_pairs={{0,64},{64,128},{128,192},{192,256},{256,320},{320,384},{384,448},... | collective-permute-start | bytes 24584 | tf_op jit(solution)/shard_map/ppermute | solution.py:521
  49.7 15.5 %collective-permute-start.5 = (f32[16,1024]{1,0:T(8,128)S(1)}, f32[16,1024]{1,0:T(8,128)S(1)}, u32[]{:S(2)}, u32[]{:S(2)}) collective-permute-start(f32[16,1024]{1,0:T(8,128)S(1)} %get-tuple-element.27), channel_id=1, source_target_pairs={{1,2},{3,4},{5,6},{7,8},{9,10},{11,12},{13,14},{15,16},{17,18},{19... | collective-permute-start | bytes 196616 | tf_op jit(solution)/shard_map/ppermute | solution.py:447
  55.3 13.3 %collective-permute-start.7 = (f32[16,1024]{1,0:T(8,128)S(1)}, f32[16,1024]{1,0:T(8,128)S(1)}, u32[]{:S(2)}, u32[]{:S(2)}) collective-permute-start(f32[16,1024]{1,0:T(8,128)S(1)} %get-tuple-element.32), channel_id=1, source_target_pairs={{2,4},{3,5},{6,8},{7,9},{10,12},{11,13},{14,16},{15,17},{18,20},{1... | collective-permute-start | bytes 196616 | tf_op jit(solution)/shard_map/ppermute | solution.py:447
  57.3 11.3 %collective-permute-start.8 = (f32[16,1024]{1,0:T(8,128)S(1)}, f32[16,1024]{1,0:T(8,128)S(1)}, u32[]{:S(2)}, u32[]{:S(2)}) collective-permute-start(f32[16,1024]{1,0:T(8,128)S(1)} %get-tuple-element.33), channel_id=1, source_target_pairs={{0,2},{1,3},{4,6},{5,7},{8,10},{9,11},{12,14},{13,15},{16,18},{17,... | collective-permute-start | bytes 196616 | tf_op jit(solution)/shard_map/ppermute | solution.py:447
  59.2 9.4 %collective-permute-start.9 = (f32[16,1024]{1,0:T(8,128)S(1)}, f32[16,1024]{1,0:T(8,128)S(1)}, u32[]{:S(2)}, u32[]{:S(2)}) collective-permute-start(f32[16,1024]{1,0:T(8,128)S(1)} %get-tuple-element.34), channel_id=1, source_target_pairs={{0,1},{2,3},{4,5},{6,7},{8,9},{10,11},{12,13},{14,15},{16,17},{18,... | collective-permute-start | bytes 196616 | tf_op jit(solution)/shard_map/ppermute | solution.py:447

commit v5 on v4

--- a/solution.py
+++ b/solution.py
@@ -94,7 +94,7 @@
                 out[pair, rows(tile), :] = jnp.where(lane < 64, pick(first, index), pick(second, index))
 
 
-def strips_kernel(gas, kappa, send_q, send_p, recv_q, recv_p, _, strips, send_a, send_wall):
+def strips_kernel(gas, kappa, send_q, send_p, recv_q, recv_p, strips, send_a, send_wall):
     lane = lanes()
     low_side = (lane & 1) == 1
     cell = jnp.clip((lane >> 1) - 3, 0, GX - 1)
@@ -177,15 +177,17 @@
     return sums
 
 
-def radial_sum_of(src, c, at, values):
+def radial_sum_of(src, c, at, t, value):
     sub = lax.broadcasted_iota(jnp.int32, (8, 128), 0)
-    sums = []
-    for t in range(TILES):
-        first, last = t == 0, t == TILES - 1
-        below = jnp.where(sub == 0, values[t], pltpu.roll(values[t], 1, 0)) if first else src[c, at, 8 * t - 1 : 8 * t + 7, :]
-        above = jnp.where(sub == 7, values[t], pltpu.roll(values[t], 7, 0)) if last else src[c, at, 8 * t + 1 : 8 * t + 9, :]
-        sums.append(below + above)
-    return sums
+    if t == 0:
+        below = jnp.where(sub == 0, value, pltpu.roll(value, 1, 0))
+    else:
+        below = src[c, at, 8 * t - 1 : 8 * t + 7, :]
+    if t == TILES - 1:
+        above = jnp.where(sub == 7, value, pltpu.roll(value, 7, 0))
+    else:
+        above = src[c, at, 8 * t + 1 : 8 * t + 9, :]
+    return below + above
 
 
 def strip_levels(strips, low_corner, high_corner, mix, edge, tiles):
@@ -225,18 +227,18 @@
     lane = lanes()
     first, last = lane == 0, lane == 127
     shift = 121 - 2 * x
-    values = [[src[c, at, rows(t), :] for t in range(count)] for c in range(COMP)]
     kap = [kappa[at, rows(t), :] for t in range(count)]
     out = {}
-    for c in comps:
-        radial = radial_sum(values[c], True) if count == 1 else radial_sum_of(src, c, at, values[c])
-        for t in range(count):
-            value = values[c][t]
+    for t in range(count):
+        values = [src[c, at, rows(t), :] for c in range(COMP)]
+        for c in comps:
+            value = values[c]
             beyond = pltpu.roll(edge[step, c, rows(t), :], shift, 1)
-            around = src[c, at - 1, rows(t), :] + src[c, at + 1, rows(t), :] + radial[t]
+            around = src[c, at - 1, rows(t), :] + src[c, at + 1, rows(t), :]
+            around = around + (radial_sum([value], True)[0] if count == 1 else radial_sum_of(src, c, at, t, value))
             around = around + jnp.where(first, beyond, pltpu.roll(value, 1, 1))
             around = around + jnp.where(last, beyond, pltpu.roll(value, 127, 1))
-            out[c, t] = updated(c, [values[d][t] for d in range(COMP)], around, kap[t], mix)
+            out[c, t] = updated(c, values, around, kap[t], mix)
     return out
 
 
@@ -466,6 +468,45 @@
     )(gas, kappa)
     recv_q = swap(send_q, "blk", pairs_q)
     recv_p = swap(send_p, "blk", pairs_p)
+    strips, send_a, send_wall = call(
+        strips_kernel,
+        (f32(len(STRIPS), GR, GA), f32(LAYERS, GR, GA), f32(2 * (LAYERS - 1) + TILES, 8, GA)),
+        specs=[VMEM] * 6,
+        moved=2 << 20,
+    )(gas, kappa, send_q, send_p, recv_q, recv_p)
+    recv_wall = swap(send_wall, "sect", pairs_b)
+    recv_a = swap(send_a, "sect", pairs_a)
+
+    whole = f32(COMP, GX, GR, GA)
+    first, second, middle = call(
+        inner_kernel,
+        (f32(COMP, len(SEAM), GR, GA), f32(COMP, len(SEAM), GR, GA), f32(COMP, GX - 6, GR, GA)),
+        scratch=[
+            pltpu.VMEM((COMP, GX, GR, GA), jnp.float32),
+            pltpu.VMEM((COMP, GX, GR, GA), jnp.float32),
+            pltpu.VMEM((ITERS, COMP, GR, GA), jnp.float32),
+        ],
+        specs=[VMEM] * 3 + [SMEM],
+        moved=12 << 20,
+    )(gas, kappa, strips, reaction)
+
+    send_rest = call(rest_kernel, f32(LAYERS - 1, GR // 2, GA), specs=[VMEM] * 2 + [ANY], moved=1 << 18)(gas, kappa, middle)
+    recv_rest = swap(send_rest, "sect", pairs_b)
+
+    wall = call(
+        wall_kernel,
+        f32(GX, GA),
+        scratch=[
+            pltpu.VMEM((COMP, EXT, 8, GA), jnp.float32),
+            pltpu.VMEM((COMP, EXT, 8, GA), jnp.float32),
+            pltpu.VMEM((EXT, 8, GA), jnp.float32),
+            pltpu.VMEM((ITERS, COMP, 8, GA), jnp.float32),
+        ],
+        specs=[VMEM] * 5 + [SMEM, ANY],
+        moved=4 << 20,
+    )(gas, kappa, strips, recv_wall, recv_a, reaction, send_rest)
+    earlier = lax.ppermute(wall, "sect", [(i, i + 1) for i in range(sections - 1)])
+
     heating_column = heating.reshape(VALS, 1)
     packed, cells = call(
         pack_kernel,
@@ -479,47 +520,7 @@
         ],
         specs=[VMEM] * 5 + [ANY],
         moved=4 << 20,
-    )(tile_hop.reshape(CHUNKS, 128), wall_cell.reshape(CHUNKS, 128), particles, mixing, heating_column, send_p)
-
-    strips, send_a, send_wall = call(
-        strips_kernel,
-        (f32(len(STRIPS), GR, GA), f32(LAYERS, GR, GA), f32(2 * (LAYERS - 1) + TILES, 8, GA)),
-        specs=[VMEM] * 6 + [ANY],
-        moved=2 << 20,
-    )(gas, kappa, send_q, send_p, recv_q, recv_p, cells)
-    recv_wall = swap(send_wall, "sect", pairs_b)
-    recv_a = swap(send_a, "sect", pairs_a)
-
-    whole = f32(COMP, GX, GR, GA)
-    first, second, middle = call(
-        inner_kernel,
-        (f32(COMP, len(SEAM), GR, GA), f32(COMP, len(SEAM), GR, GA), f32(COMP, GX - 6, GR, GA)),
-        scratch=[
-            pltpu.VMEM((COMP, GX, GR, GA), jnp.float32),
-            pltpu.VMEM((COMP, GX, GR, GA), jnp.float32),
-            pltpu.VMEM((ITERS, COMP, GR, GA), jnp.float32),
-        ],
-        specs=[VMEM] * 3 + [SMEM],
-        moved=12 << 20,
-    )(gas, kappa, strips, reaction)
-
-    send_rest = call(rest_kernel, f32(LAYERS - 1, GR // 2, GA), specs=[VMEM] * 2 + [ANY], moved=1 << 18)(gas, kappa, middle)
-    recv_rest = swap(send_rest, "sect", pairs_b)
-
-    wall = call(
-        wall_kernel,
-        f32(GX, GA),
-        scratch=[
-            pltpu.VMEM((COMP, EXT, 8, GA), jnp.float32),
-            pltpu.VMEM((COMP, EXT, 8, GA), jnp.float32),
-            pltpu.VMEM((EXT, 8, GA), jnp.float32),
-            pltpu.VMEM((ITERS, COMP, 8, GA), jnp.float32),
-        ],
-        specs=[VMEM] * 5 + [SMEM, ANY],
-        moved=4 << 20,
-    )(gas, kappa, strips, recv_wall, recv_a, reaction, send_rest)
-    earlier = lax.ppermute(wall, "sect", [(i, i + 1) for i in range(sections - 1)])
-
+    )(tile_hop.reshape(CHUNKS, 128), wall_cell.reshape(CHUNKS, 128), particles, mixing, heating_column, wall)
     own, *sends = call(
         heat_kernel,
         (f32(VALS, CAP),) * MOVES,

time: 69.8 us -> 74.4 us (1.066)
  waiting for transfers between devices: 0.79 us -> 3.21 us
  starting transfers between devices: 50.1 us -> 51.1 us
    ppermute x9, waiting for transfers between devices: 0.02 us -> 3.21 us  [swap(): return lax.ppermute(x, axis, pairs + [(j, i) for i, j in pairs])]
    ppermute x9, starting transfers between devices: 42.6 us -> 43.5 us  [swap(): return lax.ppermute(x, axis, pairs + [(j, i) for i, j in pairs])]
    ppermute x1, waiting for transfers between devices: 0.77 us -> 0.01 us  [local(): lax.ppermute(wall, 'sect', [(i, i + 1) for i in range(sections - 1)])]
    unnamed x16 -> x24, local copies, waits for them, and re-layouts: 2.32 us -> 2.89 us
where the time goes in v5:
time: 74.4 us; the launch traced here: 73.8 us
  starting transfers between devices  51.1 us (69%)
  Pallas kernels  15.6 us (21%)
  waiting for transfers between devices  3.21 us (4%)
  local copies, waits for them, and re-layouts  2.97 us (4%)
  between operations  0.94 us (1%)
    ppermute x9, starting transfers between devices, swap(): return lax.ppermute(x, axis, pairs + [(j, i) for i, j in pairs])  43.5 us
    ppermute x1, starting transfers between devices, local(): lax.ppermute(wall, 'sect', [(i, i + 1) for i in range(sections - 1)])  7.55 us
    pallas_call x1, Pallas kernels, local(): call(inner_kernel, (f32(COMP, len(SEAM), GR, GA), f32(COMP, len(SEAM), GR...  4.53 us
    pallas_call x1, Pallas kernels, local(): call(outer_kernel, (whole, f32(8, 128)), scratch=[pltpu.VMEM((COMP, EXT,...  3.9 us
    ppermute x9, waiting for transfers between devices, swap(): return lax.ppermute(x, axis, pairs + [(j, i) for i, j in pairs])  3.21 us
    unnamed x24, local copies, waits for them, and re-layouts  2.89 us
    pallas_call x1, Pallas kernels, local(): call(edges_kernel, (f32(3, GR, GA), f32(3, GR, GA)), scratch=[pltpu.VMEM(...  2.18 us
    pallas_call x1, Pallas kernels, local(): call(pack_kernel, (f32(MOVES, VALS, CAP), i32(MOVES, SPOTS, 128)), scratc...  1.74 us
  transfers between devices with their start and end apart: 10, of which 1 were waited for; matrix products, arithmetic and copies ran while one was open for 0% of the time, Pallas kernels for 16%

profile of v5, /device:TPU:1, one launch (start us, length us, event | category | flops | bytes accessed | tf_op | source)
XLA Modules:
  0.0 73.8 jit_solution(16205532464203155101)
XLA Ops:
  0.6 0.0 copy-start.1
  0.6 0.0 copy-start
  0.6 0.0 copy-start.7
  0.7 2.2 %shard_map.95 = (f32[3,32,128]{2,1,0:T(8,128)S(1)}, f32[3,32,128]{2,1,0:T(8,128)S(1)}) custom-call(f32[5,16,32,128]{3,2,1,0:T(8,128)} %gas.11, f32[16,32,128]{2,1,0:T(8,128)} %kappa.11), custom_call_target="tpu_custom_call" | custom-call | bytes 2097152 | tf_op jit(solution)/shard_map/pallas_call | solution.py:461
  2.8 11.7 %collective-permute-start = (f32[3,32,128]{2,1,0:T(8,128)S(1)}, f32[3,32,128]{2,1,0:T(8,128)S(1)}, u32[]{:S(2)}, u32[]{:S(2)}) collective-permute-start(f32[3,32,128]{2,1,0:T(8,128)S(1)} %get-tuple-element.19.send_q), channel_id=1, source_target_pairs={{1,2},{3,4},{5,6},{7,8},{9,10},{11,12},{13,14},{15,16},{17,18},{19... | collective-permute-start | bytes 147464 | tf_op jit(solution)/shard_map/ppermute | solution.py:449
  14.6 1.9 %collective-permute-start.1 = (f32[3,32,128]{2,1,0:T(8,128)S(1)}, f32[3,32,128]{2,1,0:T(8,128)S(1)}, u32[]{:S(2)}, u32[]{:S(2)}) collective-permute-start(f32[3,32,128]{2,1,0:T(8,128)S(1)} %get-tuple-element.20.send_p), channel_id=1, source_target_pairs={{0,1},{2,3},{4,5},{6,7},{8,9},{10,11},{12,13},{14,15},{16,17},{18,... | collective-permute-start | bytes 147464 | tf_op jit(solution)/shard_map/ppermute | solution.py:449
  16.5 0.0 collective-permute-done.recv_q
  16.5 3.2 %collective-permute-done.1.recv_p = f32[3,32,128]{2,1,0:T(8,128)S(1)} collective-permute-done((f32[3,32,128]{2,1,0:T(8,128)S(1)}, f32[3,32,128]{2,1,0:T(8,128)S(1)}, u32[]{:S(2)}, u32[]{:S(2)}) %collective-permute-start.1) | collective-permute-done | bytes 49184 | tf_op jit(solution)/shard_map/ppermute | solution.py:449
  19.7 0.0 copy-done.1
  19.7 0.0 copy-done
  19.7 0.8 %shard_map.96 = (f32[28,32,128]{2,1,0:T(8,128)S(1)}, f32[18,32,128]{2,1,0:T(8,128)S(1)}, f32[38,8,128]{2,1,0:T(8,128)S(1)}) custom-call(f32[5,16,32,128]{3,2,1,0:T(8,128)S(1)} %copy-done, f32[16,32,128]{2,1,0:T(8,128)S(1)} %copy-done.1, f32[3,32,128]{2,1,0:T(8,128)S(1)} %get-tuple-element.19.send_q, f32[3,32,128]{2,1,0:T(8,128)S(1)} %get-tuple-element.20.send_p, ...), custom_call_target="tpu_custom_call" | custom-call | bytes 2097152 | tf_op jit(solution)/shard_map/pallas_call | solution.py:471
  20.6 4.0 %collective-permute-start.3 = (f32[18,32,128]{2,1,0:T(8,128)S(1)}, f32[18,32,128]{2,1,0:T(8,128)S(1)}, u32[]{:S(2)}, u32[]{:S(2)}) collective-permute-start(f32[18,32,128]{2,1,0:T(8,128)S(1)} %get-tuple-element.23), channel_id=1, source_target_pairs={{0,64},{128,192},{256,320},{384,448},{64,0},{192,128},{320,256},{4... | collective-permute-start | bytes 884744 | tf_op jit(solution)/shard_map/ppermute | solution.py:449
  24.6 8.4 %collective-permute-start.2 = (f32[38,8,128]{2,1,0:T(8,128)S(1)}, f32[38,8,128]{2,1,0:T(8,128)S(1)}, u32[]{:S(2)}, u32[]{:S(2)}) collective-permute-start(f32[38,8,128]{2,1,0:T(8,128)S(1)} %get-tuple-element.22), channel_id=1, source_target_pairs={{64,128},{192,256},{320,384},{128,64},{256,192},{384,320},{65,129}... | collective-permute-start | bytes 466952 | tf_op jit(solution)/shard_map/ppermute | solution.py:449
  33.0 0.0 copy-done.7
  33.0 4.5 %shard_map.97 = (f32[5,4,32,128]{3,2,1,0:T(8,128)S(1)}, f32[5,4,32,128]{3,2,1,0:T(8,128)S(1)}, f32[5,10,32,128]{3,2,1,0:T(8,128)S(1)}) custom-call(f32[5,16,32,128]{3,2,1,0:T(8,128)S(1)} %copy-done, f32[16,32,128]{2,1,0:T(8,128)S(1)} %copy-done.1, f32[28,32,128]{2,1,0:T(8,128)S(1)} %get-tuple-element.21.strips, f32[5,5]{1,0:T(8,128)S(1)} %copy-done.7), custom_call_target="tpu_custom_call" | custom-call | bytes 12582912 | tf_op jit(solution)/shard_map/pallas_call | solution.py:481
  37.6 0.0 copy-start.2
  37.6 0.0 copy-start.4
  37.6 0.0 copy-start.11
  37.6 0.0 copy-start.8
  37.6 0.0 copy-start.9
  37.7 0.0 copy-start.10
  37.7 2.1 %collective-permute-start.6 = (f32[17,16,128]{2,1,0:T(8,128)S(1)}, f32[17,16,128]{2,1,0:T(8,128)}, u32[]{:S(2)}, u32[]{:S(2)}) collective-permute-start(f32[17,16,128]{2,1,0:T(8,128)S(1)} %shard_map.98._), channel_id=1, source_target_pairs={{64,128},{192,256},{320,384},{128,64},{256,192},{384,320},{65,129}... | collective-permute-start | bytes 417800 | tf_op jit(solution)/shard_map/ppermute | solution.py:449
  39.7 0.0 collective-permute-done.2.recv_wall
  39.7 0.0 collective-permute-done.3.recv_a
  39.8 1.4 %shard_map.99._.wall = f32[16,128]{1,0:T(8,128)S(1)} custom-call(f32[5,16,32,128]{3,2,1,0:T(8,128)S(1)} %copy-done, f32[16,32,128]{2,1,0:T(8,128)S(1)} %copy-done.1, f32[28,32,128]{2,1,0:T(8,128)S(1)} %get-tuple-element.21.strips, f32[38,8,128]{2,1,0:T(8,128)S(1)} %collective-permute-done.2.recv_wall, f32[18,32,128]{2,1,0:T(8,128)S(1)} %collective-permute-done.3.recv_a, ...), custom_call_target="tpu_custom_call" | custom-call | bytes 4194304 | tf_op jit(solution)/shard_map/pallas_call | solution.py:496
  41.2 0.0 copy-done.2
  41.2 0.0 copy-done.4
  41.2 7.5 %collective-permute-start.4 = (f32[16,128]{1,0:T(8,128)S(1)}, f32[16,128]{1,0:T(8,128)S(1)}, u32[]{:S(2)}, u32[]{:S(2)}) collective-permute-start(f32[16,128]{1,0:T(8,128)S(1)} %shard_map.99._.wall), channel_id=1, source_target_pairs={{0,64},{64,128},{128,192},{192,256},{256,320},{320,384},{384,448},... | collective-permute-start | bytes 24584 | tf_op jit(solution)/shard_map/ppermute | solution.py:508
  48.8 0.1 copy.10.heating
  48.9 0.0 copy-start.6
  48.9 0.9 %copy-done.6 = f32[16,2048]{1,0:T(8,128)S(1)} copy-done((f32[16,2048]{1,0:T(8,128)S(1)}, f32[16,2048]{1,0:T(8,128)}, u32[]{:S(2)}) %copy-start.6) | copy-done | bytes 131096
  49.8 1.7 %shard_map.100 = (f32[5,16,1024]{2,1,0:T(8,128)S(1)}, s32[5,8,128]{2,1,0:T(8,128)S(1)}) custom-call(s32[16,128]{1,0:T(8,128)S(1)} %bitcast.3, s32[16,128]{1,0:T(8,128)S(1)} %bitcast.4, f32[16,2048]{1,0:T(8,128)S(1)} %copy-done.6, f32[16,16]{1,0:T(8,128)S(1)} %copy-done.10, f32[16,1]{1,0:T(8,128)S(1)} %copy.10.heating, f32[16,128]{1,0:T(8,128)S(1)} %shard_map.99._.wall), custom_call_target="tpu_custom_call" | custom-call | bytes 4194304 | tf_op jit(solution)/shard_map/pallas_call | solution.py:511
  51.5 0.0 collective-permute-done.4.earlier
  51.6 0.2 shard_map.101
  51.8 5.7 %collective-permute-start.5 = (f32[16,1024]{1,0:T(8,128)S(1)}, f32[16,1024]{1,0:T(8,128)S(1)}, u32[]{:S(2)}, u32[]{:S(2)}) collective-permute-start(f32[16,1024]{1,0:T(8,128)S(1)} %get-tuple-element.27), channel_id=1, source_target_pairs={{1,2},{3,4},{5,6},{7,8},{9,10},{11,12},{13,14},{15,16},{17,18},{19... | collective-permute-start | bytes 196616 | tf_op jit(solution)/shard_map/ppermute | solution.py:449
  57.5 1.9 %collective-permute-start.7 = (f32[16,1024]{1,0:T(8,128)S(1)}, f32[16,1024]{1,0:T(8,128)S(1)}, u32[]{:S(2)}, u32[]{:S(2)}) collective-permute-start(f32[16,1024]{1,0:T(8,128)S(1)} %get-tuple-element.32), channel_id=1, source_target_pairs={{2,4},{3,5},{6,8},{7,9},{10,12},{11,13},{14,16},{15,17},{18,20},{1... | collective-permute-start | bytes 196616 | tf_op jit(solution)/shard_map/ppermute | solution.py:449
  59.4 1.9 %collective-permute-start.8 = (f32[16,1024]{1,0:T(8,128)S(1)}, f32[16,1024]{1,0:T(8,128)S(1)}, u32[]{:S(2)}, u32[]{:S(2)}) collective-permute-start(f32[16,1024]{1,0:T(8,128)S(1)} %get-tuple-element.33), channel_id=1, source_target_pairs={{0,2},{1,3},{4,6},{5,7},{8,10},{9,11},{12,14},{13,15},{16,18},{17,... | collective-permute-start | bytes 196616 | tf_op jit(solution)/shard_map/ppermute | solution.py:449
  61.4 5.8 %collective-permute-start.9 = (f32[16,1024]{1,0:T(8,128)S(1)}, f32[16,1024]{1,0:T(8,128)S(1)}, u32[]{:S(2)}, u32[]{:S(2)}) collective-permute-start(f32[16,1024]{1,0:T(8,128)S(1)} %get-tuple-element.34), channel_id=1, source_target_pairs={{0,1},{2,3},{4,5},{6,7},{8,9},{10,11},{12,13},{14,15},{16,17},{18,... | collective-permute-start | bytes 196616 | tf_op jit(solution)/shard_map/ppermute | solution.py:449
  67.2 0.0 collective-permute-done.6.recv_rest
  67.2 0.0 collective-permute-done.5._.recv_q
  67.2 0.0 copy-start.3
  67.2 1.0 %copy-done.3 = f32[5,4,32,128]{3,2,1,0:T(8,128)S(1)} copy-done((f32[5,4,32,128]{3,2,1,0:T(8,128)S(1)}, f32[5,4,32,128]{3,2,1,0:T(8,128)}, u32[]{:S(2)}) %copy-start.3) | copy-done | bytes 327704
  68.2 1.0 %copy-done.5 = f32[5,4,32,128]{3,2,1,0:T(8,128)S(1)} copy-done((f32[5,4,32,128]{3,2,1,0:T(8,128)S(1)}, f32[5,4,32,128]{3,2,1,0:T(8,128)}, u32[]{:S(2)}) %copy-start.5) | copy-done | bytes 327704
  69.2 3.9 %shard_map.102 = (f32[5,16,32,128]{3,2,1,0:T(8,128)}, f32[8,128]{1,0:T(8,128)S(1)}) custom-call(f32[16,1024]{1,0:T(8,128)S(1)} %collective-permute-done.5._.recv_q, f32[5,16,32,128]{3,2,1,0:T(8,128)S(1)} %copy-done, f32[16,32,128]{2,1,0:T(8,128)S(1)} %copy-done.1, f32[28,32,128]{2,1,0:T(8,128)S(1)} %get-tuple-element.21.strips, ...), custom_call_target="tpu_custom_call" | custom-call | bytes 8388608 | tf_op jit(solution)/shard_map/pallas_call | solution.py:533
  73.1 0.0 collective-permute-done.7.recv_s
  73.1 0.0 collective-permute-done.8.recv_r
  73.1 0.0 collective-permute-done.9.recv_p
  73.1 0.8 %shard_map.103 = f32[16,5120]{1,0:T(8,128)} custom-call(f32[16,1024]{1,0:T(8,128)S(1)} %get-tuple-element.31.own, f32[16,1024]{1,0:T(8,128)S(1)} %collective-permute-done.5._.recv_q, f32[16,1024]{1,0:T(8,128)S(1)} %collective-permute-done.7.recv_s, f32[16,1024]{1,0:T(8,128)S(1)} %collective-permute-done.8.recv_r, ...), custom_call_target="tpu_custom_call" | custom-call | bytes 1048576 | tf_op jit(solution)/shard_map/pallas_call | solution.py:545
  (6 shorter events, 0.0 us)
Async XLA Ops:
  0.6 19.1 %copy-start.1 = (f32[16,32,128]{2,1,0:T(8,128)S(1)}, f32[16,32,128]{2,1,0:T(8,128)}, u32[]{:S(2)}) copy-start(f32[16,32,128]{2,1,0:T(8,128)} %kappa.11) | copy-start | bytes 786436
  0.6 19.1 %copy-start = (f32[5,16,32,128]{3,2,1,0:T(8,128)S(1)}, f32[5,16,32,128]{3,2,1,0:T(8,128)}, u32[]{:S(2)}) copy-start(f32[5,16,32,128]{3,2,1,0:T(8,128)} %gas.11) | copy-start | bytes 3932164
  0.6 32.4 %copy-start.7 = (f32[5,5]{1,0:T(8,128)S(1)}, f32[5,5]{1,0:T(8,128)}, u32[]{:S(2)}) copy-start(f32[5,5]{1,0:T(8,128)} %reaction.5) | copy-start | bytes 304
  2.8 13.7 %collective-permute-start = (f32[3,32,128]{2,1,0:T(8,128)S(1)}, f32[3,32,128]{2,1,0:T(8,128)S(1)}, u32[]{:S(2)}, u32[]{:S(2)}) collective-permute-start(f32[3,32,128]{2,1,0:T(8,128)S(1)} %get-tuple-element.19.send_q), channel_id=1, source_target_pairs={{1,2},{3,4},{5,6},{7,8},{9,10},{11,12},{13,14},{15,16},{17,18},{19... | collective-permute-start | bytes 147464 | tf_op jit(solution)/shard_map/ppermute | solution.py:449
  14.6 5.1 %collective-permute-start.1 = (f32[3,32,128]{2,1,0:T(8,128)S(1)}, f32[3,32,128]{2,1,0:T(8,128)S(1)}, u32[]{:S(2)}, u32[]{:S(2)}) collective-permute-start(f32[3,32,128]{2,1,0:T(8,128)S(1)} %get-tuple-element.20.send_p), channel_id=1, source_target_pairs={{0,1},{2,3},{4,5},{6,7},{8,9},{10,11},{12,13},{14,15},{16,17},{18,... | collective-permute-start | bytes 147464 | tf_op jit(solution)/shard_map/ppermute | solution.py:449
  20.6 19.2 %collective-permute-start.3 = (f32[18,32,128]{2,1,0:T(8,128)S(1)}, f32[18,32,128]{2,1,0:T(8,128)S(1)}, u32[]{:S(2)}, u32[]{:S(2)}) collective-permute-start(f32[18,32,128]{2,1,0:T(8,128)S(1)} %get-tuple-element.23), channel_id=1, source_target_pairs={{0,64},{128,192},{256,320},{384,448},{64,0},{192,128},{320,256},{4... | collective-permute-start | bytes 884744 | tf_op jit(solution)/shard_map/ppermute | solution.py:449
  24.6 15.1 %collective-permute-start.2 = (f32[38,8,128]{2,1,0:T(8,128)S(1)}, f32[38,8,128]{2,1,0:T(8,128)S(1)}, u32[]{:S(2)}, u32[]{:S(2)}) collective-permute-start(f32[38,8,128]{2,1,0:T(8,128)S(1)} %get-tuple-element.22), channel_id=1, source_target_pairs={{64,128},{192,256},{320,384},{128,64},{256,192},{384,320},{65,129}... | collective-permute-start | bytes 466952 | tf_op jit(solution)/shard_map/ppermute | solution.py:449
  37.6 3.6 %copy-start.2 = (f32[5,4,32,128]{3,2,1,0:T(8,128)}, f32[5,4,32,128]{3,2,1,0:T(8,128)S(1)}, u32[]{:S(2)}) copy-start(f32[5,4,32,128]{3,2,1,0:T(8,128)S(1)} %get-tuple-element.28.first) | copy-start | bytes 983044
  37.6 3.6 %copy-start.4 = (f32[5,4,32,128]{3,2,1,0:T(8,128)}, f32[5,4,32,128]{3,2,1,0:T(8,128)S(1)}, u32[]{:S(2)}) copy-start(f32[5,4,32,128]{3,2,1,0:T(8,128)S(1)} %get-tuple-element.29.second) | copy-start | bytes 983044
  37.6 11.2 %copy-start.11 = (f32[16]{0:T(128)S(1)}, f32[16]{0:T(128)}, u32[]{:S(2)}) copy-start(f32[16]{0:T(128)} %param.13) | copy-start | bytes 196
  37.6 11.2 %copy-start.8 = (s32[2048,1]{0,1:T(1,128)S(1)}, s32[2048,1]{0,1:T(1,128)}, u32[]{:S(2)}) copy-start(s32[2048,1]{0,1:T(1,128)} %param.15) | copy-start | bytes 24580
  37.6 11.2 %copy-start.9 = (s32[2048]{0:T(1024)S(1)}, s32[2048]{0:T(1024)}, u32[]{:S(2)}) copy-start(s32[2048]{0:T(1024)} %param.14) | copy-start | bytes 24580
  37.7 11.2 %copy-start.10 = (f32[16,16]{1,0:T(8,128)S(1)}, f32[16,16]{1,0:T(8,128)}, u32[]{:S(2)}) copy-start(f32[16,16]{1,0:T(8,128)} %mixing.1) | copy-start | bytes 3076
  37.7 29.5 %collective-permute-start.6 = (f32[17,16,128]{2,1,0:T(8,128)S(1)}, f32[17,16,128]{2,1,0:T(8,128)}, u32[]{:S(2)}, u32[]{:S(2)}) collective-permute-start(f32[17,16,128]{2,1,0:T(8,128)S(1)} %shard_map.98._), channel_id=1, source_target_pairs={{64,128},{192,256},{320,384},{128,64},{256,192},{384,320},{65,129}... | collective-permute-start | bytes 417800 | tf_op jit(solution)/shard_map/ppermute | solution.py:449
  41.2 10.3 %collective-permute-start.4 = (f32[16,128]{1,0:T(8,128)S(1)}, f32[16,128]{1,0:T(8,128)S(1)}, u32[]{:S(2)}, u32[]{:S(2)}) collective-permute-start(f32[16,128]{1,0:T(8,128)S(1)} %shard_map.99._.wall), channel_id=1, source_target_pairs={{0,64},{64,128},{128,192},{192,256},{256,320},{320,384},{384,448},... | collective-permute-start | bytes 24584 | tf_op jit(solution)/shard_map/ppermute | solution.py:508
  48.9 0.9 %copy-start.6 = (f32[16,2048]{1,0:T(8,128)S(1)}, f32[16,2048]{1,0:T(8,128)}, u32[]{:S(2)}) copy-start(f32[16,2048]{1,0:T(8,128)} %particles.1) | copy-start | bytes 393220
  51.8 15.5 %collective-permute-start.5 = (f32[16,1024]{1,0:T(8,128)S(1)}, f32[16,1024]{1,0:T(8,128)S(1)}, u32[]{:S(2)}, u32[]{:S(2)}) collective-permute-start(f32[16,1024]{1,0:T(8,128)S(1)} %get-tuple-element.27), channel_id=1, source_target_pairs={{1,2},{3,4},{5,6},{7,8},{9,10},{11,12},{13,14},{15,16},{17,18},{19... | collective-permute-start | bytes 196616 | tf_op jit(solution)/shard_map/ppermute | solution.py:449
  57.5 15.6 %collective-permute-start.7 = (f32[16,1024]{1,0:T(8,128)S(1)}, f32[16,1024]{1,0:T(8,128)S(1)}, u32[]{:S(2)}, u32[]{:S(2)}) collective-permute-start(f32[16,1024]{1,0:T(8,128)S(1)} %get-tuple-element.32), channel_id=1, source_target_pairs={{2,4},{3,5},{6,8},{7,9},{10,12},{11,13},{14,16},{15,17},{18,20},{1... | collective-permute-start | bytes 196616 | tf_op jit(solution)/shard_map/ppermute | solution.py:449
  59.4 13.6 %collective-permute-start.8 = (f32[16,1024]{1,0:T(8,128)S(1)}, f32[16,1024]{1,0:T(8,128)S(1)}, u32[]{:S(2)}, u32[]{:S(2)}) collective-permute-start(f32[16,1024]{1,0:T(8,128)S(1)} %get-tuple-element.33), channel_id=1, source_target_pairs={{0,2},{1,3},{4,6},{5,7},{8,10},{9,11},{12,14},{13,15},{16,18},{17,... | collective-permute-start | bytes 196616 | tf_op jit(solution)/shard_map/ppermute | solution.py:449
  61.4 11.7 %collective-permute-start.9 = (f32[16,1024]{1,0:T(8,128)S(1)}, f32[16,1024]{1,0:T(8,128)S(1)}, u32[]{:S(2)}, u32[]{:S(2)}) collective-permute-start(f32[16,1024]{1,0:T(8,128)S(1)} %get-tuple-element.34), channel_id=1, source_target_pairs={{0,1},{2,3},{4,5},{6,7},{8,9},{10,11},{12,13},{14,15},{16,17},{18,... | collective-permute-start | bytes 196616 | tf_op jit(solution)/shard_map/ppermute | solution.py:449
  67.2 1.0 %copy-start.3 = (f32[5,4,32,128]{3,2,1,0:T(8,128)S(1)}, f32[5,4,32,128]{3,2,1,0:T(8,128)}, u32[]{:S(2)}) copy-start(f32[5,4,32,128]{3,2,1,0:T(8,128)} %copy-done.2) | copy-start | bytes 983044
  68.2 1.0 %copy-start.5 = (f32[5,4,32,128]{3,2,1,0:T(8,128)S(1)}, f32[5,4,32,128]{3,2,1,0:T(8,128)}, u32[]{:S(2)}) copy-start(f32[5,4,32,128]{3,2,1,0:T(8,128)} %copy-done.4) | copy-start | bytes 983044

commit v6 on v4

--- a/solution.py
+++ b/solution.py
@@ -221,6 +221,22 @@
         held = later
 
 
+class Shifted:
+    def __init__(self, ref, offset):
+        self.ref, self.offset = ref, offset
+
+    def __getitem__(self, index):
+        return self.ref[(index[0] + self.offset,) + index[1:]]
+
+
+class Wrapped:
+    def __init__(self, ref):
+        self.ref = ref
+
+    def __getitem__(self, index):
+        return self.ref[index[1:]]
+
+
 def plane(src, kappa, edge, step, at, x, mix, count, comps):
     lane = lanes()
     first, last = lane == 0, lane == 127
@@ -273,27 +289,26 @@
                 dst[c, at] = out[c, 0]
 
 
-def inner_kernel(gas, kappa, strips, reaction, first, second, middle, one, two, edge):
+def inner_kernel(gas, kappa, strips, reaction, first, second, edges, one, edge):
     mix = coupling(reaction)
     strip_levels(strips, None, None, mix, edge, list(range(TILES)))
-    for step, (src, dst) in enumerate(((gas, one), (one, two), (two, middle))):
+    edges[...] = edge[ITERS - 1]
+    for step, (src, dst) in enumerate(((gas, one), (one, second))):
 
         def body(x, carry, step=step, src=src, dst=dst):
             out = plane(src, kappa, edge, step, x, x, mix, TILES, range(COMP))
-            into = x - 3 if step == ITERS - 1 else x
             for (c, t), value in out.items():
-                dst[c, into, rows(t), :] = value
+                dst[c, x - 2 * step, rows(t), :] = value
             return carry
 
         lax.fori_loop(step + 1, GX - 1 - step, body, 0, unroll=2)
     for c in range(COMP):
         for i, x in enumerate(SEAM):
             first[c, i] = one[c, x]
-            second[c, i] = two[c, x + 1 if i < 2 else x - 1]
 
 
 def outer_kernel(
-    _, gas, kappa, strips, first, second, middle, recv_wall, recv_a, recv_rest, reaction, result, token, now, later, kap, edge
+    _, gas, kappa, strips, first, second, edges, recv_wall, recv_a, recv_rest, reaction, result, token, now, later, now_two, kap, edge
 ):
     token[...] = jnp.zeros((8, 128), jnp.float32)
     even = lax.rem(lax.axis_index("sect"), 2) == 0
@@ -326,20 +341,33 @@
         high.append(jnp.where(even, corner_a, corner_b))
     strip_levels(strips, low, high, mix, edge, list(range(TILES)))
     for c in range(COMP):
-        result[c, 3 : GX - 3] = middle[c]
-    for step, (src, dst) in enumerate(((now, later), (later, now), (now, None))):
-        if step == ITERS - 1:
-            for c in range(COMP):
-                for i, x in enumerate(SEAM):
-                    now[c, (x + 1 if i < 2 else x - 1) + 3] = second[c, i]
-        for i in range(3):
+        for x in (2, 3, GX - 4, GX - 3):
+            now_two[c, x + 3] = second[c, x - 2]
+
+    def store(at, out, dst, shift):
+        for (c, t), value in out.items():
+            dst[c, at - shift, rows(t), :] = value
+
+    for step, (src, dst, shift) in enumerate(((now, later, 0), (later, now_two, 0), (now_two, result, 3))):
+
+        def body(i, carry, step=step, src=src, dst=dst, shift=shift):
             for at in (step + 1 + i, GX + 2 - step + i):
-                out = plane(src, kap, edge, step, at, at - 3, mix, TILES, range(COMP))
-                for (c, t), value in out.items():
-                    if step == ITERS - 1:
-                        result[c, at - 3, rows(t), :] = value
-                    else:
-                        dst[c, at, rows(t), :] = value
+                store(at, plane(src, kap, edge, step, at, at - 3, mix, TILES, range(COMP)), dst, shift)
+            return carry
+
+        lax.fori_loop(0, 3, body, 0)
+
+    def body(x, carry):
+        out = third_plane(x)
+        store(x, out, result, 0)
+        return carry
+
+    def third_plane(x):
+        return plane(second, kap_inner, edge_inner, 0, x - 2, x, mix, TILES, range(COMP))
+
+    kap_inner = Shifted(kappa, 2)
+    edge_inner = Wrapped(edges)
+    lax.fori_loop(3, GX - 3, body, 0, unroll=2)
 
 
 def pack_kernel(hop, cell, particles, mixing, heating, _, packed, cells, spread, ordered, source, begin, end):
@@ -491,11 +519,10 @@
     recv_a = swap(send_a, "sect", pairs_a)
 
     whole = f32(COMP, GX, GR, GA)
-    first, second, middle = call(
+    first, second, edges = call(
         inner_kernel,
-        (f32(COMP, len(SEAM), GR, GA), f32(COMP, len(SEAM), GR, GA), f32(COMP, GX - 6, GR, GA)),
+        (f32(COMP, len(SEAM), GR, GA), f32(COMP, GX - 4, GR, GA), f32(COMP, GR, GA)),
         scratch=[
-            pltpu.VMEM((COMP, GX, GR, GA), jnp.float32),
             pltpu.VMEM((COMP, GX, GR, GA), jnp.float32),
             pltpu.VMEM((ITERS, COMP, GR, GA), jnp.float32),
         ],
@@ -503,7 +530,7 @@
         moved=12 << 20,
     )(gas, kappa, strips, reaction)
 
-    send_rest = call(rest_kernel, f32(LAYERS - 1, GR // 2, GA), specs=[VMEM] * 2 + [ANY], moved=1 << 18)(gas, kappa, middle)
+    send_rest = call(rest_kernel, f32(LAYERS - 1, GR // 2, GA), specs=[VMEM] * 2 + [ANY], moved=1 << 18)(gas, kappa, second)
     recv_rest = swap(send_rest, "sect", pairs_b)
 
     wall = call(
@@ -535,12 +562,13 @@
         scratch=[
             pltpu.VMEM((COMP, EXT, GR, GA), jnp.float32),
             pltpu.VMEM((COMP, EXT, GR, GA), jnp.float32),
+            pltpu.VMEM((COMP, EXT, GR, GA), jnp.float32),
             pltpu.VMEM((EXT, GR, GA), jnp.float32),
             pltpu.VMEM((ITERS, COMP, GR, GA), jnp.float32),
         ],
         specs=[ANY] + [VMEM] * 9 + [SMEM],
         moved=8 << 20,
-    )(pieces[0], gas, kappa, strips, first, second, middle, recv_wall, recv_a, recv_rest, reaction)
+    )(pieces[0], gas, kappa, strips, first, second, edges, recv_wall, recv_a, recv_rest, reaction)
     arrived = call(
         join_kernel,
         f32(VALS, MOVES * CAP),

time: 69.8 us -> 70.8 us (1.014)
    pallas_call x1, Pallas kernels: 3.41 us -> 5.07 us  [local(): call(outer_kernel, (whole, f32(8, 128)), scratch=[pltpu.VMEM((COMP, EXT,...]
    pallas_call x1, Pallas kernels: 4.56 us -> 3.53 us  [local(): call(inner_kernel, (f32(COMP, len(SEAM), GR, GA), f32(COMP, GX - 4, GR, G...]
  transfers between devices with their start and end apart: 10 -> 10, of which waited for: 1 -> 1; matrix products, arithmetic and copies ran while one was open for 0% -> 0% of each run, Pallas kernels for 16% -> 17%
where the time goes in v6:
time: 70.8 us; the launch traced here: 70 us
  starting transfers between devices  50.1 us (71%)
  Pallas kernels  15.8 us (22%)
  local copies, waits for them, and re-layouts  2.4 us (3%)
  between operations  0.89 us (1%)
  waiting for transfers between devices  0.79 us (1%)
    ppermute x9, starting transfers between devices, swap(): return lax.ppermute(x, axis, pairs + [(j, i) for i, j in pairs])  42.6 us
    ppermute x1, starting transfers between devices, local(): lax.ppermute(wall, 'sect', [(i, i + 1) for i in range(sections - 1)])  7.55 us
    pallas_call x1, Pallas kernels, local(): call(outer_kernel, (whole, f32(8, 128)), scratch=[pltpu.VMEM((COMP, EXT,...  5.07 us
    pallas_call x1, Pallas kernels, local(): call(inner_kernel, (f32(COMP, len(SEAM), GR, GA), f32(COMP, GX - 4, GR, G...  3.53 us
    unnamed x16, local copies, waits for them, and re-layouts  2.32 us
    pallas_call x1, Pallas kernels, local(): call(edges_kernel, (f32(3, GR, GA), f32(3, GR, GA)), scratch=[pltpu.VMEM(...  2.18 us
    pallas_call x1, Pallas kernels, local(): call(pack_kernel, (f32(MOVES, VALS, CAP), i32(MOVES, SPOTS, 128)), scratc...  1.74 us
    pallas_call x1, Pallas kernels, local(): call(wall_kernel, f32(GX, GA), scratch=[pltpu.VMEM((COMP, EXT, 8, GA), jn...  1.45 us
  transfers between devices with their start and end apart: 10, of which 1 were waited for; matrix products, arithmetic and copies ran while one was open for 0% of the time, Pallas kernels for 17%

profile of v6, /device:TPU:1, one launch (start us, length us, event | category | flops | bytes accessed | tf_op | source)
XLA Modules:
  0.0 70.0 jit_solution(16657713450061609240)
XLA Ops:
  0.6 0.0 copy-start.1
  0.6 0.0 copy-start
  0.7 0.0 copy-start.7
  0.7 0.0 copy-start.4
  0.7 2.2 %shard_map.95 = (f32[3,32,128]{2,1,0:T(8,128)S(1)}, f32[3,32,128]{2,1,0:T(8,128)S(1)}) custom-call(f32[5,16,32,128]{3,2,1,0:T(8,128)} %gas.11, f32[16,32,128]{2,1,0:T(8,128)} %kappa.11), custom_call_target="tpu_custom_call" | custom-call | bytes 2097152 | tf_op jit(solution)/shard_map/pallas_call | solution.py:487
  2.9 0.0 copy-start.3
  2.9 11.7 %collective-permute-start = (f32[3,32,128]{2,1,0:T(8,128)S(1)}, f32[3,32,128]{2,1,0:T(8,128)S(1)}, u32[]{:S(2)}, u32[]{:S(2)}) collective-permute-start(f32[3,32,128]{2,1,0:T(8,128)S(1)} %get-tuple-element.19.send_q), channel_id=1, source_target_pairs={{1,2},{3,4},{5,6},{7,8},{9,10},{11,12},{13,14},{15,16},{17,18},{19... | collective-permute-start | bytes 147464 | tf_op jit(solution)/shard_map/ppermute | solution.py:475
  14.6 1.9 %collective-permute-start.1 = (f32[3,32,128]{2,1,0:T(8,128)S(1)}, f32[3,32,128]{2,1,0:T(8,128)S(1)}, u32[]{:S(2)}, u32[]{:S(2)}) collective-permute-start(f32[3,32,128]{2,1,0:T(8,128)S(1)} %get-tuple-element.20._.send_p), channel_id=1, source_target_pairs={{0,1},{2,3},{4,5},{6,7},{8,9},{10,11},{12,13},{14,15},{16,17},{18,... | collective-permute-start | bytes 147464 | tf_op jit(solution)/shard_map/ppermute | solution.py:475
  16.5 0.0 copy-done.7
  16.5 0.1 copy.10.heating
  16.6 0.0 copy-done.4
  16.6 0.0 copy-start.2
  16.6 0.9 %copy-done.2 = f32[16,2048]{1,0:T(8,128)S(1)} copy-done((f32[16,2048]{1,0:T(8,128)S(1)}, f32[16,2048]{1,0:T(8,128)}, u32[]{:S(2)}) %copy-start.2) | copy-done | bytes 131096
  17.5 0.0 copy-start.5
  17.5 0.7 copy-done.5
  18.2 0.0 copy-start.6
  18.2 0.7 copy-done.6
  18.9 1.7 %shard_map.96 = (f32[5,16,1024]{2,1,0:T(8,128)S(1)}, s32[5,8,128]{2,1,0:T(8,128)S(1)}) custom-call(s32[16,128]{1,0:T(8,128)S(1)} %bitcast.3, s32[16,128]{1,0:T(8,128)S(1)} %bitcast.4, f32[16,2048]{1,0:T(8,128)S(1)} %copy-done.2, f32[16,16]{1,0:T(8,128)S(1)} %copy-done.6, f32[16,1]{1,0:T(8,128)S(1)} %copy.10.heating, f32[3,32,128]{2,1,0:T(8,128)S(1)} %get-tuple-element.20._.send_p), custom_call_target="tpu_custom_call" | custom-call | bytes 4194304 | tf_op jit(solution)/shard_map/pallas_call | solution.py:498
  20.7 0.0 collective-permute-done.recv_q
  20.7 0.0 collective-permute-done.1.recv_p
  20.7 0.0 copy-done.1
  20.7 0.0 copy-done
  20.7 0.8 %shard_map.97 = (f32[28,32,128]{2,1,0:T(8,128)S(1)}, f32[18,32,128]{2,1,0:T(8,128)S(1)}, f32[38,8,128]{2,1,0:T(8,128)S(1)}) custom-call(f32[5,16,32,128]{3,2,1,0:T(8,128)S(1)} %copy-done, f32[16,32,128]{2,1,0:T(8,128)S(1)} %copy-done.1, f32[3,32,128]{2,1,0:T(8,128)S(1)} %get-tuple-element.19.send_q, f32[3,32,128]{2,1,0:T(8,128)S(1)} %get-tuple-element.20._.send_p, ...), custom_call_target="tpu_custom_call" | custom-call | bytes 2097152 | tf_op jit(solution)/shard_map/pallas_call | solution.py:512
  21.6 3.1 %collective-permute-start.3 = (f32[18,32,128]{2,1,0:T(8,128)S(1)}, f32[18,32,128]{2,1,0:T(8,128)S(1)}, u32[]{:S(2)}, u32[]{:S(2)}) collective-permute-start(f32[18,32,128]{2,1,0:T(8,128)S(1)} %get-tuple-element.24), channel_id=1, source_target_pairs={{0,64},{128,192},{256,320},{384,448},{64,0},{192,128},{320,256},{4... | collective-permute-start | bytes 884744 | tf_op jit(solution)/shard_map/ppermute | solution.py:475
  24.6 8.5 %collective-permute-start.2 = (f32[38,8,128]{2,1,0:T(8,128)S(1)}, f32[38,8,128]{2,1,0:T(8,128)S(1)}, u32[]{:S(2)}, u32[]{:S(2)}) collective-permute-start(f32[38,8,128]{2,1,0:T(8,128)S(1)} %get-tuple-element.23), channel_id=1, source_target_pairs={{64,128},{192,256},{320,384},{128,64},{256,192},{384,320},{65,129}... | collective-permute-start | bytes 466952 | tf_op jit(solution)/shard_map/ppermute | solution.py:475
  33.2 0.0 copy-done.3
  33.2 3.5 %shard_map.98 = (f32[5,4,32,128]{3,2,1,0:T(8,128)S(1)}, f32[5,12,32,128]{3,2,1,0:T(8,128)S(1)}, f32[5,32,128]{2,1,0:T(8,128)S(1)}) custom-call(f32[5,16,32,128]{3,2,1,0:T(8,128)S(1)} %copy-done, f32[16,32,128]{2,1,0:T(8,128)S(1)} %copy-done.1, f32[28,32,128]{2,1,0:T(8,128)S(1)} %get-tuple-element.22.strips, f32[5,5]{1,0:T(8,128)S(1)} %copy-done.3), custom_call_target="tpu_custom_call" | custom-call | bytes 12582912 | tf_op jit(solution)/shard_map/pallas_call | solution.py:522
  36.7 1.9 %collective-permute-start.6 = (f32[17,16,128]{2,1,0:T(8,128)S(1)}, f32[17,16,128]{2,1,0:T(8,128)S(1)}, u32[]{:S(2)}, u32[]{:S(2)}) collective-permute-start(f32[17,16,128]{2,1,0:T(8,128)S(1)} %shard_map.99._), channel_id=1, source_target_pairs={{64,128},{192,256},{320,384},{128,64},{256,192},{384,320},{65,129}... | collective-permute-start | bytes 417800 | tf_op jit(solution)/shard_map/ppermute | solution.py:475
  38.7 0.0 collective-permute-done.2.recv_wall
  38.7 0.0 collective-permute-done.3.recv_a
  38.7 1.5 %shard_map.100.wall = f32[16,128]{1,0:T(8,128)S(1)} custom-call(f32[5,16,32,128]{3,2,1,0:T(8,128)S(1)} %copy-done, f32[16,32,128]{2,1,0:T(8,128)S(1)} %copy-done.1, f32[28,32,128]{2,1,0:T(8,128)S(1)} %get-tuple-element.22.strips, f32[38,8,128]{2,1,0:T(8,128)S(1)} %collective-permute-done.2.recv_wall, f32[18,32,128]{2,1,0:T(8,128)S(1)} %collective-permute-done.3.recv_a, ...), custom_call_target="tpu_custom_call" | custom-call | bytes 4194304 | tf_op jit(solution)/shard_map/pallas_call | solution.py:536
  40.1 7.5 %collective-permute-start.4 = (f32[16,128]{1,0:T(8,128)S(1)}, f32[16,128]{1,0:T(8,128)S(1)}, u32[]{:S(2)}, u32[]{:S(2)}) collective-permute-start(f32[16,128]{1,0:T(8,128)S(1)} %shard_map.100.wall), channel_id=1, source_target_pairs={{0,64},{64,128},{128,192},{192,256},{256,320},{320,384},{384,448},... | collective-permute-start | bytes 24584 | tf_op jit(solution)/shard_map/ppermute | solution.py:548
  47.7 0.8 %collective-permute-done.4.earlier = f32[16,128]{1,0:T(8,128)S(1)} collective-permute-done((f32[16,128]{1,0:T(8,128)S(1)}, f32[16,128]{1,0:T(8,128)S(1)}, u32[]{:S(2)}, u32[]{:S(2)}) %collective-permute-start.4) | collective-permute-done | bytes 8224 | tf_op jit(solution)/shard_map/ppermute | solution.py:548
  48.5 0.2 shard_map.101
  48.7 5.8 %collective-permute-start.5 = (f32[16,1024]{1,0:T(8,128)S(1)}, f32[16,1024]{1,0:T(8,128)S(1)}, u32[]{:S(2)}, u32[]{:S(2)}) collective-permute-start(f32[16,1024]{1,0:T(8,128)S(1)} %get-tuple-element.27), channel_id=1, source_target_pairs={{1,2},{3,4},{5,6},{7,8},{9,10},{11,12},{13,14},{15,16},{17,18},{19... | collective-permute-start | bytes 196616 | tf_op jit(solution)/shard_map/ppermute | solution.py:475
  54.5 1.9 %collective-permute-start.7 = (f32[16,1024]{1,0:T(8,128)S(1)}, f32[16,1024]{1,0:T(8,128)S(1)}, u32[]{:S(2)}, u32[]{:S(2)}) collective-permute-start(f32[16,1024]{1,0:T(8,128)S(1)} %get-tuple-element.32), channel_id=1, source_target_pairs={{2,4},{3,5},{6,8},{7,9},{10,12},{11,13},{14,16},{15,17},{18,20},{1... | collective-permute-start | bytes 196616 | tf_op jit(solution)/shard_map/ppermute | solution.py:475
  56.4 1.9 %collective-permute-start.8 = (f32[16,1024]{1,0:T(8,128)S(1)}, f32[16,1024]{1,0:T(8,128)S(1)}, u32[]{:S(2)}, u32[]{:S(2)}) collective-permute-start(f32[16,1024]{1,0:T(8,128)S(1)} %get-tuple-element.33), channel_id=1, source_target_pairs={{0,2},{1,3},{4,6},{5,7},{8,10},{9,11},{12,14},{13,15},{16,18},{17,... | collective-permute-start | bytes 196616 | tf_op jit(solution)/shard_map/ppermute | solution.py:475
  58.3 5.8 %collective-permute-start.9 = (f32[16,1024]{1,0:T(8,128)S(1)}, f32[16,1024]{1,0:T(8,128)S(1)}, u32[]{:S(2)}, u32[]{:S(2)}) collective-permute-start(f32[16,1024]{1,0:T(8,128)S(1)} %get-tuple-element.34), channel_id=1, source_target_pairs={{0,1},{2,3},{4,5},{6,7},{8,9},{10,11},{12,13},{14,15},{16,17},{18,... | collective-permute-start | bytes 196616 | tf_op jit(solution)/shard_map/ppermute | solution.py:475
  64.1 0.0 collective-permute-done.6.recv_rest
  64.1 0.0 collective-permute-done.5._.recv_q
  64.1 5.1 %shard_map.102 = (f32[5,16,32,128]{3,2,1,0:T(8,128)}, f32[8,128]{1,0:T(8,128)S(1)}) custom-call(f32[16,1024]{1,0:T(8,128)S(1)} %collective-permute-done.5._.recv_q, f32[5,16,32,128]{3,2,1,0:T(8,128)S(1)} %copy-done, f32[16,32,128]{2,1,0:T(8,128)S(1)} %copy-done.1, f32[28,32,128]{2,1,0:T(8,128)S(1)} %get-tuple-element.22.strips, ...), custom_call_target="tpu_custom_call" | custom-call | bytes 8388608 | tf_op jit(solution)/shard_map/pallas_call | solution.py:559
  69.2 0.0 collective-permute-done.7.recv_s
  69.2 0.0 collective-permute-done.8.recv_r
  69.2 0.0 collective-permute-done.9.recv_p
  69.2 0.8 %shard_map.103 = f32[16,5120]{1,0:T(8,128)} custom-call(f32[16,1024]{1,0:T(8,128)S(1)} %get-tuple-element.31.own, f32[16,1024]{1,0:T(8,128)S(1)} %collective-permute-done.5._.recv_q, f32[16,1024]{1,0:T(8,128)S(1)} %collective-permute-done.7.recv_s, f32[16,1024]{1,0:T(8,128)S(1)} %collective-permute-done.8.recv_r, ...), custom_call_target="tpu_custom_call" | custom-call | bytes 1048576 | tf_op jit(solution)/shard_map/pallas_call | solution.py:572
  (1 shorter events, 0.0 us)
Async XLA Ops:
  0.6 20.1 %copy-start.1 = (f32[16,32,128]{2,1,0:T(8,128)S(1)}, f32[16,32,128]{2,1,0:T(8,128)}, u32[]{:S(2)}) copy-start(f32[16,32,128]{2,1,0:T(8,128)} %kappa.11) | copy-start | bytes 786436
  0.6 20.1 %copy-start = (f32[5,16,32,128]{3,2,1,0:T(8,128)S(1)}, f32[5,16,32,128]{3,2,1,0:T(8,128)}, u32[]{:S(2)}) copy-start(f32[5,16,32,128]{3,2,1,0:T(8,128)} %gas.11) | copy-start | bytes 3932164
  0.7 15.9 %copy-start.7 = (f32[16]{0:T(128)S(1)}, f32[16]{0:T(128)}, u32[]{:S(2)}) copy-start(f32[16]{0:T(128)} %param.13) | copy-start | bytes 196
  0.7 16.0 %copy-start.4 = (s32[2048,1]{0,1:T(1,128)S(1)}, s32[2048,1]{0,1:T(1,128)}, u32[]{:S(2)}) copy-start(s32[2048,1]{0,1:T(1,128)} %param.15) | copy-start | bytes 24580
  2.9 30.3 %copy-start.3 = (f32[5,5]{1,0:T(8,128)S(1)}, f32[5,5]{1,0:T(8,128)}, u32[]{:S(2)}) copy-start(f32[5,5]{1,0:T(8,128)} %reaction.5) | copy-start | bytes 304
  2.9 17.8 %collective-permute-start = (f32[3,32,128]{2,1,0:T(8,128)S(1)}, f32[3,32,128]{2,1,0:T(8,128)S(1)}, u32[]{:S(2)}, u32[]{:S(2)}) collective-permute-start(f32[3,32,128]{2,1,0:T(8,128)S(1)} %get-tuple-element.19.send_q), channel_id=1, source_target_pairs={{1,2},{3,4},{5,6},{7,8},{9,10},{11,12},{13,14},{15,16},{17,18},{19... | collective-permute-start | bytes 147464 | tf_op jit(solution)/shard_map/ppermute | solution.py:475
  14.6 6.1 %collective-permute-start.1 = (f32[3,32,128]{2,1,0:T(8,128)S(1)}, f32[3,32,128]{2,1,0:T(8,128)S(1)}, u32[]{:S(2)}, u32[]{:S(2)}) collective-permute-start(f32[3,32,128]{2,1,0:T(8,128)S(1)} %get-tuple-element.20._.send_p), channel_id=1, source_target_pairs={{0,1},{2,3},{4,5},{6,7},{8,9},{10,11},{12,13},{14,15},{16,17},{18,... | collective-permute-start | bytes 147464 | tf_op jit(solution)/shard_map/ppermute | solution.py:475
  16.6 0.9 %copy-start.2 = (f32[16,2048]{1,0:T(8,128)S(1)}, f32[16,2048]{1,0:T(8,128)}, u32[]{:S(2)}) copy-start(f32[16,2048]{1,0:T(8,128)} %particles.1) | copy-start | bytes 393220
  17.5 0.7 copy-start.5
  18.2 0.7 copy-start.6
  21.6 17.1 %collective-permute-start.3 = (f32[18,32,128]{2,1,0:T(8,128)S(1)}, f32[18,32,128]{2,1,0:T(8,128)S(1)}, u32[]{:S(2)}, u32[]{:S(2)}) collective-permute-start(f32[18,32,128]{2,1,0:T(8,128)S(1)} %get-tuple-element.24), channel_id=1, source_target_pairs={{0,64},{128,192},{256,320},{384,448},{64,0},{192,128},{320,256},{4... | collective-permute-start | bytes 884744 | tf_op jit(solution)/shard_map/ppermute | solution.py:475
  24.6 14.0 %collective-permute-start.2 = (f32[38,8,128]{2,1,0:T(8,128)S(1)}, f32[38,8,128]{2,1,0:T(8,128)S(1)}, u32[]{:S(2)}, u32[]{:S(2)}) collective-permute-start(f32[38,8,128]{2,1,0:T(8,128)S(1)} %get-tuple-element.23), channel_id=1, source_target_pairs={{64,128},{192,256},{320,384},{128,64},{256,192},{384,320},{65,129}... | collective-permute-start | bytes 466952 | tf_op jit(solution)/shard_map/ppermute | solution.py:475
  36.7 27.4 %collective-permute-start.6 = (f32[17,16,128]{2,1,0:T(8,128)S(1)}, f32[17,16,128]{2,1,0:T(8,128)S(1)}, u32[]{:S(2)}, u32[]{:S(2)}) collective-permute-start(f32[17,16,128]{2,1,0:T(8,128)S(1)} %shard_map.99._), channel_id=1, source_target_pairs={{64,128},{192,256},{320,384},{128,64},{256,192},{384,320},{65,129}... | collective-permute-start | bytes 417800 | tf_op jit(solution)/shard_map/ppermute | solution.py:475
  40.1 8.3 %collective-permute-start.4 = (f32[16,128]{1,0:T(8,128)S(1)}, f32[16,128]{1,0:T(8,128)S(1)}, u32[]{:S(2)}, u32[]{:S(2)}) collective-permute-start(f32[16,128]{1,0:T(8,128)S(1)} %shard_map.100.wall), channel_id=1, source_target_pairs={{0,64},{64,128},{128,192},{192,256},{256,320},{320,384},{384,448},... | collective-permute-start | bytes 24584 | tf_op jit(solution)/shard_map/ppermute | solution.py:548
  48.7 15.5 %collective-permute-start.5 = (f32[16,1024]{1,0:T(8,128)S(1)}, f32[16,1024]{1,0:T(8,128)S(1)}, u32[]{:S(2)}, u32[]{:S(2)}) collective-permute-start(f32[16,1024]{1,0:T(8,128)S(1)} %get-tuple-element.27), channel_id=1, source_target_pairs={{1,2},{3,4},{5,6},{7,8},{9,10},{11,12},{13,14},{15,16},{17,18},{19... | collective-permute-start | bytes 196616 | tf_op jit(solution)/shard_map/ppermute | solution.py:475
  54.5 14.7 %collective-permute-start.7 = (f32[16,1024]{1,0:T(8,128)S(1)}, f32[16,1024]{1,0:T(8,128)S(1)}, u32[]{:S(2)}, u32[]{:S(2)}) collective-permute-start(f32[16,1024]{1,0:T(8,128)S(1)} %get-tuple-element.32), channel_id=1, source_target_pairs={{2,4},{3,5},{6,8},{7,9},{10,12},{11,13},{14,16},{15,17},{18,20},{1... | collective-permute-start | bytes 196616 | tf_op jit(solution)/shard_map/ppermute | solution.py:475
  56.4 12.8 %collective-permute-start.8 = (f32[16,1024]{1,0:T(8,128)S(1)}, f32[16,1024]{1,0:T(8,128)S(1)}, u32[]{:S(2)}, u32[]{:S(2)}) collective-permute-start(f32[16,1024]{1,0:T(8,128)S(1)} %get-tuple-element.33), channel_id=1, source_target_pairs={{0,2},{1,3},{4,6},{5,7},{8,10},{9,11},{12,14},{13,15},{16,18},{17,... | collective-permute-start | bytes 196616 | tf_op jit(solution)/shard_map/ppermute | solution.py:475
  58.3 10.9 %collective-permute-start.9 = (f32[16,1024]{1,0:T(8,128)S(1)}, f32[16,1024]{1,0:T(8,128)S(1)}, u32[]{:S(2)}, u32[]{:S(2)}) collective-permute-start(f32[16,1024]{1,0:T(8,128)S(1)} %get-tuple-element.34), channel_id=1, source_target_pairs={{0,1},{2,3},{4,5},{6,7},{8,9},{10,11},{12,13},{14,15},{16,17},{18,... | collective-permute-start | bytes 196616 | tf_op jit(solution)/shard_map/ppermute | solution.py:475

commit v7 on v4

--- a/solution.py
+++ b/solution.py
@@ -124,23 +124,21 @@
         for_a = jnp.where(even, top, bottom)
         for_b = jnp.where(even, bottom, top)
         send_a[LAYERS - 1, rows(tile), :] = for_a
-        send_wall[2 * (LAYERS - 1) + tile] = for_b
+        send_wall[LAYERS - 1 + tile] = for_b
     at_a, at_b = jnp.where(even, GX - 3, 0), jnp.where(even, 0, GX - 3)
     kappa_a, kappa_b = jnp.where(even, GX - 2, 0), jnp.where(even, 0, GX - 2)
     for c in range(COMP):
         for layer in range(3):
             send_a[3 * c + layer] = gas[c, at_a + layer]
-            for half in range(2):
-                send_wall[2 * (3 * c + layer) + half] = gas[c, at_b + layer, rows(2 + half), :]
+            send_wall[3 * c + layer] = gas[c, at_b + layer, GR - 8 :, :]
     for layer in range(2):
         send_a[3 * COMP + layer] = kappa[kappa_a + layer]
-        for half in range(2):
-            send_wall[2 * (3 * COMP + layer) + half] = kappa[kappa_b + layer, rows(2 + half), :]
+        send_wall[3 * COMP + layer] = kappa[kappa_b + layer, GR - 8 :, :]
 
 
 def rest_kernel(gas, kappa, _, send_rest):
     even = lax.rem(lax.axis_index("sect"), 2) == 0
-    split = GR // 2
+    split = GR - 8
     from_b, from_kappa = jnp.where(even, 0, GX - 3), jnp.where(even, 0, GX - 2)
     for c in range(COMP):
         for layer in range(3):
@@ -252,13 +250,13 @@
             now[c, x + 3] = gas[c, x, top, :]
         for layer in range(3):
             now[c, at_a + layer] = recv_a[3 * c + layer, top, :]
-            now[c, at_b + layer] = recv_wall[2 * (3 * c + layer) + 1]
+            now[c, at_b + layer] = recv_wall[3 * c + layer]
     for x in range(GX):
         kap[x + 3] = kappa[x, top, :]
     for layer in range(2):
         kap[kappa_a + layer] = recv_a[3 * COMP + layer, top, :]
-        kap[kappa_b + layer] = recv_wall[2 * (3 * COMP + layer) + 1]
-    corner_a, corner_b = recv_a[LAYERS - 1, top, :], recv_wall[2 * (LAYERS - 1) + TILES - 1]
+        kap[kappa_b + layer] = recv_wall[3 * COMP + layer]
+    corner_a, corner_b = recv_a[LAYERS - 1, top, :], recv_wall[LAYERS - 1 + TILES - 1]
     low, high = jnp.where(even, corner_b, corner_a), jnp.where(even, corner_a, corner_b)
     strip_levels(strips, [low], [high], mix, edge, [TILES - 1])
 
@@ -298,7 +296,7 @@
     token[...] = jnp.zeros((8, 128), jnp.float32)
     even = lax.rem(lax.axis_index("sect"), 2) == 0
     mix = coupling(reaction)
-    split = GR // 2
+    split = GR - 8
     at_a, at_b = jnp.where(even, GX + 3, 0), jnp.where(even, 0, GX + 3)
     kappa_a, kappa_b = jnp.where(even, GX + 3, 1), jnp.where(even, 1, GX + 3)
     for c in range(COMP):
@@ -306,8 +304,7 @@
             now[c, x + 3] = gas[c, x]
         for layer in range(3):
             now[c, at_a + layer] = recv_a[3 * c + layer]
-            for half in range(2):
-                now[c, at_b + layer, rows(2 + half), :] = recv_wall[2 * (3 * c + layer) + half]
+            now[c, at_b + layer, split:, :] = recv_wall[3 * c + layer]
             now[c, at_b + layer, :split, :] = recv_rest[3 * c + layer]
         for i, x in enumerate(SEAM):
             later[c, x + 3] = first[c, i]
@@ -315,13 +312,12 @@
         kap[x + 3] = kappa[x]
     for layer in range(2):
         kap[kappa_a + layer] = recv_a[3 * COMP + layer]
-        for half in range(2):
-            kap[kappa_b + layer, rows(2 + half), :] = recv_wall[2 * (3 * COMP + layer) + half]
+        kap[kappa_b + layer, split:, :] = recv_wall[3 * COMP + layer]
         kap[kappa_b + layer, :split, :] = recv_rest[3 * COMP + layer]
     low, high = [], []
     for t in range(TILES):
         corner_a = recv_a[LAYERS - 1, rows(t), :]
-        corner_b = recv_wall[2 * (LAYERS - 1) + t]
+        corner_b = recv_wall[LAYERS - 1 + t]
         low.append(jnp.where(even, corner_b, corner_a))
         high.append(jnp.where(even, corner_a, corner_b))
     strip_levels(strips, low, high, mix, edge, list(range(TILES)))
@@ -483,7 +479,7 @@
 
     strips, send_a, send_wall = call(
         strips_kernel,
-        (f32(len(STRIPS), GR, GA), f32(LAYERS, GR, GA), f32(2 * (LAYERS - 1) + TILES, 8, GA)),
+        (f32(len(STRIPS), GR, GA), f32(LAYERS, GR, GA), f32(LAYERS - 1 + TILES, 8, GA)),
         specs=[VMEM] * 6 + [ANY],
         moved=2 << 20,
     )(gas, kappa, send_q, send_p, recv_q, recv_p, cells)
@@ -503,7 +499,7 @@
         moved=12 << 20,
     )(gas, kappa, strips, reaction)
 
-    send_rest = call(rest_kernel, f32(LAYERS - 1, GR // 2, GA), specs=[VMEM] * 2 + [ANY], moved=1 << 18)(gas, kappa, middle)
+    send_rest = call(rest_kernel, f32(LAYERS - 1, GR - 8, GA), specs=[VMEM] * 2 + [ANY], moved=1 << 18)(gas, kappa, middle)
     recv_rest = swap(send_rest, "sect", pairs_b)
 
     wall = call(
@@ -526,6 +522,7 @@
         scratch=[pltpu.VMEM((MOVES, SPOTS, 128), jnp.float32)],
         specs=[VMEM] * 5,
         moved=2 << 20,
+        flops=1 << 34,
     )(wall, earlier, packed, cells, heating_column)
     pieces = [swap(x, "blk", pairs) for x, pairs in zip(sends, (pairs_q, pairs_s, pairs_r, pairs_p))]
 

time: 69.8 us -> 68 us (0.974)
  starting transfers between devices: 50.1 us -> 49.1 us
  waiting for transfers between devices: 0.79 us -> 0.03 us
    ppermute x1, starting transfers between devices: 7.55 us -> 5.11 us  [local(): lax.ppermute(wall, 'sect', [(i, i + 1) for i in range(sections - 1)])]
    ppermute x9, starting transfers between devices: 42.6 us -> 44 us  [swap(): return lax.ppermute(x, axis, pairs + [(j, i) for i, j in pairs])]
    ppermute x1, waiting for transfers between devices: 0.77 us -> 0.01 us  [local(): lax.ppermute(wall, 'sect', [(i, i + 1) for i in range(sections - 1)])]
  transfers between devices with their start and end apart: 10 -> 10, of which waited for: 1 -> 0; matrix products, arithmetic and copies ran while one was open for 0% -> 0% of each run, Pallas kernels for 16% -> 15%
where the time goes in v7:
time: 68 us; the launch traced here: 67.5 us
  starting transfers between devices  49.1 us (72%)
  Pallas kernels  15.1 us (22%)
  local copies, waits for them, and re-layouts  2.4 us (4%)
  between operations  0.9 us (1%)
    ppermute x9, starting transfers between devices, swap(): return lax.ppermute(x, axis, pairs + [(j, i) for i, j in pairs])  44 us
    ppermute x1, starting transfers between devices, local(): lax.ppermute(wall, 'sect', [(i, i + 1) for i in range(sections - 1)])  5.11 us
    pallas_call x1, Pallas kernels, local(): call(inner_kernel, (f32(COMP, len(SEAM), GR, GA), f32(COMP, len(SEAM), GR...  4.56 us
    pallas_call x1, Pallas kernels, local(): call(outer_kernel, (whole, f32(8, 128)), scratch=[pltpu.VMEM((COMP, EXT,...  3.39 us
    unnamed x16, local copies, waits for them, and re-layouts  2.32 us
    pallas_call x1, Pallas kernels, local(): call(edges_kernel, (f32(3, GR, GA), f32(3, GR, GA)), scratch=[pltpu.VMEM(...  2.18 us
    pallas_call x1, Pallas kernels, local(): call(pack_kernel, (f32(MOVES, VALS, CAP), i32(MOVES, SPOTS, 128)), scratc...  1.73 us
    pallas_call x1, Pallas kernels, local(): call(wall_kernel, f32(GX, GA), scratch=[pltpu.VMEM((COMP, EXT, 8, GA), jn...  1.45 us
  transfers between devices with their start and end apart: 10, of which 0 were waited for; matrix products, arithmetic and copies ran while one was open for 0% of the time, Pallas kernels for 15%

profile of v7, /device:TPU:1, one launch (start us, length us, event | category | flops | bytes accessed | tf_op | source)
XLA Modules:
  0.0 67.5 jit_solution(1838563183365171369)
XLA Ops:
  0.6 0.0 copy-start.1
  0.6 0.0 copy-start
  0.7 0.0 copy-start.7
  0.7 0.0 copy-start.4
  0.7 2.2 %shard_map.95 = (f32[3,32,128]{2,1,0:T(8,128)S(1)}, f32[3,32,128]{2,1,0:T(8,128)S(1)}) custom-call(f32[5,16,32,128]{3,2,1,0:T(8,128)} %gas.11, f32[16,32,128]{2,1,0:T(8,128)} %kappa.11), custom_call_target="tpu_custom_call" | custom-call | bytes 2097152 | tf_op jit(solution)/shard_map/pallas_call | solution.py:455
  2.9 0.0 copy-start.3
  2.9 11.7 %collective-permute-start = (f32[3,32,128]{2,1,0:T(8,128)S(1)}, f32[3,32,128]{2,1,0:T(8,128)S(1)}, u32[]{:S(2)}, u32[]{:S(2)}) collective-permute-start(f32[3,32,128]{2,1,0:T(8,128)S(1)} %get-tuple-element.19.send_q), channel_id=1, source_target_pairs={{1,2},{3,4},{5,6},{7,8},{9,10},{11,12},{13,14},{15,16},{17,18},{19... | collective-permute-start | bytes 147464 | tf_op jit(solution)/shard_map/ppermute | solution.py:443
  14.6 1.9 %collective-permute-start.1 = (f32[3,32,128]{2,1,0:T(8,128)S(1)}, f32[3,32,128]{2,1,0:T(8,128)S(1)}, u32[]{:S(2)}, u32[]{:S(2)}) collective-permute-start(f32[3,32,128]{2,1,0:T(8,128)S(1)} %get-tuple-element.20._.send_p), channel_id=1, source_target_pairs={{0,1},{2,3},{4,5},{6,7},{8,9},{10,11},{12,13},{14,15},{16,17},{18,... | collective-permute-start | bytes 147464 | tf_op jit(solution)/shard_map/ppermute | solution.py:443
  16.5 0.0 copy-done.7
  16.5 0.1 copy.10.heating
  16.6 0.0 copy-done.4
  16.6 0.0 copy-start.2
  16.6 0.9 %copy-done.2 = f32[16,2048]{1,0:T(8,128)S(1)} copy-done((f32[16,2048]{1,0:T(8,128)S(1)}, f32[16,2048]{1,0:T(8,128)}, u32[]{:S(2)}) %copy-start.2) | copy-done | bytes 131096
  17.5 0.0 copy-start.5
  17.5 0.7 %copy-done.5 = s32[2048]{0:T(1024)S(1)} copy-done((s32[2048]{0:T(1024)S(1)}, s32[2048]{0:T(1024)}, u32[]{:S(2)}) %copy-start.5) | copy-done | bytes 8216
  18.2 0.0 copy-start.6
  18.2 0.7 %copy-done.6 = f32[16,16]{1,0:T(8,128)S(1)} copy-done((f32[16,16]{1,0:T(8,128)S(1)}, f32[16,16]{1,0:T(8,128)}, u32[]{:S(2)}) %copy-start.6) | copy-done | bytes 1048
  18.9 1.7 %shard_map.96 = (f32[5,16,1024]{2,1,0:T(8,128)S(1)}, s32[5,8,128]{2,1,0:T(8,128)S(1)}) custom-call(s32[16,128]{1,0:T(8,128)S(1)} %bitcast.3, s32[16,128]{1,0:T(8,128)S(1)} %bitcast.4, f32[16,2048]{1,0:T(8,128)S(1)} %copy-done.2, f32[16,16]{1,0:T(8,128)S(1)} %copy-done.6, f32[16,1]{1,0:T(8,128)S(1)} %copy.10.heating, f32[3,32,128]{2,1,0:T(8,128)S(1)} %get-tuple-element.20._.send_p), custom_call_target="tpu_custom_call" | custom-call | bytes 4194304 | tf_op jit(solution)/shard_map/pallas_call | solution.py:466
  20.7 0.0 collective-permute-done.recv_q
  20.7 0.0 collective-permute-done.1.recv_p
  20.7 0.0 copy-done.1
  20.7 0.0 copy-done
  20.7 0.8 %shard_map.97 = (f32[28,32,128]{2,1,0:T(8,128)S(1)}, f32[18,32,128]{2,1,0:T(8,128)S(1)}, f32[21,8,128]{2,1,0:T(8,128)S(1)}) custom-call(f32[5,16,32,128]{3,2,1,0:T(8,128)S(1)} %copy-done, f32[16,32,128]{2,1,0:T(8,128)S(1)} %copy-done.1, f32[3,32,128]{2,1,0:T(8,128)S(1)} %get-tuple-element.19.send_q, f32[3,32,128]{2,1,0:T(8,128)S(1)} %get-tuple-element.20._.send_p, ...), custom_call_target="tpu_custom_call" | custom-call | bytes 2097152 | tf_op jit(solution)/shard_map/pallas_call | solution.py:480
  21.6 3.1 %collective-permute-start.3 = (f32[18,32,128]{2,1,0:T(8,128)S(1)}, f32[18,32,128]{2,1,0:T(8,128)S(1)}, u32[]{:S(2)}, u32[]{:S(2)}) collective-permute-start(f32[18,32,128]{2,1,0:T(8,128)S(1)} %get-tuple-element.24), channel_id=1, source_target_pairs={{0,64},{128,192},{256,320},{384,448},{64,0},{192,128},{320,256},{4... | collective-permute-start | bytes 884744 | tf_op jit(solution)/shard_map/ppermute | solution.py:443
  24.6 8.5 %collective-permute-start.2 = (f32[21,8,128]{2,1,0:T(8,128)S(1)}, f32[21,8,128]{2,1,0:T(8,128)S(1)}, u32[]{:S(2)}, u32[]{:S(2)}) collective-permute-start(f32[21,8,128]{2,1,0:T(8,128)S(1)} %get-tuple-element.23), channel_id=1, source_target_pairs={{64,128},{192,256},{320,384},{128,64},{256,192},{384,320},{65,129}... | collective-permute-start | bytes 258056 | tf_op jit(solution)/shard_map/ppermute | solution.py:443
  33.2 0.0 copy-done.3
  33.2 4.6 %shard_map.98 = (f32[5,4,32,128]{3,2,1,0:T(8,128)S(1)}, f32[5,4,32,128]{3,2,1,0:T(8,128)S(1)}, f32[5,10,32,128]{3,2,1,0:T(8,128)S(1)}) custom-call(f32[5,16,32,128]{3,2,1,0:T(8,128)S(1)} %copy-done, f32[16,32,128]{2,1,0:T(8,128)S(1)} %copy-done.1, f32[28,32,128]{2,1,0:T(8,128)S(1)} %get-tuple-element.22.strips, f32[5,5]{1,0:T(8,128)S(1)} %copy-done.3), custom_call_target="tpu_custom_call" | custom-call | bytes 12582912 | tf_op jit(solution)/shard_map/pallas_call | solution.py:490
  37.8 0.0 collective-permute-done.2.recv_wall
  37.8 0.0 collective-permute-done.3.recv_a
  37.8 1.5 %shard_map.100.wall = f32[16,128]{1,0:T(8,128)S(1)} custom-call(f32[5,16,32,128]{3,2,1,0:T(8,128)S(1)} %copy-done, f32[16,32,128]{2,1,0:T(8,128)S(1)} %copy-done.1, f32[28,32,128]{2,1,0:T(8,128)S(1)} %get-tuple-element.22.strips, f32[21,8,128]{2,1,0:T(8,128)S(1)} %collective-permute-done.2.recv_wall, f32[18,32,128]{2,1,0:T(8,128)S(1)} %collective-permute-done.3.recv_a, ...), custom_call_target="tpu_custom_call" | custom-call | bytes 4194304 | tf_op jit(solution)/shard_map/pallas_call | solution.py:505
  39.2 5.1 %collective-permute-start.4 = (f32[16,128]{1,0:T(8,128)S(1)}, f32[16,128]{1,0:T(8,128)S(1)}, u32[]{:S(2)}, u32[]{:S(2)}) collective-permute-start(f32[16,128]{1,0:T(8,128)S(1)} %shard_map.100.wall), channel_id=1, source_target_pairs={{0,64},{64,128},{128,192},{192,256},{256,320},{320,384},{384,448},... | collective-permute-start | bytes 24584 | tf_op jit(solution)/shard_map/ppermute | solution.py:517
  44.4 3.3 %collective-permute-start.6 = (f32[17,24,128]{2,1,0:T(8,128)S(1)}, f32[17,24,128]{2,1,0:T(8,128)S(1)}, u32[]{:S(2)}, u32[]{:S(2)}) collective-permute-start(f32[17,24,128]{2,1,0:T(8,128)S(1)} %shard_map.99._), channel_id=1, source_target_pairs={{64,128},{192,256},{320,384},{128,64},{256,192},{384,320},{65,129}... | collective-permute-start | bytes 626696 | tf_op jit(solution)/shard_map/ppermute | solution.py:443
  47.7 0.0 collective-permute-done.4.earlier
  47.7 0.2 shard_map.101
  47.9 5.6 %collective-permute-start.5 = (f32[16,1024]{1,0:T(8,128)S(1)}, f32[16,1024]{1,0:T(8,128)S(1)}, u32[]{:S(2)}, u32[]{:S(2)}) collective-permute-start(f32[16,1024]{1,0:T(8,128)S(1)} %get-tuple-element.27), channel_id=1, source_target_pairs={{1,2},{3,4},{5,6},{7,8},{9,10},{11,12},{13,14},{15,16},{17,18},{19... | collective-permute-start | bytes 196616 | tf_op jit(solution)/shard_map/ppermute | solution.py:443
  53.5 1.9 %collective-permute-start.7 = (f32[16,1024]{1,0:T(8,128)S(1)}, f32[16,1024]{1,0:T(8,128)S(1)}, u32[]{:S(2)}, u32[]{:S(2)}) collective-permute-start(f32[16,1024]{1,0:T(8,128)S(1)} %get-tuple-element.32), channel_id=1, source_target_pairs={{2,4},{3,5},{6,8},{7,9},{10,12},{11,13},{14,16},{15,17},{18,20},{1... | collective-permute-start | bytes 196616 | tf_op jit(solution)/shard_map/ppermute | solution.py:443
  55.5 1.9 %collective-permute-start.8 = (f32[16,1024]{1,0:T(8,128)S(1)}, f32[16,1024]{1,0:T(8,128)S(1)}, u32[]{:S(2)}, u32[]{:S(2)}) collective-permute-start(f32[16,1024]{1,0:T(8,128)S(1)} %get-tuple-element.33), channel_id=1, source_target_pairs={{0,2},{1,3},{4,6},{5,7},{8,10},{9,11},{12,14},{13,15},{16,18},{17,... | collective-permute-start | bytes 196616 | tf_op jit(solution)/shard_map/ppermute | solution.py:443
  57.4 6.0 %collective-permute-start.9 = (f32[16,1024]{1,0:T(8,128)S(1)}, f32[16,1024]{1,0:T(8,128)S(1)}, u32[]{:S(2)}, u32[]{:S(2)}) collective-permute-start(f32[16,1024]{1,0:T(8,128)S(1)} %get-tuple-element.34), channel_id=1, source_target_pairs={{0,1},{2,3},{4,5},{6,7},{8,9},{10,11},{12,13},{14,15},{16,17},{18,... | collective-permute-start | bytes 196616 | tf_op jit(solution)/shard_map/ppermute | solution.py:443
  63.3 0.0 collective-permute-done.6.recv_rest
  63.4 0.0 collective-permute-done.5._.recv_q
  63.4 3.4 %shard_map.102 = (f32[5,16,32,128]{3,2,1,0:T(8,128)}, f32[8,128]{1,0:T(8,128)S(1)}) custom-call(f32[16,1024]{1,0:T(8,128)S(1)} %collective-permute-done.5._.recv_q, f32[5,16,32,128]{3,2,1,0:T(8,128)S(1)} %copy-done, f32[16,32,128]{2,1,0:T(8,128)S(1)} %copy-done.1, f32[28,32,128]{2,1,0:T(8,128)S(1)} %get-tuple-element.22.strips, ...), custom_call_target="tpu_custom_call" | custom-call | bytes 8388608 | tf_op jit(solution)/shard_map/pallas_call | solution.py:529
  66.8 0.0 collective-permute-done.7.recv_s
  66.8 0.0 collective-permute-done.8.recv_r
  66.8 0.0 collective-permute-done.9.recv_p
  66.8 0.8 %shard_map.103 = f32[16,5120]{1,0:T(8,128)} custom-call(f32[16,1024]{1,0:T(8,128)S(1)} %get-tuple-element.31.own, f32[16,1024]{1,0:T(8,128)S(1)} %collective-permute-done.5._.recv_q, f32[16,1024]{1,0:T(8,128)S(1)} %collective-permute-done.7.recv_s, f32[16,1024]{1,0:T(8,128)S(1)} %collective-permute-done.8.recv_r, ...), custom_call_target="tpu_custom_call" | custom-call | bytes 1048576 | tf_op jit(solution)/shard_map/pallas_call | solution.py:541
  (1 shorter events, 0.0 us)
Async XLA Ops:
  0.6 20.1 %copy-start.1 = (f32[16,32,128]{2,1,0:T(8,128)S(1)}, f32[16,32,128]{2,1,0:T(8,128)}, u32[]{:S(2)}) copy-start(f32[16,32,128]{2,1,0:T(8,128)} %kappa.11) | copy-start | bytes 786436
  0.6 20.1 %copy-start = (f32[5,16,32,128]{3,2,1,0:T(8,128)S(1)}, f32[5,16,32,128]{3,2,1,0:T(8,128)}, u32[]{:S(2)}) copy-start(f32[5,16,32,128]{3,2,1,0:T(8,128)} %gas.11) | copy-start | bytes 3932164
  0.7 15.9 %copy-start.7 = (f32[16]{0:T(128)S(1)}, f32[16]{0:T(128)}, u32[]{:S(2)}) copy-start(f32[16]{0:T(128)} %param.13) | copy-start | bytes 196
  0.7 16.0 %copy-start.4 = (s32[2048,1]{0,1:T(1,128)S(1)}, s32[2048,1]{0,1:T(1,128)}, u32[]{:S(2)}) copy-start(s32[2048,1]{0,1:T(1,128)} %param.15) | copy-start | bytes 24580
  2.9 30.3 %copy-start.3 = (f32[5,5]{1,0:T(8,128)S(1)}, f32[5,5]{1,0:T(8,128)}, u32[]{:S(2)}) copy-start(f32[5,5]{1,0:T(8,128)} %reaction.5) | copy-start | bytes 304
  2.9 17.8 %collective-permute-start = (f32[3,32,128]{2,1,0:T(8,128)S(1)}, f32[3,32,128]{2,1,0:T(8,128)S(1)}, u32[]{:S(2)}, u32[]{:S(2)}) collective-permute-start(f32[3,32,128]{2,1,0:T(8,128)S(1)} %get-tuple-element.19.send_q), channel_id=1, source_target_pairs={{1,2},{3,4},{5,6},{7,8},{9,10},{11,12},{13,14},{15,16},{17,18},{19... | collective-permute-start | bytes 147464 | tf_op jit(solution)/shard_map/ppermute | solution.py:443
  14.6 6.1 %collective-permute-start.1 = (f32[3,32,128]{2,1,0:T(8,128)S(1)}, f32[3,32,128]{2,1,0:T(8,128)S(1)}, u32[]{:S(2)}, u32[]{:S(2)}) collective-permute-start(f32[3,32,128]{2,1,0:T(8,128)S(1)} %get-tuple-element.20._.send_p), channel_id=1, source_target_pairs={{0,1},{2,3},{4,5},{6,7},{8,9},{10,11},{12,13},{14,15},{16,17},{18,... | collective-permute-start | bytes 147464 | tf_op jit(solution)/shard_map/ppermute | solution.py:443
  16.6 0.9 %copy-start.2 = (f32[16,2048]{1,0:T(8,128)S(1)}, f32[16,2048]{1,0:T(8,128)}, u32[]{:S(2)}) copy-start(f32[16,2048]{1,0:T(8,128)} %particles.1) | copy-start | bytes 393220
  17.5 0.7 %copy-start.5 = (s32[2048]{0:T(1024)S(1)}, s32[2048]{0:T(1024)}, u32[]{:S(2)}) copy-start(s32[2048]{0:T(1024)} %param.14) | copy-start | bytes 24580
  18.2 0.7 %copy-start.6 = (f32[16,16]{1,0:T(8,128)S(1)}, f32[16,16]{1,0:T(8,128)}, u32[]{:S(2)}) copy-start(f32[16,16]{1,0:T(8,128)} %mixing.1) | copy-start | bytes 3076
  21.6 16.2 %collective-permute-start.3 = (f32[18,32,128]{2,1,0:T(8,128)S(1)}, f32[18,32,128]{2,1,0:T(8,128)S(1)}, u32[]{:S(2)}, u32[]{:S(2)}) collective-permute-start(f32[18,32,128]{2,1,0:T(8,128)S(1)} %get-tuple-element.24), channel_id=1, source_target_pairs={{0,64},{128,192},{256,320},{384,448},{64,0},{192,128},{320,256},{4... | collective-permute-start | bytes 884744 | tf_op jit(solution)/shard_map/ppermute | solution.py:443
  24.6 13.1 %collective-permute-start.2 = (f32[21,8,128]{2,1,0:T(8,128)S(1)}, f32[21,8,128]{2,1,0:T(8,128)S(1)}, u32[]{:S(2)}, u32[]{:S(2)}) collective-permute-start(f32[21,8,128]{2,1,0:T(8,128)S(1)} %get-tuple-element.23), channel_id=1, source_target_pairs={{64,128},{192,256},{320,384},{128,64},{256,192},{384,320},{65,129}... | collective-permute-start | bytes 258056 | tf_op jit(solution)/shard_map/ppermute | solution.py:443
  39.2 8.4 %collective-permute-start.4 = (f32[16,128]{1,0:T(8,128)S(1)}, f32[16,128]{1,0:T(8,128)S(1)}, u32[]{:S(2)}, u32[]{:S(2)}) collective-permute-start(f32[16,128]{1,0:T(8,128)S(1)} %shard_map.100.wall), channel_id=1, source_target_pairs={{0,64},{64,128},{128,192},{192,256},{256,320},{320,384},{384,448},... | collective-permute-start | bytes 24584 | tf_op jit(solution)/shard_map/ppermute | solution.py:517
  44.4 19.0 %collective-permute-start.6 = (f32[17,24,128]{2,1,0:T(8,128)S(1)}, f32[17,24,128]{2,1,0:T(8,128)S(1)}, u32[]{:S(2)}, u32[]{:S(2)}) collective-permute-start(f32[17,24,128]{2,1,0:T(8,128)S(1)} %shard_map.99._), channel_id=1, source_target_pairs={{64,128},{192,256},{320,384},{128,64},{256,192},{384,320},{65,129}... | collective-permute-start | bytes 626696 | tf_op jit(solution)/shard_map/ppermute | solution.py:443
  47.9 15.5 %collective-permute-start.5 = (f32[16,1024]{1,0:T(8,128)S(1)}, f32[16,1024]{1,0:T(8,128)S(1)}, u32[]{:S(2)}, u32[]{:S(2)}) collective-permute-start(f32[16,1024]{1,0:T(8,128)S(1)} %get-tuple-element.27), channel_id=1, source_target_pairs={{1,2},{3,4},{5,6},{7,8},{9,10},{11,12},{13,14},{15,16},{17,18},{19... | collective-permute-start | bytes 196616 | tf_op jit(solution)/shard_map/ppermute | solution.py:443
  53.5 13.2 %collective-permute-start.7 = (f32[16,1024]{1,0:T(8,128)S(1)}, f32[16,1024]{1,0:T(8,128)S(1)}, u32[]{:S(2)}, u32[]{:S(2)}) collective-permute-start(f32[16,1024]{1,0:T(8,128)S(1)} %get-tuple-element.32), channel_id=1, source_target_pairs={{2,4},{3,5},{6,8},{7,9},{10,12},{11,13},{14,16},{15,17},{18,20},{1... | collective-permute-start | bytes 196616 | tf_op jit(solution)/shard_map/ppermute | solution.py:443
  55.5 11.3 %collective-permute-start.8 = (f32[16,1024]{1,0:T(8,128)S(1)}, f32[16,1024]{1,0:T(8,128)S(1)}, u32[]{:S(2)}, u32[]{:S(2)}) collective-permute-start(f32[16,1024]{1,0:T(8,128)S(1)} %get-tuple-element.33), channel_id=1, source_target_pairs={{0,2},{1,3},{4,6},{5,7},{8,10},{9,11},{12,14},{13,15},{16,18},{17,... | collective-permute-start | bytes 196616 | tf_op jit(solution)/shard_map/ppermute | solution.py:443
  57.4 9.4 %collective-permute-start.9 = (f32[16,1024]{1,0:T(8,128)S(1)}, f32[16,1024]{1,0:T(8,128)S(1)}, u32[]{:S(2)}, u32[]{:S(2)}) collective-permute-start(f32[16,1024]{1,0:T(8,128)S(1)} %get-tuple-element.34), channel_id=1, source_target_pairs={{0,1},{2,3},{4,5},{6,7},{8,9},{10,11},{12,13},{14,15},{16,17},{18,... | collective-permute-start | bytes 196616 | tf_op jit(solution)/shard_map/ppermute | solution.py:443

commit v8 on v7

--- a/solution.py
+++ b/solution.py
@@ -94,37 +94,47 @@
                 out[pair, rows(tile), :] = jnp.where(lane < 64, pick(first, index), pick(second, index))
 
 
-def strips_kernel(gas, kappa, send_q, send_p, recv_q, recv_p, _, strips, send_a, send_wall):
+def edge_sides(send_q, send_p, recv_q, recv_p, tile):
+    odd = lax.rem(lax.axis_index("blk"), 2) == 1
+    slabs = [[ref[s, rows(tile), :] for s in range(3)] for ref in (send_q, send_p, recv_q, recv_p)]
+    own_q, own_p, got_q, got_p = slabs
+    left = [jnp.where(odd, p, q) for q, p in zip(own_q, own_p)]
+    right = [jnp.where(odd, q, p) for q, p in zip(own_q, own_p)]
+    from_left = [jnp.where(odd, p, q) for q, p in zip(got_q, got_p)]
+    from_right = [jnp.where(odd, q, p) for q, p in zip(got_q, got_p)]
+    return (left, right), (from_left, from_right)
+
+
+def strip_of(sides, q, k):
     lane = lanes()
-    low_side = (lane & 1) == 1
-    cell = jnp.clip((lane >> 1) - 3, 0, GX - 1)
+    own, got = sides
+    low, high = got if k > 0 else own
+    depth = k - 1 if k > 0 else -k
+    index = jnp.clip((lane >> 1) - 3, 0, GX - 1) + ((q % 2) * 64 + depth * 16)
+    return jnp.where((lane & 1) == 1, pick(low[q // 2], index), pick(high[q // 2], index))
+
+
+def strips_kernel(send_q, send_p, recv_q, recv_p, _, strips):
+    for tile in range(TILES):
+        sides = edge_sides(send_q, send_p, recv_q, recv_p, tile)
+        for i, (q, k) in enumerate(STRIPS):
+            strips[i, rows(tile), :] = strip_of(sides, q, k)
+
+
+def sends_kernel(gas, kappa, send_q, send_p, recv_q, recv_p, _, send_a, send_wall):
+    lane = lanes()
     even = lax.rem(lax.axis_index("sect"), 2) == 0
-    odd_tile = lax.rem(lax.axis_index("blk"), 2) == 1
     for tile in range(TILES):
-        held = {}
-        slabs = [[ref[s, rows(tile), :] for s in range(3)] for ref in (send_q, send_p, recv_q, recv_p)]
-        own_q, own_p, got_q, got_p = slabs
-        to_left = [jnp.where(odd_tile, p, q) for q, p in zip(own_q, own_p)]
-        to_right = [jnp.where(odd_tile, q, p) for q, p in zip(own_q, own_p)]
-        from_left = [jnp.where(odd_tile, p, q) for q, p in zip(got_q, got_p)]
-        from_right = [jnp.where(odd_tile, q, p) for q, p in zip(got_q, got_p)]
-        for q, k in STRIPS:
-            depth = k - 1 if k > 0 else -k
-            index = cell + ((q % 2) * 64 + depth * 16)
-            low, high = (from_left, from_right) if k > 0 else (to_left, to_right)
-            value = jnp.where(low_side, pick(low[q // 2], index), pick(high[q // 2], index))
-            strips[STRIP_AT[q, k], rows(tile), :] = value
-            held[q, k] = value
+        sides = edge_sides(send_q, send_p, recv_q, recv_p, tile)
         top = jnp.zeros((8, 128), jnp.float32)
         bottom = top
-        for i, key in enumerate(CORNERS):
+        for i, (q, k) in enumerate(CORNERS):
             here = (lane >> 2) == i
-            top = jnp.where(here, pltpu.roll(held[key], (4 * i - 34) % 128, 1), top)
-            bottom = jnp.where(here, pltpu.roll(held[key], (4 * i - 6) % 128, 1), bottom)
-        for_a = jnp.where(even, top, bottom)
-        for_b = jnp.where(even, bottom, top)
-        send_a[LAYERS - 1, rows(tile), :] = for_a
-        send_wall[LAYERS - 1 + tile] = for_b
+            strip = strip_of(sides, q, k)
+            top = jnp.where(here, pltpu.roll(strip, (4 * i - 34) % 128, 1), top)
+            bottom = jnp.where(here, pltpu.roll(strip, (4 * i - 6) % 128, 1), bottom)
+        send_a[LAYERS - 1, rows(tile), :] = jnp.where(even, top, bottom)
+        send_wall[LAYERS - 1 + tile] = jnp.where(even, bottom, top)
     at_a, at_b = jnp.where(even, GX - 3, 0), jnp.where(even, 0, GX - 3)
     kappa_a, kappa_b = jnp.where(even, GX - 2, 0), jnp.where(even, 0, GX - 2)
     for c in range(COMP):
@@ -238,20 +248,23 @@
     return out
 
 
-def wall_kernel(gas, kappa, strips, recv_wall, recv_a, reaction, _, wall, now, later, kap, edge):
-    odd = lax.rem(lax.axis_index("sect"), 2)
-    even = odd == 0
+def wall_kernel(
+    gas, kappa, strips, recv_wall, recv_a, first, second, middle, reaction, _, wall, now, later, kap, edge
+):
+    even = lax.rem(lax.axis_index("sect"), 2) == 0
     mix = coupling(reaction)
     top = slice(GR - 8, GR)
     at_a, at_b = jnp.where(even, GX + 3, 0), jnp.where(even, 0, GX + 3)
     kappa_a, kappa_b = jnp.where(even, GX + 3, 1), jnp.where(even, 1, GX + 3)
     for c in range(COMP):
-        for x in range(GX):
+        for x in (0, 1, GX - 2, GX - 1):
             now[c, x + 3] = gas[c, x, top, :]
         for layer in range(3):
             now[c, at_a + layer] = recv_a[3 * c + layer, top, :]
             now[c, at_b + layer] = recv_wall[3 * c + layer]
-    for x in range(GX):
+        for i, x in enumerate(SEAM):
+            later[c, x + 3] = first[c, i, top, :]
+    for x in (0, 1, 2, GX - 3, GX - 2, GX - 1):
         kap[x + 3] = kappa[x, top, :]
     for layer in range(2):
         kap[kappa_a + layer] = recv_a[3 * COMP + layer, top, :]
@@ -259,16 +272,21 @@
     corner_a, corner_b = recv_a[LAYERS - 1, top, :], recv_wall[LAYERS - 1 + TILES - 1]
     low, high = jnp.where(even, corner_b, corner_a), jnp.where(even, corner_a, corner_b)
     strip_levels(strips, [low], [high], mix, edge, [TILES - 1])
-
+    wall[3 : GX - 3, :] = middle[0, :, GR - 1, :]
     for step, (src, dst) in enumerate(((now, later), (later, now), (now, None))):
-        comps = (0,) if step == ITERS - 1 else range(COMP)
-        for at in range(step + 1, EXT - 1 - step):
-            out = plane(src, kap, edge, step, at, at - 3, mix, 1, comps)
-            if step == ITERS - 1:
-                wall[at - 3 : at - 2, :] = out[0, 0][7:8, :]
-                continue
-            for c in comps:
-                dst[c, at] = out[c, 0]
+        last = step == ITERS - 1
+        if last:
+            for c in range(COMP):
+                for i, x in enumerate(SEAM):
+                    now[c, (x + 1 if i < 2 else x - 1) + 3] = second[c, i, top, :]
+        for i in range(3):
+            for at in (step + 1 + i, GX + 2 - step + i):
+                out = plane(src, kap, edge, step, at, at - 3, mix, 1, (0,) if last else range(COMP))
+                if last:
+                    wall[at - 3 : at - 2, :] = out[0, 0][7:8, :]
+                    continue
+                for c in range(COMP):
+                    dst[c, at] = out[c, 0]
 
 
 def inner_kernel(gas, kappa, strips, reaction, first, second, middle, one, two, edge):
@@ -477,14 +495,18 @@
         moved=4 << 20,
     )(tile_hop.reshape(CHUNKS, 128), wall_cell.reshape(CHUNKS, 128), particles, mixing, heating_column, send_p)
 
-    strips, send_a, send_wall = call(
-        strips_kernel,
-        (f32(len(STRIPS), GR, GA), f32(LAYERS, GR, GA), f32(LAYERS - 1 + TILES, 8, GA)),
+    send_a, send_wall = call(
+        sends_kernel,
+        (f32(LAYERS, GR, GA), f32(LAYERS - 1 + TILES, 8, GA)),
         specs=[VMEM] * 6 + [ANY],
         moved=2 << 20,
     )(gas, kappa, send_q, send_p, recv_q, recv_p, cells)
     recv_wall = swap(send_wall, "sect", pairs_b)
     recv_a = swap(send_a, "sect", pairs_a)
+
+    strips = call(strips_kernel, f32(len(STRIPS), GR, GA), specs=[VMEM] * 4 + [ANY], moved=1 << 20)(
+        send_q, send_p, recv_q, recv_p, send_a
+    )
 
     whole = f32(COMP, GX, GR, GA)
     first, second, middle = call(
@@ -511,9 +533,9 @@
             pltpu.VMEM((EXT, 8, GA), jnp.float32),
             pltpu.VMEM((ITERS, COMP, 8, GA), jnp.float32),
         ],
-        specs=[VMEM] * 5 + [SMEM, ANY],
+        specs=[VMEM] * 8 + [SMEM, ANY],
         moved=4 << 20,
-    )(gas, kappa, strips, recv_wall, recv_a, reaction, send_rest)
+    )(gas, kappa, strips, recv_wall, recv_a, first, second, middle, reaction, send_rest)
     earlier = lax.ppermute(wall, "sect", [(i, i + 1) for i in range(sections - 1)])
 
     own, *sends = call(

time: 68 us -> 70 us (1.029)
  Pallas kernels: 15.1 us -> 17.3 us
    pallas_call x1 -> x2, Pallas kernels: 0.84 us -> 3.42 us  [the longest x1 2.87 us: local(): call(sends_kernel, (f32(LAYERS, GR, GA), f32(LAYERS - 1 + TILES, 8, GA)),...]
    ppermute x9, starting transfers between devices: 44 us -> 45 us  [swap(): return lax.ppermute(x, axis, pairs + [(j, i) for i, j in pairs])]
where the time goes in v8:
time: 70 us; the launch traced here: 69.6 us
  starting transfers between devices  49.6 us (71%)
  Pallas kernels  17.3 us (25%)
  local copies, waits for them, and re-layouts  1.71 us (2%)
  between operations  0.91 us (1%)
    ppermute x9, starting transfers between devices, swap(): return lax.ppermute(x, axis, pairs + [(j, i) for i, j in pairs])  45 us
    ppermute x1, starting transfers between devices, local(): lax.ppermute(wall, 'sect', [(i, i + 1) for i in range(sections - 1)])  4.62 us
    pallas_call x1, Pallas kernels, local(): call(inner_kernel, (f32(COMP, len(SEAM), GR, GA), f32(COMP, len(SEAM), GR...  4.55 us
    pallas_call x1, Pallas kernels, local(): call(outer_kernel, (whole, f32(8, 128)), scratch=[pltpu.VMEM((COMP, EXT,...  3.41 us
    pallas_call x1, Pallas kernels, local(): call(sends_kernel, (f32(LAYERS, GR, GA), f32(LAYERS - 1 + TILES, 8, GA)),...  2.87 us
    pallas_call x1, Pallas kernels, local(): call(edges_kernel, (f32(3, GR, GA), f32(3, GR, GA)), scratch=[pltpu.VMEM(...  2.18 us
    pallas_call x1, Pallas kernels, local(): call(pack_kernel, (f32(MOVES, VALS, CAP), i32(MOVES, SPOTS, 128)), scratc...  1.74 us
    unnamed x16, local copies, waits for them, and re-layouts  1.63 us
  transfers between devices with their start and end apart: 10, of which 0 were waited for; matrix products, arithmetic and copies ran while one was open for 0% of the time, Pallas kernels for 15%

profile of v8, /device:TPU:1, one launch (start us, length us, event | category | flops | bytes accessed | tf_op | source)
XLA Modules:
  0.0 69.6 jit_solution(13678120033338097825)
XLA Ops:
  0.6 0.0 copy-start.1
  0.6 0.0 copy-start
  0.7 0.0 copy-start.7
  0.7 0.0 copy-start.4
  0.7 0.0 copy-start.5
  0.7 2.2 %shard_map.95 = (f32[3,32,128]{2,1,0:T(8,128)S(1)}, f32[3,32,128]{2,1,0:T(8,128)S(1)}) custom-call(f32[5,16,32,128]{3,2,1,0:T(8,128)} %gas.11, f32[16,32,128]{2,1,0:T(8,128)} %kappa.11), custom_call_target="tpu_custom_call" | custom-call | bytes 2097152 | tf_op jit(solution)/shard_map/pallas_call | solution.py:473
  2.9 11.7 %collective-permute-start = (f32[3,32,128]{2,1,0:T(8,128)S(1)}, f32[3,32,128]{2,1,0:T(8,128)S(1)}, u32[]{:S(2)}, u32[]{:S(2)}) collective-permute-start(f32[3,32,128]{2,1,0:T(8,128)S(1)} %get-tuple-element.18.send_q), channel_id=1, source_target_pairs={{1,2},{3,4},{5,6},{7,8},{9,10},{11,12},{13,14},{15,16},{17,18},{19... | collective-permute-start | bytes 147464 | tf_op jit(solution)/shard_map/ppermute | solution.py:461
  14.6 1.9 %collective-permute-start.1 = (f32[3,32,128]{2,1,0:T(8,128)S(1)}, f32[3,32,128]{2,1,0:T(8,128)S(1)}, u32[]{:S(2)}, u32[]{:S(2)}) collective-permute-start(f32[3,32,128]{2,1,0:T(8,128)S(1)} %get-tuple-element.19._.send_p), channel_id=1, source_target_pairs={{0,1},{2,3},{4,5},{6,7},{8,9},{10,11},{12,13},{14,15},{16,17},{18,... | collective-permute-start | bytes 147464 | tf_op jit(solution)/shard_map/ppermute | solution.py:461
  16.5 0.0 copy-done.7
  16.5 0.1 copy.10.heating
  16.6 0.0 copy-done.4
  16.6 0.0 copy-done.5
  16.6 0.0 copy-start.2
  16.6 0.9 %copy-done.2 = f32[16,2048]{1,0:T(8,128)S(1)} copy-done((f32[16,2048]{1,0:T(8,128)S(1)}, f32[16,2048]{1,0:T(8,128)}, u32[]{:S(2)}) %copy-start.2) | copy-done | bytes 131096
  17.5 0.0 copy-start.6
  17.5 0.7 copy-done.6
  18.2 1.7 %shard_map.96 = (f32[5,16,1024]{2,1,0:T(8,128)S(1)}, s32[5,8,128]{2,1,0:T(8,128)S(1)}) custom-call(s32[16,128]{1,0:T(8,128)S(1)} %bitcast.3, s32[16,128]{1,0:T(8,128)S(1)} %bitcast.4, f32[16,2048]{1,0:T(8,128)S(1)} %copy-done.2, f32[16,16]{1,0:T(8,128)S(1)} %copy-done.6, f32[16,1]{1,0:T(8,128)S(1)} %copy.10.heating, f32[3,32,128]{2,1,0:T(8,128)S(1)} %get-tuple-element.19._.send_p), custom_call_target="tpu_custom_call" | custom-call | bytes 4194304 | tf_op jit(solution)/shard_map/pallas_call | solution.py:484
  20.0 0.0 collective-permute-done.recv_q
  20.0 0.0 collective-permute-done.1.recv_p
  20.0 0.0 copy-done.1
  20.0 0.0 copy-done
  20.0 0.0 copy-start.3
  20.0 2.9 %shard_map.97 = (f32[18,32,128]{2,1,0:T(8,128)S(1)}, f32[21,8,128]{2,1,0:T(8,128)S(1)}) custom-call(f32[5,16,32,128]{3,2,1,0:T(8,128)S(1)} %copy-done, f32[16,32,128]{2,1,0:T(8,128)S(1)} %copy-done.1, f32[3,32,128]{2,1,0:T(8,128)S(1)} %get-tuple-element.18.send_q, f32[3,32,128]{2,1,0:T(8,128)S(1)} %get-tuple-element.19._.send_p, ...), custom_call_target="tpu_custom_call" | custom-call | bytes 2097152 | tf_op jit(solution)/shard_map/pallas_call | solution.py:498
  22.9 3.8 %collective-permute-start.3 = (f32[18,32,128]{2,1,0:T(8,128)S(1)}, f32[18,32,128]{2,1,0:T(8,128)S(1)}, u32[]{:S(2)}, u32[]{:S(2)}) collective-permute-start(f32[18,32,128]{2,1,0:T(8,128)S(1)} %get-tuple-element.21._), channel_id=1, source_target_pairs={{0,64},{128,192},{256,320},{384,448},{64,0},{192,128},{320,256},{4... | collective-permute-start | bytes 884744 | tf_op jit(solution)/shard_map/ppermute | solution.py:461
  26.7 8.4 %collective-permute-start.2 = (f32[21,8,128]{2,1,0:T(8,128)S(1)}, f32[21,8,128]{2,1,0:T(8,128)S(1)}, u32[]{:S(2)}, u32[]{:S(2)}) collective-permute-start(f32[21,8,128]{2,1,0:T(8,128)S(1)} %get-tuple-element.22), channel_id=1, source_target_pairs={{64,128},{192,256},{320,384},{128,64},{256,192},{384,320},{65,129}... | collective-permute-start | bytes 258056 | tf_op jit(solution)/shard_map/ppermute | solution.py:461
  35.1 0.5 shard_map.98.strips
  35.6 0.0 copy-done.3
  35.6 4.5 %shard_map.99 = (f32[5,4,32,128]{3,2,1,0:T(8,128)S(1)}, f32[5,4,32,128]{3,2,1,0:T(8,128)S(1)}, f32[5,10,32,128]{3,2,1,0:T(8,128)S(1)}) custom-call(f32[5,16,32,128]{3,2,1,0:T(8,128)S(1)} %copy-done, f32[16,32,128]{2,1,0:T(8,128)S(1)} %copy-done.1, f32[28,32,128]{2,1,0:T(8,128)S(1)} %shard_map.98.strips, f32[5,5]{1,0:T(8,128)S(1)} %copy-done.3), custom_call_target="tpu_custom_call" | custom-call | bytes 12582912 | tf_op jit(solution)/shard_map/pallas_call | solution.py:512
  40.2 0.0 collective-permute-done.2.recv_wall
  40.2 0.0 collective-permute-done.3.recv_a
  40.2 1.0 %shard_map.101.wall = f32[16,128]{1,0:T(8,128)S(1)} custom-call(f32[5,16,32,128]{3,2,1,0:T(8,128)S(1)} %copy-done, f32[16,32,128]{2,1,0:T(8,128)S(1)} %copy-done.1, f32[28,32,128]{2,1,0:T(8,128)S(1)} %shard_map.98.strips, f32[21,8,128]{2,1,0:T(8,128)S(1)} %collective-permute-done.2.recv_wall, f32[18,32,128]{2,1,0:T(8,128)S(1)} %collective-permute-done.3.recv_a, ...), custom_call_target="tpu_custom_call" | custom-call | bytes 4194304 | tf_op jit(solution)/shard_map/pallas_call | solution.py:527
  41.3 4.6 %collective-permute-start.4 = (f32[16,128]{1,0:T(8,128)S(1)}, f32[16,128]{1,0:T(8,128)S(1)}, u32[]{:S(2)}, u32[]{:S(2)}) collective-permute-start(f32[16,128]{1,0:T(8,128)S(1)} %shard_map.101.wall), channel_id=1, source_target_pairs={{0,64},{64,128},{128,192},{192,256},{256,320},{320,384},{384,448},... | collective-permute-start | bytes 24584 | tf_op jit(solution)/shard_map/ppermute | solution.py:539
  45.9 3.8 %collective-permute-start.6 = (f32[17,24,128]{2,1,0:T(8,128)S(1)}, f32[17,24,128]{2,1,0:T(8,128)S(1)}, u32[]{:S(2)}, u32[]{:S(2)}) collective-permute-start(f32[17,24,128]{2,1,0:T(8,128)S(1)} %shard_map.100._), channel_id=1, source_target_pairs={{64,128},{192,256},{320,384},{128,64},{256,192},{384,320},{65,129}... | collective-permute-start | bytes 626696 | tf_op jit(solution)/shard_map/ppermute | solution.py:461
  49.7 0.0 collective-permute-done.4.earlier
  49.7 0.2 shard_map.102
  49.9 7.0 %collective-permute-start.5 = (f32[16,1024]{1,0:T(8,128)S(1)}, f32[16,1024]{1,0:T(8,128)S(1)}, u32[]{:S(2)}, u32[]{:S(2)}) collective-permute-start(f32[16,1024]{1,0:T(8,128)S(1)} %get-tuple-element.27), channel_id=1, source_target_pairs={{1,2},{3,4},{5,6},{7,8},{9,10},{11,12},{13,14},{15,16},{17,18},{19... | collective-permute-start | bytes 196616 | tf_op jit(solution)/shard_map/ppermute | solution.py:461
  56.9 1.9 %collective-permute-start.7 = (f32[16,1024]{1,0:T(8,128)S(1)}, f32[16,1024]{1,0:T(8,128)S(1)}, u32[]{:S(2)}, u32[]{:S(2)}) collective-permute-start(f32[16,1024]{1,0:T(8,128)S(1)} %get-tuple-element.30), channel_id=1, source_target_pairs={{2,4},{3,5},{6,8},{7,9},{10,12},{11,13},{14,16},{15,17},{18,20},{1... | collective-permute-start | bytes 196616 | tf_op jit(solution)/shard_map/ppermute | solution.py:461
  58.9 1.9 %collective-permute-start.8 = (f32[16,1024]{1,0:T(8,128)S(1)}, f32[16,1024]{1,0:T(8,128)S(1)}, u32[]{:S(2)}, u32[]{:S(2)}) collective-permute-start(f32[16,1024]{1,0:T(8,128)S(1)} %get-tuple-element.31), channel_id=1, source_target_pairs={{0,2},{1,3},{4,6},{5,7},{8,10},{9,11},{12,14},{13,15},{16,18},{17,... | collective-permute-start | bytes 196616 | tf_op jit(solution)/shard_map/ppermute | solution.py:461
  60.8 4.6 %collective-permute-start.9 = (f32[16,1024]{1,0:T(8,128)S(1)}, f32[16,1024]{1,0:T(8,128)S(1)}, u32[]{:S(2)}, u32[]{:S(2)}) collective-permute-start(f32[16,1024]{1,0:T(8,128)S(1)} %get-tuple-element.32), channel_id=1, source_target_pairs={{0,1},{2,3},{4,5},{6,7},{8,9},{10,11},{12,13},{14,15},{16,17},{18,... | collective-permute-start | bytes 196616 | tf_op jit(solution)/shard_map/ppermute | solution.py:461
  65.4 0.0 collective-permute-done.6.recv_rest
  65.4 0.0 collective-permute-done.5._.recv_q
  65.4 3.4 %shard_map.103 = (f32[5,16,32,128]{3,2,1,0:T(8,128)}, f32[8,128]{1,0:T(8,128)S(1)}) custom-call(f32[16,1024]{1,0:T(8,128)S(1)} %collective-permute-done.5._.recv_q, f32[5,16,32,128]{3,2,1,0:T(8,128)S(1)} %copy-done, f32[16,32,128]{2,1,0:T(8,128)S(1)} %copy-done.1, f32[28,32,128]{2,1,0:T(8,128)S(1)} %shard_map.98.strips, ...), custom_call_target="tpu_custom_call" | custom-call | bytes 8388608 | tf_op jit(solution)/shard_map/pallas_call | solution.py:551
  68.8 0.0 collective-permute-done.7.recv_s
  68.8 0.0 collective-permute-done.8.recv_r
  68.8 0.0 collective-permute-done.9.recv_p
  68.8 0.8 %shard_map.104 = f32[16,5120]{1,0:T(8,128)} custom-call(f32[16,1024]{1,0:T(8,128)S(1)} %get-tuple-element.29.own, f32[16,1024]{1,0:T(8,128)S(1)} %collective-permute-done.5._.recv_q, f32[16,1024]{1,0:T(8,128)S(1)} %collective-permute-done.7.recv_s, f32[16,1024]{1,0:T(8,128)S(1)} %collective-permute-done.8.recv_r, ...), custom_call_target="tpu_custom_call" | custom-call | bytes 1048576 | tf_op jit(solution)/shard_map/pallas_call | solution.py:563
  (1 shorter events, 0.0 us)
Async XLA Ops:
  0.6 19.4 %copy-start.1 = (f32[16,32,128]{2,1,0:T(8,128)S(1)}, f32[16,32,128]{2,1,0:T(8,128)}, u32[]{:S(2)}) copy-start(f32[16,32,128]{2,1,0:T(8,128)} %kappa.11) | copy-start | bytes 786436
  0.6 19.4 %copy-start = (f32[5,16,32,128]{3,2,1,0:T(8,128)S(1)}, f32[5,16,32,128]{3,2,1,0:T(8,128)}, u32[]{:S(2)}) copy-start(f32[5,16,32,128]{3,2,1,0:T(8,128)} %gas.11) | copy-start | bytes 3932164
  0.7 15.9 %copy-start.7 = (f32[16]{0:T(128)S(1)}, f32[16]{0:T(128)}, u32[]{:S(2)}) copy-start(f32[16]{0:T(128)} %param.13) | copy-start | bytes 196
  0.7 16.0 %copy-start.4 = (s32[2048,1]{0,1:T(1,128)S(1)}, s32[2048,1]{0,1:T(1,128)}, u32[]{:S(2)}) copy-start(s32[2048,1]{0,1:T(1,128)} %param.15) | copy-start | bytes 24580
  0.7 16.0 %copy-start.5 = (s32[2048]{0:T(1024)S(1)}, s32[2048]{0:T(1024)}, u32[]{:S(2)}) copy-start(s32[2048]{0:T(1024)} %param.14) | copy-start | bytes 24580
  2.9 17.1 %collective-permute-start = (f32[3,32,128]{2,1,0:T(8,128)S(1)}, f32[3,32,128]{2,1,0:T(8,128)S(1)}, u32[]{:S(2)}, u32[]{:S(2)}) collective-permute-start(f32[3,32,128]{2,1,0:T(8,128)S(1)} %get-tuple-element.18.send_q), channel_id=1, source_target_pairs={{1,2},{3,4},{5,6},{7,8},{9,10},{11,12},{13,14},{15,16},{17,18},{19... | collective-permute-start | bytes 147464 | tf_op jit(solution)/shard_map/ppermute | solution.py:461
  14.6 5.4 %collective-permute-start.1 = (f32[3,32,128]{2,1,0:T(8,128)S(1)}, f32[3,32,128]{2,1,0:T(8,128)S(1)}, u32[]{:S(2)}, u32[]{:S(2)}) collective-permute-start(f32[3,32,128]{2,1,0:T(8,128)S(1)} %get-tuple-element.19._.send_p), channel_id=1, source_target_pairs={{0,1},{2,3},{4,5},{6,7},{8,9},{10,11},{12,13},{14,15},{16,17},{18,... | collective-permute-start | bytes 147464 | tf_op jit(solution)/shard_map/ppermute | solution.py:461
  16.6 0.9 %copy-start.2 = (f32[16,2048]{1,0:T(8,128)S(1)}, f32[16,2048]{1,0:T(8,128)}, u32[]{:S(2)}) copy-start(f32[16,2048]{1,0:T(8,128)} %particles.1) | copy-start | bytes 393220
  17.5 0.7 %copy-start.6 = (f32[16,16]{1,0:T(8,128)S(1)}, f32[16,16]{1,0:T(8,128)}, u32[]{:S(2)}) copy-start(f32[16,16]{1,0:T(8,128)} %mixing.1) | copy-start | bytes 3076
  20.0 15.6 %copy-start.3 = (f32[5,5]{1,0:T(8,128)S(1)}, f32[5,5]{1,0:T(8,128)}, u32[]{:S(2)}) copy-start(f32[5,5]{1,0:T(8,128)} %reaction.5) | copy-start | bytes 304
  22.9 17.3 %collective-permute-start.3 = (f32[18,32,128]{2,1,0:T(8,128)S(1)}, f32[18,32,128]{2,1,0:T(8,128)S(1)}, u32[]{:S(2)}, u32[]{:S(2)}) collective-permute-start(f32[18,32,128]{2,1,0:T(8,128)S(1)} %get-tuple-element.21._), channel_id=1, source_target_pairs={{0,64},{128,192},{256,320},{384,448},{64,0},{192,128},{320,256},{4... | collective-permute-start | bytes 884744 | tf_op jit(solution)/shard_map/ppermute | solution.py:461
  26.7 13.6 %collective-permute-start.2 = (f32[21,8,128]{2,1,0:T(8,128)S(1)}, f32[21,8,128]{2,1,0:T(8,128)S(1)}, u32[]{:S(2)}, u32[]{:S(2)}) collective-permute-start(f32[21,8,128]{2,1,0:T(8,128)S(1)} %get-tuple-element.22), channel_id=1, source_target_pairs={{64,128},{192,256},{320,384},{128,64},{256,192},{384,320},{65,129}... | collective-permute-start | bytes 258056 | tf_op jit(solution)/shard_map/ppermute | solution.py:461
  41.3 8.4 %collective-permute-start.4 = (f32[16,128]{1,0:T(8,128)S(1)}, f32[16,128]{1,0:T(8,128)S(1)}, u32[]{:S(2)}, u32[]{:S(2)}) collective-permute-start(f32[16,128]{1,0:T(8,128)S(1)} %shard_map.101.wall), channel_id=1, source_target_pairs={{0,64},{64,128},{128,192},{192,256},{256,320},{320,384},{384,448},... | collective-permute-start | bytes 24584 | tf_op jit(solution)/shard_map/ppermute | solution.py:539
  45.9 19.5 %collective-permute-start.6 = (f32[17,24,128]{2,1,0:T(8,128)S(1)}, f32[17,24,128]{2,1,0:T(8,128)S(1)}, u32[]{:S(2)}, u32[]{:S(2)}) collective-permute-start(f32[17,24,128]{2,1,0:T(8,128)S(1)} %shard_map.100._), channel_id=1, source_target_pairs={{64,128},{192,256},{320,384},{128,64},{256,192},{384,320},{65,129}... | collective-permute-start | bytes 626696 | tf_op jit(solution)/shard_map/ppermute | solution.py:461
  49.9 15.5 %collective-permute-start.5 = (f32[16,1024]{1,0:T(8,128)S(1)}, f32[16,1024]{1,0:T(8,128)S(1)}, u32[]{:S(2)}, u32[]{:S(2)}) collective-permute-start(f32[16,1024]{1,0:T(8,128)S(1)} %get-tuple-element.27), channel_id=1, source_target_pairs={{1,2},{3,4},{5,6},{7,8},{9,10},{11,12},{13,14},{15,16},{17,18},{19... | collective-permute-start | bytes 196616 | tf_op jit(solution)/shard_map/ppermute | solution.py:461
  56.9 11.9 %collective-permute-start.7 = (f32[16,1024]{1,0:T(8,128)S(1)}, f32[16,1024]{1,0:T(8,128)S(1)}, u32[]{:S(2)}, u32[]{:S(2)}) collective-permute-start(f32[16,1024]{1,0:T(8,128)S(1)} %get-tuple-element.30), channel_id=1, source_target_pairs={{2,4},{3,5},{6,8},{7,9},{10,12},{11,13},{14,16},{15,17},{18,20},{1... | collective-permute-start | bytes 196616 | tf_op jit(solution)/shard_map/ppermute | solution.py:461
  58.9 9.9 %collective-permute-start.8 = (f32[16,1024]{1,0:T(8,128)S(1)}, f32[16,1024]{1,0:T(8,128)S(1)}, u32[]{:S(2)}, u32[]{:S(2)}) collective-permute-start(f32[16,1024]{1,0:T(8,128)S(1)} %get-tuple-element.31), channel_id=1, source_target_pairs={{0,2},{1,3},{4,6},{5,7},{8,10},{9,11},{12,14},{13,15},{16,18},{17,... | collective-permute-start | bytes 196616 | tf_op jit(solution)/shard_map/ppermute | solution.py:461
  60.8 8.0 %collective-permute-start.9 = (f32[16,1024]{1,0:T(8,128)S(1)}, f32[16,1024]{1,0:T(8,128)S(1)}, u32[]{:S(2)}, u32[]{:S(2)}) collective-permute-start(f32[16,1024]{1,0:T(8,128)S(1)} %get-tuple-element.32), channel_id=1, source_target_pairs={{0,1},{2,3},{4,5},{6,7},{8,9},{10,11},{12,13},{14,15},{16,17},{18,... | collective-permute-start | bytes 196616 | tf_op jit(solution)/shard_map/ppermute | solution.py:461

commit v9 on v7

--- a/solution.py
+++ b/solution.py
@@ -238,20 +238,23 @@
     return out
 
 
-def wall_kernel(gas, kappa, strips, recv_wall, recv_a, reaction, _, wall, now, later, kap, edge):
-    odd = lax.rem(lax.axis_index("sect"), 2)
-    even = odd == 0
+def wall_kernel(
+    gas, kappa, strips, recv_wall, recv_a, first, second, middle, reaction, _, wall, now, later, kap, edge
+):
+    even = lax.rem(lax.axis_index("sect"), 2) == 0
     mix = coupling(reaction)
     top = slice(GR - 8, GR)
     at_a, at_b = jnp.where(even, GX + 3, 0), jnp.where(even, 0, GX + 3)
     kappa_a, kappa_b = jnp.where(even, GX + 3, 1), jnp.where(even, 1, GX + 3)
     for c in range(COMP):
-        for x in range(GX):
+        for x in (0, 1, GX - 2, GX - 1):
             now[c, x + 3] = gas[c, x, top, :]
         for layer in range(3):
             now[c, at_a + layer] = recv_a[3 * c + layer, top, :]
             now[c, at_b + layer] = recv_wall[3 * c + layer]
-    for x in range(GX):
+        for i, x in enumerate(SEAM):
+            later[c, x + 3] = first[c, i, top, :]
+    for x in (0, 1, 2, GX - 3, GX - 2, GX - 1):
         kap[x + 3] = kappa[x, top, :]
     for layer in range(2):
         kap[kappa_a + layer] = recv_a[3 * COMP + layer, top, :]
@@ -259,16 +262,21 @@
     corner_a, corner_b = recv_a[LAYERS - 1, top, :], recv_wall[LAYERS - 1 + TILES - 1]
     low, high = jnp.where(even, corner_b, corner_a), jnp.where(even, corner_a, corner_b)
     strip_levels(strips, [low], [high], mix, edge, [TILES - 1])
-
+    wall[3 : GX - 3, :] = middle[0, :, GR - 1, :]
     for step, (src, dst) in enumerate(((now, later), (later, now), (now, None))):
-        comps = (0,) if step == ITERS - 1 else range(COMP)
-        for at in range(step + 1, EXT - 1 - step):
-            out = plane(src, kap, edge, step, at, at - 3, mix, 1, comps)
-            if step == ITERS - 1:
-                wall[at - 3 : at - 2, :] = out[0, 0][7:8, :]
-                continue
-            for c in comps:
-                dst[c, at] = out[c, 0]
+        last = step == ITERS - 1
+        if last:
+            for c in range(COMP):
+                for i, x in enumerate(SEAM):
+                    now[c, (x + 1 if i < 2 else x - 1) + 3] = second[c, i, top, :]
+        for i in range(3):
+            for at in (step + 1 + i, GX + 2 - step + i):
+                out = plane(src, kap, edge, step, at, at - 3, mix, 1, (0,) if last else range(COMP))
+                if last:
+                    wall[at - 3 : at - 2, :] = out[0, 0][7:8, :]
+                    continue
+                for c in range(COMP):
+                    dst[c, at] = out[c, 0]
 
 
 def inner_kernel(gas, kappa, strips, reaction, first, second, middle, one, two, edge):
@@ -511,9 +519,9 @@
             pltpu.VMEM((EXT, 8, GA), jnp.float32),
             pltpu.VMEM((ITERS, COMP, 8, GA), jnp.float32),
         ],
-        specs=[VMEM] * 5 + [SMEM, ANY],
+        specs=[VMEM] * 8 + [SMEM, ANY],
         moved=4 << 20,
-    )(gas, kappa, strips, recv_wall, recv_a, reaction, send_rest)
+    )(gas, kappa, strips, recv_wall, recv_a, first, second, middle, reaction, send_rest)
     earlier = lax.ppermute(wall, "sect", [(i, i + 1) for i in range(sections - 1)])
 
     own, *sends = call(

time: 68 us -> 67.6 us (level)
  no operation moved by 1% of the time
where the time goes in v9:
time: 67.6 us; the launch traced here: 67.1 us
  starting transfers between devices  49.1 us (73%)
  Pallas kernels  14.7 us (22%)
  local copies, waits for them, and re-layouts  2.4 us (4%)
  between operations  0.9 us (1%)
    ppermute x9, starting transfers between devices, swap(): return lax.ppermute(x, axis, pairs + [(j, i) for i, j in pairs])  43.9 us
    ppermute x1, starting transfers between devices, local(): lax.ppermute(wall, 'sect', [(i, i + 1) for i in range(sections - 1)])  5.11 us
    pallas_call x1, Pallas kernels, local(): call(inner_kernel, (f32(COMP, len(SEAM), GR, GA), f32(COMP, len(SEAM), GR...  4.55 us
    pallas_call x1, Pallas kernels, local(): call(outer_kernel, (whole, f32(8, 128)), scratch=[pltpu.VMEM((COMP, EXT,...  3.41 us
    unnamed x16, local copies, waits for them, and re-layouts  2.32 us
    pallas_call x1, Pallas kernels, local(): call(edges_kernel, (f32(3, GR, GA), f32(3, GR, GA)), scratch=[pltpu.VMEM(...  2.18 us
    pallas_call x1, Pallas kernels, local(): call(pack_kernel, (f32(MOVES, VALS, CAP), i32(MOVES, SPOTS, 128)), scratc...  1.73 us
  transfers between devices with their start and end apart: 10, of which 0 were waited for; matrix products, arithmetic and copies ran while one was open for 0% of the time, Pallas kernels for 15%

profile of v9, /device:TPU:1, one launch (start us, length us, event | category | flops | bytes accessed | tf_op | source)
XLA Modules:
  0.0 67.1 jit_solution(17300956135195915440)
XLA Ops:
  0.6 0.0 copy-start.1
  0.6 0.0 copy-start
  0.7 0.0 copy-start.7
  0.7 0.0 copy-start.4
  0.7 2.2 %shard_map.95 = (f32[3,32,128]{2,1,0:T(8,128)S(1)}, f32[3,32,128]{2,1,0:T(8,128)S(1)}) custom-call(f32[5,16,32,128]{3,2,1,0:T(8,128)} %gas.11, f32[16,32,128]{2,1,0:T(8,128)} %kappa.11), custom_call_target="tpu_custom_call" | custom-call | bytes 2097152 | tf_op jit(solution)/shard_map/pallas_call | solution.py:463
  2.9 0.0 copy-start.3
  2.9 11.7 %collective-permute-start = (f32[3,32,128]{2,1,0:T(8,128)S(1)}, f32[3,32,128]{2,1,0:T(8,128)S(1)}, u32[]{:S(2)}, u32[]{:S(2)}) collective-permute-start(f32[3,32,128]{2,1,0:T(8,128)S(1)} %get-tuple-element.19.send_q), channel_id=1, source_target_pairs={{1,2},{3,4},{5,6},{7,8},{9,10},{11,12},{13,14},{15,16},{17,18},{19... | collective-permute-start | bytes 147464 | tf_op jit(solution)/shard_map/ppermute | solution.py:451
  14.6 1.9 %collective-permute-start.1 = (f32[3,32,128]{2,1,0:T(8,128)S(1)}, f32[3,32,128]{2,1,0:T(8,128)S(1)}, u32[]{:S(2)}, u32[]{:S(2)}) collective-permute-start(f32[3,32,128]{2,1,0:T(8,128)S(1)} %get-tuple-element.20._.send_p), channel_id=1, source_target_pairs={{0,1},{2,3},{4,5},{6,7},{8,9},{10,11},{12,13},{14,15},{16,17},{18,... | collective-permute-start | bytes 147464 | tf_op jit(solution)/shard_map/ppermute | solution.py:451
  16.5 0.0 copy-done.7
  16.5 0.1 copy.10.heating
  16.6 0.0 copy-done.4
  16.6 0.0 copy-start.2
  16.6 0.9 %copy-done.2 = f32[16,2048]{1,0:T(8,128)S(1)} copy-done((f32[16,2048]{1,0:T(8,128)S(1)}, f32[16,2048]{1,0:T(8,128)}, u32[]{:S(2)}) %copy-start.2) | copy-done | bytes 131096
  17.5 0.0 copy-start.5
  17.5 0.7 %copy-done.5 = s32[2048]{0:T(1024)S(1)} copy-done((s32[2048]{0:T(1024)S(1)}, s32[2048]{0:T(1024)}, u32[]{:S(2)}) %copy-start.5) | copy-done | bytes 8216
  18.2 0.0 copy-start.6
  18.2 0.7 %copy-done.6 = f32[16,16]{1,0:T(8,128)S(1)} copy-done((f32[16,16]{1,0:T(8,128)S(1)}, f32[16,16]{1,0:T(8,128)}, u32[]{:S(2)}) %copy-start.6) | copy-done | bytes 1048
  18.9 1.7 %shard_map.96 = (f32[5,16,1024]{2,1,0:T(8,128)S(1)}, s32[5,8,128]{2,1,0:T(8,128)S(1)}) custom-call(s32[16,128]{1,0:T(8,128)S(1)} %bitcast.3, s32[16,128]{1,0:T(8,128)S(1)} %bitcast.4, f32[16,2048]{1,0:T(8,128)S(1)} %copy-done.2, f32[16,16]{1,0:T(8,128)S(1)} %copy-done.6, f32[16,1]{1,0:T(8,128)S(1)} %copy.10.heating, f32[3,32,128]{2,1,0:T(8,128)S(1)} %get-tuple-element.20._.send_p), custom_call_target="tpu_custom_call" | custom-call | bytes 4194304 | tf_op jit(solution)/shard_map/pallas_call | solution.py:474
  20.7 0.0 collective-permute-done.recv_q
  20.7 0.0 collective-permute-done.1.recv_p
  20.7 0.0 copy-done.1
  20.7 0.0 copy-done
  20.7 0.8 %shard_map.97 = (f32[28,32,128]{2,1,0:T(8,128)S(1)}, f32[18,32,128]{2,1,0:T(8,128)S(1)}, f32[21,8,128]{2,1,0:T(8,128)S(1)}) custom-call(f32[5,16,32,128]{3,2,1,0:T(8,128)S(1)} %copy-done, f32[16,32,128]{2,1,0:T(8,128)S(1)} %copy-done.1, f32[3,32,128]{2,1,0:T(8,128)S(1)} %get-tuple-element.19.send_q, f32[3,32,128]{2,1,0:T(8,128)S(1)} %get-tuple-element.20._.send_p, ...), custom_call_target="tpu_custom_call" | custom-call | bytes 2097152 | tf_op jit(solution)/shard_map/pallas_call | solution.py:488
  21.6 3.1 %collective-permute-start.3 = (f32[18,32,128]{2,1,0:T(8,128)S(1)}, f32[18,32,128]{2,1,0:T(8,128)S(1)}, u32[]{:S(2)}, u32[]{:S(2)}) collective-permute-start(f32[18,32,128]{2,1,0:T(8,128)S(1)} %get-tuple-element.24), channel_id=1, source_target_pairs={{0,64},{128,192},{256,320},{384,448},{64,0},{192,128},{320,256},{4... | collective-permute-start | bytes 884744 | tf_op jit(solution)/shard_map/ppermute | solution.py:451
  24.6 8.5 %collective-permute-start.2 = (f32[21,8,128]{2,1,0:T(8,128)S(1)}, f32[21,8,128]{2,1,0:T(8,128)S(1)}, u32[]{:S(2)}, u32[]{:S(2)}) collective-permute-start(f32[21,8,128]{2,1,0:T(8,128)S(1)} %get-tuple-element.23), channel_id=1, source_target_pairs={{64,128},{192,256},{320,384},{128,64},{256,192},{384,320},{65,129}... | collective-permute-start | bytes 258056 | tf_op jit(solution)/shard_map/ppermute | solution.py:451
  33.2 0.0 copy-done.3
  33.2 4.5 %shard_map.98 = (f32[5,4,32,128]{3,2,1,0:T(8,128)S(1)}, f32[5,4,32,128]{3,2,1,0:T(8,128)S(1)}, f32[5,10,32,128]{3,2,1,0:T(8,128)S(1)}) custom-call(f32[5,16,32,128]{3,2,1,0:T(8,128)S(1)} %copy-done, f32[16,32,128]{2,1,0:T(8,128)S(1)} %copy-done.1, f32[28,32,128]{2,1,0:T(8,128)S(1)} %get-tuple-element.22.strips, f32[5,5]{1,0:T(8,128)S(1)} %copy-done.3), custom_call_target="tpu_custom_call" | custom-call | bytes 12582912 | tf_op jit(solution)/shard_map/pallas_call | solution.py:498
  37.8 0.0 collective-permute-done.2.recv_wall
  37.8 0.0 collective-permute-done.3.recv_a
  37.8 1.0 %shard_map.100.wall = f32[16,128]{1,0:T(8,128)S(1)} custom-call(f32[5,16,32,128]{3,2,1,0:T(8,128)S(1)} %copy-done, f32[16,32,128]{2,1,0:T(8,128)S(1)} %copy-done.1, f32[28,32,128]{2,1,0:T(8,128)S(1)} %get-tuple-element.22.strips, f32[21,8,128]{2,1,0:T(8,128)S(1)} %collective-permute-done.2.recv_wall, f32[18,32,128]{2,1,0:T(8,128)S(1)} %collective-permute-done.3.recv_a, ...), custom_call_target="tpu_custom_call" | custom-call | bytes 4194304 | tf_op jit(solution)/shard_map/pallas_call | solution.py:513
  38.8 5.1 %collective-permute-start.4 = (f32[16,128]{1,0:T(8,128)S(1)}, f32[16,128]{1,0:T(8,128)S(1)}, u32[]{:S(2)}, u32[]{:S(2)}) collective-permute-start(f32[16,128]{1,0:T(8,128)S(1)} %shard_map.100.wall), channel_id=1, source_target_pairs={{0,64},{64,128},{128,192},{192,256},{256,320},{320,384},{384,448},... | collective-permute-start | bytes 24584 | tf_op jit(solution)/shard_map/ppermute | solution.py:525
  43.9 3.3 %collective-permute-start.6 = (f32[17,24,128]{2,1,0:T(8,128)S(1)}, f32[17,24,128]{2,1,0:T(8,128)S(1)}, u32[]{:S(2)}, u32[]{:S(2)}) collective-permute-start(f32[17,24,128]{2,1,0:T(8,128)S(1)} %shard_map.99._), channel_id=1, source_target_pairs={{64,128},{192,256},{320,384},{128,64},{256,192},{384,320},{65,129}... | collective-permute-start | bytes 626696 | tf_op jit(solution)/shard_map/ppermute | solution.py:451
  47.2 0.0 collective-permute-done.4.earlier
  47.3 0.2 shard_map.101
  47.5 5.6 %collective-permute-start.5 = (f32[16,1024]{1,0:T(8,128)S(1)}, f32[16,1024]{1,0:T(8,128)S(1)}, u32[]{:S(2)}, u32[]{:S(2)}) collective-permute-start(f32[16,1024]{1,0:T(8,128)S(1)} %get-tuple-element.29), channel_id=1, source_target_pairs={{1,2},{3,4},{5,6},{7,8},{9,10},{11,12},{13,14},{15,16},{17,18},{19... | collective-permute-start | bytes 196616 | tf_op jit(solution)/shard_map/ppermute | solution.py:451
  53.1 1.9 %collective-permute-start.7 = (f32[16,1024]{1,0:T(8,128)S(1)}, f32[16,1024]{1,0:T(8,128)S(1)}, u32[]{:S(2)}, u32[]{:S(2)}) collective-permute-start(f32[16,1024]{1,0:T(8,128)S(1)} %get-tuple-element.32), channel_id=1, source_target_pairs={{2,4},{3,5},{6,8},{7,9},{10,12},{11,13},{14,16},{15,17},{18,20},{1... | collective-permute-start | bytes 196616 | tf_op jit(solution)/shard_map/ppermute | solution.py:451
  55.0 1.9 %collective-permute-start.8 = (f32[16,1024]{1,0:T(8,128)S(1)}, f32[16,1024]{1,0:T(8,128)S(1)}, u32[]{:S(2)}, u32[]{:S(2)}) collective-permute-start(f32[16,1024]{1,0:T(8,128)S(1)} %get-tuple-element.33), channel_id=1, source_target_pairs={{0,2},{1,3},{4,6},{5,7},{8,10},{9,11},{12,14},{13,15},{16,18},{17,... | collective-permute-start | bytes 196616 | tf_op jit(solution)/shard_map/ppermute | solution.py:451
  56.9 6.0 %collective-permute-start.9 = (f32[16,1024]{1,0:T(8,128)S(1)}, f32[16,1024]{1,0:T(8,128)S(1)}, u32[]{:S(2)}, u32[]{:S(2)}) collective-permute-start(f32[16,1024]{1,0:T(8,128)S(1)} %get-tuple-element.34), channel_id=1, source_target_pairs={{0,1},{2,3},{4,5},{6,7},{8,9},{10,11},{12,13},{14,15},{16,17},{18,... | collective-permute-start | bytes 196616 | tf_op jit(solution)/shard_map/ppermute | solution.py:451
  62.9 0.0 collective-permute-done.6.recv_rest
  62.9 0.0 collective-permute-done.5._.recv_q
  62.9 3.4 %shard_map.102 = (f32[5,16,32,128]{3,2,1,0:T(8,128)}, f32[8,128]{1,0:T(8,128)S(1)}) custom-call(f32[16,1024]{1,0:T(8,128)S(1)} %collective-permute-done.5._.recv_q, f32[5,16,32,128]{3,2,1,0:T(8,128)S(1)} %copy-done, f32[16,32,128]{2,1,0:T(8,128)S(1)} %copy-done.1, f32[28,32,128]{2,1,0:T(8,128)S(1)} %get-tuple-element.22.strips, ...), custom_call_target="tpu_custom_call" | custom-call | bytes 8388608 | tf_op jit(solution)/shard_map/pallas_call | solution.py:537
  66.3 0.0 collective-permute-done.7.recv_s
  66.3 0.0 collective-permute-done.8.recv_r
  66.3 0.0 collective-permute-done.9.recv_p
  66.3 0.8 %shard_map.103 = f32[16,5120]{1,0:T(8,128)} custom-call(f32[16,1024]{1,0:T(8,128)S(1)} %get-tuple-element.31.own, f32[16,1024]{1,0:T(8,128)S(1)} %collective-permute-done.5._.recv_q, f32[16,1024]{1,0:T(8,128)S(1)} %collective-permute-done.7.recv_s, f32[16,1024]{1,0:T(8,128)S(1)} %collective-permute-done.8.recv_r, ...), custom_call_target="tpu_custom_call" | custom-call | bytes 1048576 | tf_op jit(solution)/shard_map/pallas_call | solution.py:549
  (1 shorter events, 0.0 us)
Async XLA Ops:
  0.6 20.1 %copy-start.1 = (f32[16,32,128]{2,1,0:T(8,128)S(1)}, f32[16,32,128]{2,1,0:T(8,128)}, u32[]{:S(2)}) copy-start(f32[16,32,128]{2,1,0:T(8,128)} %kappa.11) | copy-start | bytes 786436
  0.6 20.1 %copy-start = (f32[5,16,32,128]{3,2,1,0:T(8,128)S(1)}, f32[5,16,32,128]{3,2,1,0:T(8,128)}, u32[]{:S(2)}) copy-start(f32[5,16,32,128]{3,2,1,0:T(8,128)} %gas.11) | copy-start | bytes 3932164
  0.7 15.9 %copy-start.7 = (f32[16]{0:T(128)S(1)}, f32[16]{0:T(128)}, u32[]{:S(2)}) copy-start(f32[16]{0:T(128)} %param.13) | copy-start | bytes 196
  0.7 16.0 %copy-start.4 = (s32[2048,1]{0,1:T(1,128)S(1)}, s32[2048,1]{0,1:T(1,128)}, u32[]{:S(2)}) copy-start(s32[2048,1]{0,1:T(1,128)} %param.15) | copy-start | bytes 24580
  2.9 30.3 %copy-start.3 = (f32[5,5]{1,0:T(8,128)S(1)}, f32[5,5]{1,0:T(8,128)}, u32[]{:S(2)}) copy-start(f32[5,5]{1,0:T(8,128)} %reaction.5) | copy-start | bytes 304
  2.9 17.8 %collective-permute-start = (f32[3,32,128]{2,1,0:T(8,128)S(1)}, f32[3,32,128]{2,1,0:T(8,128)S(1)}, u32[]{:S(2)}, u32[]{:S(2)}) collective-permute-start(f32[3,32,128]{2,1,0:T(8,128)S(1)} %get-tuple-element.19.send_q), channel_id=1, source_target_pairs={{1,2},{3,4},{5,6},{7,8},{9,10},{11,12},{13,14},{15,16},{17,18},{19... | collective-permute-start | bytes 147464 | tf_op jit(solution)/shard_map/ppermute | solution.py:451
  14.6 6.1 %collective-permute-start.1 = (f32[3,32,128]{2,1,0:T(8,128)S(1)}, f32[3,32,128]{2,1,0:T(8,128)S(1)}, u32[]{:S(2)}, u32[]{:S(2)}) collective-permute-start(f32[3,32,128]{2,1,0:T(8,128)S(1)} %get-tuple-element.20._.send_p), channel_id=1, source_target_pairs={{0,1},{2,3},{4,5},{6,7},{8,9},{10,11},{12,13},{14,15},{16,17},{18,... | collective-permute-start | bytes 147464 | tf_op jit(solution)/shard_map/ppermute | solution.py:451
  16.6 0.9 %copy-start.2 = (f32[16,2048]{1,0:T(8,128)S(1)}, f32[16,2048]{1,0:T(8,128)}, u32[]{:S(2)}) copy-start(f32[16,2048]{1,0:T(8,128)} %particles.1) | copy-start | bytes 393220
  17.5 0.7 %copy-start.5 = (s32[2048]{0:T(1024)S(1)}, s32[2048]{0:T(1024)}, u32[]{:S(2)}) copy-start(s32[2048]{0:T(1024)} %param.14) | copy-start | bytes 24580
  18.2 0.7 %copy-start.6 = (f32[16,16]{1,0:T(8,128)S(1)}, f32[16,16]{1,0:T(8,128)}, u32[]{:S(2)}) copy-start(f32[16,16]{1,0:T(8,128)} %mixing.1) | copy-start | bytes 3076
  21.6 16.2 %collective-permute-start.3 = (f32[18,32,128]{2,1,0:T(8,128)S(1)}, f32[18,32,128]{2,1,0:T(8,128)S(1)}, u32[]{:S(2)}, u32[]{:S(2)}) collective-permute-start(f32[18,32,128]{2,1,0:T(8,128)S(1)} %get-tuple-element.24), channel_id=1, source_target_pairs={{0,64},{128,192},{256,320},{384,448},{64,0},{192,128},{320,256},{4... | collective-permute-start | bytes 884744 | tf_op jit(solution)/shard_map/ppermute | solution.py:451
  24.6 13.1 %collective-permute-start.2 = (f32[21,8,128]{2,1,0:T(8,128)S(1)}, f32[21,8,128]{2,1,0:T(8,128)S(1)}, u32[]{:S(2)}, u32[]{:S(2)}) collective-permute-start(f32[21,8,128]{2,1,0:T(8,128)S(1)} %get-tuple-element.23), channel_id=1, source_target_pairs={{64,128},{192,256},{320,384},{128,64},{256,192},{384,320},{65,129}... | collective-permute-start | bytes 258056 | tf_op jit(solution)/shard_map/ppermute | solution.py:451
  38.8 8.4 %collective-permute-start.4 = (f32[16,128]{1,0:T(8,128)S(1)}, f32[16,128]{1,0:T(8,128)S(1)}, u32[]{:S(2)}, u32[]{:S(2)}) collective-permute-start(f32[16,128]{1,0:T(8,128)S(1)} %shard_map.100.wall), channel_id=1, source_target_pairs={{0,64},{64,128},{128,192},{192,256},{256,320},{320,384},{384,448},... | collective-permute-start | bytes 24584 | tf_op jit(solution)/shard_map/ppermute | solution.py:525
  43.9 19.0 %collective-permute-start.6 = (f32[17,24,128]{2,1,0:T(8,128)S(1)}, f32[17,24,128]{2,1,0:T(8,128)S(1)}, u32[]{:S(2)}, u32[]{:S(2)}) collective-permute-start(f32[17,24,128]{2,1,0:T(8,128)S(1)} %shard_map.99._), channel_id=1, source_target_pairs={{64,128},{192,256},{320,384},{128,64},{256,192},{384,320},{65,129}... | collective-permute-start | bytes 626696 | tf_op jit(solution)/shard_map/ppermute | solution.py:451
  47.5 15.5 %collective-permute-start.5 = (f32[16,1024]{1,0:T(8,128)S(1)}, f32[16,1024]{1,0:T(8,128)S(1)}, u32[]{:S(2)}, u32[]{:S(2)}) collective-permute-start(f32[16,1024]{1,0:T(8,128)S(1)} %get-tuple-element.29), channel_id=1, source_target_pairs={{1,2},{3,4},{5,6},{7,8},{9,10},{11,12},{13,14},{15,16},{17,18},{19... | collective-permute-start | bytes 196616 | tf_op jit(solution)/shard_map/ppermute | solution.py:451
  53.1 13.3 %collective-permute-start.7 = (f32[16,1024]{1,0:T(8,128)S(1)}, f32[16,1024]{1,0:T(8,128)S(1)}, u32[]{:S(2)}, u32[]{:S(2)}) collective-permute-start(f32[16,1024]{1,0:T(8,128)S(1)} %get-tuple-element.32), channel_id=1, source_target_pairs={{2,4},{3,5},{6,8},{7,9},{10,12},{11,13},{14,16},{15,17},{18,20},{1... | collective-permute-start | bytes 196616 | tf_op jit(solution)/shard_map/ppermute | solution.py:451
  55.0 11.3 %collective-permute-start.8 = (f32[16,1024]{1,0:T(8,128)S(1)}, f32[16,1024]{1,0:T(8,128)S(1)}, u32[]{:S(2)}, u32[]{:S(2)}) collective-permute-start(f32[16,1024]{1,0:T(8,128)S(1)} %get-tuple-element.33), channel_id=1, source_target_pairs={{0,2},{1,3},{4,6},{5,7},{8,10},{9,11},{12,14},{13,15},{16,18},{17,... | collective-permute-start | bytes 196616 | tf_op jit(solution)/shard_map/ppermute | solution.py:451
  56.9 9.4 %collective-permute-start.9 = (f32[16,1024]{1,0:T(8,128)S(1)}, f32[16,1024]{1,0:T(8,128)S(1)}, u32[]{:S(2)}, u32[]{:S(2)}) collective-permute-start(f32[16,1024]{1,0:T(8,128)S(1)} %get-tuple-element.34), channel_id=1, source_target_pairs={{0,1},{2,3},{4,5},{6,7},{8,9},{10,11},{12,13},{14,15},{16,17},{18,... | collective-permute-start | bytes 196616 | tf_op jit(solution)/shard_map/ppermute | solution.py:451

commit v10 on v9

--- a/solution.py
+++ b/solution.py
@@ -416,10 +416,10 @@
 def moves_of_swaps():
     tile = lax.axis_index("blk")
     odd, late = lax.rem(tile, 2), lax.rem(tile, 4) >> 1
-    return [REACH - 1 + 2 * odd, 2 * REACH * late, 2 * REACH * (1 - late), REACH + 1 - 2 * odd]
-
-
-def heat_kernel(wall, earlier, packed, cells, heating, own, send_q, send_s, send_r, send_p, look):
+    return [REACH - 1 + 2 * odd, 2 * REACH * (1 - late), 2 * REACH * late, REACH + 1 - 2 * odd]
+
+
+def heat_kernel(wall, earlier, packed, cells, heating, own, send_q, send_r, send_s, send_p, look):
     flux = 0.5 * (wall[...] + earlier[...])
     heat = jnp.broadcast_to(heating[...], (VALS, 128))
     for j in range(MOVES):
@@ -430,15 +430,15 @@
             line = jnp.broadcast_to(flux[x : x + 1, :], (8, 128))
             found = jnp.where(row == x, pick(line, column), found)
         look[j] = found
-    for out, j in zip((own, send_q, send_s, send_r, send_p), [REACH] + moves_of_swaps()):
+    for out, j in zip((own, send_q, send_r, send_s, send_p), [REACH] + moves_of_swaps()):
         for spot in range(SPOTS):
             part = slice(128 * spot, 128 * (spot + 1))
             out[:, part] = packed[j, :, part] + heat * look[j, spot : spot + 1, :]
 
 
-def join_kernel(own, recv_q, recv_s, recv_r, recv_p, _, out, done):
+def join_kernel(own, recv_q, recv_r, recv_s, recv_p, _, out, done):
     copies = []
-    for n, (piece, j) in enumerate(zip((own, recv_q, recv_s, recv_r, recv_p), [REACH] + moves_of_swaps())):
+    for n, (piece, j) in enumerate(zip((own, recv_q, recv_r, recv_s, recv_p), [REACH] + moves_of_swaps())):
         place = pl.multiple_of((2 * REACH - j) * CAP, CAP)
         copies.append(pltpu.make_async_copy(piece, out.at[:, pl.ds(place, CAP)], done.at[n]))
     for copy in copies:
@@ -532,7 +532,7 @@
         moved=2 << 20,
         flops=1 << 34,
     )(wall, earlier, packed, cells, heating_column)
-    pieces = [swap(x, "blk", pairs) for x, pairs in zip(sends, (pairs_q, pairs_s, pairs_r, pairs_p))]
+    pieces = [swap(x, "blk", pairs) for x, pairs in zip(sends, (pairs_q, pairs_r, pairs_s, pairs_p))]
 
     field, token = call(
         outer_kernel,

time: 67.6 us -> 67.6 us (level)
  no operation moved by 1% of the time
where the time goes in v10:
time: 67.6 us; the launch traced here: 67.1 us
  starting transfers between devices  49.1 us (73%)
  Pallas kernels  14.7 us (22%)
  local copies, waits for them, and re-layouts  2.4 us (4%)
  between operations  0.9 us (1%)
    ppermute x9, starting transfers between devices, swap(): return lax.ppermute(x, axis, pairs + [(j, i) for i, j in pairs])  43.9 us
    ppermute x1, starting transfers between devices, local(): lax.ppermute(wall, 'sect', [(i, i + 1) for i in range(sections - 1)])  5.11 us
    pallas_call x1, Pallas kernels, local(): call(inner_kernel, (f32(COMP, len(SEAM), GR, GA), f32(COMP, len(SEAM), GR...  4.55 us
    pallas_call x1, Pallas kernels, local(): call(outer_kernel, (whole, f32(8, 128)), scratch=[pltpu.VMEM((COMP, EXT,...  3.41 us
    unnamed x16, local copies, waits for them, and re-layouts  2.32 us
    pallas_call x1, Pallas kernels, local(): call(edges_kernel, (f32(3, GR, GA), f32(3, GR, GA)), scratch=[pltpu.VMEM(...  2.18 us
    pallas_call x1, Pallas kernels, local(): call(pack_kernel, (f32(MOVES, VALS, CAP), i32(MOVES, SPOTS, 128)), scratc...  1.73 us
  transfers between devices with their start and end apart: 10, of which 0 were waited for; matrix products, arithmetic and copies ran while one was open for 0% of the time, Pallas kernels for 15%

profile of v10, /device:TPU:1, one launch (start us, length us, event | category | flops | bytes accessed | tf_op | source)
XLA Modules:
  0.0 67.1 jit_solution(16213451363504231034)
XLA Ops:
  0.6 0.0 copy-start.1
  0.6 0.0 copy-start
  0.7 0.0 copy-start.7
  0.7 0.0 copy-start.4
  0.7 2.2 %shard_map.95 = (f32[3,32,128]{2,1,0:T(8,128)S(1)}, f32[3,32,128]{2,1,0:T(8,128)S(1)}) custom-call(f32[5,16,32,128]{3,2,1,0:T(8,128)} %gas.11, f32[16,32,128]{2,1,0:T(8,128)} %kappa.11), custom_call_target="tpu_custom_call" | custom-call | bytes 2097152 | tf_op jit(solution)/shard_map/pallas_call | solution.py:463
  2.9 0.0 copy-start.3
  2.9 11.7 %collective-permute-start = (f32[3,32,128]{2,1,0:T(8,128)S(1)}, f32[3,32,128]{2,1,0:T(8,128)S(1)}, u32[]{:S(2)}, u32[]{:S(2)}) collective-permute-start(f32[3,32,128]{2,1,0:T(8,128)S(1)} %get-tuple-element.19.send_q), channel_id=1, source_target_pairs={{1,2},{3,4},{5,6},{7,8},{9,10},{11,12},{13,14},{15,16},{17,18},{19... | collective-permute-start | bytes 147464 | tf_op jit(solution)/shard_map/ppermute | solution.py:451
  14.6 1.9 %collective-permute-start.1 = (f32[3,32,128]{2,1,0:T(8,128)S(1)}, f32[3,32,128]{2,1,0:T(8,128)S(1)}, u32[]{:S(2)}, u32[]{:S(2)}) collective-permute-start(f32[3,32,128]{2,1,0:T(8,128)S(1)} %get-tuple-element.20._.send_p), channel_id=1, source_target_pairs={{0,1},{2,3},{4,5},{6,7},{8,9},{10,11},{12,13},{14,15},{16,17},{18,... | collective-permute-start | bytes 147464 | tf_op jit(solution)/shard_map/ppermute | solution.py:451
  16.5 0.0 copy-done.7
  16.5 0.1 copy.10.heating
  16.6 0.0 copy-done.4
  16.6 0.0 copy-start.2
  16.6 0.9 %copy-done.2 = f32[16,2048]{1,0:T(8,128)S(1)} copy-done((f32[16,2048]{1,0:T(8,128)S(1)}, f32[16,2048]{1,0:T(8,128)}, u32[]{:S(2)}) %copy-start.2) | copy-done | bytes 131096
  17.5 0.0 copy-start.5
  17.5 0.7 %copy-done.5 = s32[2048]{0:T(1024)S(1)} copy-done((s32[2048]{0:T(1024)S(1)}, s32[2048]{0:T(1024)}, u32[]{:S(2)}) %copy-start.5) | copy-done | bytes 8216
  18.2 0.0 copy-start.6
  18.2 0.7 %copy-done.6 = f32[16,16]{1,0:T(8,128)S(1)} copy-done((f32[16,16]{1,0:T(8,128)S(1)}, f32[16,16]{1,0:T(8,128)}, u32[]{:S(2)}) %copy-start.6) | copy-done | bytes 1048
  18.9 1.7 %shard_map.96 = (f32[5,16,1024]{2,1,0:T(8,128)S(1)}, s32[5,8,128]{2,1,0:T(8,128)S(1)}) custom-call(s32[16,128]{1,0:T(8,128)S(1)} %bitcast.3, s32[16,128]{1,0:T(8,128)S(1)} %bitcast.4, f32[16,2048]{1,0:T(8,128)S(1)} %copy-done.2, f32[16,16]{1,0:T(8,128)S(1)} %copy-done.6, f32[16,1]{1,0:T(8,128)S(1)} %copy.10.heating, f32[3,32,128]{2,1,0:T(8,128)S(1)} %get-tuple-element.20._.send_p), custom_call_target="tpu_custom_call" | custom-call | bytes 4194304 | tf_op jit(solution)/shard_map/pallas_call | solution.py:474
  20.7 0.0 collective-permute-done.recv_q
  20.7 0.0 collective-permute-done.1.recv_p
  20.7 0.0 copy-done.1
  20.7 0.0 copy-done
  20.7 0.8 %shard_map.97 = (f32[28,32,128]{2,1,0:T(8,128)S(1)}, f32[18,32,128]{2,1,0:T(8,128)S(1)}, f32[21,8,128]{2,1,0:T(8,128)S(1)}) custom-call(f32[5,16,32,128]{3,2,1,0:T(8,128)S(1)} %copy-done, f32[16,32,128]{2,1,0:T(8,128)S(1)} %copy-done.1, f32[3,32,128]{2,1,0:T(8,128)S(1)} %get-tuple-element.19.send_q, f32[3,32,128]{2,1,0:T(8,128)S(1)} %get-tuple-element.20._.send_p, ...), custom_call_target="tpu_custom_call" | custom-call | bytes 2097152 | tf_op jit(solution)/shard_map/pallas_call | solution.py:488
  21.6 3.1 %collective-permute-start.3 = (f32[18,32,128]{2,1,0:T(8,128)S(1)}, f32[18,32,128]{2,1,0:T(8,128)S(1)}, u32[]{:S(2)}, u32[]{:S(2)}) collective-permute-start(f32[18,32,128]{2,1,0:T(8,128)S(1)} %get-tuple-element.24), channel_id=1, source_target_pairs={{0,64},{128,192},{256,320},{384,448},{64,0},{192,128},{320,256},{4... | collective-permute-start | bytes 884744 | tf_op jit(solution)/shard_map/ppermute | solution.py:451
  24.6 8.5 %collective-permute-start.2 = (f32[21,8,128]{2,1,0:T(8,128)S(1)}, f32[21,8,128]{2,1,0:T(8,128)S(1)}, u32[]{:S(2)}, u32[]{:S(2)}) collective-permute-start(f32[21,8,128]{2,1,0:T(8,128)S(1)} %get-tuple-element.23), channel_id=1, source_target_pairs={{64,128},{192,256},{320,384},{128,64},{256,192},{384,320},{65,129}... | collective-permute-start | bytes 258056 | tf_op jit(solution)/shard_map/ppermute | solution.py:451
  33.2 0.0 copy-done.3
  33.2 4.5 %shard_map.98 = (f32[5,4,32,128]{3,2,1,0:T(8,128)S(1)}, f32[5,4,32,128]{3,2,1,0:T(8,128)S(1)}, f32[5,10,32,128]{3,2,1,0:T(8,128)S(1)}) custom-call(f32[5,16,32,128]{3,2,1,0:T(8,128)S(1)} %copy-done, f32[16,32,128]{2,1,0:T(8,128)S(1)} %copy-done.1, f32[28,32,128]{2,1,0:T(8,128)S(1)} %get-tuple-element.22.strips, f32[5,5]{1,0:T(8,128)S(1)} %copy-done.3), custom_call_target="tpu_custom_call" | custom-call | bytes 12582912 | tf_op jit(solution)/shard_map/pallas_call | solution.py:498
  37.8 0.0 collective-permute-done.2.recv_wall
  37.8 0.0 collective-permute-done.3.recv_a
  37.8 1.0 %shard_map.100.wall = f32[16,128]{1,0:T(8,128)S(1)} custom-call(f32[5,16,32,128]{3,2,1,0:T(8,128)S(1)} %copy-done, f32[16,32,128]{2,1,0:T(8,128)S(1)} %copy-done.1, f32[28,32,128]{2,1,0:T(8,128)S(1)} %get-tuple-element.22.strips, f32[21,8,128]{2,1,0:T(8,128)S(1)} %collective-permute-done.2.recv_wall, f32[18,32,128]{2,1,0:T(8,128)S(1)} %collective-permute-done.3.recv_a, ...), custom_call_target="tpu_custom_call" | custom-call | bytes 4194304 | tf_op jit(solution)/shard_map/pallas_call | solution.py:513
  38.8 5.1 %collective-permute-start.4 = (f32[16,128]{1,0:T(8,128)S(1)}, f32[16,128]{1,0:T(8,128)S(1)}, u32[]{:S(2)}, u32[]{:S(2)}) collective-permute-start(f32[16,128]{1,0:T(8,128)S(1)} %shard_map.100.wall), channel_id=1, source_target_pairs={{0,64},{64,128},{128,192},{192,256},{256,320},{320,384},{384,448},... | collective-permute-start | bytes 24584 | tf_op jit(solution)/shard_map/ppermute | solution.py:525
  43.9 3.3 %collective-permute-start.6 = (f32[17,24,128]{2,1,0:T(8,128)S(1)}, f32[17,24,128]{2,1,0:T(8,128)S(1)}, u32[]{:S(2)}, u32[]{:S(2)}) collective-permute-start(f32[17,24,128]{2,1,0:T(8,128)S(1)} %shard_map.99._), channel_id=1, source_target_pairs={{64,128},{192,256},{320,384},{128,64},{256,192},{384,320},{65,129}... | collective-permute-start | bytes 626696 | tf_op jit(solution)/shard_map/ppermute | solution.py:451
  47.2 0.0 collective-permute-done.4.earlier
  47.3 0.2 shard_map.101
  47.5 5.6 %collective-permute-start.5 = (f32[16,1024]{1,0:T(8,128)S(1)}, f32[16,1024]{1,0:T(8,128)S(1)}, u32[]{:S(2)}, u32[]{:S(2)}) collective-permute-start(f32[16,1024]{1,0:T(8,128)S(1)} %get-tuple-element.29), channel_id=1, source_target_pairs={{1,2},{3,4},{5,6},{7,8},{9,10},{11,12},{13,14},{15,16},{17,18},{19... | collective-permute-start | bytes 196616 | tf_op jit(solution)/shard_map/ppermute | solution.py:451
  53.1 1.9 %collective-permute-start.7 = (f32[16,1024]{1,0:T(8,128)S(1)}, f32[16,1024]{1,0:T(8,128)S(1)}, u32[]{:S(2)}, u32[]{:S(2)}) collective-permute-start(f32[16,1024]{1,0:T(8,128)S(1)} %get-tuple-element.32), channel_id=1, source_target_pairs={{0,2},{1,3},{4,6},{5,7},{8,10},{9,11},{12,14},{13,15},{16,18},{17,... | collective-permute-start | bytes 196616 | tf_op jit(solution)/shard_map/ppermute | solution.py:451
  55.0 3.1 %collective-permute-start.8 = (f32[16,1024]{1,0:T(8,128)S(1)}, f32[16,1024]{1,0:T(8,128)S(1)}, u32[]{:S(2)}, u32[]{:S(2)}) collective-permute-start(f32[16,1024]{1,0:T(8,128)S(1)} %get-tuple-element.33), channel_id=1, source_target_pairs={{2,4},{3,5},{6,8},{7,9},{10,12},{11,13},{14,16},{15,17},{18,20},{1... | collective-permute-start | bytes 196616 | tf_op jit(solution)/shard_map/ppermute | solution.py:451
  58.1 4.8 %collective-permute-start.9 = (f32[16,1024]{1,0:T(8,128)S(1)}, f32[16,1024]{1,0:T(8,128)S(1)}, u32[]{:S(2)}, u32[]{:S(2)}) collective-permute-start(f32[16,1024]{1,0:T(8,128)S(1)} %get-tuple-element.34), channel_id=1, source_target_pairs={{0,1},{2,3},{4,5},{6,7},{8,9},{10,11},{12,13},{14,15},{16,17},{18,... | collective-permute-start | bytes 196616 | tf_op jit(solution)/shard_map/ppermute | solution.py:451
  62.9 0.0 collective-permute-done.6.recv_rest
  62.9 0.0 collective-permute-done.5._.recv_q
  62.9 3.4 %shard_map.102 = (f32[5,16,32,128]{3,2,1,0:T(8,128)}, f32[8,128]{1,0:T(8,128)S(1)}) custom-call(f32[16,1024]{1,0:T(8,128)S(1)} %collective-permute-done.5._.recv_q, f32[5,16,32,128]{3,2,1,0:T(8,128)S(1)} %copy-done, f32[16,32,128]{2,1,0:T(8,128)S(1)} %copy-done.1, f32[28,32,128]{2,1,0:T(8,128)S(1)} %get-tuple-element.22.strips, ...), custom_call_target="tpu_custom_call" | custom-call | bytes 8388608 | tf_op jit(solution)/shard_map/pallas_call | solution.py:537
  66.3 0.0 collective-permute-done.7.recv_r
  66.3 0.0 collective-permute-done.8.recv_s
  66.3 0.0 collective-permute-done.9.recv_p
  66.3 0.8 %shard_map.103 = f32[16,5120]{1,0:T(8,128)} custom-call(f32[16,1024]{1,0:T(8,128)S(1)} %get-tuple-element.31.own, f32[16,1024]{1,0:T(8,128)S(1)} %collective-permute-done.5._.recv_q, f32[16,1024]{1,0:T(8,128)S(1)} %collective-permute-done.7.recv_r, f32[16,1024]{1,0:T(8,128)S(1)} %collective-permute-done.8.recv_s, ...), custom_call_target="tpu_custom_call" | custom-call | bytes 1048576 | tf_op jit(solution)/shard_map/pallas_call | solution.py:549
  (1 shorter events, 0.0 us)
Async XLA Ops:
  0.6 20.1 %copy-start.1 = (f32[16,32,128]{2,1,0:T(8,128)S(1)}, f32[16,32,128]{2,1,0:T(8,128)}, u32[]{:S(2)}) copy-start(f32[16,32,128]{2,1,0:T(8,128)} %kappa.11) | copy-start | bytes 786436
  0.6 20.1 %copy-start = (f32[5,16,32,128]{3,2,1,0:T(8,128)S(1)}, f32[5,16,32,128]{3,2,1,0:T(8,128)}, u32[]{:S(2)}) copy-start(f32[5,16,32,128]{3,2,1,0:T(8,128)} %gas.11) | copy-start | bytes 3932164
  0.7 15.9 %copy-start.7 = (f32[16]{0:T(128)S(1)}, f32[16]{0:T(128)}, u32[]{:S(2)}) copy-start(f32[16]{0:T(128)} %param.13) | copy-start | bytes 196
  0.7 16.0 %copy-start.4 = (s32[2048,1]{0,1:T(1,128)S(1)}, s32[2048,1]{0,1:T(1,128)}, u32[]{:S(2)}) copy-start(s32[2048,1]{0,1:T(1,128)} %param.15) | copy-start | bytes 24580
  2.9 30.3 %copy-start.3 = (f32[5,5]{1,0:T(8,128)S(1)}, f32[5,5]{1,0:T(8,128)}, u32[]{:S(2)}) copy-start(f32[5,5]{1,0:T(8,128)} %reaction.5) | copy-start | bytes 304
  2.9 17.8 %collective-permute-start = (f32[3,32,128]{2,1,0:T(8,128)S(1)}, f32[3,32,128]{2,1,0:T(8,128)S(1)}, u32[]{:S(2)}, u32[]{:S(2)}) collective-permute-start(f32[3,32,128]{2,1,0:T(8,128)S(1)} %get-tuple-element.19.send_q), channel_id=1, source_target_pairs={{1,2},{3,4},{5,6},{7,8},{9,10},{11,12},{13,14},{15,16},{17,18},{19... | collective-permute-start | bytes 147464 | tf_op jit(solution)/shard_map/ppermute | solution.py:451
  14.6 6.1 %collective-permute-start.1 = (f32[3,32,128]{2,1,0:T(8,128)S(1)}, f32[3,32,128]{2,1,0:T(8,128)S(1)}, u32[]{:S(2)}, u32[]{:S(2)}) collective-permute-start(f32[3,32,128]{2,1,0:T(8,128)S(1)} %get-tuple-element.20._.send_p), channel_id=1, source_target_pairs={{0,1},{2,3},{4,5},{6,7},{8,9},{10,11},{12,13},{14,15},{16,17},{18,... | collective-permute-start | bytes 147464 | tf_op jit(solution)/shard_map/ppermute | solution.py:451
  16.6 0.9 %copy-start.2 = (f32[16,2048]{1,0:T(8,128)S(1)}, f32[16,2048]{1,0:T(8,128)}, u32[]{:S(2)}) copy-start(f32[16,2048]{1,0:T(8,128)} %particles.1) | copy-start | bytes 393220
  17.5 0.7 %copy-start.5 = (s32[2048]{0:T(1024)S(1)}, s32[2048]{0:T(1024)}, u32[]{:S(2)}) copy-start(s32[2048]{0:T(1024)} %param.14) | copy-start | bytes 24580
  18.2 0.7 %copy-start.6 = (f32[16,16]{1,0:T(8,128)S(1)}, f32[16,16]{1,0:T(8,128)}, u32[]{:S(2)}) copy-start(f32[16,16]{1,0:T(8,128)} %mixing.1) | copy-start | bytes 3076
  21.6 16.2 %collective-permute-start.3 = (f32[18,32,128]{2,1,0:T(8,128)S(1)}, f32[18,32,128]{2,1,0:T(8,128)S(1)}, u32[]{:S(2)}, u32[]{:S(2)}) collective-permute-start(f32[18,32,128]{2,1,0:T(8,128)S(1)} %get-tuple-element.24), channel_id=1, source_target_pairs={{0,64},{128,192},{256,320},{384,448},{64,0},{192,128},{320,256},{4... | collective-permute-start | bytes 884744 | tf_op jit(solution)/shard_map/ppermute | solution.py:451
  24.6 13.1 %collective-permute-start.2 = (f32[21,8,128]{2,1,0:T(8,128)S(1)}, f32[21,8,128]{2,1,0:T(8,128)S(1)}, u32[]{:S(2)}, u32[]{:S(2)}) collective-permute-start(f32[21,8,128]{2,1,0:T(8,128)S(1)} %get-tuple-element.23), channel_id=1, source_target_pairs={{64,128},{192,256},{320,384},{128,64},{256,192},{384,320},{65,129}... | collective-permute-start | bytes 258056 | tf_op jit(solution)/shard_map/ppermute | solution.py:451
  38.8 8.4 %collective-permute-start.4 = (f32[16,128]{1,0:T(8,128)S(1)}, f32[16,128]{1,0:T(8,128)S(1)}, u32[]{:S(2)}, u32[]{:S(2)}) collective-permute-start(f32[16,128]{1,0:T(8,128)S(1)} %shard_map.100.wall), channel_id=1, source_target_pairs={{0,64},{64,128},{128,192},{192,256},{256,320},{320,384},{384,448},... | collective-permute-start | bytes 24584 | tf_op jit(solution)/shard_map/ppermute | solution.py:525
  43.9 19.0 %collective-permute-start.6 = (f32[17,24,128]{2,1,0:T(8,128)S(1)}, f32[17,24,128]{2,1,0:T(8,128)S(1)}, u32[]{:S(2)}, u32[]{:S(2)}) collective-permute-start(f32[17,24,128]{2,1,0:T(8,128)S(1)} %shard_map.99._), channel_id=1, source_target_pairs={{64,128},{192,256},{320,384},{128,64},{256,192},{384,320},{65,129}... | collective-permute-start | bytes 626696 | tf_op jit(solution)/shard_map/ppermute | solution.py:451
  47.5 15.5 %collective-permute-start.5 = (f32[16,1024]{1,0:T(8,128)S(1)}, f32[16,1024]{1,0:T(8,128)S(1)}, u32[]{:S(2)}, u32[]{:S(2)}) collective-permute-start(f32[16,1024]{1,0:T(8,128)S(1)} %get-tuple-element.29), channel_id=1, source_target_pairs={{1,2},{3,4},{5,6},{7,8},{9,10},{11,12},{13,14},{15,16},{17,18},{19... | collective-permute-start | bytes 196616 | tf_op jit(solution)/shard_map/ppermute | solution.py:451
  53.1 13.3 %collective-permute-start.7 = (f32[16,1024]{1,0:T(8,128)S(1)}, f32[16,1024]{1,0:T(8,128)S(1)}, u32[]{:S(2)}, u32[]{:S(2)}) collective-permute-start(f32[16,1024]{1,0:T(8,128)S(1)} %get-tuple-element.32), channel_id=1, source_target_pairs={{0,2},{1,3},{4,6},{5,7},{8,10},{9,11},{12,14},{13,15},{16,18},{17,... | collective-permute-start | bytes 196616 | tf_op jit(solution)/shard_map/ppermute | solution.py:451
  55.0 11.3 %collective-permute-start.8 = (f32[16,1024]{1,0:T(8,128)S(1)}, f32[16,1024]{1,0:T(8,128)S(1)}, u32[]{:S(2)}, u32[]{:S(2)}) collective-permute-start(f32[16,1024]{1,0:T(8,128)S(1)} %get-tuple-element.33), channel_id=1, source_target_pairs={{2,4},{3,5},{6,8},{7,9},{10,12},{11,13},{14,16},{15,17},{18,20},{1... | collective-permute-start | bytes 196616 | tf_op jit(solution)/shard_map/ppermute | solution.py:451
  58.1 8.3 %collective-permute-start.9 = (f32[16,1024]{1,0:T(8,128)S(1)}, f32[16,1024]{1,0:T(8,128)S(1)}, u32[]{:S(2)}, u32[]{:S(2)}) collective-permute-start(f32[16,1024]{1,0:T(8,128)S(1)} %get-tuple-element.34), channel_id=1, source_target_pairs={{0,1},{2,3},{4,5},{6,7},{8,9},{10,11},{12,13},{14,15},{16,17},{18,... | collective-permute-start | bytes 196616 | tf_op jit(solution)/shard_map/ppermute | solution.py:451

commit v11 on v10

--- a/solution.py
+++ b/solution.py
@@ -94,7 +94,7 @@
                 out[pair, rows(tile), :] = jnp.where(lane < 64, pick(first, index), pick(second, index))
 
 
-def strips_kernel(gas, kappa, send_q, send_p, recv_q, recv_p, _, strips, send_a, send_wall):
+def strips_kernel(gas, kappa, send_q, send_p, recv_q, recv_p, _, strips, send_a, send_wall, corner):
     lane = lanes()
     low_side = (lane & 1) == 1
     cell = jnp.clip((lane >> 1) - 3, 0, GX - 1)
@@ -124,7 +124,10 @@
         for_a = jnp.where(even, top, bottom)
         for_b = jnp.where(even, bottom, top)
         send_a[LAYERS - 1, rows(tile), :] = for_a
-        send_wall[LAYERS - 1 + tile] = for_b
+        if tile == TILES - 1:
+            send_wall[LAYERS - 1] = for_b
+        else:
+            corner[rows(tile), :] = for_b
     at_a, at_b = jnp.where(even, GX - 3, 0), jnp.where(even, 0, GX - 3)
     kappa_a, kappa_b = jnp.where(even, GX - 2, 0), jnp.where(even, 0, GX - 2)
     for c in range(COMP):
@@ -136,7 +139,8 @@
         send_wall[3 * COMP + layer] = kappa[kappa_b + layer, GR - 8 :, :]
 
 
-def rest_kernel(gas, kappa, _, send_rest):
+def rest_kernel(gas, kappa, corner, _, send_rest):
+    send_rest[LAYERS - 1] = corner[...]
     even = lax.rem(lax.axis_index("sect"), 2) == 0
     split = GR - 8
     from_b, from_kappa = jnp.where(even, 0, GX - 3), jnp.where(even, 0, GX - 2)
@@ -259,7 +263,7 @@
     for layer in range(2):
         kap[kappa_a + layer] = recv_a[3 * COMP + layer, top, :]
         kap[kappa_b + layer] = recv_wall[3 * COMP + layer]
-    corner_a, corner_b = recv_a[LAYERS - 1, top, :], recv_wall[LAYERS - 1 + TILES - 1]
+    corner_a, corner_b = recv_a[LAYERS - 1, top, :], recv_wall[LAYERS - 1]
     low, high = jnp.where(even, corner_b, corner_a), jnp.where(even, corner_a, corner_b)
     strip_levels(strips, [low], [high], mix, edge, [TILES - 1])
     wall[3 : GX - 3, :] = middle[0, :, GR - 1, :]
@@ -325,7 +329,7 @@
     low, high = [], []
     for t in range(TILES):
         corner_a = recv_a[LAYERS - 1, rows(t), :]
-        corner_b = recv_wall[LAYERS - 1 + t]
+        corner_b = recv_wall[LAYERS - 1] if t == TILES - 1 else recv_rest[LAYERS - 1, rows(t), :]
         low.append(jnp.where(even, corner_b, corner_a))
         high.append(jnp.where(even, corner_a, corner_b))
     strip_levels(strips, low, high, mix, edge, list(range(TILES)))
@@ -485,9 +489,9 @@
         moved=4 << 20,
     )(tile_hop.reshape(CHUNKS, 128), wall_cell.reshape(CHUNKS, 128), particles, mixing, heating_column, send_p)
 
-    strips, send_a, send_wall = call(
+    strips, send_a, send_wall, corner = call(
         strips_kernel,
-        (f32(len(STRIPS), GR, GA), f32(LAYERS, GR, GA), f32(LAYERS - 1 + TILES, 8, GA)),
+        (f32(len(STRIPS), GR, GA), f32(LAYERS, GR, GA), f32(LAYERS, 8, GA), f32(GR - 8, GA)),
         specs=[VMEM] * 6 + [ANY],
         moved=2 << 20,
     )(gas, kappa, send_q, send_p, recv_q, recv_p, cells)
@@ -507,7 +511,9 @@
         moved=12 << 20,
     )(gas, kappa, strips, reaction)
 
-    send_rest = call(rest_kernel, f32(LAYERS - 1, GR - 8, GA), specs=[VMEM] * 2 + [ANY], moved=1 << 18)(gas, kappa, middle)
+    send_rest = call(rest_kernel, f32(LAYERS, GR - 8, GA), specs=[VMEM] * 3 + [ANY], moved=1 << 18)(
+        gas, kappa, corner, middle
+    )
     recv_rest = swap(send_rest, "sect", pairs_b)
 
     wall = call(

time: 67.6 us -> 67.7 us (level)
  no operation moved by 1% of the time
where the time goes in v11:
time: 67.7 us; the launch traced here: 67.1 us
  starting transfers between devices  49.1 us (73%)
  Pallas kernels  14.7 us (22%)
  local copies, waits for them, and re-layouts  2.4 us (4%)
  between operations  0.9 us (1%)
    ppermute x9, starting transfers between devices, swap(): return lax.ppermute(x, axis, pairs + [(j, i) for i, j in pairs])  44.1 us
    ppermute x1, starting transfers between devices, local(): lax.ppermute(wall, 'sect', [(i, i + 1) for i in range(sections - 1)])  4.97 us
    pallas_call x1, Pallas kernels, local(): call(inner_kernel, (f32(COMP, len(SEAM), GR, GA), f32(COMP, len(SEAM), GR...  4.55 us
    pallas_call x1, Pallas kernels, local(): call(outer_kernel, (whole, f32(8, 128)), scratch=[pltpu.VMEM((COMP, EXT,...  3.41 us
    unnamed x16, local copies, waits for them, and re-layouts  2.32 us
    pallas_call x1, Pallas kernels, local(): call(edges_kernel, (f32(3, GR, GA), f32(3, GR, GA)), scratch=[pltpu.VMEM(...  2.18 us
    pallas_call x1, Pallas kernels, local(): call(pack_kernel, (f32(MOVES, VALS, CAP), i32(MOVES, SPOTS, 128)), scratc...  1.73 us
  transfers between devices with their start and end apart: 10, of which 0 were waited for; matrix products, arithmetic and copies ran while one was open for 0% of the time, Pallas kernels for 15%

profile of v11, /device:TPU:1, one launch (start us, length us, event | category | flops | bytes accessed | tf_op | source)
XLA Modules:
  0.0 67.1 jit_solution(15010162129001495653)
XLA Ops:
  0.6 0.0 copy-start.1
  0.6 0.0 copy-start
  0.7 0.0 copy-start.7
  0.7 0.0 copy-start.4
  0.7 2.2 %shard_map.95 = (f32[3,32,128]{2,1,0:T(8,128)S(1)}, f32[3,32,128]{2,1,0:T(8,128)S(1)}) custom-call(f32[5,16,32,128]{3,2,1,0:T(8,128)} %gas.11, f32[16,32,128]{2,1,0:T(8,128)} %kappa.11), custom_call_target="tpu_custom_call" | custom-call | bytes 2097152 | tf_op jit(solution)/shard_map/pallas_call | solution.py:467
  2.9 0.0 copy-start.3
  2.9 11.7 %collective-permute-start = (f32[3,32,128]{2,1,0:T(8,128)S(1)}, f32[3,32,128]{2,1,0:T(8,128)S(1)}, u32[]{:S(2)}, u32[]{:S(2)}) collective-permute-start(f32[3,32,128]{2,1,0:T(8,128)S(1)} %get-tuple-element.20.send_q), channel_id=1, source_target_pairs={{1,2},{3,4},{5,6},{7,8},{9,10},{11,12},{13,14},{15,16},{17,18},{19... | collective-permute-start | bytes 147464 | tf_op jit(solution)/shard_map/ppermute | solution.py:455
  14.6 1.9 %collective-permute-start.1 = (f32[3,32,128]{2,1,0:T(8,128)S(1)}, f32[3,32,128]{2,1,0:T(8,128)S(1)}, u32[]{:S(2)}, u32[]{:S(2)}) collective-permute-start(f32[3,32,128]{2,1,0:T(8,128)S(1)} %get-tuple-element.21._.send_p), channel_id=1, source_target_pairs={{0,1},{2,3},{4,5},{6,7},{8,9},{10,11},{12,13},{14,15},{16,17},{18,... | collective-permute-start | bytes 147464 | tf_op jit(solution)/shard_map/ppermute | solution.py:455
  16.5 0.0 copy-done.7
  16.5 0.1 copy.10.heating
  16.6 0.0 copy-done.4
  16.6 0.0 copy-start.2
  16.6 0.9 %copy-done.2 = f32[16,2048]{1,0:T(8,128)S(1)} copy-done((f32[16,2048]{1,0:T(8,128)S(1)}, f32[16,2048]{1,0:T(8,128)}, u32[]{:S(2)}) %copy-start.2) | copy-done | bytes 131096
  17.5 0.0 copy-start.5
  17.5 0.7 %copy-done.5 = s32[2048]{0:T(1024)S(1)} copy-done((s32[2048]{0:T(1024)S(1)}, s32[2048]{0:T(1024)}, u32[]{:S(2)}) %copy-start.5) | copy-done | bytes 8216
  18.2 0.0 copy-start.6
  18.2 0.7 %copy-done.6 = f32[16,16]{1,0:T(8,128)S(1)} copy-done((f32[16,16]{1,0:T(8,128)S(1)}, f32[16,16]{1,0:T(8,128)}, u32[]{:S(2)}) %copy-start.6) | copy-done | bytes 1048
  18.9 1.7 %shard_map.96 = (f32[5,16,1024]{2,1,0:T(8,128)S(1)}, s32[5,8,128]{2,1,0:T(8,128)S(1)}) custom-call(s32[16,128]{1,0:T(8,128)S(1)} %bitcast.3, s32[16,128]{1,0:T(8,128)S(1)} %bitcast.4, f32[16,2048]{1,0:T(8,128)S(1)} %copy-done.2, f32[16,16]{1,0:T(8,128)S(1)} %copy-done.6, f32[16,1]{1,0:T(8,128)S(1)} %copy.10.heating, f32[3,32,128]{2,1,0:T(8,128)S(1)} %get-tuple-element.21._.send_p), custom_call_target="tpu_custom_call" | custom-call | bytes 4194304 | tf_op jit(solution)/shard_map/pallas_call | solution.py:478
  20.7 0.0 collective-permute-done.recv_q
  20.7 0.0 collective-permute-done.1.recv_p
  20.7 0.0 copy-done.1
  20.7 0.0 copy-done
  20.7 0.8 %shard_map.97 = (f32[28,32,128]{2,1,0:T(8,128)S(1)}, f32[18,32,128]{2,1,0:T(8,128)S(1)}, f32[18,8,128]{2,1,0:T(8,128)S(1)}, f32[24,128]{1,0:T(8,128)S(1)}) custom-call(f32[5,16,32,128]{3,2,1,0:T(8,128)S(1)} %copy-done, f32[16,32,128]{2,1,0:T(8,128)S(1)} %copy-done.1, f32[3,32,128]{2,1,0:T(8,128)S(1)} %get-tuple-element.20.send_q, ...), custom_call_target="tpu_custom_call" | custom-call | bytes 2097152 | tf_op jit(solution)/shard_map/pallas_call | solution.py:492
  21.6 3.1 %collective-permute-start.3 = (f32[18,32,128]{2,1,0:T(8,128)S(1)}, f32[18,32,128]{2,1,0:T(8,128)S(1)}, u32[]{:S(2)}, u32[]{:S(2)}) collective-permute-start(f32[18,32,128]{2,1,0:T(8,128)S(1)} %get-tuple-element.25), channel_id=1, source_target_pairs={{0,64},{128,192},{256,320},{384,448},{64,0},{192,128},{320,256},{4... | collective-permute-start | bytes 884744 | tf_op jit(solution)/shard_map/ppermute | solution.py:455
  24.6 8.5 %collective-permute-start.2 = (f32[18,8,128]{2,1,0:T(8,128)S(1)}, f32[18,8,128]{2,1,0:T(8,128)S(1)}, u32[]{:S(2)}, u32[]{:S(2)}) collective-permute-start(f32[18,8,128]{2,1,0:T(8,128)S(1)} %get-tuple-element.24), channel_id=1, source_target_pairs={{64,128},{192,256},{320,384},{128,64},{256,192},{384,320},{65,129}... | collective-permute-start | bytes 221192 | tf_op jit(solution)/shard_map/ppermute | solution.py:455
  33.2 0.0 copy-done.3
  33.2 4.5 %shard_map.98 = (f32[5,4,32,128]{3,2,1,0:T(8,128)S(1)}, f32[5,4,32,128]{3,2,1,0:T(8,128)S(1)}, f32[5,10,32,128]{3,2,1,0:T(8,128)S(1)}) custom-call(f32[5,16,32,128]{3,2,1,0:T(8,128)S(1)} %copy-done, f32[16,32,128]{2,1,0:T(8,128)S(1)} %copy-done.1, f32[28,32,128]{2,1,0:T(8,128)S(1)} %get-tuple-element.23.strips, f32[5,5]{1,0:T(8,128)S(1)} %copy-done.3), custom_call_target="tpu_custom_call" | custom-call | bytes 12582912 | tf_op jit(solution)/shard_map/pallas_call | solution.py:502
  37.8 0.0 collective-permute-done.2.recv_wall
  37.8 0.0 collective-permute-done.3.recv_a
  37.8 1.0 %shard_map.100.wall = f32[16,128]{1,0:T(8,128)S(1)} custom-call(f32[5,16,32,128]{3,2,1,0:T(8,128)S(1)} %copy-done, f32[16,32,128]{2,1,0:T(8,128)S(1)} %copy-done.1, f32[28,32,128]{2,1,0:T(8,128)S(1)} %get-tuple-element.23.strips, f32[18,8,128]{2,1,0:T(8,128)S(1)} %collective-permute-done.2.recv_wall, f32[18,32,128]{2,1,0:T(8,128)S(1)} %collective-permute-done.3.recv_a, ...), custom_call_target="tpu_custom_call" | custom-call | bytes 4194304 | tf_op jit(solution)/shard_map/pallas_call | solution.py:519
  38.8 5.0 %collective-permute-start.4 = (f32[16,128]{1,0:T(8,128)S(1)}, f32[16,128]{1,0:T(8,128)S(1)}, u32[]{:S(2)}, u32[]{:S(2)}) collective-permute-start(f32[16,128]{1,0:T(8,128)S(1)} %shard_map.100.wall), channel_id=1, source_target_pairs={{0,64},{64,128},{128,192},{192,256},{256,320},{320,384},{384,448},... | collective-permute-start | bytes 24584 | tf_op jit(solution)/shard_map/ppermute | solution.py:531
  43.8 3.5 %collective-permute-start.6 = (f32[18,24,128]{2,1,0:T(8,128)S(1)}, f32[18,24,128]{2,1,0:T(8,128)S(1)}, u32[]{:S(2)}, u32[]{:S(2)}) collective-permute-start(f32[18,24,128]{2,1,0:T(8,128)S(1)} %shard_map.99._), channel_id=1, source_target_pairs={{64,128},{192,256},{320,384},{128,64},{256,192},{384,320},{65,129}... | collective-permute-start | bytes 663560 | tf_op jit(solution)/shard_map/ppermute | solution.py:455
  47.2 0.0 collective-permute-done.4.earlier
  47.3 0.2 shard_map.101
  47.5 5.6 %collective-permute-start.5 = (f32[16,1024]{1,0:T(8,128)S(1)}, f32[16,1024]{1,0:T(8,128)S(1)}, u32[]{:S(2)}, u32[]{:S(2)}) collective-permute-start(f32[16,1024]{1,0:T(8,128)S(1)} %get-tuple-element.31), channel_id=1, source_target_pairs={{1,2},{3,4},{5,6},{7,8},{9,10},{11,12},{13,14},{15,16},{17,18},{19... | collective-permute-start | bytes 196616 | tf_op jit(solution)/shard_map/ppermute | solution.py:455
  53.1 1.9 %collective-permute-start.7 = (f32[16,1024]{1,0:T(8,128)S(1)}, f32[16,1024]{1,0:T(8,128)S(1)}, u32[]{:S(2)}, u32[]{:S(2)}) collective-permute-start(f32[16,1024]{1,0:T(8,128)S(1)} %get-tuple-element.34), channel_id=1, source_target_pairs={{0,2},{1,3},{4,6},{5,7},{8,10},{9,11},{12,14},{13,15},{16,18},{17,... | collective-permute-start | bytes 196616 | tf_op jit(solution)/shard_map/ppermute | solution.py:455
  55.0 3.1 %collective-permute-start.8 = (f32[16,1024]{1,0:T(8,128)S(1)}, f32[16,1024]{1,0:T(8,128)S(1)}, u32[]{:S(2)}, u32[]{:S(2)}) collective-permute-start(f32[16,1024]{1,0:T(8,128)S(1)} %get-tuple-element.35), channel_id=1, source_target_pairs={{2,4},{3,5},{6,8},{7,9},{10,12},{11,13},{14,16},{15,17},{18,20},{1... | collective-permute-start | bytes 196616 | tf_op jit(solution)/shard_map/ppermute | solution.py:455
  58.1 4.8 %collective-permute-start.9 = (f32[16,1024]{1,0:T(8,128)S(1)}, f32[16,1024]{1,0:T(8,128)S(1)}, u32[]{:S(2)}, u32[]{:S(2)}) collective-permute-start(f32[16,1024]{1,0:T(8,128)S(1)} %get-tuple-element.36), channel_id=1, source_target_pairs={{0,1},{2,3},{4,5},{6,7},{8,9},{10,11},{12,13},{14,15},{16,17},{18,... | collective-permute-start | bytes 196616 | tf_op jit(solution)/shard_map/ppermute | solution.py:455
  62.9 0.0 collective-permute-done.6.recv_rest
  62.9 0.0 collective-permute-done.5._.recv_q
  62.9 3.4 %shard_map.102 = (f32[5,16,32,128]{3,2,1,0:T(8,128)}, f32[8,128]{1,0:T(8,128)S(1)}) custom-call(f32[16,1024]{1,0:T(8,128)S(1)} %collective-permute-done.5._.recv_q, f32[5,16,32,128]{3,2,1,0:T(8,128)S(1)} %copy-done, f32[16,32,128]{2,1,0:T(8,128)S(1)} %copy-done.1, f32[28,32,128]{2,1,0:T(8,128)S(1)} %get-tuple-element.23.strips, ...), custom_call_target="tpu_custom_call" | custom-call | bytes 8388608 | tf_op jit(solution)/shard_map/pallas_call | solution.py:543
  66.3 0.0 collective-permute-done.7.recv_r
  66.3 0.0 collective-permute-done.8.recv_s
  66.3 0.0 collective-permute-done.9.recv_p
  66.3 0.8 %shard_map.103 = f32[16,5120]{1,0:T(8,128)} custom-call(f32[16,1024]{1,0:T(8,128)S(1)} %get-tuple-element.33.own, f32[16,1024]{1,0:T(8,128)S(1)} %collective-permute-done.5._.recv_q, f32[16,1024]{1,0:T(8,128)S(1)} %collective-permute-done.7.recv_r, f32[16,1024]{1,0:T(8,128)S(1)} %collective-permute-done.8.recv_s, ...), custom_call_target="tpu_custom_call" | custom-call | bytes 1048576 | tf_op jit(solution)/shard_map/pallas_call | solution.py:555
  (1 shorter events, 0.0 us)
Async XLA Ops:
  0.6 20.1 %copy-start.1 = (f32[16,32,128]{2,1,0:T(8,128)S(1)}, f32[16,32,128]{2,1,0:T(8,128)}, u32[]{:S(2)}) copy-start(f32[16,32,128]{2,1,0:T(8,128)} %kappa.11) | copy-start | bytes 786436
  0.6 20.1 %copy-start = (f32[5,16,32,128]{3,2,1,0:T(8,128)S(1)}, f32[5,16,32,128]{3,2,1,0:T(8,128)}, u32[]{:S(2)}) copy-start(f32[5,16,32,128]{3,2,1,0:T(8,128)} %gas.11) | copy-start | bytes 3932164
  0.7 15.9 %copy-start.7 = (f32[16]{0:T(128)S(1)}, f32[16]{0:T(128)}, u32[]{:S(2)}) copy-start(f32[16]{0:T(128)} %param.13) | copy-start | bytes 196
  0.7 16.0 %copy-start.4 = (s32[2048,1]{0,1:T(1,128)S(1)}, s32[2048,1]{0,1:T(1,128)}, u32[]{:S(2)}) copy-start(s32[2048,1]{0,1:T(1,128)} %param.15) | copy-start | bytes 24580
  2.9 30.3 %copy-start.3 = (f32[5,5]{1,0:T(8,128)S(1)}, f32[5,5]{1,0:T(8,128)}, u32[]{:S(2)}) copy-start(f32[5,5]{1,0:T(8,128)} %reaction.5) | copy-start | bytes 304
  2.9 17.8 %collective-permute-start = (f32[3,32,128]{2,1,0:T(8,128)S(1)}, f32[3,32,128]{2,1,0:T(8,128)S(1)}, u32[]{:S(2)}, u32[]{:S(2)}) collective-permute-start(f32[3,32,128]{2,1,0:T(8,128)S(1)} %get-tuple-element.20.send_q), channel_id=1, source_target_pairs={{1,2},{3,4},{5,6},{7,8},{9,10},{11,12},{13,14},{15,16},{17,18},{19... | collective-permute-start | bytes 147464 | tf_op jit(solution)/shard_map/ppermute | solution.py:455
  14.6 6.1 %collective-permute-start.1 = (f32[3,32,128]{2,1,0:T(8,128)S(1)}, f32[3,32,128]{2,1,0:T(8,128)S(1)}, u32[]{:S(2)}, u32[]{:S(2)}) collective-permute-start(f32[3,32,128]{2,1,0:T(8,128)S(1)} %get-tuple-element.21._.send_p), channel_id=1, source_target_pairs={{0,1},{2,3},{4,5},{6,7},{8,9},{10,11},{12,13},{14,15},{16,17},{18,... | collective-permute-start | bytes 147464 | tf_op jit(solution)/shard_map/ppermute | solution.py:455
  16.6 0.9 %copy-start.2 = (f32[16,2048]{1,0:T(8,128)S(1)}, f32[16,2048]{1,0:T(8,128)}, u32[]{:S(2)}) copy-start(f32[16,2048]{1,0:T(8,128)} %particles.1) | copy-start | bytes 393220
  17.5 0.7 %copy-start.5 = (s32[2048]{0:T(1024)S(1)}, s32[2048]{0:T(1024)}, u32[]{:S(2)}) copy-start(s32[2048]{0:T(1024)} %param.14) | copy-start | bytes 24580
  18.2 0.7 %copy-start.6 = (f32[16,16]{1,0:T(8,128)S(1)}, f32[16,16]{1,0:T(8,128)}, u32[]{:S(2)}) copy-start(f32[16,16]{1,0:T(8,128)} %mixing.1) | copy-start | bytes 3076
  21.6 16.2 %collective-permute-start.3 = (f32[18,32,128]{2,1,0:T(8,128)S(1)}, f32[18,32,128]{2,1,0:T(8,128)S(1)}, u32[]{:S(2)}, u32[]{:S(2)}) collective-permute-start(f32[18,32,128]{2,1,0:T(8,128)S(1)} %get-tuple-element.25), channel_id=1, source_target_pairs={{0,64},{128,192},{256,320},{384,448},{64,0},{192,128},{320,256},{4... | collective-permute-start | bytes 884744 | tf_op jit(solution)/shard_map/ppermute | solution.py:455
  24.6 13.1 %collective-permute-start.2 = (f32[18,8,128]{2,1,0:T(8,128)S(1)}, f32[18,8,128]{2,1,0:T(8,128)S(1)}, u32[]{:S(2)}, u32[]{:S(2)}) collective-permute-start(f32[18,8,128]{2,1,0:T(8,128)S(1)} %get-tuple-element.24), channel_id=1, source_target_pairs={{64,128},{192,256},{320,384},{128,64},{256,192},{384,320},{65,129}... | collective-permute-start | bytes 221192 | tf_op jit(solution)/shard_map/ppermute | solution.py:455
  38.8 8.4 %collective-permute-start.4 = (f32[16,128]{1,0:T(8,128)S(1)}, f32[16,128]{1,0:T(8,128)S(1)}, u32[]{:S(2)}, u32[]{:S(2)}) collective-permute-start(f32[16,128]{1,0:T(8,128)S(1)} %shard_map.100.wall), channel_id=1, source_target_pairs={{0,64},{64,128},{128,192},{192,256},{256,320},{320,384},{384,448},... | collective-permute-start | bytes 24584 | tf_op jit(solution)/shard_map/ppermute | solution.py:531
  43.8 19.1 %collective-permute-start.6 = (f32[18,24,128]{2,1,0:T(8,128)S(1)}, f32[18,24,128]{2,1,0:T(8,128)S(1)}, u32[]{:S(2)}, u32[]{:S(2)}) collective-permute-start(f32[18,24,128]{2,1,0:T(8,128)S(1)} %shard_map.99._), channel_id=1, source_target_pairs={{64,128},{192,256},{320,384},{128,64},{256,192},{384,320},{65,129}... | collective-permute-start | bytes 663560 | tf_op jit(solution)/shard_map/ppermute | solution.py:455
  47.5 15.5 %collective-permute-start.5 = (f32[16,1024]{1,0:T(8,128)S(1)}, f32[16,1024]{1,0:T(8,128)S(1)}, u32[]{:S(2)}, u32[]{:S(2)}) collective-permute-start(f32[16,1024]{1,0:T(8,128)S(1)} %get-tuple-element.31), channel_id=1, source_target_pairs={{1,2},{3,4},{5,6},{7,8},{9,10},{11,12},{13,14},{15,16},{17,18},{19... | collective-permute-start | bytes 196616 | tf_op jit(solution)/shard_map/ppermute | solution.py:455
  53.1 13.3 %collective-permute-start.7 = (f32[16,1024]{1,0:T(8,128)S(1)}, f32[16,1024]{1,0:T(8,128)S(1)}, u32[]{:S(2)}, u32[]{:S(2)}) collective-permute-start(f32[16,1024]{1,0:T(8,128)S(1)} %get-tuple-element.34), channel_id=1, source_target_pairs={{0,2},{1,3},{4,6},{5,7},{8,10},{9,11},{12,14},{13,15},{16,18},{17,... | collective-permute-start | bytes 196616 | tf_op jit(solution)/shard_map/ppermute | solution.py:455
  55.0 11.3 %collective-permute-start.8 = (f32[16,1024]{1,0:T(8,128)S(1)}, f32[16,1024]{1,0:T(8,128)S(1)}, u32[]{:S(2)}, u32[]{:S(2)}) collective-permute-start(f32[16,1024]{1,0:T(8,128)S(1)} %get-tuple-element.35), channel_id=1, source_target_pairs={{2,4},{3,5},{6,8},{7,9},{10,12},{11,13},{14,16},{15,17},{18,20},{1... | collective-permute-start | bytes 196616 | tf_op jit(solution)/shard_map/ppermute | solution.py:455
  58.1 8.3 %collective-permute-start.9 = (f32[16,1024]{1,0:T(8,128)S(1)}, f32[16,1024]{1,0:T(8,128)S(1)}, u32[]{:S(2)}, u32[]{:S(2)}) collective-permute-start(f32[16,1024]{1,0:T(8,128)S(1)} %get-tuple-element.36), channel_id=1, source_target_pairs={{0,1},{2,3},{4,5},{6,7},{8,9},{10,11},{12,13},{14,15},{16,17},{18,... | collective-permute-start | bytes 196616 | tf_op jit(solution)/shard_map/ppermute | solution.py:455

commit v12 on v11

--- a/solution.py
+++ b/solution.py
@@ -92,6 +92,19 @@
             first, second = packed[2 * pair, tile], packed[2 * pair + 1, tile]
             for out, index in ((send_q, index_q), (send_p, index_p)):
                 out[pair, rows(tile), :] = jnp.where(lane < 64, pick(first, index), pick(second, index))
+
+
+def section_slabs(gas, kappa, corner, at, kappa_at):
+    top = slice(GR - 8, GR)
+    slabs = [gas[c, at + layer, top, :] for c in range(COMP) for layer in range(3)]
+    return slabs + [kappa[kappa_at + layer, top, :] for layer in range(2)] + [corner]
+
+
+def halves(slabs, upper):
+    high = lax.broadcasted_iota(jnp.int32, (8, 128), 0) >= 4
+    return [
+        jnp.where(high == upper, a, pltpu.roll(b, 4, 0)) for a, b in zip(slabs[::2], slabs[1::2])
+    ]
 
 
 def strips_kernel(gas, kappa, send_q, send_p, recv_q, recv_p, _, strips, send_a, send_wall, corner):
@@ -124,31 +137,33 @@
         for_a = jnp.where(even, top, bottom)
         for_b = jnp.where(even, bottom, top)
         send_a[LAYERS - 1, rows(tile), :] = for_a
-        if tile == TILES - 1:
-            send_wall[LAYERS - 1] = for_b
-        else:
-            corner[rows(tile), :] = for_b
+        corner[rows(tile), :] = for_b
     at_a, at_b = jnp.where(even, GX - 3, 0), jnp.where(even, 0, GX - 3)
     kappa_a, kappa_b = jnp.where(even, GX - 2, 0), jnp.where(even, 0, GX - 2)
     for c in range(COMP):
         for layer in range(3):
             send_a[3 * c + layer] = gas[c, at_a + layer]
-            send_wall[3 * c + layer] = gas[c, at_b + layer, GR - 8 :, :]
     for layer in range(2):
         send_a[3 * COMP + layer] = kappa[kappa_a + layer]
-        send_wall[3 * COMP + layer] = kappa[kappa_b + layer, GR - 8 :, :]
+
+
+    for n, tile in enumerate(halves(section_slabs(gas, kappa, for_b, at_b, kappa_b), True)):
+        send_wall[n] = tile
 
 
 def rest_kernel(gas, kappa, corner, _, send_rest):
-    send_rest[LAYERS - 1] = corner[...]
     even = lax.rem(lax.axis_index("sect"), 2) == 0
-    split = GR - 8
     from_b, from_kappa = jnp.where(even, 0, GX - 3), jnp.where(even, 0, GX - 2)
-    for c in range(COMP):
-        for layer in range(3):
-            send_rest[3 * c + layer] = gas[c, from_b + layer, :split, :]
-    for layer in range(2):
-        send_rest[3 * COMP + layer] = kappa[from_kappa + layer, :split, :]
+    for t in range(TILES - 1):
+        for c in range(COMP):
+            for layer in range(3):
+                send_rest[3 * (3 * c + layer) + t] = gas[c, from_b + layer, rows(t), :]
+        for layer in range(2):
+            send_rest[3 * (3 * COMP + layer) + t] = kappa[from_kappa + layer, rows(t), :]
+        send_rest[3 * (LAYERS - 1) + t] = corner[rows(t), :]
+    slabs = section_slabs(gas, kappa, corner[rows(TILES - 1), :], from_b, from_kappa)
+    for n, tile in enumerate(halves(slabs, False)):
+        send_rest[3 * LAYERS + n] = tile
 
 
 def coupling(reaction):
@@ -248,6 +263,10 @@
     even = lax.rem(lax.axis_index("sect"), 2) == 0
     mix = coupling(reaction)
     top = slice(GR - 8, GR)
+
+    def upper(i):
+        return recv_wall[i // 2] if i % 2 == 0 else pltpu.roll(recv_wall[i // 2], 4, 0)
+
     at_a, at_b = jnp.where(even, GX + 3, 0), jnp.where(even, 0, GX + 3)
     kappa_a, kappa_b = jnp.where(even, GX + 3, 1), jnp.where(even, 1, GX + 3)
     for c in range(COMP):
@@ -255,15 +274,15 @@
             now[c, x + 3] = gas[c, x, top, :]
         for layer in range(3):
             now[c, at_a + layer] = recv_a[3 * c + layer, top, :]
-            now[c, at_b + layer] = recv_wall[3 * c + layer]
+            now[c, at_b + layer] = upper(3 * c + layer)
         for i, x in enumerate(SEAM):
             later[c, x + 3] = first[c, i, top, :]
     for x in (0, 1, 2, GX - 3, GX - 2, GX - 1):
         kap[x + 3] = kappa[x, top, :]
     for layer in range(2):
         kap[kappa_a + layer] = recv_a[3 * COMP + layer, top, :]
-        kap[kappa_b + layer] = recv_wall[3 * COMP + layer]
-    corner_a, corner_b = recv_a[LAYERS - 1, top, :], recv_wall[LAYERS - 1]
+        kap[kappa_b + layer] = upper(3 * COMP + layer)
+    corner_a, corner_b = recv_a[LAYERS - 1, top, :], upper(LAYERS - 1)
     low, high = jnp.where(even, corner_b, corner_a), jnp.where(even, corner_a, corner_b)
     strip_levels(strips, [low], [high], mix, edge, [TILES - 1])
     wall[3 : GX - 3, :] = middle[0, :, GR - 1, :]
@@ -308,7 +327,14 @@
     token[...] = jnp.zeros((8, 128), jnp.float32)
     even = lax.rem(lax.axis_index("sect"), 2) == 0
     mix = coupling(reaction)
-    split = GR - 8
+    late = lax.broadcasted_iota(jnp.int32, (8, 128), 0) >= 4
+
+    def part(i, t):
+        if t < TILES - 1:
+            return recv_rest[3 * i + t]
+        wall, other = recv_wall[i // 2], recv_rest[3 * LAYERS + i // 2]
+        return jnp.where(late, wall, other) if i % 2 == 0 else pltpu.roll(jnp.where(late, other, wall), 4, 0)
+
     at_a, at_b = jnp.where(even, GX + 3, 0), jnp.where(even, 0, GX + 3)
     kappa_a, kappa_b = jnp.where(even, GX + 3, 1), jnp.where(even, 1, GX + 3)
     for c in range(COMP):
@@ -316,20 +342,20 @@
             now[c, x + 3] = gas[c, x]
         for layer in range(3):
             now[c, at_a + layer] = recv_a[3 * c + layer]
-            now[c, at_b + layer, split:, :] = recv_wall[3 * c + layer]
-            now[c, at_b + layer, :split, :] = recv_rest[3 * c + layer]
+            for t in range(TILES):
+                now[c, at_b + layer, rows(t), :] = part(3 * c + layer, t)
         for i, x in enumerate(SEAM):
             later[c, x + 3] = first[c, i]
     for x in (0, 1, 2, GX - 3, GX - 2, GX - 1):
         kap[x + 3] = kappa[x]
     for layer in range(2):
         kap[kappa_a + layer] = recv_a[3 * COMP + layer]
-        kap[kappa_b + layer, split:, :] = recv_wall[3 * COMP + layer]
-        kap[kappa_b + layer, :split, :] = recv_rest[3 * COMP + layer]
+        for t in range(TILES):
+            kap[kappa_b + layer, rows(t), :] = part(3 * COMP + layer, t)
     low, high = [], []
     for t in range(TILES):
         corner_a = recv_a[LAYERS - 1, rows(t), :]
-        corner_b = recv_wall[LAYERS - 1] if t == TILES - 1 else recv_rest[LAYERS - 1, rows(t), :]
+        corner_b = part(LAYERS - 1, t)
         low.append(jnp.where(even, corner_b, corner_a))
         high.append(jnp.where(even, corner_a, corner_b))
     strip_levels(strips, low, high, mix, edge, list(range(TILES)))
@@ -491,7 +517,7 @@
 
     strips, send_a, send_wall, corner = call(
         strips_kernel,
-        (f32(len(STRIPS), GR, GA), f32(LAYERS, GR, GA), f32(LAYERS, 8, GA), f32(GR - 8, GA)),
+        (f32(len(STRIPS), GR, GA), f32(LAYERS, GR, GA), f32(LAYERS // 2, 8, GA), f32(GR, GA)),
         specs=[VMEM] * 6 + [ANY],
         moved=2 << 20,
     )(gas, kappa, send_q, send_p, recv_q, recv_p, cells)
@@ -511,7 +537,7 @@
         moved=12 << 20,
     )(gas, kappa, strips, reaction)
 
-    send_rest = call(rest_kernel, f32(LAYERS, GR - 8, GA), specs=[VMEM] * 3 + [ANY], moved=1 << 18)(
+    send_rest = call(rest_kernel, f32(3 * LAYERS + LAYERS // 2, 8, GA), specs=[VMEM] * 3 + [ANY], moved=1 << 18)(
         gas, kappa, corner, middle
     )
     recv_rest = swap(send_rest, "sect", pairs_b)

time: 67.7 us -> 68.2 us (level)
  transfers between devices with their start and end apart: 10 -> 10, of which waited for: 0 -> 1; matrix products, arithmetic and copies ran while one was open for 0% -> 0% of each run, Pallas kernels for 15% -> 15%
where the time goes in v12:
time: 68.2 us; the launch traced here: 67.8 us
  starting transfers between devices  49.1 us (72%)
  Pallas kernels  14.7 us (22%)
  local copies, waits for them, and re-layouts  2.4 us (4%)
  between operations  0.89 us (1%)
    ppermute x9, starting transfers between devices, swap(): return lax.ppermute(x, axis, pairs + [(j, i) for i, j in pairs])  44.5 us
    pallas_call x1, Pallas kernels, local(): call(inner_kernel, (f32(COMP, len(SEAM), GR, GA), f32(COMP, len(SEAM), GR...  4.55 us
    ppermute x1, starting transfers between devices, local(): lax.ppermute(wall, 'sect', [(i, i + 1) for i in range(sections - 1)])  4.54 us
    pallas_call x1, Pallas kernels, local(): call(outer_kernel, (whole, f32(8, 128)), scratch=[pltpu.VMEM((COMP, EXT,...  3.42 us
    unnamed x16, local copies, waits for them, and re-layouts  2.32 us
    pallas_call x1, Pallas kernels, local(): call(edges_kernel, (f32(3, GR, GA), f32(3, GR, GA)), scratch=[pltpu.VMEM(...  2.18 us
    pallas_call x1, Pallas kernels, local(): call(pack_kernel, (f32(MOVES, VALS, CAP), i32(MOVES, SPOTS, 128)), scratc...  1.73 us
  transfers between devices with their start and end apart: 10, of which 1 were waited for; matrix products, arithmetic and copies ran while one was open for 0% of the time, Pallas kernels for 15%

profile of v12, /device:TPU:1, one launch (start us, length us, event | category | flops | bytes accessed | tf_op | source)
XLA Modules:
  0.0 67.8 jit_solution(13527473261174819473)
XLA Ops:
  0.6 0.0 copy-start.1
  0.6 0.0 copy-start
  0.7 0.0 copy-start.7
  0.7 0.0 copy-start.4
  0.7 2.2 %shard_map.95 = (f32[3,32,128]{2,1,0:T(8,128)S(1)}, f32[3,32,128]{2,1,0:T(8,128)S(1)}) custom-call(f32[5,16,32,128]{3,2,1,0:T(8,128)} %gas.11, f32[16,32,128]{2,1,0:T(8,128)} %kappa.11), custom_call_target="tpu_custom_call" | custom-call | bytes 2097152 | tf_op jit(solution)/shard_map/pallas_call | solution.py:493
  2.9 0.0 copy-start.3
  2.9 11.7 %collective-permute-start = (f32[3,32,128]{2,1,0:T(8,128)S(1)}, f32[3,32,128]{2,1,0:T(8,128)S(1)}, u32[]{:S(2)}, u32[]{:S(2)}) collective-permute-start(f32[3,32,128]{2,1,0:T(8,128)S(1)} %get-tuple-element.20.send_q), channel_id=1, source_target_pairs={{1,2},{3,4},{5,6},{7,8},{9,10},{11,12},{13,14},{15,16},{17,18},{19... | collective-permute-start | bytes 147464 | tf_op jit(solution)/shard_map/ppermute | solution.py:481
  14.6 1.9 %collective-permute-start.1 = (f32[3,32,128]{2,1,0:T(8,128)S(1)}, f32[3,32,128]{2,1,0:T(8,128)S(1)}, u32[]{:S(2)}, u32[]{:S(2)}) collective-permute-start(f32[3,32,128]{2,1,0:T(8,128)S(1)} %get-tuple-element.21._.send_p), channel_id=1, source_target_pairs={{0,1},{2,3},{4,5},{6,7},{8,9},{10,11},{12,13},{14,15},{16,17},{18,... | collective-permute-start | bytes 147464 | tf_op jit(solution)/shard_map/ppermute | solution.py:481
  16.5 0.0 copy-done.7
  16.5 0.1 copy.10.heating
  16.6 0.0 copy-done.4
  16.6 0.0 copy-start.2
  16.6 0.9 %copy-done.2 = f32[16,2048]{1,0:T(8,128)S(1)} copy-done((f32[16,2048]{1,0:T(8,128)S(1)}, f32[16,2048]{1,0:T(8,128)}, u32[]{:S(2)}) %copy-start.2) | copy-done | bytes 131096
  17.5 0.0 copy-start.5
  17.5 0.7 %copy-done.5 = s32[2048]{0:T(1024)S(1)} copy-done((s32[2048]{0:T(1024)S(1)}, s32[2048]{0:T(1024)}, u32[]{:S(2)}) %copy-start.5) | copy-done | bytes 8216
  18.2 0.0 copy-start.6
  18.2 0.7 %copy-done.6 = f32[16,16]{1,0:T(8,128)S(1)} copy-done((f32[16,16]{1,0:T(8,128)S(1)}, f32[16,16]{1,0:T(8,128)}, u32[]{:S(2)}) %copy-start.6) | copy-done | bytes 1048
  18.9 1.7 %shard_map.96 = (f32[5,16,1024]{2,1,0:T(8,128)S(1)}, s32[5,8,128]{2,1,0:T(8,128)S(1)}) custom-call(s32[16,128]{1,0:T(8,128)S(1)} %bitcast.3, s32[16,128]{1,0:T(8,128)S(1)} %bitcast.4, f32[16,2048]{1,0:T(8,128)S(1)} %copy-done.2, f32[16,16]{1,0:T(8,128)S(1)} %copy-done.6, f32[16,1]{1,0:T(8,128)S(1)} %copy.10.heating, f32[3,32,128]{2,1,0:T(8,128)S(1)} %get-tuple-element.21._.send_p), custom_call_target="tpu_custom_call" | custom-call | bytes 4194304 | tf_op jit(solution)/shard_map/pallas_call | solution.py:504
  20.7 0.0 collective-permute-done.recv_q
  20.7 0.0 collective-permute-done.1.recv_p
  20.7 0.0 copy-done.1
  20.7 0.0 copy-done
  20.7 0.8 %shard_map.97 = (f32[28,32,128]{2,1,0:T(8,128)S(1)}, f32[18,32,128]{2,1,0:T(8,128)S(1)}, f32[9,8,128]{2,1,0:T(8,128)S(1)}, f32[32,128]{1,0:T(8,128)S(1)}) custom-call(f32[5,16,32,128]{3,2,1,0:T(8,128)S(1)} %copy-done, f32[16,32,128]{2,1,0:T(8,128)S(1)} %copy-done.1, f32[3,32,128]{2,1,0:T(8,128)S(1)} %get-tuple-element.20.send_q, ...), custom_call_target="tpu_custom_call" | custom-call | bytes 2097152 | tf_op jit(solution)/shard_map/pallas_call | solution.py:518
  21.6 3.1 %collective-permute-start.3 = (f32[18,32,128]{2,1,0:T(8,128)S(1)}, f32[18,32,128]{2,1,0:T(8,128)S(1)}, u32[]{:S(2)}, u32[]{:S(2)}) collective-permute-start(f32[18,32,128]{2,1,0:T(8,128)S(1)} %get-tuple-element.25), channel_id=1, source_target_pairs={{0,64},{128,192},{256,320},{384,448},{64,0},{192,128},{320,256},{4... | collective-permute-start | bytes 884744 | tf_op jit(solution)/shard_map/ppermute | solution.py:481
  24.6 8.5 %collective-permute-start.2 = (f32[9,8,128]{2,1,0:T(8,128)S(1)}, f32[9,8,128]{2,1,0:T(8,128)S(1)}, u32[]{:S(2)}, u32[]{:S(2)}) collective-permute-start(f32[9,8,128]{2,1,0:T(8,128)S(1)} %get-tuple-element.24), channel_id=1, source_target_pairs={{64,128},{192,256},{320,384},{128,64},{256,192},{384,320},{65,129}... | collective-permute-start | bytes 110600 | tf_op jit(solution)/shard_map/ppermute | solution.py:481
  33.2 0.0 copy-done.3
  33.2 4.5 %shard_map.98 = (f32[5,4,32,128]{3,2,1,0:T(8,128)S(1)}, f32[5,4,32,128]{3,2,1,0:T(8,128)S(1)}, f32[5,10,32,128]{3,2,1,0:T(8,128)S(1)}) custom-call(f32[5,16,32,128]{3,2,1,0:T(8,128)S(1)} %copy-done, f32[16,32,128]{2,1,0:T(8,128)S(1)} %copy-done.1, f32[28,32,128]{2,1,0:T(8,128)S(1)} %get-tuple-element.23.strips, f32[5,5]{1,0:T(8,128)S(1)} %copy-done.3), custom_call_target="tpu_custom_call" | custom-call | bytes 12582912 | tf_op jit(solution)/shard_map/pallas_call | solution.py:528
  37.8 0.0 collective-permute-done.2.recv_wall
  37.8 0.0 collective-permute-done.3.recv_a
  37.8 1.0 %shard_map.100.wall = f32[16,128]{1,0:T(8,128)S(1)} custom-call(f32[5,16,32,128]{3,2,1,0:T(8,128)S(1)} %copy-done, f32[16,32,128]{2,1,0:T(8,128)S(1)} %copy-done.1, f32[28,32,128]{2,1,0:T(8,128)S(1)} %get-tuple-element.23.strips, f32[9,8,128]{2,1,0:T(8,128)S(1)} %collective-permute-done.2.recv_wall, f32[18,32,128]{2,1,0:T(8,128)S(1)} %collective-permute-done.3.recv_a, ...), custom_call_target="tpu_custom_call" | custom-call | bytes 4194304 | tf_op jit(solution)/shard_map/pallas_call | solution.py:545
  38.8 4.5 %collective-permute-start.4 = (f32[16,128]{1,0:T(8,128)S(1)}, f32[16,128]{1,0:T(8,128)S(1)}, u32[]{:S(2)}, u32[]{:S(2)}) collective-permute-start(f32[16,128]{1,0:T(8,128)S(1)} %shard_map.100.wall), channel_id=1, source_target_pairs={{0,64},{64,128},{128,192},{192,256},{256,320},{320,384},{384,448},... | collective-permute-start | bytes 24584 | tf_op jit(solution)/shard_map/ppermute | solution.py:557
  43.4 3.9 %collective-permute-start.6 = (f32[63,8,128]{2,1,0:T(8,128)S(1)}, f32[63,8,128]{2,1,0:T(8,128)S(1)}, u32[]{:S(2)}, u32[]{:S(2)}) collective-permute-start(f32[63,8,128]{2,1,0:T(8,128)S(1)} %shard_map.99._), channel_id=1, source_target_pairs={{64,128},{192,256},{320,384},{128,64},{256,192},{384,320},{65,129}... | collective-permute-start | bytes 774152 | tf_op jit(solution)/shard_map/ppermute | solution.py:481
  47.3 0.0 collective-permute-done.4.earlier
  47.3 0.2 shard_map.101
  47.5 5.6 %collective-permute-start.5 = (f32[16,1024]{1,0:T(8,128)S(1)}, f32[16,1024]{1,0:T(8,128)S(1)}, u32[]{:S(2)}, u32[]{:S(2)}) collective-permute-start(f32[16,1024]{1,0:T(8,128)S(1)} %get-tuple-element.31), channel_id=1, source_target_pairs={{1,2},{3,4},{5,6},{7,8},{9,10},{11,12},{13,14},{15,16},{17,18},{19... | collective-permute-start | bytes 196616 | tf_op jit(solution)/shard_map/ppermute | solution.py:481
  53.1 1.9 %collective-permute-start.7 = (f32[16,1024]{1,0:T(8,128)S(1)}, f32[16,1024]{1,0:T(8,128)S(1)}, u32[]{:S(2)}, u32[]{:S(2)}) collective-permute-start(f32[16,1024]{1,0:T(8,128)S(1)} %get-tuple-element.34), channel_id=1, source_target_pairs={{0,2},{1,3},{4,6},{5,7},{8,10},{9,11},{12,14},{13,15},{16,18},{17,... | collective-permute-start | bytes 196616 | tf_op jit(solution)/shard_map/ppermute | solution.py:481
  55.0 3.1 %collective-permute-start.8 = (f32[16,1024]{1,0:T(8,128)S(1)}, f32[16,1024]{1,0:T(8,128)S(1)}, u32[]{:S(2)}, u32[]{:S(2)}) collective-permute-start(f32[16,1024]{1,0:T(8,128)S(1)} %get-tuple-element.35), channel_id=1, source_target_pairs={{2,4},{3,5},{6,8},{7,9},{10,12},{11,13},{14,16},{15,17},{18,20},{1... | collective-permute-start | bytes 196616 | tf_op jit(solution)/shard_map/ppermute | solution.py:481
  58.1 4.8 %collective-permute-start.9 = (f32[16,1024]{1,0:T(8,128)S(1)}, f32[16,1024]{1,0:T(8,128)S(1)}, u32[]{:S(2)}, u32[]{:S(2)}) collective-permute-start(f32[16,1024]{1,0:T(8,128)S(1)} %get-tuple-element.36), channel_id=1, source_target_pairs={{0,1},{2,3},{4,5},{6,7},{8,9},{10,11},{12,13},{14,15},{16,17},{18,... | collective-permute-start | bytes 196616 | tf_op jit(solution)/shard_map/ppermute | solution.py:481
  62.9 0.0 collective-permute-done.6.recv_rest
  62.9 0.0 collective-permute-done.5._.recv_q
  62.9 3.4 %shard_map.102 = (f32[5,16,32,128]{3,2,1,0:T(8,128)}, f32[8,128]{1,0:T(8,128)S(1)}) custom-call(f32[16,1024]{1,0:T(8,128)S(1)} %collective-permute-done.5._.recv_q, f32[5,16,32,128]{3,2,1,0:T(8,128)S(1)} %copy-done, f32[16,32,128]{2,1,0:T(8,128)S(1)} %copy-done.1, f32[28,32,128]{2,1,0:T(8,128)S(1)} %get-tuple-element.23.strips, ...), custom_call_target="tpu_custom_call" | custom-call | bytes 8388608 | tf_op jit(solution)/shard_map/pallas_call | solution.py:569
  66.4 0.0 collective-permute-done.7.recv_r
  66.4 0.6 collective-permute-done.8.recv_s
  67.0 0.0 collective-permute-done.9.recv_p
  67.0 0.8 %shard_map.103 = f32[16,5120]{1,0:T(8,128)} custom-call(f32[16,1024]{1,0:T(8,128)S(1)} %get-tuple-element.33.own, f32[16,1024]{1,0:T(8,128)S(1)} %collective-permute-done.5._.recv_q, f32[16,1024]{1,0:T(8,128)S(1)} %collective-permute-done.7.recv_r, f32[16,1024]{1,0:T(8,128)S(1)} %collective-permute-done.8.recv_s, ...), custom_call_target="tpu_custom_call" | custom-call | bytes 1048576 | tf_op jit(solution)/shard_map/pallas_call | solution.py:581
  (1 shorter events, 0.0 us)
Async XLA Ops:
  0.6 20.1 %copy-start.1 = (f32[16,32,128]{2,1,0:T(8,128)S(1)}, f32[16,32,128]{2,1,0:T(8,128)}, u32[]{:S(2)}) copy-start(f32[16,32,128]{2,1,0:T(8,128)} %kappa.11) | copy-start | bytes 786436
  0.6 20.1 %copy-start = (f32[5,16,32,128]{3,2,1,0:T(8,128)S(1)}, f32[5,16,32,128]{3,2,1,0:T(8,128)}, u32[]{:S(2)}) copy-start(f32[5,16,32,128]{3,2,1,0:T(8,128)} %gas.11) | copy-start | bytes 3932164
  0.7 15.9 %copy-start.7 = (f32[16]{0:T(128)S(1)}, f32[16]{0:T(128)}, u32[]{:S(2)}) copy-start(f32[16]{0:T(128)} %param.13) | copy-start | bytes 196
  0.7 16.0 %copy-start.4 = (s32[2048,1]{0,1:T(1,128)S(1)}, s32[2048,1]{0,1:T(1,128)}, u32[]{:S(2)}) copy-start(s32[2048,1]{0,1:T(1,128)} %param.15) | copy-start | bytes 24580
  2.9 30.3 %copy-start.3 = (f32[5,5]{1,0:T(8,128)S(1)}, f32[5,5]{1,0:T(8,128)}, u32[]{:S(2)}) copy-start(f32[5,5]{1,0:T(8,128)} %reaction.5) | copy-start | bytes 304
  2.9 17.8 %collective-permute-start = (f32[3,32,128]{2,1,0:T(8,128)S(1)}, f32[3,32,128]{2,1,0:T(8,128)S(1)}, u32[]{:S(2)}, u32[]{:S(2)}) collective-permute-start(f32[3,32,128]{2,1,0:T(8,128)S(1)} %get-tuple-element.20.send_q), channel_id=1, source_target_pairs={{1,2},{3,4},{5,6},{7,8},{9,10},{11,12},{13,14},{15,16},{17,18},{19... | collective-permute-start | bytes 147464 | tf_op jit(solution)/shard_map/ppermute | solution.py:481
  14.6 6.1 %collective-permute-start.1 = (f32[3,32,128]{2,1,0:T(8,128)S(1)}, f32[3,32,128]{2,1,0:T(8,128)S(1)}, u32[]{:S(2)}, u32[]{:S(2)}) collective-permute-start(f32[3,32,128]{2,1,0:T(8,128)S(1)} %get-tuple-element.21._.send_p), channel_id=1, source_target_pairs={{0,1},{2,3},{4,5},{6,7},{8,9},{10,11},{12,13},{14,15},{16,17},{18,... | collective-permute-start | bytes 147464 | tf_op jit(solution)/shard_map/ppermute | solution.py:481
  16.6 0.9 %copy-start.2 = (f32[16,2048]{1,0:T(8,128)S(1)}, f32[16,2048]{1,0:T(8,128)}, u32[]{:S(2)}) copy-start(f32[16,2048]{1,0:T(8,128)} %particles.1) | copy-start | bytes 393220
  17.5 0.7 %copy-start.5 = (s32[2048]{0:T(1024)S(1)}, s32[2048]{0:T(1024)}, u32[]{:S(2)}) copy-start(s32[2048]{0:T(1024)} %param.14) | copy-start | bytes 24580
  18.2 0.7 %copy-start.6 = (f32[16,16]{1,0:T(8,128)S(1)}, f32[16,16]{1,0:T(8,128)}, u32[]{:S(2)}) copy-start(f32[16,16]{1,0:T(8,128)} %mixing.1) | copy-start | bytes 3076
  21.6 16.2 %collective-permute-start.3 = (f32[18,32,128]{2,1,0:T(8,128)S(1)}, f32[18,32,128]{2,1,0:T(8,128)S(1)}, u32[]{:S(2)}, u32[]{:S(2)}) collective-permute-start(f32[18,32,128]{2,1,0:T(8,128)S(1)} %get-tuple-element.25), channel_id=1, source_target_pairs={{0,64},{128,192},{256,320},{384,448},{64,0},{192,128},{320,256},{4... | collective-permute-start | bytes 884744 | tf_op jit(solution)/shard_map/ppermute | solution.py:481
  24.6 13.1 %collective-permute-start.2 = (f32[9,8,128]{2,1,0:T(8,128)S(1)}, f32[9,8,128]{2,1,0:T(8,128)S(1)}, u32[]{:S(2)}, u32[]{:S(2)}) collective-permute-start(f32[9,8,128]{2,1,0:T(8,128)S(1)} %get-tuple-element.24), channel_id=1, source_target_pairs={{64,128},{192,256},{320,384},{128,64},{256,192},{384,320},{65,129}... | collective-permute-start | bytes 110600 | tf_op jit(solution)/shard_map/ppermute | solution.py:481
  38.8 8.4 %collective-permute-start.4 = (f32[16,128]{1,0:T(8,128)S(1)}, f32[16,128]{1,0:T(8,128)S(1)}, u32[]{:S(2)}, u32[]{:S(2)}) collective-permute-start(f32[16,128]{1,0:T(8,128)S(1)} %shard_map.100.wall), channel_id=1, source_target_pairs={{0,64},{64,128},{128,192},{192,256},{256,320},{320,384},{384,448},... | collective-permute-start | bytes 24584 | tf_op jit(solution)/shard_map/ppermute | solution.py:557
  43.4 19.6 %collective-permute-start.6 = (f32[63,8,128]{2,1,0:T(8,128)S(1)}, f32[63,8,128]{2,1,0:T(8,128)S(1)}, u32[]{:S(2)}, u32[]{:S(2)}) collective-permute-start(f32[63,8,128]{2,1,0:T(8,128)S(1)} %shard_map.99._), channel_id=1, source_target_pairs={{64,128},{192,256},{320,384},{128,64},{256,192},{384,320},{65,129}... | collective-permute-start | bytes 774152 | tf_op jit(solution)/shard_map/ppermute | solution.py:481
  47.5 15.5 %collective-permute-start.5 = (f32[16,1024]{1,0:T(8,128)S(1)}, f32[16,1024]{1,0:T(8,128)S(1)}, u32[]{:S(2)}, u32[]{:S(2)}) collective-permute-start(f32[16,1024]{1,0:T(8,128)S(1)} %get-tuple-element.31), channel_id=1, source_target_pairs={{1,2},{3,4},{5,6},{7,8},{9,10},{11,12},{13,14},{15,16},{17,18},{19... | collective-permute-start | bytes 196616 | tf_op jit(solution)/shard_map/ppermute | solution.py:481
  53.1 13.3 %collective-permute-start.7 = (f32[16,1024]{1,0:T(8,128)S(1)}, f32[16,1024]{1,0:T(8,128)S(1)}, u32[]{:S(2)}, u32[]{:S(2)}) collective-permute-start(f32[16,1024]{1,0:T(8,128)S(1)} %get-tuple-element.34), channel_id=1, source_target_pairs={{0,2},{1,3},{4,6},{5,7},{8,10},{9,11},{12,14},{13,15},{16,18},{17,... | collective-permute-start | bytes 196616 | tf_op jit(solution)/shard_map/ppermute | solution.py:481
  55.0 12.0 %collective-permute-start.8 = (f32[16,1024]{1,0:T(8,128)S(1)}, f32[16,1024]{1,0:T(8,128)S(1)}, u32[]{:S(2)}, u32[]{:S(2)}) collective-permute-start(f32[16,1024]{1,0:T(8,128)S(1)} %get-tuple-element.35), channel_id=1, source_target_pairs={{2,4},{3,5},{6,8},{7,9},{10,12},{11,13},{14,16},{15,17},{18,20},{1... | collective-permute-start | bytes 196616 | tf_op jit(solution)/shard_map/ppermute | solution.py:481
  58.1 8.9 %collective-permute-start.9 = (f32[16,1024]{1,0:T(8,128)S(1)}, f32[16,1024]{1,0:T(8,128)S(1)}, u32[]{:S(2)}, u32[]{:S(2)}) collective-permute-start(f32[16,1024]{1,0:T(8,128)S(1)} %get-tuple-element.36), channel_id=1, source_target_pairs={{0,1},{2,3},{4,5},{6,7},{8,9},{10,11},{12,13},{14,15},{16,17},{18,... | collective-permute-start | bytes 196616 | tf_op jit(solution)/shard_map/ppermute | solution.py:481
